TPU v7x, 32 devices: a whole 2x2x4 slice. The times are simulated.
32 devices in a mesh: seq: 8 (over z, y), mp: 4 (over x, core).
Axes of the slice: x: 2, y: 2, z: 4, core: 2. Of those that a mesh axis runs over, the one named last changes fastest.
Arguments:
- scored_token_targets: int32 [2048], P('seq'), may hold values from 0 to 15999
- valid: int32 [2048], P('seq'), may hold values 0 or 1
- lengths: int32 [48], replicated, may hold values from 1 to 256, 2048 in all
- owners: int32 [48], replicated, may hold values from 0 to 7
- holders: int32 [48], replicated, may hold values from -1 to 7, as said below
- mixer_input_x: bfloat16 [2, 2048, 3584], P(None, 'seq', 'mp'), may hold values from -6 to 6
- mixer_gate_input: bfloat16 [2, 2048, 3584], P(None, 'seq', 'mp'), may hold values from -6 to 6
- input_projection_b: bfloat16 [2, 2048, 64], P(None, 'seq'), may hold values from -2.390625 to 2.390625
- output_projection_c: bfloat16 [2, 2048, 64], P(None, 'seq'), may hold values from -2.390625 to 2.390625
- token_step_sizes: float32 [2, 2048, 56], P(None, 'seq', 'mp'), may hold values from 0.01 to 0.3
- head_decay_rate: float32 [2, 56], P(None, 'mp'), may hold values from 0.0002 to 1
- head_skip_scale: float32 [2, 56], P(None, 'mp'), may hold values from 0.5 to 1.5
- prompt_held_states: bfloat16 [2, 8, 56, 64, 64], P(None, 'seq', 'mp'), may hold values from -6 to 6
- shared_output_weight: bfloat16 [3584, 3584], P('mp'), may hold values from -0.09375 to 0.09375
- adapter_down_weight: bfloat16 [3584, 128], P('mp'), may hold values from -0.09375 to 0.09375
- adapter_up_weight: bfloat16 [128, 3584], replicated, may hold values from -0.5 to 0.5
- residual: bfloat16 [2048, 2, 3584], P('seq'), may hold values from -16 to 16
- final_norm_scale: float32 [3584], replicated, may hold values from 0.5 to 1.5
- vocab_head_weight: bfloat16 [3584, 16000], P('seq', 'mp'), may hold values from -8 to 8
Outputs:
- owner_sums: float32 [8, 48], P('seq')
- token_delta: float32 [2048], P('seq')
Inputs may be any that keep to these rules, and one draw needn't show every extreme that they name: `holders`: exactly 24 rollouts continue a prompt state; the others start from zeros.
All inputs are finite; a program needn't handle non-finite values. No bound on the sum of `valid` on one device may be relied on, other than what follows from the above.
Results may differ from a plain program's by a relative error of at most 0.035.
Values may be sent and summed in bfloat16 or wider, within the bound.
No kernel may reach another device: no remote copies, remote signals or barrier semaphores. Data moves between devices by JAX's collectives and lax.ppermute only.
A program may use at most 128 MiB of HBM per device.

v0:
```python
import jax
import jax.numpy as jnp
from jax import lax
from jax.sharding import PartitionSpec as P

highest = lax.Precision.HIGHEST


def shifted(x, axis, by):
    count = lax.axis_size(axis)
    pairs = [(i, i + by) for i in range(count) if 0 <= i + by < count]
    return lax.ppermute(x, axis, pairs)


def root_norm(hidden, final_norm_scale):
    mean_sq = jnp.mean(hidden * hidden, axis=-1, keepdims=True)
    return (hidden * lax.rsqrt(mean_sq + 1e-05) * final_norm_scale).astype(jnp.bfloat16)


def shards(
    scored_token_targets,
    valid,
    lengths,
    owners,
    holders,
    mixer_input_x,
    mixer_gate_input,
    input_projection_b,
    output_projection_c,
    token_step_sizes,
    head_decay_rate,
    head_skip_scale,
    prompt_held_states,
    shared_output_weight,
    adapter_down_weight,
    adapter_up_weight,
    residual,
    final_norm_scale,
    vocab_head_weight,
):
    seq_count = lax.axis_size("seq")
    mp_count = lax.axis_size("mp")
    tok_rows = scored_token_targets.shape[0]
    models = mixer_input_x.shape[0]
    inner_local = mixer_input_x.shape[2]
    head_count = token_step_sizes.shape[2]
    head_dim = inner_local // head_count
    state_dim = input_projection_b.shape[2]
    roll_count = lengths.shape[0]
    first_row = lax.axis_index("seq") * tok_rows
    offsets = jnp.arange(tok_rows, dtype=jnp.int32)
    position = first_row + offsets
    starts = jnp.cumsum(lengths) - lengths
    rollout = jnp.sum((starts[None, :] <= position[:, None]).astype(jnp.int32), axis=1) - 1
    member_table = rollout[:, None] == jnp.arange(roll_count, dtype=jnp.int32)[None, :]
    start_local = jnp.sum(jnp.where(member_table, starts[None, :], 0), axis=1) - first_row
    holder_tok = jnp.sum(jnp.where(member_table, holders[None, :], 0), axis=1)
    borrowed = (start_local >= 0) & (holder_tok >= 0)
    prompt_pick = (
        (holder_tok[:, None] == jnp.arange(seq_count, dtype=jnp.int32)[None, :]) & borrowed[:, None]
    ).astype(jnp.float32)
    neg_rates = -head_decay_rate
    log_decay = jnp.cumsum(token_step_sizes * neg_rates[:, None, :], axis=1)
    before = jnp.take(log_decay, jnp.maximum(start_local - 1, 0), axis=1)
    before = jnp.where((start_local >= 1)[None, :, None], before, 0.0)
    x_values = mixer_input_x.astype(jnp.float32).reshape(models, tok_rows, head_count, head_dim)
    b_values = input_projection_b.astype(jnp.float32)
    c_values = output_projection_c.astype(jnp.float32)
    gram_matrix = jnp.einsum(
        "mtn,msn->mts", output_projection_c, input_projection_b, preferred_element_type=jnp.float32
    )
    causal = (rollout[:, None] == rollout[None, :]) & (offsets[None, :] <= offsets[:, None])
    log_gap = log_decay[:, :, None, :] - log_decay[:, None, :, :]
    mixing = jnp.where(
        causal[None, :, :, None], jnp.exp(jnp.where(causal[None, :, :, None], log_gap, 0.0)), 0.0
    )
    mixing = mixing * gram_matrix[..., None] * token_step_sizes[:, None, :, :]
    intra_out = jnp.einsum("mtsh,mshp->mthp", mixing, x_values, precision=highest)
    last_pick = prompt_pick[tok_rows - 1]
    zeros_state = jnp.zeros((models, head_count, head_dim, state_dim), jnp.float32)
    piece = lax.all_gather(prompt_held_states, "seq", axis=1, tiled=True)
    last_weight = last_pick.astype(jnp.bfloat16)
    picked = (prompt_pick[None, :, :, None] * c_values[:, :, None, :]).astype(jnp.bfloat16)
    projected = jnp.einsum("mtjn,mjhpn->mthp", picked, piece, preferred_element_type=jnp.float32)
    end_states = jnp.einsum("j,mjhpn->mhpn", last_weight, piece, preferred_element_type=jnp.float32)
    entry_decay = jnp.exp(log_decay - before)
    final_log = log_decay[:, tok_rows - 1, :]
    tail_mask = (rollout == rollout[tok_rows - 1]).astype(jnp.float32)
    end_weight = (
        jnp.exp(final_log[:, None, :] - log_decay) * token_step_sizes * tail_mask[None, :, None]
    )
    local_end = jnp.einsum("msh,mshp,msn->mhpn", end_weight, x_values, b_values, precision=highest)
    local_end = (
        local_end + jnp.exp(final_log - before[:, tok_rows - 1, :])[:, :, None, None] * end_states
    )
    carry_through = jnp.where(start_local[tok_rows - 1] < 0, jnp.exp(final_log), 0.0)

    def relay_step(step_index, incoming):
        outgoing = carry_through[:, :, None, None] * incoming + local_end
        return shifted(outgoing, "seq", 1)

    arriving = lax.fori_loop(0, seq_count - 1, relay_step, zeros_state)
    inherited = (start_local < 0).astype(jnp.float32)
    carried = jnp.einsum("mhpn,mtn->mthp", arriving, c_values, precision=highest)
    carried = carried * (jnp.exp(log_decay) * inherited[None, :, None])[..., None]
    output = (
        intra_out
        + carried
        + entry_decay[..., None] * projected
        + head_skip_scale[:, None, :, None] * x_values
    )
    output = output.reshape(models, tok_rows, inner_local)
    gated_output = (output * jax.nn.silu(mixer_gate_input.astype(jnp.float32))).astype(jnp.bfloat16)
    share_rows = tok_rows // mp_count
    base_output = jnp.einsum(
        "mti,id->tmd", gated_output, shared_output_weight, preferred_element_type=jnp.float32
    )
    low_rank_rows = jnp.dot(
        gated_output[0], adapter_down_weight, preferred_element_type=jnp.float32
    ).astype(jnp.bfloat16)
    adapter_output = jnp.dot(low_rank_rows, adapter_up_weight, preferred_element_type=jnp.float32)
    mixed = lax.psum_scatter(
        jnp.stack([base_output[:, 0] + adapter_output, base_output[:, 1]], axis=1).astype(
            jnp.bfloat16
        ),
        "mp",
        scatter_dimension=0,
        tiled=True,
    ).astype(jnp.float32)
    own_rows = lax.dynamic_slice_in_dim(residual, lax.axis_index("mp") * share_rows, share_rows, 0)
    normed_own = root_norm(own_rows.astype(jnp.float32) + mixed, final_norm_scale)
    normed = lax.all_gather(normed_own, "mp", axis=0, tiled=True)
    vocab_local = vocab_head_weight.shape[1]
    logits = jnp.einsum(
        "tmk,kv->mtv",
        normed,
        lax.all_gather(vocab_head_weight, "seq", axis=0, tiled=True),
        preferred_element_type=jnp.float32,
    )
    vocab_first = lax.axis_index("mp") * vocab_local
    target_hit = (
        scored_token_targets[:, None]
        == vocab_first + jnp.arange(vocab_local, dtype=jnp.int32)[None, :]
    )
    target_local = jnp.sum(jnp.where(target_hit[None], logits, 0.0), axis=2)
    local_max = jnp.max(logits, axis=2)
    vocab_top = lax.pmax(local_max, "mp")
    exp_sums = jnp.sum(jnp.exp(logits - vocab_top[..., None]), axis=2)
    vocab_total, target_logit = lax.psum((exp_sums, target_local), "mp")
    logprob = target_logit - vocab_top - jnp.log(vocab_total)
    token_delta = (logprob[0] - logprob[1]) * valid.astype(jnp.float32)
    roll_sums = jnp.dot(
        token_delta, member_table.astype(jnp.float32), precision=highest
    ) / lengths.astype(jnp.float32)
    owner_rows = (owners[None, :] == jnp.arange(seq_count, dtype=jnp.int32)[:, None]).astype(
        jnp.float32
    ) * roll_sums[None, :]
    owner_sums = lax.psum_scatter(owner_rows, "seq", scatter_dimension=0, tiled=True)
    return (owner_sums, token_delta)


def solution(mesh):
    placed = (
        P("seq"),
        P("seq"),
        P(),
        P(),
        P(),
        P(None, "seq", "mp"),
        P(None, "seq", "mp"),
        P(None, "seq", None),
        P(None, "seq", None),
        P(None, "seq", "mp"),
        P(None, "mp"),
        P(None, "mp"),
        P(None, "seq", "mp", None, None),
        P("mp", None),
        P("mp", None),
        P(),
        P("seq", None, None),
        P(),
        P("seq", "mp"),
    )
    return jax.shard_map(
        shards, mesh=mesh, in_specs=placed, out_specs=(P("seq", None), P("seq")), check_vma=False
    )
```

profile of v0, /device:TPU:0, one launch (start us, length us, event | category | flops | bytes accessed | tf_op | source)
XLA Modules:
  0.0 989.0 jit_solution(14702583418642034165)
XLA Ops:
  7.2 0.7 all-gather.4.cloned.1.call-update
  8.0 0.7 neg.7
  8.8 0.8 multiply_bitcast_fusion
  9.7 1.2 reduce-window.20
  11.4 0.6 copy.116
  12.0 1.3 copy.118
  13.4 0.7 copy.112
  14.3 0.7 sub.84
  15.7 0.7 select_reduce_fusion.1
  16.4 0.6 compare_convert_fusion
  17.7 1.0 gather_fusion
  19.0 0.8 subtract_exponential_fusion
  20.6 1.5 copy.119
  22.1 0.6 copy.127
  22.8 0.6 copy.128
  24.8 0.7 fusion.42
  25.8 54.0 %all-gather.4.cloned.1.call-done = bf16[2,8,14,64,64]{4,3,1,2,0:T(8,128)(2,1)} async-done(((bf16[2,1,14,64,64]{4,3,1,2,0:T(8,128)(2,1)}), bf16[2,8,14,64,64]{4,3,1,2,0:T(8,128)(2,1)}) %all-gather.4.cloned.1.call-update) | async-done | bytes 1835024 | tf_op jit(solution)/shard_map/all_gather | solution.py:81
  79.8 4.5 fusion.15
  84.3 1.1 fusion.34
  85.4 151.1 %while.10 = (s32[]{:T(128)}, f32[2,14,64,64]{3,2,1,0:T(8,128)S(1)}, f32[2,14]{1,0:T(2,128)S(1)}, f32[2,14,64,64]{3,2,1,0:T(8,128)S(1)}, s32[]{:T(128)}) while((s32[]{:T(128)}, f32[2,14,64,64]{3,2,1,0:T(8,128)S(1)}, f32[2,14]{1,0:T(2,128)S(1)}, f32[2,14,64,64]{3,2,1,0:T(8,128)S(1)}, s32[]{:T(128)}) %tuple.33), condition=%wide.region_7.8_spmd, body=%wide.region_6.7_spmd.sunk | while | flops 229378 | bytes 3211477 | solution.py:102
  85.5 1.1 multiply_add_fusion.2
  86.5 2.5 collective-permute-start
  89.1 18.8 %collective-permute-done = f32[2,14,64,64]{3,2,1,0:T(8,128)S(1)} collective-permute-done((f32[2,14,64,64]{3,2,1,0:T(8,128)}, f32[2,14,64,64]{3,2,1,0:T(8,128)S(1)}, u32[]{:S(2)}, u32[]{:S(2)}) %collective-permute-start) | collective-permute-done | bytes 458784 | tf_op jit(solution)/shard_map/while/body/eval_jaxpr/ppermute | solution.py:12
  107.9 1.1 multiply_add_fusion.2
  109.0 4.3 collective-permute-start
  113.3 17.9 %collective-permute-done = f32[2,14,64,64]{3,2,1,0:T(8,128)S(1)} collective-permute-done((f32[2,14,64,64]{3,2,1,0:T(8,128)}, f32[2,14,64,64]{3,2,1,0:T(8,128)S(1)}, u32[]{:S(2)}, u32[]{:S(2)}) %collective-permute-start) | collective-permute-done | bytes 458784 | tf_op jit(solution)/shard_map/while/body/eval_jaxpr/ppermute | solution.py:12
  131.2 1.1 multiply_add_fusion.2
  132.3 4.3 collective-permute-start
  136.7 17.0 %collective-permute-done = f32[2,14,64,64]{3,2,1,0:T(8,128)S(1)} collective-permute-done((f32[2,14,64,64]{3,2,1,0:T(8,128)}, f32[2,14,64,64]{3,2,1,0:T(8,128)S(1)}, u32[]{:S(2)}, u32[]{:S(2)}) %collective-permute-start) | collective-permute-done | bytes 458784 | tf_op jit(solution)/shard_map/while/body/eval_jaxpr/ppermute | solution.py:12
  153.7 1.1 multiply_add_fusion.2
  154.7 4.9 collective-permute-start
  159.7 15.8 %collective-permute-done = f32[2,14,64,64]{3,2,1,0:T(8,128)S(1)} collective-permute-done((f32[2,14,64,64]{3,2,1,0:T(8,128)}, f32[2,14,64,64]{3,2,1,0:T(8,128)S(1)}, u32[]{:S(2)}, u32[]{:S(2)}) %collective-permute-start) | collective-permute-done | bytes 458784 | tf_op jit(solution)/shard_map/while/body/eval_jaxpr/ppermute | solution.py:12
  175.4 1.1 multiply_add_fusion.2
  176.5 5.2 collective-permute-start
  181.8 14.8 %collective-permute-done = f32[2,14,64,64]{3,2,1,0:T(8,128)S(1)} collective-permute-done((f32[2,14,64,64]{3,2,1,0:T(8,128)}, f32[2,14,64,64]{3,2,1,0:T(8,128)S(1)}, u32[]{:S(2)}, u32[]{:S(2)}) %collective-permute-start) | collective-permute-done | bytes 458784 | tf_op jit(solution)/shard_map/while/body/eval_jaxpr/ppermute | solution.py:12
  196.6 1.1 multiply_add_fusion.2
  197.7 5.2 collective-permute-start
  202.9 14.2 %collective-permute-done = f32[2,14,64,64]{3,2,1,0:T(8,128)S(1)} collective-permute-done((f32[2,14,64,64]{3,2,1,0:T(8,128)}, f32[2,14,64,64]{3,2,1,0:T(8,128)S(1)}, u32[]{:S(2)}, u32[]{:S(2)}) %collective-permute-start) | collective-permute-done | bytes 458784 | tf_op jit(solution)/shard_map/while/body/eval_jaxpr/ppermute | solution.py:12
  217.1 1.1 multiply_add_fusion.2
  218.2 4.9 collective-permute-start
  223.2 13.3 %collective-permute-done = f32[2,14,64,64]{3,2,1,0:T(8,128)S(1)} collective-permute-done((f32[2,14,64,64]{3,2,1,0:T(8,128)}, f32[2,14,64,64]{3,2,1,0:T(8,128)S(1)}, u32[]{:S(2)}, u32[]{:S(2)}) %collective-permute-start) | collective-permute-done | bytes 458784 | tf_op jit(solution)/shard_map/while/body/eval_jaxpr/ppermute | solution.py:12
  236.5 0.9 fusion.43
  237.5 3.1 fusion.38
  240.7 7.2 fusion.24
  247.9 1.8 copy.129
  249.7 1.8 fusion.31
  251.5 6.4 convolution_bitcast_fusion
  257.9 3.0 copy-done.2
  261.1 0.7 copy-done.8
  261.8 4.4 fusion.14
  266.2 3.6 pad_maximum_fusion
  269.9 1.8 constant_dynamic-slice_fusion.1
  271.7 52.3 %reduce-scatter.2.cloned.1.call-done = bf16[64,2,3584]{2,0,1:T(8,128)(2,1)} async-done(((bf16[256,2,3584]{2,0,1:T(8,128)(2,1)}), bf16[64,2,3584]{2,0,1:T(8,128)(2,1)}) %reduce-scatter.2.cloned.1.call-update) | async-done | bytes 917520 | tf_op jit(solution)/shard_map/reduce_scatter | solution.py:122
  324.0 1.5 multiply_reduce_fusion
  325.5 2.5 multiply_convert_fusion
  329.2 1.8 broadcast_compare_fusion
  331.0 28.7 %all-gather.6.cloned.1.call-done = bf16[256,2,3584]{2,0,1:T(8,128)(2,1)} async-done(((bf16[64,2,3584]{2,0,1:T(8,128)(2,1)}), bf16[256,2,3584]{2,0,1:T(8,128)(2,1)}) %all-gather.6.cloned.1.call-update) | async-done | bytes 3670032 | tf_op jit(solution)/shard_map/all_gather | solution.py:132
  359.7 560.6 %all-gather.8.cloned.1.call-done = bf16[3584,4000]{1,0:T(8,128)(2,1)} async-done(((bf16[448,4000]{1,0:T(8,128)(2,1)}), bf16[3584,4000]{1,0:T(8,128)(2,1)}) %all-gather.8.cloned.1.call-update) | async-done | bytes 28672016 | tf_op jit(solution)/shard_map/all_gather | solution.py:137
  920.3 23.4 %fusion.2 = (f32[2,256]{1,0:T(2,128)S(1)}, f32[2,256]{1,0:T(2,128)S(1)}, f32[256,2,4000]{0,2,1:T(8,128)}) fusion(pred[256,4000]{0,1:T(8,128)(4,1)S(1)} %broadcast_compare_fusion, bf16[256,2,3584]{2,0,1:T(8,128)(2,1)} %all-gather.6.cloned.1.call-done, bf16[3584,4000]{1,0:T(8,128)(2,1)} %all-gather.8.cloned.1.call-done), kind=kOutput, calls=%fused_computation.7 | convolution fusion | flops 14686208000 | bytes 41562112 | tf_op jit(solution)/shard_map/tmk,kv->mtv/dot_general | solution.py:134
  943.7 6.8 pmax.7
  950.6 4.5 fusion.4
  955.0 5.9 all-reduce.1
  961.2 20.3 %all-reduce = f32[8,48]{1,0:T(8,128)S(1)} all-reduce(f32[8,48]{1,0:T(8,128)S(1)} %fusion.49), channel_id=3, replica_groups=mesh['seq'=8,'mp'=4] {'seq'}, use_global_device_ids=true, to_apply=%region_16.17.clone | all-reduce | flops 384 | bytes 3072
  981.4 1.1 constant_dynamic-slice_fusion
  (95 shorter events, 6.2 us)
Async XLA Ops:
  7.2 253.9 %copy-start = (bf16[128,3584]{1,0:T(8,128)(2,1)S(1)}, bf16[128,3584]{1,0:T(8,128)(2,1)}, u32[]{:S(2)}) copy-start(bf16[128,3584]{1,0:T(8,128)(2,1)} %param.36) | copy-start | bytes 2752516
  7.2 16.2 %copy-start.6 = (bf16[2,256,64]{1,2,0:T(8,128)(2,1)S(1)}, bf16[2,256,64]{1,2,0:T(8,128)(2,1)}, u32[]{:S(2)}) copy-start(bf16[2,256,64]{1,2,0:T(8,128)(2,1)} %param.29) | copy-start | bytes 196612
  7.2 18.4 %copy-start.7 = (bf16[2,256,64]{1,2,0:T(8,128)(2,1)S(1)}, bf16[2,256,64]{1,2,0:T(8,128)(2,1)}, u32[]{:S(2)}) copy-start(bf16[2,256,64]{1,2,0:T(8,128)(2,1)} %param.28) | copy-start | bytes 196612
  7.2 72.6 %all-gather.4.cloned.1.call-start = ((), (), s32[]{:S(2)}) async-start(), calls=%async_computation.1 | async-start | bytes 4128768 | tf_op jit(solution)/shard_map/all_gather | solution.py:81
  7.9 316.0 %reduce-scatter.2.cloned.1.call-start = ((), (), s32[]{:S(2)}) async-start(), calls=%async_computation.2 | async-start | bytes 4587520 | tf_op jit(solution)/shard_map/reduce_scatter | solution.py:122
  22.1 63.2 %copy-start.3 = (bf16[2,256,896]{1,2,0:T(8,128)(2,1)}, bf16[2,256,896]{1,2,0:T(8,128)(2,1)S(1)}, u32[]{:S(2)}) copy-start(bf16[2,256,896]{1,2,0:T(8,128)(2,1)S(1)} %copy.119) | copy-start | bytes 2752516
  79.8 4.5 copy-start.9
  79.8 4.5 copy-start.16
  86.5 21.3 %collective-permute-start = (f32[2,14,64,64]{3,2,1,0:T(8,128)}, f32[2,14,64,64]{3,2,1,0:T(8,128)S(1)}, u32[]{:S(2)}, u32[]{:S(2)}) collective-permute-start(f32[2,14,64,64]{3,2,1,0:T(8,128)} %multiply_add_fusion.2), channel_id=1, source_target_pairs={{0,4},{4,8},{8,12},{12,16},{16,20},{20,24},{24,28},{1,5},{5,9},{9,... | collective-permute-start | bytes 1376264 | tf_op jit(solution)/shard_map/while/body/eval_jaxpr/ppermute | solution.py:12
  109.0 22.3 %collective-permute-start = (f32[2,14,64,64]{3,2,1,0:T(8,128)}, f32[2,14,64,64]{3,2,1,0:T(8,128)S(1)}, u32[]{:S(2)}, u32[]{:S(2)}) collective-permute-start(f32[2,14,64,64]{3,2,1,0:T(8,128)} %multiply_add_fusion.2), channel_id=1, source_target_pairs={{0,4},{4,8},{8,12},{12,16},{16,20},{20,24},{24,28},{1,5},{5,9},{9,... | collective-permute-start | bytes 1376264 | tf_op jit(solution)/shard_map/while/body/eval_jaxpr/ppermute | solution.py:12
  132.3 21.3 %collective-permute-start = (f32[2,14,64,64]{3,2,1,0:T(8,128)}, f32[2,14,64,64]{3,2,1,0:T(8,128)S(1)}, u32[]{:S(2)}, u32[]{:S(2)}) collective-permute-start(f32[2,14,64,64]{3,2,1,0:T(8,128)} %multiply_add_fusion.2), channel_id=1, source_target_pairs={{0,4},{4,8},{8,12},{12,16},{16,20},{20,24},{24,28},{1,5},{5,9},{9,... | collective-permute-start | bytes 1376264 | tf_op jit(solution)/shard_map/while/body/eval_jaxpr/ppermute | solution.py:12
  154.7 20.7 %collective-permute-start = (f32[2,14,64,64]{3,2,1,0:T(8,128)}, f32[2,14,64,64]{3,2,1,0:T(8,128)S(1)}, u32[]{:S(2)}, u32[]{:S(2)}) collective-permute-start(f32[2,14,64,64]{3,2,1,0:T(8,128)} %multiply_add_fusion.2), channel_id=1, source_target_pairs={{0,4},{4,8},{8,12},{12,16},{16,20},{20,24},{24,28},{1,5},{5,9},{9,... | collective-permute-start | bytes 1376264 | tf_op jit(solution)/shard_map/while/body/eval_jaxpr/ppermute | solution.py:12
  176.5 20.1 %collective-permute-start = (f32[2,14,64,64]{3,2,1,0:T(8,128)}, f32[2,14,64,64]{3,2,1,0:T(8,128)S(1)}, u32[]{:S(2)}, u32[]{:S(2)}) collective-permute-start(f32[2,14,64,64]{3,2,1,0:T(8,128)} %multiply_add_fusion.2), channel_id=1, source_target_pairs={{0,4},{4,8},{8,12},{12,16},{16,20},{20,24},{24,28},{1,5},{5,9},{9,... | collective-permute-start | bytes 1376264 | tf_op jit(solution)/shard_map/while/body/eval_jaxpr/ppermute | solution.py:12
  197.7 19.4 %collective-permute-start = (f32[2,14,64,64]{3,2,1,0:T(8,128)}, f32[2,14,64,64]{3,2,1,0:T(8,128)S(1)}, u32[]{:S(2)}, u32[]{:S(2)}) collective-permute-start(f32[2,14,64,64]{3,2,1,0:T(8,128)} %multiply_add_fusion.2), channel_id=1, source_target_pairs={{0,4},{4,8},{8,12},{12,16},{16,20},{20,24},{24,28},{1,5},{5,9},{9,... | collective-permute-start | bytes 1376264 | tf_op jit(solution)/shard_map/while/body/eval_jaxpr/ppermute | solution.py:12
  218.2 18.3 %collective-permute-start = (f32[2,14,64,64]{3,2,1,0:T(8,128)}, f32[2,14,64,64]{3,2,1,0:T(8,128)S(1)}, u32[]{:S(2)}, u32[]{:S(2)}) collective-permute-start(f32[2,14,64,64]{3,2,1,0:T(8,128)} %multiply_add_fusion.2), channel_id=1, source_target_pairs={{0,4},{4,8},{8,12},{12,16},{16,20},{20,24},{24,28},{1,5},{5,9},{9,... | collective-permute-start | bytes 1376264 | tf_op jit(solution)/shard_map/while/body/eval_jaxpr/ppermute | solution.py:12
  237.4 3.2 copy-start.4
  237.4 3.2 copy-start.10
  237.4 3.2 copy-start.11
  237.4 3.2 copy-start.12
  237.4 3.2 copy-start.13
  237.4 3.2 copy-start.14
  237.4 3.2 copy-start.22
  251.5 6.4 copy-start.5
  257.9 3.0 copy-start.2
  260.9 0.9 copy-start.8
  269.8 55.7 %copy-start.15 = (f32[3584]{0:T(1024)S(1)}, f32[3584]{0:T(1024)}, u32[]{:S(2)}) copy-start(f32[3584]{0:T(1024)} %param.38) | copy-start | bytes 43012
  269.8 89.8 %all-gather.6.cloned.1.call-start = ((), (), s32[]{:S(2)}) async-start(), calls=%async_computation.3 | async-start | bytes 4587520 | tf_op jit(solution)/shard_map/all_gather | solution.py:132
  325.5 3.1 copy-start.23
  325.5 3.7 copy-start.17
  328.0 592.3 %all-gather.8.cloned.1.call-start = ((), (), s32[]{:S(2)}) async-start(), calls=%async_computation.4 | async-start | bytes 33030144 | tf_op jit(solution)/shard_map/all_gather | solution.py:137
  950.5 32.0 %copy-start.1 = (bf16[128,3584]{1,0:T(8,128)(2,1)S(1)}, bf16[128,3584]{1,0:T(8,128)(2,1)}, u32[]{:S(2)}) copy-start(bf16[128,3584]{1,0:T(8,128)(2,1)} %param.36) | copy-start | bytes 2752516
  950.5 10.4 %copy-start.18 = (s32[256]{0:T(256)S(1)}, s32[256]{0:T(256)}, u32[]{:S(2)}) copy-start(s32[256]{0:T(256)} %param.22) | copy-start | bytes 3076
  950.5 10.5 %copy-start.20 = (s32[48]{0:T(128)S(1)}, s32[48]{0:T(128)}, u32[]{:S(2)}) copy-start(s32[48]{0:T(128)} %param.23) | copy-start | bytes 580
  950.6 10.6 %copy-start.21 = (s32[48]{0:T(128)S(1)}, s32[48]{0:T(128)}, u32[]{:S(2)}) copy-start(s32[48]{0:T(128)} %param.24) | copy-start | bytes 580
  961.0 21.5 %copy-start.19 = (f32[256]{0:T(256)}, f32[256]{0:T(256)S(1)}, u32[]{:S(2)}) copy-start(f32[256]{0:T(256)S(1)} %convert_multiply_fusion.6) | copy-start | bytes 3076
Sparse Core Ops, SparseCore 0:
  10.2 69.5 all-gather.3
  270.0 53.9 reduce-scatter.1
  328.1 31.5 all-gather.5
  361.1 559.0 all-gather.7
where the time goes:
time: 990 us; the launch traced here: 989 us
  waiting for transfers between devices  809 us (82%)
  matrix products  51.4 us (5%)
  blocking collectives  33 us (3%)
  starting transfers between devices  31.6 us (3%)
  other arithmetic  30.7 us (3%)
  local copies, waits for them, and re-layouts  18.8 us (2%)
  between operations  14.9 us (2%)
    all_gather x1, waiting for transfers between devices, shards(): lax.all_gather(vocab_head_weight, 'seq', axis=0, tiled=True)  561 us
    ppermute x7, waiting for transfers between devices, shifted(): return lax.ppermute(x, axis, pairs)  112 us
    all_gather x1, waiting for transfers between devices, shards(): piece = lax.all_gather(prompt_held_states, 'seq', axis=1, tiled=True)  54 us
    reduce_scatter x1, waiting for transfers between devices, shards(): lax.psum_scatter(jnp.stack([base_output[:, 0] + adapter_output, base_outp...  52.3 us
    ppermute x7, starting transfers between devices, shifted(): return lax.ppermute(x, axis, pairs)  31.5 us
    all_gather x1, waiting for transfers between devices, shards(): normed = lax.all_gather(normed_own, 'mp', axis=0, tiled=True)  28.7 us
    dot_general x1, matrix products, shards(): jnp.einsum('tmk,kv->mtv', normed, lax.all_gather(vocab_head_weight, 'seq'...  23.4 us
    unnamed x1, blocking collectives  20.3 us
  transfers between devices with their start and end apart: 11, of which 11 were waited for; matrix products, arithmetic and copies ran while one was open for 2% of the time, Pallas kernels for 0%

commit v1 on v0

v1 whole, which is shorter than its diff:
```python
import functools
import itertools

import jax
import jax.numpy as jnp
from jax import lax
from jax.experimental import pallas as pl
from jax.experimental.pallas import tpu as pltpu
from jax.sharding import PartitionSpec as P

highest = lax.Precision.HIGHEST
CHAIN = 4
SIDE = 2


def place_of(i):
    return (i // SIDE) % CHAIN


def turned(i, by):
    return i ^ (by * SIDE)


def partner(i, side, block, count):
    return ((i ^ side) + block * CHAIN * SIDE) % count


def turn(x, by):
    count = lax.axis_size("seq")
    return lax.ppermute(x, "seq", [(i, turned(i, by)) for i in range(count)])


def to_partner(x, side, block):
    count = lax.axis_size("seq")
    return lax.ppermute(x, "seq", [(i, partner(i, side, block, count)) for i in range(count)])


def chain_groups():
    count = lax.axis_size("seq")
    return [
        [first + k * SIDE for k in range(CHAIN)] for first in range(count) if place_of(first) == 0
    ]


def other_core(x):
    count = lax.axis_size("mp")
    return lax.ppermute(x, "mp", [(i, i ^ 1) for i in range(count)])


def along_x(x, by):
    count = lax.axis_size("mp")
    return lax.ppermute(x, "mp", [(i, (i + 2 * by) % count) for i in range(count)])


def tied(*values):
    return lax.optimization_barrier(values)


def dot(a, b, over=((1,), (0,))):
    return lax.dot_general(a, b, (over, ((), ())), preferred_element_type=jnp.float32)


def head_pairs(head_count, head_dim):
    return [
        (first, slice(first * head_dim, min(first + 2, head_count) * head_dim))
        for first in range(0, head_count, 2)
    ]


def pair_lanes(values, first, head_dim):
    if first + 1 == values.shape[1]:
        return jnp.broadcast_to(values[:, first : first + 1], (values.shape[0], head_dim))
    lane = lax.broadcasted_iota(jnp.int32, (values.shape[0], 2 * head_dim), 1)
    return jnp.where(lane < head_dim, values[:, first : first + 1], values[:, first + 1 : first + 2])


def local_kernel(
    x_ref, b_ref, c_ref, step_ref, step_row_ref, log_ref, log_row_ref, start_ref,
    skip_ref, out_ref, end_ref,
):
    tok_rows, inner = x_ref.shape
    head_count = step_ref.shape[1]
    head_dim = inner // head_count
    state_dim = b_ref.shape[1]
    row = lax.broadcasted_iota(jnp.int32, (tok_rows, tok_rows), 0)
    col = lax.broadcasted_iota(jnp.int32, (tok_rows, tok_rows), 1)
    causal = (col >= start_ref[...]) & (col <= row)
    gram = jnp.where(causal, dot(c_ref[...], b_ref[...], ((1,), (1,))), 0.0)
    logs = log_ref[...]
    steps = step_ref[...]
    last_log = logs[tok_rows - 1 :, :]
    last_start = start_ref[tok_rows - 1 :, :]
    place = lax.broadcasted_iota(jnp.int32, (tok_rows, 1), 0)
    weight = jnp.where(place >= last_start, jnp.exp(last_log - logs) * steps, 0.0)
    skip = jnp.broadcast_to(skip_ref[...], (8, head_count))
    for first, span in head_pairs(head_count, head_dim):
        x_pair = x_ref[:, span]
        sides = []
        for head in range(first, min(first + 2, head_count)):
            gap = jnp.minimum(logs[:, head : head + 1] - log_row_ref[head : head + 1, :], 0.0)
            mixing = jnp.exp(gap) * gram * step_row_ref[head : head + 1, :]
            sides.append(dot(mixing.astype(jnp.bfloat16), x_pair))
        x_wide = x_pair.astype(jnp.float32)
        lane = lax.broadcasted_iota(jnp.int32, x_pair.shape, 1)
        out_ref[:, span] = (
            jnp.where(lane < head_dim, sides[0], sides[-1])
            + pair_lanes(skip, first, head_dim)[:1] * x_wide
        )
        weighted = (pair_lanes(weight, first, head_dim) * x_wide).astype(jnp.bfloat16)
        end_ref[:, span] = dot(b_ref[...], weighted, ((0,), (0,))).astype(end_ref.dtype)


def project_kernel(slots, order_ref, *refs):
    prompt_refs = refs[:slots]
    (local_ref, c_ref, pick_ref, inherited_ref, decay_ref, arriving_ref, tail_ref, gate_ref,
     weight_ref, down_ref, up_ref, kept_ref, sent_ref, gated, low_rank) = refs[slots:]
    models, tok_rows, inner = local_ref.shape
    head_count = decay_ref.shape[2]
    head_dim = inner // head_count
    state_dim = c_ref.shape[2]
    share = tok_rows // order_ref.shape[0]
    half = models * tok_rows // 2

    @pl.when(pl.program_id(0) == 0)
    def _():
        for model in range(models):
            c_values = c_ref[model].astype(jnp.float32)
            inherited = inherited_ref[...]
            tail = jnp.broadcast_to(tail_ref[model], (8, head_count))
            mine = dot((c_values * inherited).astype(jnp.bfloat16), arriving_ref[model])
            borrowed = jnp.zeros((tok_rows, inner), jnp.float32)
            for slot in range(0, slots, 4):
                chosen = [c_values * pick_ref[:, i : i + 1] for i in range(slot, slot + 4)]
                states = [prompt_refs[i][model] for i in range(slot, slot + 4)]
                borrowed = borrowed + dot(
                    jnp.concatenate(chosen, axis=1).astype(jnp.bfloat16),
                    jnp.concatenate(states, axis=0),
                )
            decay = decay_ref[model]
            for first, span in head_pairs(head_count, head_dim):
                log_wide = pair_lanes(decay, first, head_dim)
                log_prompt = log_wide + inherited * pair_lanes(tail, first, head_dim)[:1]
                output = (
                    local_ref[model, :, span]
                    + jnp.exp(log_wide) * mine[:, span]
                    + jnp.exp(log_prompt) * borrowed[:, span]
                )
                gate = gate_ref[model, :, span].astype(jnp.float32)
                output = (output * gate / (1.0 + jnp.exp(-gate))).astype(jnp.bfloat16)
                for quarter in range(tok_rows // share):
                    rows = pl.ds(pl.multiple_of(order_ref[quarter] + model * share, share), share)
                    gated[rows, span] = output[quarter * share : (quarter + 1) * share]
        low_rank[...] = dot(gated[...], down_ref[...]).astype(jnp.bfloat16)

    policy = lax.broadcasted_iota(jnp.int32, (models * tok_rows, 1), 0) % (models * share) < share
    adapter = jnp.where(policy, dot(low_rank[...], up_ref[...]), 0.0)
    terms = (dot(gated[...], weight_ref[...]) + adapter).astype(jnp.bfloat16)
    kept_ref[...] = terms[:half]
    sent_ref[...] = terms[half:]


def head_kernel(parts, limit_ref, *refs):
    row_refs = refs[:parts]
    weight_ref, target_ref, out_ref, total = refs[parts:]
    step = pl.program_id(0)
    each = row_refs[0].shape[0]

    @pl.when(step == 0)
    def _():
        total[...] = jnp.zeros_like(total)

    total[...] += dot(jnp.concatenate([rows[...] for rows in row_refs], axis=0), weight_ref[...])

    @pl.when(step == pl.num_programs(0) - 1)
    def _():
        count = total.shape[1]
        for part in range(parts):
            rows = slice(part * each, (part + 1) * each)
            column = lax.broadcasted_iota(jnp.int32, (each, count), 1)
            in_range = column < limit_ref[0]
            logits = jnp.where(in_range, total[rows, :], -jnp.inf)
            top = jnp.max(logits, axis=1, keepdims=True)
            sums = jnp.sum(jnp.exp(logits - top), axis=1, keepdims=True)
            hit = (target_ref[rows, :] - limit_ref[1] == column) & in_range
            target = jnp.sum(jnp.where(hit, logits, 0.0), axis=1, keepdims=True)
            lane = lax.broadcasted_iota(jnp.int32, (each, 128), 1)
            stats = jnp.where(lane == 0, top, jnp.where(lane == 1, sums, target))
            out_ref[:, rows] = jnp.transpose(stats)[:8]


def place_kernel(count, first_ref, *refs):
    whole, held, arrived, left = refs[count:]
    into, out = [], []
    for i in range(count):
        blocks, size = refs[i].shape[:2]
        into.append(pltpu.make_async_copy(refs[i], held.at[i], arrived.at[i]))
        for j in range(blocks):
            rows = pl.ds(pl.multiple_of(first_ref[i * blocks + j], 16), size)
            out.append(
                pltpu.make_async_copy(held.at[i, j], whole.at[rows, :], left.at[i * blocks + j])
            )
    for copy in into:
        copy.start()
    for i in range(count):
        into[i].wait()
        for copy in out[i * blocks : (i + 1) * blocks]:
            copy.start()
    for copy in out:
        copy.wait()


def split_kernel(head_ref, *out_refs):
    size = out_refs[0].shape[0]
    for cut, out_ref in enumerate(out_refs):
        out_ref[...] = head_ref[cut * size : (cut + 1) * size, :]


def cost(flops, moved, exps=0):
    return pl.CostEstimate(flops=flops, bytes_accessed=moved, transcendentals=exps)


def whole_spec():
    return pl.BlockSpec(memory_space=pltpu.VMEM)


def shards(
    scored_token_targets,
    valid,
    lengths,
    owners,
    holders,
    mixer_input_x,
    mixer_gate_input,
    input_projection_b,
    output_projection_c,
    token_step_sizes,
    head_decay_rate,
    head_skip_scale,
    prompt_held_states,
    shared_output_weight,
    adapter_down_weight,
    adapter_up_weight,
    residual,
    final_norm_scale,
    vocab_head_weight,
):
    seq_count = lax.axis_size("seq")
    mp_count = lax.axis_size("mp")
    seq_index = lax.axis_index("seq")
    mp_index = lax.axis_index("mp")
    place = place_of(seq_index)
    core = mp_index % 2
    x_count = mp_count // 2
    x_index = mp_index // 2
    tok_rows = scored_token_targets.shape[0]
    models = mixer_input_x.shape[0]
    inner_local = mixer_input_x.shape[2]
    head_count = token_step_sizes.shape[2]
    state_dim = input_projection_b.shape[2]
    roll_count = lengths.shape[0]
    width = residual.shape[2]
    blocks = seq_count // (CHAIN * SIDE)
    partners = list(itertools.product(range(SIDE), range(blocks)))[1:]
    share_rows = tok_rows // mp_count

    def from_partner(side, block):
        return partner(seq_index, side, blocks - block, seq_count)

    def beside(value):
        return [to_partner(value, side, block) for side, block in partners]

    held = jnp.transpose(prompt_held_states[:, 0], (0, 3, 1, 2)).reshape(
        models, state_dim, inner_local
    )
    states = [held, turn(held, 1), turn(held, 2)]
    states.append(turn(states[2], 1))
    beside_held = beside(held)
    targets = lax.all_gather(
        scored_token_targets, "seq", axis_index_groups=chain_groups(), tiled=False
    )

    first_row = seq_index * tok_rows
    offsets = jnp.arange(tok_rows, dtype=jnp.int32)
    position = first_row + offsets
    starts = jnp.cumsum(lengths) - lengths
    rollout = jnp.sum((starts[None, :] <= position[:, None]).astype(jnp.int32), axis=1) - 1
    member_table = rollout[:, None] == jnp.arange(roll_count, dtype=jnp.int32)[None, :]
    start_local = jnp.sum(jnp.where(member_table, starts[None, :], 0), axis=1) - first_row
    holder_tok = jnp.sum(jnp.where(member_table, holders[None, :], 0), axis=1)
    prompt_holder = jnp.stack(
        [
            turned(source, k)
            for k in range(CHAIN)
            for source in [seq_index] + [from_partner(side, block) for side, block in partners]
        ]
    )
    pick = (holder_tok[:, None] == prompt_holder[None, :]).astype(jnp.float32)
    inherited = (start_local < 0).astype(jnp.float32)
    neg_rates = -head_decay_rate
    log_decay = jnp.cumsum(token_step_sizes * neg_rates[:, None, :], axis=1)
    before = jnp.take(log_decay, jnp.maximum(start_local - 1, 0), axis=1)
    before = jnp.where((start_local >= 1)[None, :, None], before, 0.0)

    mixer_x, states[1], *beside_held = tied(mixer_input_x, states[1], *beside_held)
    per_model = lambda *shape: pl.BlockSpec((None,) + shape, lambda m: (m,) + (0,) * len(shape))
    local_out, local_end = pl.pallas_call(
        local_kernel,
        grid=(models,),
        in_specs=[
            per_model(tok_rows, inner_local),
            per_model(tok_rows, state_dim),
            per_model(tok_rows, state_dim),
            per_model(tok_rows, head_count),
            per_model(head_count, tok_rows),
            per_model(tok_rows, head_count),
            per_model(head_count, tok_rows),
            pl.BlockSpec((tok_rows, 1), lambda m: (0, 0)),
            per_model(1, head_count),
        ],
        out_specs=[per_model(tok_rows, inner_local), per_model(state_dim, inner_local)],
        out_shape=[
            jax.ShapeDtypeStruct((models, tok_rows, inner_local), jnp.float32),
            jax.ShapeDtypeStruct((models, state_dim, inner_local), jnp.bfloat16),
        ],
        compiler_params=pltpu.CompilerParams(vmem_limit_bytes=32 * 2**20),
        cost_estimate=cost(10**9, 8 * 2**20, 2 * 10**6),
        name="local_tokens",
    )(
        mixer_x,
        input_projection_b,
        output_projection_c,
        token_step_sizes,
        jnp.swapaxes(token_step_sizes, 1, 2),
        log_decay,
        jnp.swapaxes(log_decay, 1, 2),
        start_local[:, None],
        head_skip_scale[:, None, :],
    )

    hops = max(1, -(-(seq_count * tok_rows // 8) // tok_rows))
    next_one = [(i, i + 1) for i in range(seq_count - 1)]
    local_tail = log_decay[:, -1] - before[:, -1]
    arriving = lax.ppermute(local_end, "seq", next_one)
    tail = lax.ppermute(local_tail, "seq", next_one)
    if hops > 1:
        through = jnp.repeat(jnp.exp(log_decay[:, -1]), inner_local // head_count, axis=1)
        through = through[:, None, :] * inherited[-1]
        for _ in range(hops - 1):
            moved = through * arriving.astype(jnp.float32) + local_end.astype(jnp.float32)
            arriving = lax.ppermute(moved.astype(jnp.bfloat16), "seq", next_one)
            tail = lax.ppermute(inherited[-1] * tail + local_tail, "seq", next_one)

    head_rows, vocab_local = vocab_head_weight.shape
    part = -(-vocab_local // (CHAIN * 128)) * 128
    cuts = 2 if head_rows % 32 == 0 else 1
    cut_rows = head_rows // cuts
    head = pl.pallas_call(
        split_kernel,
        grid=(CHAIN,),
        in_specs=[pl.BlockSpec((head_rows, part), lambda j: (0, j))],
        out_specs=[pl.BlockSpec((None, cut_rows, part), lambda j: (j, 0, 0))] * cuts,
        out_shape=[jax.ShapeDtypeStruct((CHAIN, cut_rows, part), vocab_head_weight.dtype)] * cuts,
        cost_estimate=cost(0, 2 * vocab_head_weight.size * 2),
        name="split_head_columns",
    )(vocab_head_weight)
    arriving, tail, states[2], states[3], *head = tied(arriving, tail, states[2], states[3], *head)
    came_head = [
        lax.all_to_all(head[cut], "seq", 0, 0, axis_index_groups=chain_groups())
        for cut in range(cuts)
    ]

    prompts = [held] + beside_held
    for state in states[1:]:
        prompts += [state] + beside(state)

    quarter = jnp.arange(mp_count, dtype=jnp.int32)
    order = (quarter % 2 != core) * x_count + (quarter // 2 - x_index) % x_count
    order = order.astype(jnp.int32) * (models * share_rows)
    half = models * tok_rows // 2
    tile = 512 if width % 512 == 0 else width
    kept, sent = pl.pallas_call(
        functools.partial(project_kernel, len(prompts)),
        grid=(width // tile,),
        in_specs=[pl.BlockSpec(memory_space=pltpu.SMEM)]
        + [whole_spec()] * (len(prompts) + 8)
        + [
            pl.BlockSpec((inner_local, tile), lambda j: (0, j)),
            whole_spec(),
            pl.BlockSpec((adapter_up_weight.shape[0], tile), lambda j: (0, j)),
        ],
        out_specs=[pl.BlockSpec((half, tile), lambda j: (0, j))] * 2,
        out_shape=[jax.ShapeDtypeStruct((half, width), jnp.bfloat16)] * 2,
        scratch_shapes=[
            pltpu.VMEM((models * tok_rows, inner_local), jnp.bfloat16),
            pltpu.VMEM((models * tok_rows, adapter_up_weight.shape[0]), jnp.bfloat16),
        ],
        compiler_params=pltpu.CompilerParams(vmem_limit_bytes=48 * 2**20),
        cost_estimate=cost(
            2 * models * tok_rows * inner_local * width, 4 * inner_local * width, 2 * 10**6
        ),
        name="gate_and_project",
    )(
        order,
        *prompts,
        local_out,
        output_projection_c,
        pick,
        inherited[:, None],
        log_decay - before,
        arriving,
        tail[:, None, :],
        mixer_gate_input,
        shared_output_weight,
        adapter_down_weight,
        adapter_up_weight,
    )

    came, targets = tied(other_core(sent), targets)
    each = models * share_rows
    chip_sum = kept.astype(jnp.float32) + came.astype(jnp.float32)
    mixed = chip_sum[:each]
    for by in range(1, x_count):
        away = chip_sum[by * each : (by + 1) * each].astype(jnp.bfloat16)
        mixed = mixed + along_x(away, by).astype(jnp.float32)
    own_rows = lax.dynamic_slice_in_dim(residual, mp_index * share_rows, share_rows, 0)
    hidden = jnp.transpose(own_rows, (1, 0, 2)).reshape(each, width).astype(jnp.float32) + mixed
    mean_sq = jnp.mean(hidden * hidden, axis=-1, keepdims=True)
    normed_own = (hidden * lax.rsqrt(mean_sq + 1e-05) * final_norm_scale).astype(jnp.bfloat16)

    came_head[-1], _ = tied(came_head[-1], normed_own)
    rows_of = [normed_own, turn(normed_own, 1), turn(normed_own, 2)]
    pieces, firsts = [], []
    for cut in range(cuts):
        sources = [seq_index] + [from_partner(side, block) for side, block in partners]
        pieces += [came_head[cut]] + beside(came_head[cut])
        for source in sources:
            first_of_chain = source - place_of(source) * SIDE
            firsts += [
                (first_of_chain + k * SIDE) * head_rows + cut * cut_rows for k in range(CHAIN)
            ]
    head_part = pl.pallas_call(
        functools.partial(place_kernel, len(pieces)),
        in_specs=[pl.BlockSpec(memory_space=pltpu.SMEM)]
        + [pl.BlockSpec(memory_space=pl.ANY)] * len(pieces),
        out_specs=pl.BlockSpec(memory_space=pl.ANY),
        out_shape=jax.ShapeDtypeStruct((seq_count * head_rows, part), vocab_head_weight.dtype),
        scratch_shapes=[
            pltpu.VMEM((len(pieces), CHAIN, cut_rows, part), vocab_head_weight.dtype),
            pltpu.SemaphoreType.DMA((len(pieces),)),
            pltpu.SemaphoreType.DMA((len(pieces) * CHAIN,)),
        ],
        compiler_params=pltpu.CompilerParams(vmem_limit_bytes=16 * 2**20),
        cost_estimate=cost(0, 4 * seq_count * head_rows * part),
        name="place_head_rows",
    )(jnp.stack(firsts).astype(jnp.int32), *pieces)
    last_rows, head_part = tied(turn(rows_of[2], 1), head_part)
    rows_of.append(last_rows)

    limit = jnp.stack(
        [
            jnp.minimum(vocab_local - place * part, part),
            mp_index * vocab_local + place * part,
        ]
    ).astype(jnp.int32)
    depth = 512 if width % 512 == 0 else width
    parts = mp_count
    chain_stats = []
    mp_order = jnp.stack(
        [(x_index - k) % x_count * 2 + (core + other) % 2 for other in (0, 1) for k in range(x_count)]
    )
    def head_stats(rows, targets):
        near = [rows] + [along_x(rows, by) for by in range(1, x_count)]
        all_rows = near + [other_core(value) for value in near]
        targets = jnp.repeat(targets.reshape(mp_count, 1, share_rows)[mp_order], models, axis=1)
        stats = pl.pallas_call(
            functools.partial(head_kernel, parts),
            grid=(width // depth,),
            in_specs=[pl.BlockSpec(memory_space=pltpu.SMEM)]
            + [pl.BlockSpec((each, depth), lambda j: (0, j))] * parts
            + [pl.BlockSpec((depth, part), lambda j: (j, 0)), whole_spec()],
            out_specs=whole_spec(),
            out_shape=jax.ShapeDtypeStruct((8, parts * each), jnp.float32),
            scratch_shapes=[pltpu.VMEM((parts * each, part), jnp.float32)],
            compiler_params=pltpu.CompilerParams(vmem_limit_bytes=48 * 2**20),
            cost_estimate=cost(
                2 * parts * each * width * part, 2 * (parts * each + part) * width, parts * each * part
            ),
            name="head_stats",
        )(limit, *all_rows, head_part, targets.reshape(parts * each, 1))
        return stats.reshape(8, 2, x_count, models, share_rows)

    for k in range(CHAIN):
        stats = head_stats(rows_of[k], targets[place ^ k])
        chain_stats.append(stats if k == 0 else turn(stats, k))

    def merged(several):
        top = functools.reduce(jnp.maximum, [stats[0] for stats in several])
        total = sum(stats[1] * jnp.exp(stats[0] - top) for stats in several)
        return jnp.stack([top, total, sum(stats[2] for stats in several)])

    stats = merged(chain_stats)
    stats = merged([stats, other_core(stats)[:, ::-1]])
    stats = merged(
        [stats] + [jnp.roll(along_x(stats, by), by, axis=2) for by in range(1, x_count)]
    )
    logprob = stats[2] - stats[0] - jnp.log(stats[1])
    delta = (logprob[:, :, 0] - logprob[:, :, 1]).reshape(mp_count, share_rows)
    token_delta = jnp.sum(
        jnp.where(mp_order[None, :, None] == quarter[:, None, None], delta[None], 0.0), axis=1
    ).reshape(tok_rows)
    token_delta = token_delta * valid.astype(jnp.float32)
    roll_sums = jnp.dot(token_delta, member_table.astype(jnp.float32), precision=highest)
    distance = 1
    while distance < seq_count:
        pairs = [(i, i ^ distance) for i in range(seq_count)]
        roll_sums = roll_sums + lax.ppermute(roll_sums, "seq", pairs)
        distance *= 2
    owner_sums = jnp.where(owners == seq_index, roll_sums / lengths.astype(jnp.float32), 0.0)
    return (owner_sums[None, :], token_delta)


def solution(mesh):
    placed = (
        P("seq"),
        P("seq"),
        P(),
        P(),
        P(),
        P(None, "seq", "mp"),
        P(None, "seq", "mp"),
        P(None, "seq", None),
        P(None, "seq", None),
        P(None, "seq", "mp"),
        P(None, "mp"),
        P(None, "mp"),
        P(None, "seq", "mp", None, None),
        P("mp", None),
        P("mp", None),
        P(),
        P("seq", None, None),
        P(),
        P("seq", "mp"),
    )
    return jax.shard_map(
        shards, mesh=mesh, in_specs=placed, out_specs=(P("seq", None), P("seq")), check_vma=False
    )
```

time: 990 us -> 306 us (0.31)
  waiting for transfers between devices: 809 us -> 135 us
  Pallas kernels: 0 us -> 67.7 us
  matrix products: 51.4 us -> 0.12 us
  blocking collectives: 33 us -> 11.1 us
  other arithmetic: 30.7 us -> 12.2 us
  starting transfers between devices: 31.6 us -> 46.2 us
  between operations: 14.9 us -> 1.27 us
  local copies, waits for them, and re-layouts: 18.8 us -> 30.6 us
    all_gather x3 -> x0, waiting for transfers between devices: 643 us -> none  [the longest x1 561 us: shards(): lax.all_gather(vocab_head_weight, 'seq', axis=0, tiled=True)]
    pallas_call x0 -> x8, Pallas kernels: none -> 67.7 us  [the longest x4 40.4 us: head_stats(): pl.pallas_call(functools.partial(head_kernel, parts), grid=(width // dept...]
    reduce_scatter x1 -> x0, waiting for transfers between devices: 52.3 us -> none  [shards(): lax.psum_scatter(jnp.stack([base_output[:, 0] + adapter_output, base_outp...]
    dot_general x9 -> x0, matrix products: 51.2 us -> none  [the longest x1 23.4 us: shards(): jnp.einsum('tmk,kv->mtv', normed, lax.all_gather(vocab_head_weight, 'seq'...]
    unnamed x1 -> x0, blocking collectives: 20.3 us -> none
    all_to_all x0 -> x2, waiting for transfers between devices: none -> 12.5 us  [shards(): lax.all_to_all(head[cut], 'seq', 0, 0, axis_index_groups=chain_groups())]
    all_gather x0 -> x1, blocking collectives: none -> 11.1 us  [shards(): lax.all_gather(scored_token_targets, 'seq', axis_index_groups=chain_group...]
    ppermute x7 -> x36, waiting for transfers between devices: 112 us -> 123 us  [the longest x6 53.5 us: along_x(): lax.ppermute(x, 'mp', [(i, (i + 2 * by) % count) for i in range(count)])]
  transfers between devices with their start and end apart: 11 -> 38, of which waited for: 11 -> 18; matrix products, arithmetic and copies ran while one was open for 2% -> 8% of each run, Pallas kernels for 0% -> 22%
where the time goes in v1:
time: 306 us; the launch traced here: 304 us
  waiting for transfers between devices  135 us (44%)
  Pallas kernels  67.7 us (22%)
  starting transfers between devices  46.2 us (15%)
  local copies, waits for them, and re-layouts  30.6 us (10%)
  other arithmetic  12.2 us (4%)
  blocking collectives  11.1 us (4%)
    ppermute x6, waiting for transfers between devices, along_x(): lax.ppermute(x, 'mp', [(i, (i + 2 * by) % count) for i in range(count)])  53.5 us
    ppermute x9, waiting for transfers between devices, turn(): return lax.ppermute(x, 'seq', [(i, turned(i, by)) for i in range(count)])  43.4 us
    pallas_call x4, Pallas kernels, head_stats(): pl.pallas_call(functools.partial(head_kernel, parts), grid=(width // dept...  40.4 us
    unnamed x63, local copies, waits for them, and re-layouts  18.9 us
    ppermute x6, waiting for transfers between devices, to_partner(): lax.ppermute(x, 'seq', [(i, partner(i, side, block, count)) for i in rang...  15.9 us
    pallas_call x1, Pallas kernels, shards(): pl.pallas_call(functools.partial(project_kernel, len(prompts)), grid=(wid...  13.9 us
    ppermute x9, starting transfers between devices, turn(): return lax.ppermute(x, 'seq', [(i, turned(i, by)) for i in range(count)])  12.8 us
    all_to_all x2, waiting for transfers between devices, shards(): lax.all_to_all(head[cut], 'seq', 0, 0, axis_index_groups=chain_groups())  12.5 us
  transfers between devices with their start and end apart: 38, of which 18 were waited for; matrix products, arithmetic and copies ran while one was open for 8% of the time, Pallas kernels for 22%

profile of v1, /device:TPU:0, one launch (start us, length us, event | category | flops | bytes accessed | tf_op | source)
XLA Modules:
  0.0 304.5 jit_solution(5438122084491311302)
XLA Ops:
  0.7 1.3 copy.127.refs_0_
  2.0 3.1 %collective-permute-start = (bf16[2,64,896]{2,1,0:T(8,128)(2,1)S(1)}, bf16[2,64,896]{2,1,0:T(8,128)(2,1)S(1)}, u32[]{:S(2)}, u32[]{:S(2)}) collective-permute-start(bf16[2,64,896]{2,1,0:T(8,128)(2,1)S(1)} %copy.127.refs_0_), channel_id=1, source_target_pairs={{0,8},{4,12},{8,0},{12,4},{16,24},{20,28},{24,16},{28,20},{1,9},{5... | collective-permute-start | bytes 688136 | tf_op jit(solution)/shard_map/ppermute | solution.py:30
  5.1 1.5 collective-permute-start.1
  6.6 2.6 collective-permute-start.5
  13.3 1.2 reduce-window.19
  18.0 1.9 gather_fusion
  20.0 3.2 %local_tokens.1 = (f32[2,256,896]{2,1,0:T(8,128)S(1)}, bf16[2,64,896]{2,1,0:T(8,128)(2,1)S(1)}) custom-call(bf16[2,256,896]{2,1,0:T(8,128)(2,1)S(1)} %copy-done.15, bf16[2,256,64]{2,1,0:T(8,128)(2,1)S(1)} %copy.111.b_ref, bf16[2,256,64]{2,1,0:T(8,128)(2,1)S(1)} %copy.112.c_ref.refs_9_, f32[2,256,14]{2,1,0:T(8,128)S(1)} %copy.113.step_ref, ...), custom_call_target="tpu_custom_call" | custom-call | flops 1000000000 | bytes 8388608 | tf_op jit(solution)/shard_map/local_tokens/pallas_call | solution.py:306
  23.2 1.2 copy-done.3
  24.4 2.4 collective-permute-start.3
  27.5 3.3 %collective-permute-start.4 = (f32[2,14]{1,0:T(2,128)S(1)}, f32[2,14]{1,0:T(2,128)S(1)}, u32[]{:S(2)}, u32[]{:S(2)}) collective-permute-start(f32[2,14]{1,0:T(2,128)S(1)} %bitcast.242), channel_id=1, source_target_pairs={{0,4},{4,8},{8,12},{12,16},{16,20},{20,24},{24,28},{1,5},{5,9},{9,... | collective-permute-start | bytes 344 | tf_op jit(solution)/shard_map/ppermute | solution.py:344
  30.9 4.5 %split_head_columns.1 = (bf16[4,224,1024]{2,1,0:T(8,128)(2,1)}, bf16[4,224,1024]{2,1,0:T(8,128)(2,1)}) custom-call(bf16[448,4000]{1,0:T(8,128)(2,1)} %head_ref.1), custom_call_target="tpu_custom_call" | custom-call | bytes 7168000 | tf_op jit(solution)/shard_map/split_head_columns/pallas_call | solution.py:357
  36.1 5.1 %all-to-all-start = ((bf16[4,224,1024]{2,1,0:T(8,128)(2,1)}), bf16[4,224,1024]{2,1,0:T(8,128)(2,1)S(1)}, u32[]{:S(2)}, u32[]{:S(2)}) async-start(bf16[4,224,1024]{2,1,0:T(8,128)(2,1)} %get-tuple-element.36), calls=%async_computation | async-start | bytes 3670016 | tf_op jit(solution)/shard_map/all_to_all | solution.py:368
  41.8 1.5 collective-permute-start.7
  44.2 5.9 %collective-permute-done.2.refs_3_ = bf16[2,64,896]{2,1,0:T(8,128)(2,1)} collective-permute-done((bf16[2,64,896]{2,1,0:T(8,128)(2,1)}, bf16[2,64,896]{2,1,0:T(8,128)(2,1)}, u32[]{:S(2)}, u32[]{:S(2)}) %collective-permute-start.2) | collective-permute-done | bytes 229408 | tf_op jit(solution)/shard_map/ppermute | solution.py:35
  50.1 3.8 %collective-permute-done.7.refs_5_ = bf16[2,64,896]{2,1,0:T(8,128)(2,1)} collective-permute-done((bf16[2,64,896]{2,1,0:T(8,128)(2,1)}, bf16[2,64,896]{2,1,0:T(8,128)(2,1)}, u32[]{:S(2)}, u32[]{:S(2)}) %collective-permute-start.7) | collective-permute-done | bytes 229408 | tf_op jit(solution)/shard_map/ppermute | solution.py:35
  53.9 2.5 collective-permute-done.8.refs_7_
  56.4 1.2 copy-done.5
  57.6 0.9 copy-done.6
  59.5 0.9 copy-done.10
  60.4 0.9 copy-done.12
  62.3 13.9 %gate_and_project.1 = (bf16[256,3584]{1,0:T(8,128)(2,1)}, bf16[256,3584]{1,0:T(8,128)(2,1)}) custom-call(s32[4]{0:T(128)S(1)} %fusion.35.order_ref, bf16[2,64,896]{2,1,0:T(8,128)(2,1)S(1)} %copy.127.refs_0_, bf16[2,64,896]{2,1,0:T(8,128)(2,1)S(1)} %copy-done.10, bf16[2,64,896]{2,1,0:T(8,128)(2,1)S(1)} %copy-done.8, ...), custom_call_target="tpu_custom_call" | custom-call | flops 3288334336 | bytes 12845056 | tf_op jit(solution)/shard_map/gate_and_project/pallas_call | solution.py:381
  76.2 11.1 %all-gather.1 = s32[4,1,256]{2,1,0:T(1,128)S(1)} all-gather(s32[1,1,256]{2,1,0:T(1,128)S(1)} %bitcast.240), channel_id=2, replica_groups={{0,8,16,24},{4,12,20,28},{1,9,17,25},{5,13,21,29},{2,10,18,26},{6,14,22..., dimensions={0}, use_global_device_ids=true | all-gather | bytes 5120 | tf_op jit(solution)/shard_map/all_gather | solution.py:278
  87.3 1.2 copy-done.20
  88.5 4.6 %all-to-all-start.1 = ((bf16[4,224,1024]{2,1,0:T(8,128)(2,1)}), bf16[4,224,1024]{2,1,0:T(8,128)(2,1)}, u32[]{:S(2)}, u32[]{:S(2)}) async-start(bf16[4,224,1024]{2,1,0:T(8,128)(2,1)} %get-tuple-element.37), calls=%async_computation.1 | async-start | bytes 3670016 | tf_op jit(solution)/shard_map/all_to_all | solution.py:368
  93.1 2.6 convert_add_fusion
  95.7 1.8 copy-done.17
  97.4 1.0 slice.241
  98.5 1.5 collective-permute-start.10
  100.0 1.8 convert_bitcast_fusion
  102.2 1.0 collective-permute-start.16
  103.2 16.2 %collective-permute-done.10 = bf16[128,3584]{1,0:T(8,128)(2,1)S(1)} collective-permute-done((bf16[128,3584]{1,0:T(8,128)(2,1)}, bf16[128,3584]{1,0:T(8,128)(2,1)S(1)}, u32[]{:S(2)}, u32[]{:S(2)}) %collective-permute-start.10) | collective-permute-done | bytes 917536 | tf_op jit(solution)/shard_map/ppermute | solution.py:52
  120.4 1.6 multiply_convert_fusion.refs_0_
  122.0 12.5 %all-to-all-done.1.refs_2_ = bf16[4,224,1024]{2,1,0:T(8,128)(2,1)} async-done(((bf16[4,224,1024]{2,1,0:T(8,128)(2,1)}), bf16[4,224,1024]{2,1,0:T(8,128)(2,1)}, u32[]{:S(2)}, u32[]{:S(2)}) %all-to-all-start.1) | async-done | bytes 1835040 | tf_op jit(solution)/shard_map/all_to_all | solution.py:368
  134.5 1.0 collective-permute-start.17
  135.4 2.0 collective-permute-start.18
  137.5 1.5 collective-permute-start.11
  139.0 35.6 %collective-permute-done.14.refs_0_ = bf16[128,3584]{1,0:T(8,128)(2,1)} collective-permute-done((bf16[128,3584]{1,0:T(8,128)(2,1)S(1)}, bf16[128,3584]{1,0:T(8,128)(2,1)}, u32[]{:S(2)}, u32[]{:S(2)}) %collective-permute-start.14) | collective-permute-done | bytes 917536 | tf_op jit(solution)/shard_map/ppermute | solution.py:30
  174.6 1.7 collective-permute-done.18.refs_0_
  176.2 1.5 collective-permute-start.19
  178.0 3.7 %collective-permute-done.17.refs_3_ = bf16[4,224,1024]{2,1,0:T(8,128)(2,1)S(1)} collective-permute-done((bf16[4,224,1024]{2,1,0:T(8,128)(2,1)}, bf16[4,224,1024]{2,1,0:T(8,128)(2,1)S(1)}, u32[]{:S(2)}, u32[]{:S(2)}) %collective-permute-start.17) | collective-permute-done | bytes 1835040 | tf_op jit(solution)/shard_map/ppermute | solution.py:35
  181.7 1.3 copy-done.1
  183.6 1.5 copy-done.2
  185.1 5.6 %place_head_rows.1.refs_4_ = bf16[3584,1024]{1,0:T(8,128)(2,1)S(1)} custom-call(s32[16]{0:T(128)S(1)} %stack.157.first_ref, bf16[4,224,1024]{2,1,0:T(8,128)(2,1)S(1)} %all-to-all-done.refs_0_, bf16[4,224,1024]{2,1,0:T(8,128)(2,1)} %collective-permute-done.16.refs_1_, bf16[4,224,1024]{2,1,0:T(8,128)(2,1)} %all-to-all-done.1.refs_2_, ...), custom_call_target="tpu_custom_call" | custom-call | bytes 14680064 | tf_op jit(solution)/shard_map/place_head_rows/pallas_call | solution.py:441
  190.7 2.9 copy-done
  193.6 3.5 %collective-permute-done.15.refs_0_ = bf16[128,3584]{1,0:T(8,128)(2,1)} collective-permute-done((bf16[128,3584]{1,0:T(8,128)(2,1)}, bf16[128,3584]{1,0:T(8,128)(2,1)}, u32[]{:S(2)}, u32[]{:S(2)}) %collective-permute-start.15) | collective-permute-done | bytes 917536 | tf_op jit(solution)/shard_map/ppermute | solution.py:30
  197.1 1.5 collective-permute-start.27
  198.6 1.1 collective-permute-done.19.refs_1_
  200.3 19.1 %collective-permute-done.23.refs_1_ = bf16[128,3584]{1,0:T(8,128)(2,1)} collective-permute-done((bf16[128,3584]{1,0:T(8,128)(2,1)}, bf16[128,3584]{1,0:T(8,128)(2,1)}, u32[]{:S(2)}, u32[]{:S(2)}) %collective-permute-start.23) | collective-permute-done | bytes 917536 | tf_op jit(solution)/shard_map/ppermute | solution.py:52
  223.5 15.1 %collective-permute-done.27.refs_1_ = bf16[128,3584]{1,0:T(8,128)(2,1)} collective-permute-done((bf16[128,3584]{1,0:T(8,128)(2,1)}, bf16[128,3584]{1,0:T(8,128)(2,1)}, u32[]{:S(2)}, u32[]{:S(2)}) %collective-permute-start.27) | collective-permute-done | bytes 917536 | tf_op jit(solution)/shard_map/ppermute | solution.py:52
  238.6 9.9 %head_stats.4 = f32[8,512]{1,0:T(8,128)S(1)} custom-call(s32[2]{0:T(128)S(1)} %pad_add_fusion.1.limit_ref, bf16[128,3584]{1,0:T(8,128)(2,1)S(1)} %multiply_convert_fusion.refs_0_, bf16[128,3584]{1,0:T(8,128)(2,1)} %collective-permute-done.11.refs_1_, bf16[128,3584]{1,0:T(8,128)(2,1)} %collective-permute-done.12.refs_2_, ...), custom_call_target="tpu_custom_call" | custom-call | flops 3758096384 | bytes 11010048 | tf_op jit(solution)/shard_map/head_stats/pallas_call | solution.py:475
  248.6 10.1 %head_stats.5 = f32[8,512]{1,0:T(8,128)S(1)} custom-call(s32[2]{0:T(128)S(1)} %pad_add_fusion.1.limit_ref, bf16[128,3584]{1,0:T(8,128)(2,1)} %collective-permute-done.18.refs_0_, bf16[128,3584]{1,0:T(8,128)(2,1)} %collective-permute-done.19.refs_1_, bf16[128,3584]{1,0:T(8,128)(2,1)} %collective-permute-done.20.refs_2_, ...), custom_call_target="tpu_custom_call" | custom-call | flops 3758096384 | bytes 11010048 | tf_op jit(solution)/shard_map/head_stats/pallas_call | solution.py:475
  259.2 10.1 %head_stats.6 = f32[8,512]{1,0:T(8,128)S(1)} custom-call(s32[2]{0:T(128)S(1)} %pad_add_fusion.1.limit_ref, bf16[128,3584]{1,0:T(8,128)(2,1)} %collective-permute-done.14.refs_0_, bf16[128,3584]{1,0:T(8,128)(2,1)} %collective-permute-done.23.refs_1_, bf16[128,3584]{1,0:T(8,128)(2,1)} %collective-permute-done.24.refs_2_, ...), custom_call_target="tpu_custom_call" | custom-call | flops 3758096384 | bytes 11010048 | tf_op jit(solution)/shard_map/head_stats/pallas_call | solution.py:475
  269.4 1.3 collective-permute-start.26
  270.7 10.3 %head_stats.7 = f32[8,512]{1,0:T(8,128)S(1)} custom-call(s32[2]{0:T(128)S(1)} %pad_add_fusion.1.limit_ref, bf16[128,3584]{1,0:T(8,128)(2,1)} %collective-permute-done.15.refs_0_, bf16[128,3584]{1,0:T(8,128)(2,1)} %collective-permute-done.27.refs_1_, bf16[128,3584]{1,0:T(8,128)(2,1)} %collective-permute-done.28.refs_2_, ...), custom_call_target="tpu_custom_call" | custom-call | flops 3758096384 | bytes 11010048 | tf_op jit(solution)/shard_map/head_stats/pallas_call | solution.py:475
  281.1 2.8 collective-permute-start.30
  284.3 2.6 collective-permute-done.30
  287.1 1.1 collective-permute-done.31
  288.3 1.6 collective-permute-start.32
  290.1 2.0 collective-permute-done.32
  292.4 1.1 collective-permute-start.33
  293.5 2.5 collective-permute-done.33
  296.1 3.4 %collective-permute-done.34 = f32[48]{0:T(128)S(1)} collective-permute-done((f32[48]{0:T(128)S(1)}, f32[48]{0:T(128)S(1)}, u32[]{:S(2)}, u32[]{:S(2)}) %collective-permute-start.34) | collective-permute-done | bytes 224 | tf_op jit(solution)/shard_map/ppermute | solution.py:516
  299.5 1.3 collective-permute-start.35
  300.8 3.1 %collective-permute-done.35 = f32[48]{0:T(128)S(1)} collective-permute-done((f32[48]{0:T(128)S(1)}, f32[48]{0:T(128)S(1)}, u32[]{:S(2)}, u32[]{:S(2)}) %collective-permute-start.35) | collective-permute-done | bytes 224 | tf_op jit(solution)/shard_map/ppermute | solution.py:516
  (175 shorter events, 21.7 us)
Async XLA Ops:
  0.6 17.1 %copy-start.21 = (bf16[2,256,64]{1,2,0:T(8,128)(2,1)S(1)}, bf16[2,256,64]{1,2,0:T(8,128)(2,1)}, u32[]{:S(2)}) copy-start(bf16[2,256,64]{1,2,0:T(8,128)(2,1)} %param.27) | copy-start | bytes 196612
  0.6 17.2 %copy-start.22 = (bf16[2,256,64]{1,2,0:T(8,128)(2,1)S(1)}, bf16[2,256,64]{1,2,0:T(8,128)(2,1)}, u32[]{:S(2)}) copy-start(bf16[2,256,64]{1,2,0:T(8,128)(2,1)} %param.26) | copy-start | bytes 196612
  0.7 19.4 %copy-start.15 = (bf16[2,256,896]{2,1,0:T(8,128)(2,1)S(1)}, bf16[2,256,896]{2,1,0:T(8,128)(2,1)}, u32[]{:S(2)}) copy-start(bf16[2,256,896]{2,1,0:T(8,128)(2,1)} %x_ref) | copy-start | bytes 2752516
  0.7 19.4 %copy-start.16 = (f32[2,14]{1,0:T(2,128)S(1)}, f32[2,14]{1,0:T(2,128)}, u32[]{:S(2)}) copy-start(f32[2,14]{1,0:T(2,128)} %param.30) | copy-start | bytes 340
  2.0 18.0 %collective-permute-start = (bf16[2,64,896]{2,1,0:T(8,128)(2,1)S(1)}, bf16[2,64,896]{2,1,0:T(8,128)(2,1)S(1)}, u32[]{:S(2)}, u32[]{:S(2)}) collective-permute-start(bf16[2,64,896]{2,1,0:T(8,128)(2,1)S(1)} %copy.127.refs_0_), channel_id=1, source_target_pairs={{0,8},{4,12},{8,0},{12,4},{16,24},{20,28},{24,16},{28,20},{1,9},{5... | collective-permute-start | bytes 688136 | tf_op jit(solution)/shard_map/ppermute | solution.py:30
  5.1 14.9 %collective-permute-start.1 = (bf16[2,64,896]{2,1,0:T(8,128)(2,1)S(1)}, bf16[2,64,896]{2,1,0:T(8,128)(2,1)S(1)}, u32[]{:S(2)}, u32[]{:S(2)}) collective-permute-start(bf16[2,64,896]{2,1,0:T(8,128)(2,1)S(1)} %copy.127.refs_0_), channel_id=1, source_target_pairs={{0,4},{4,0},{8,12},{12,8},{16,20},{20,16},{24,28},{28,24},{1,5},{5... | collective-permute-start | bytes 688136 | tf_op jit(solution)/shard_map/ppermute | solution.py:35
  6.6 20.3 %collective-permute-start.5 = (bf16[2,64,896]{2,1,0:T(8,128)(2,1)S(1)}, bf16[2,64,896]{2,1,0:T(8,128)(2,1)S(1)}, u32[]{:S(2)}, u32[]{:S(2)}) collective-permute-start(bf16[2,64,896]{2,1,0:T(8,128)(2,1)S(1)} %copy.127.refs_0_), channel_id=1, source_target_pairs={{0,16},{4,20},{8,24},{12,28},{16,0},{20,4},{24,8},{28,12},{1,17},{... | collective-permute-start | bytes 688136 | tf_op jit(solution)/shard_map/ppermute | solution.py:30
  20.0 16.1 %copy-start.7 = (bf16[2,64,896]{2,1,0:T(8,128)(2,1)}, bf16[2,64,896]{2,1,0:T(8,128)(2,1)S(1)}, u32[]{:S(2)}) copy-start(bf16[2,64,896]{2,1,0:T(8,128)(2,1)S(1)} %collective-permute-done.refs_2_) | copy-start | bytes 688132
  20.0 3.2 %copy-start.9 = (bf16[2,64,896]{2,1,0:T(8,128)(2,1)}, bf16[2,64,896]{2,1,0:T(8,128)(2,1)S(1)}, u32[]{:S(2)}) copy-start(bf16[2,64,896]{2,1,0:T(8,128)(2,1)S(1)} %collective-permute-done.1.refs_1_) | copy-start | bytes 688132
  23.2 1.2 copy-start.3
  24.4 11.0 %collective-permute-start.3 = (bf16[2,64,896]{2,1,0:T(8,128)(2,1)S(1)}, bf16[2,64,896]{2,1,0:T(8,128)(2,1)S(1)}, u32[]{:S(2)}, u32[]{:S(2)}) collective-permute-start(bf16[2,64,896]{2,1,0:T(8,128)(2,1)S(1)} %get-tuple-element.25), channel_id=1, source_target_pairs={{0,4},{4,8},{8,12},{12,16},{16,20},{20,24},{24,28},{1,5},{5,9},{9,... | collective-permute-start | bytes 688136 | tf_op jit(solution)/shard_map/ppermute | solution.py:343
  26.9 9.3 %copy-start.11 = (bf16[2,64,896]{2,1,0:T(8,128)(2,1)}, bf16[2,64,896]{2,1,0:T(8,128)(2,1)S(1)}, u32[]{:S(2)}) copy-start(bf16[2,64,896]{2,1,0:T(8,128)(2,1)S(1)} %collective-permute-done.5.refs_4_) | copy-start | bytes 688132
  26.9 9.3 %collective-permute-start.6 = (bf16[2,64,896]{2,1,0:T(8,128)(2,1)S(1)}, bf16[2,64,896]{2,1,0:T(8,128)(2,1)}, u32[]{:S(2)}, u32[]{:S(2)}) collective-permute-start(bf16[2,64,896]{2,1,0:T(8,128)(2,1)S(1)} %collective-permute-done.5.refs_4_), channel_id=1, source_target_pairs={{0,8},{4,12},{8,0},{12,4},{16,24},{20,28},{24,16},{28,20},{1,9},{5... | collective-permute-start | bytes 688136 | tf_op jit(solution)/shard_map/ppermute | solution.py:30
  27.5 7.9 %collective-permute-start.4 = (f32[2,14]{1,0:T(2,128)S(1)}, f32[2,14]{1,0:T(2,128)S(1)}, u32[]{:S(2)}, u32[]{:S(2)}) collective-permute-start(f32[2,14]{1,0:T(2,128)S(1)} %bitcast.242), channel_id=1, source_target_pairs={{0,4},{4,8},{8,12},{12,16},{16,20},{20,24},{24,28},{1,5},{5,9},{9,... | collective-permute-start | bytes 344 | tf_op jit(solution)/shard_map/ppermute | solution.py:344
  36.1 20.3 %copy-start.4 = (bf16[2,256,896]{2,1,0:T(8,128)(2,1)S(1)}, bf16[2,256,896]{2,1,0:T(8,128)(2,1)}, u32[]{:S(2)}) copy-start(bf16[2,256,896]{2,1,0:T(8,128)(2,1)} %refs_15_.1) | copy-start | bytes 2752516
  36.1 52.4 %all-to-all-start = ((bf16[4,224,1024]{2,1,0:T(8,128)(2,1)}), bf16[4,224,1024]{2,1,0:T(8,128)(2,1)S(1)}, u32[]{:S(2)}, u32[]{:S(2)}) async-start(bf16[4,224,1024]{2,1,0:T(8,128)(2,1)} %get-tuple-element.36), calls=%async_computation | async-start | bytes 3670016 | tf_op jit(solution)/shard_map/all_to_all | solution.py:368
  41.3 8.9 %collective-permute-start.2 = (bf16[2,64,896]{2,1,0:T(8,128)(2,1)}, bf16[2,64,896]{2,1,0:T(8,128)(2,1)}, u32[]{:S(2)}, u32[]{:S(2)}) collective-permute-start(bf16[2,64,896]{2,1,0:T(8,128)(2,1)} %copy-done.7), channel_id=1, source_target_pairs={{0,4},{4,0},{8,12},{12,8},{16,20},{20,16},{24,28},{28,24},{1,5},{5... | collective-permute-start | bytes 688136 | tf_op jit(solution)/shard_map/ppermute | solution.py:35
  41.8 12.2 %collective-permute-start.7 = (bf16[2,64,896]{2,1,0:T(8,128)(2,1)}, bf16[2,64,896]{2,1,0:T(8,128)(2,1)}, u32[]{:S(2)}, u32[]{:S(2)}) collective-permute-start(bf16[2,64,896]{2,1,0:T(8,128)(2,1)} %copy-done.11), channel_id=1, source_target_pairs={{0,4},{4,0},{8,12},{12,8},{16,20},{20,16},{24,28},{28,24},{1,5},{5... | collective-permute-start | bytes 688136 | tf_op jit(solution)/shard_map/ppermute | solution.py:35
  43.3 13.1 %collective-permute-start.8 = (bf16[2,64,896]{2,1,0:T(8,128)(2,1)}, bf16[2,64,896]{2,1,0:T(8,128)(2,1)}, u32[]{:S(2)}, u32[]{:S(2)}) collective-permute-start(bf16[2,64,896]{2,1,0:T(8,128)(2,1)} %collective-permute-done.6.refs_6_), channel_id=1, source_target_pairs={{0,4},{4,0},{8,12},{12,8},{16,20},{20,16},{24,28},{28,24},{1,5},{5... | collective-permute-start | bytes 688136 | tf_op jit(solution)/shard_map/ppermute | solution.py:35
  56.4 1.2 copy-start.5
  57.6 0.9 copy-start.6
  58.5 0.9 copy-start.8
  59.5 0.9 copy-start.10
  62.3 13.9 %copy-start.25 = (s32[256]{0:T(256)S(1)}, s32[256]{0:T(256)}, u32[]{:S(2)}) copy-start(s32[256]{0:T(256)} %param.19) | copy-start | bytes 3076
  76.2 11.1 %collective-permute-start.9 = (bf16[256,3584]{1,0:T(8,128)(2,1)}, bf16[256,3584]{1,0:T(8,128)(2,1)S(1)}, u32[]{:S(2)}, u32[]{:S(2)}) collective-permute-start(bf16[256,3584]{1,0:T(8,128)(2,1)} %get-tuple-element.34), channel_id=1, source_target_pairs={{0,1},{1,0},{2,3},{3,2},{4,5},{5,4},{6,7},{7,6},{8,9},{9,8},{10,11... | collective-permute-start | bytes 5505032 | tf_op jit(solution)/shard_map/ppermute | solution.py:47
  87.3 1.2 copy-start.20
  88.5 45.9 %all-to-all-start.1 = ((bf16[4,224,1024]{2,1,0:T(8,128)(2,1)}), bf16[4,224,1024]{2,1,0:T(8,128)(2,1)}, u32[]{:S(2)}, u32[]{:S(2)}) async-start(bf16[4,224,1024]{2,1,0:T(8,128)(2,1)} %get-tuple-element.37), calls=%async_computation.1 | async-start | bytes 3670016 | tf_op jit(solution)/shard_map/all_to_all | solution.py:368
  95.7 1.8 copy-start.17
  98.5 20.9 %collective-permute-start.10 = (bf16[128,3584]{1,0:T(8,128)(2,1)}, bf16[128,3584]{1,0:T(8,128)(2,1)S(1)}, u32[]{:S(2)}, u32[]{:S(2)}) collective-permute-start(bf16[128,3584]{1,0:T(8,128)(2,1)} %slice.241), channel_id=1, source_target_pairs={{0,2},{1,3},{2,0},{3,1},{4,6},{5,7},{6,4},{7,5},{8,10},{9,11},{10,... | collective-permute-start | bytes 2752520 | tf_op jit(solution)/shard_map/ppermute | solution.py:52
  101.8 17.6 %copy-start.18 = (f32[256,3584]{1,0:T(8,128)S(1)}, f32[256,3584]{1,0:T(8,128)}, u32[]{:S(2)}) copy-start(f32[256,3584]{1,0:T(8,128)} %copy-done.17) | copy-start | bytes 11010052
  102.1 18.2 %copy-start.23 = (f32[3584]{0:T(1024)S(1)}, f32[3584]{0:T(1024)}, u32[]{:S(2)}) copy-start(f32[3584]{0:T(1024)} %param.36) | copy-start | bytes 43012
  102.2 75.6 %collective-permute-start.16 = (bf16[4,224,1024]{2,1,0:T(8,128)(2,1)S(1)}, bf16[4,224,1024]{2,1,0:T(8,128)(2,1)}, u32[]{:S(2)}, u32[]{:S(2)}) collective-permute-start(bf16[4,224,1024]{2,1,0:T(8,128)(2,1)S(1)} %all-to-all-done.refs_0_), channel_id=1, source_target_pairs={{0,4},{4,0},{8,12},{12,8},{16,20},{20,16},{24,28},{28,24},{1,5},{5... | collective-permute-start | bytes 5505032 | tf_op jit(solution)/shard_map/ppermute | solution.py:35
  119.4 1.0 copy-start.19
  134.5 47.2 %collective-permute-start.17 = (bf16[4,224,1024]{2,1,0:T(8,128)(2,1)}, bf16[4,224,1024]{2,1,0:T(8,128)(2,1)S(1)}, u32[]{:S(2)}, u32[]{:S(2)}) collective-permute-start(bf16[4,224,1024]{2,1,0:T(8,128)(2,1)} %all-to-all-done.1.refs_2_), channel_id=1, source_target_pairs={{0,4},{4,0},{8,12},{12,8},{16,20},{20,16},{24,28},{28,24},{1,5},{5... | collective-permute-start | bytes 5505032 | tf_op jit(solution)/shard_map/ppermute | solution.py:35
  135.4 39.1 %collective-permute-start.14 = (bf16[128,3584]{1,0:T(8,128)(2,1)S(1)}, bf16[128,3584]{1,0:T(8,128)(2,1)}, u32[]{:S(2)}, u32[]{:S(2)}) collective-permute-start(bf16[128,3584]{1,0:T(8,128)(2,1)S(1)} %multiply_convert_fusion.refs_0_), channel_id=1, source_target_pairs={{0,16},{4,20},{8,24},{12,28},{16,0},{20,4},{24,8},{28,12},{1,17},{... | collective-permute-start | bytes 2752520 | tf_op jit(solution)/shard_map/ppermute | solution.py:30
  135.4 40.8 %collective-permute-start.18 = (bf16[128,3584]{1,0:T(8,128)(2,1)S(1)}, bf16[128,3584]{1,0:T(8,128)(2,1)}, u32[]{:S(2)}, u32[]{:S(2)}) collective-permute-start(bf16[128,3584]{1,0:T(8,128)(2,1)S(1)} %multiply_convert_fusion.refs_0_), channel_id=1, source_target_pairs={{0,8},{4,12},{8,0},{12,4},{16,24},{20,28},{24,16},{28,20},{1,9},{5... | collective-permute-start | bytes 2752520 | tf_op jit(solution)/shard_map/ppermute | solution.py:30
  137.5 38.8 %collective-permute-start.11 = (bf16[128,3584]{1,0:T(8,128)(2,1)S(1)}, bf16[128,3584]{1,0:T(8,128)(2,1)}, u32[]{:S(2)}, u32[]{:S(2)}) collective-permute-start(bf16[128,3584]{1,0:T(8,128)(2,1)S(1)} %multiply_convert_fusion.refs_0_), channel_id=1, source_target_pairs={{0,2},{1,3},{2,0},{3,1},{4,6},{5,7},{6,4},{7,5},{8,10},{9,11},{10,... | collective-permute-start | bytes 2752520 | tf_op jit(solution)/shard_map/ppermute | solution.py:52
  174.5 22.5 %collective-permute-start.15 = (bf16[128,3584]{1,0:T(8,128)(2,1)}, bf16[128,3584]{1,0:T(8,128)(2,1)}, u32[]{:S(2)}, u32[]{:S(2)}) collective-permute-start(bf16[128,3584]{1,0:T(8,128)(2,1)} %collective-permute-done.14.refs_0_), channel_id=1, source_target_pairs={{0,8},{4,12},{8,0},{12,4},{16,24},{20,28},{24,16},{28,20},{1,9},{5... | collective-permute-start | bytes 2752520 | tf_op jit(solution)/shard_map/ppermute | solution.py:30
  176.2 20.9 %collective-permute-start.12 = (bf16[128,3584]{1,0:T(8,128)(2,1)S(1)}, bf16[128,3584]{1,0:T(8,128)(2,1)}, u32[]{:S(2)}, u32[]{:S(2)}) collective-permute-start(bf16[128,3584]{1,0:T(8,128)(2,1)S(1)} %multiply_convert_fusion.refs_0_), channel_id=1, source_target_pairs={{0,1},{1,0},{2,3},{3,2},{4,5},{5,4},{6,7},{7,6},{8,9},{9,8},{10,11... | collective-permute-start | bytes 2752520 | tf_op jit(solution)/shard_map/ppermute | solution.py:47
  176.2 23.5 %collective-permute-start.19 = (bf16[128,3584]{1,0:T(8,128)(2,1)}, bf16[128,3584]{1,0:T(8,128)(2,1)}, u32[]{:S(2)}, u32[]{:S(2)}) collective-permute-start(bf16[128,3584]{1,0:T(8,128)(2,1)} %collective-permute-done.18.refs_0_), channel_id=1, source_target_pairs={{0,2},{1,3},{2,0},{3,1},{4,6},{5,7},{6,4},{7,5},{8,10},{9,11},{10,... | collective-permute-start | bytes 2752520 | tf_op jit(solution)/shard_map/ppermute | solution.py:52
  177.7 22.0 %collective-permute-start.20 = (bf16[128,3584]{1,0:T(8,128)(2,1)}, bf16[128,3584]{1,0:T(8,128)(2,1)}, u32[]{:S(2)}, u32[]{:S(2)}) collective-permute-start(bf16[128,3584]{1,0:T(8,128)(2,1)} %collective-permute-done.18.refs_0_), channel_id=1, source_target_pairs={{0,1},{1,0},{2,3},{3,2},{4,5},{5,4},{6,7},{7,6},{8,9},{9,8},{10,11... | collective-permute-start | bytes 2752520 | tf_op jit(solution)/shard_map/ppermute | solution.py:47
  181.7 1.3 copy-start.1
  182.9 36.4 %collective-permute-start.23 = (bf16[128,3584]{1,0:T(8,128)(2,1)}, bf16[128,3584]{1,0:T(8,128)(2,1)}, u32[]{:S(2)}, u32[]{:S(2)}) collective-permute-start(bf16[128,3584]{1,0:T(8,128)(2,1)} %collective-permute-done.14.refs_0_), channel_id=1, source_target_pairs={{0,2},{1,3},{2,0},{3,1},{4,6},{5,7},{6,4},{7,5},{8,10},{9,11},{10,... | collective-permute-start | bytes 2752520 | tf_op jit(solution)/shard_map/ppermute | solution.py:52
  183.5 1.5 copy-start.2
  190.7 2.9 copy-start
  197.1 25.9 %collective-permute-start.13 = (bf16[128,3584]{1,0:T(8,128)(2,1)}, bf16[128,3584]{1,0:T(8,128)(2,1)}, u32[]{:S(2)}, u32[]{:S(2)}) collective-permute-start(bf16[128,3584]{1,0:T(8,128)(2,1)} %collective-permute-done.11.refs_1_), channel_id=1, source_target_pairs={{0,1},{1,0},{2,3},{3,2},{4,5},{5,4},{6,7},{7,6},{8,9},{9,8},{10,11... | collective-permute-start | bytes 2752520 | tf_op jit(solution)/shard_map/ppermute | solution.py:47
  197.1 41.6 %collective-permute-start.27 = (bf16[128,3584]{1,0:T(8,128)(2,1)}, bf16[128,3584]{1,0:T(8,128)(2,1)}, u32[]{:S(2)}, u32[]{:S(2)}) collective-permute-start(bf16[128,3584]{1,0:T(8,128)(2,1)} %collective-permute-done.15.refs_0_), channel_id=1, source_target_pairs={{0,2},{1,3},{2,0},{3,1},{4,6},{5,7},{6,4},{7,5},{8,10},{9,11},{10,... | collective-permute-start | bytes 2752520 | tf_op jit(solution)/shard_map/ppermute | solution.py:52
  199.7 48.9 %collective-permute-start.21 = (bf16[128,3584]{1,0:T(8,128)(2,1)}, bf16[128,3584]{1,0:T(8,128)(2,1)}, u32[]{:S(2)}, u32[]{:S(2)}) collective-permute-start(bf16[128,3584]{1,0:T(8,128)(2,1)} %collective-permute-done.19.refs_1_), channel_id=1, source_target_pairs={{0,1},{1,0},{2,3},{3,2},{4,5},{5,4},{6,7},{7,6},{8,9},{9,8},{10,11... | collective-permute-start | bytes 2752520 | tf_op jit(solution)/shard_map/ppermute | solution.py:47
  199.8 59.4 %collective-permute-start.24 = (bf16[128,3584]{1,0:T(8,128)(2,1)}, bf16[128,3584]{1,0:T(8,128)(2,1)}, u32[]{:S(2)}, u32[]{:S(2)}) collective-permute-start(bf16[128,3584]{1,0:T(8,128)(2,1)} %collective-permute-done.14.refs_0_), channel_id=1, source_target_pairs={{0,1},{1,0},{2,3},{3,2},{4,5},{5,4},{6,7},{7,6},{8,9},{9,8},{10,11... | collective-permute-start | bytes 2752520 | tf_op jit(solution)/shard_map/ppermute | solution.py:47
  219.4 39.8 %collective-permute-start.25 = (bf16[128,3584]{1,0:T(8,128)(2,1)}, bf16[128,3584]{1,0:T(8,128)(2,1)}, u32[]{:S(2)}, u32[]{:S(2)}) collective-permute-start(bf16[128,3584]{1,0:T(8,128)(2,1)} %collective-permute-done.23.refs_1_), channel_id=1, source_target_pairs={{0,1},{1,0},{2,3},{3,2},{4,5},{5,4},{6,7},{7,6},{8,9},{9,8},{10,11... | collective-permute-start | bytes 2752520 | tf_op jit(solution)/shard_map/ppermute | solution.py:47
  222.9 47.8 %collective-permute-start.28 = (bf16[128,3584]{1,0:T(8,128)(2,1)}, bf16[128,3584]{1,0:T(8,128)(2,1)}, u32[]{:S(2)}, u32[]{:S(2)}) collective-permute-start(bf16[128,3584]{1,0:T(8,128)(2,1)} %collective-permute-done.15.refs_0_), channel_id=1, source_target_pairs={{0,1},{1,0},{2,3},{3,2},{4,5},{5,4},{6,7},{7,6},{8,9},{9,8},{10,11... | collective-permute-start | bytes 2752520 | tf_op jit(solution)/shard_map/ppermute | solution.py:47
  238.6 32.1 %collective-permute-start.29 = (bf16[128,3584]{1,0:T(8,128)(2,1)}, bf16[128,3584]{1,0:T(8,128)(2,1)}, u32[]{:S(2)}, u32[]{:S(2)}) collective-permute-start(bf16[128,3584]{1,0:T(8,128)(2,1)} %collective-permute-done.27.refs_1_), channel_id=1, source_target_pairs={{0,1},{1,0},{2,3},{3,2},{4,5},{5,4},{6,7},{7,6},{8,9},{9,8},{10,11... | collective-permute-start | bytes 2752520 | tf_op jit(solution)/shard_map/ppermute | solution.py:47
  258.8 25.5 %collective-permute-start.22 = (f32[8,2,2,2,64]{4,3,2,1,0:T(2,128)S(1)}, f32[8,2,2,2,64]{4,3,2,1,0:T(2,128)S(1)}, u32[]{:S(2)}, u32[]{:S(2)}) collective-permute-start(f32[8,2,2,2,64]{4,3,2,1,0:T(2,128)S(1)} %reshape.335), channel_id=1, source_target_pairs={{0,8},{4,12},{8,0},{12,4},{16,24},{20,28},{24,16},{28,20},{1,9},{5... | collective-permute-start | bytes 49160 | tf_op jit(solution)/shard_map/ppermute | solution.py:30
  269.4 22.9 %copy-start.26 = (s32[256]{0:T(256)S(1)}, s32[256]{0:T(256)}, u32[]{:S(2)}) copy-start(s32[256]{0:T(256)} %param.20) | copy-start | bytes 3076
  269.4 34.6 %copy-start.24 = (s32[48]{0:T(128)S(1)}, s32[48]{0:T(128)}, u32[]{:S(2)}) copy-start(s32[48]{0:T(128)} %param.21) | copy-start | bytes 580
  269.4 34.5 %copy-start.28 = (s32[48]{0:T(128)S(1)}, s32[48]{0:T(128)}, u32[]{:S(2)}) copy-start(s32[48]{0:T(128)} %param.22) | copy-start | bytes 580
  269.4 14.9 %collective-permute-start.26 = (f32[8,2,2,2,64]{4,3,2,1,0:T(2,128)S(1)}, f32[8,2,2,2,64]{4,3,2,1,0:T(2,128)S(1)}, u32[]{:S(2)}, u32[]{:S(2)}) collective-permute-start(f32[8,2,2,2,64]{4,3,2,1,0:T(2,128)S(1)} %reshape.336), channel_id=1, source_target_pairs={{0,16},{4,20},{8,24},{12,28},{16,0},{20,4},{24,8},{28,12},{1,17},{... | collective-permute-start | bytes 49160 | tf_op jit(solution)/shard_map/ppermute | solution.py:30
  281.1 5.8 %collective-permute-start.30 = (f32[8,2,2,2,64]{4,3,2,1,0:T(2,128)S(1)}, f32[8,2,2,2,64]{4,3,2,1,0:T(2,128)S(1)}, u32[]{:S(2)}, u32[]{:S(2)}) collective-permute-start(f32[8,2,2,2,64]{4,3,2,1,0:T(2,128)S(1)} %reshape.337), channel_id=1, source_target_pairs={{0,24},{4,28},{8,16},{12,20},{16,8},{20,12},{24,0},{28,4},{1,25},{... | collective-permute-start | bytes 49160 | tf_op jit(solution)/shard_map/ppermute | solution.py:30
  287.0 1.2 collective-permute-start.31
  288.3 3.8 %collective-permute-start.32 = (f32[3,2,2,2,64]{4,3,2,1,0:T(2,128)S(1)}, f32[3,2,2,2,64]{4,3,2,1,0:T(2,128)S(1)}, u32[]{:S(2)}, u32[]{:S(2)}) collective-permute-start(f32[3,2,2,2,64]{4,3,2,1,0:T(2,128)S(1)} %pad_maximum_fusion.1), channel_id=1, source_target_pairs={{0,2},{1,3},{2,0},{3,1},{4,6},{5,7},{6,4},{7,5},{8,10},{9,11},{10,... | collective-permute-start | bytes 18440 | tf_op jit(solution)/shard_map/ppermute | solution.py:52
  292.3 12.2 %copy-start.27 = (f32[256]{0:T(256)}, f32[256]{0:T(256)S(1)}, u32[]{:S(2)}) copy-start(f32[256]{0:T(256)S(1)} %convert_multiply_fusion) | copy-start | bytes 3076
  292.4 3.6 %collective-permute-start.33 = (f32[48]{0:T(128)S(1)}, f32[48]{0:T(128)S(1)}, u32[]{:S(2)}, u32[]{:S(2)}) collective-permute-start(f32[48]{0:T(128)S(1)} %convolution_bitcast_fusion), channel_id=1, source_target_pairs={{0,4},{4,0},{8,12},{12,8},{16,20},{20,16},{24,28},{28,24},{1,5},{5... | collective-permute-start | bytes 584 | tf_op jit(solution)/shard_map/ppermute | solution.py:516
  296.0 3.5 %collective-permute-start.34 = (f32[48]{0:T(128)S(1)}, f32[48]{0:T(128)S(1)}, u32[]{:S(2)}, u32[]{:S(2)}) collective-permute-start(f32[48]{0:T(128)S(1)} %add.339), channel_id=1, source_target_pairs={{0,8},{4,12},{8,0},{12,4},{16,24},{20,28},{24,16},{28,20},{1,9},{5... | collective-permute-start | bytes 584 | tf_op jit(solution)/shard_map/ppermute | solution.py:516
  299.5 4.4 %collective-permute-start.35 = (f32[48]{0:T(128)S(1)}, f32[48]{0:T(128)S(1)}, u32[]{:S(2)}, u32[]{:S(2)}) collective-permute-start(f32[48]{0:T(128)S(1)} %add.340), channel_id=1, source_target_pairs={{0,16},{4,20},{8,24},{12,28},{16,0},{20,4},{24,8},{28,12},{1,17},{... | collective-permute-start | bytes 584 | tf_op jit(solution)/shard_map/ppermute | solution.py:516
  (3 other events, 2.6 us)

commit v2 on v1

--- a/solution.py
+++ b/solution.py
@@ -35,6 +35,13 @@
     return lax.ppermute(x, "seq", [(i, partner(i, side, block, count)) for i in range(count)])
 
 
+def passed_on(up, down, step):
+    count = lax.axis_size("seq")
+    ups = [(i, i + SIDE) for i in range(count) if step - 1 <= place_of(i) < CHAIN - 1]
+    downs = [(i, i - SIDE) for i in range(count) if 0 < place_of(i) <= CHAIN - step]
+    return lax.ppermute(up, "seq", ups), lax.ppermute(down, "seq", downs)
+
+
 def chain_groups():
     count = lax.axis_size("seq")
     return [
@@ -60,6 +67,12 @@
     return lax.dot_general(a, b, (over, ((), ())), preferred_element_type=jnp.float32)
 
 
+def exact(a, b):
+    return lax.dot_general(
+        a, b, (((1,), (0,)), ((), ())), precision=highest, preferred_element_type=jnp.float32
+    )
+
+
 def head_pairs(head_count, head_dim):
     return [
         (first, slice(first * head_dim, min(first + 2, head_count) * head_dim))
@@ -75,8 +88,7 @@
 
 
 def local_kernel(
-    x_ref, b_ref, c_ref, step_ref, step_row_ref, log_ref, log_row_ref, start_ref,
-    skip_ref, out_ref, end_ref,
+    x_ref, b_ref, c_ref, step_ref, rate_ref, start_ref, skip_ref, out_ref, end_ref, decay_ref,
 ):
     tok_rows, inner = x_ref.shape
     head_count = step_ref.shape[1]
@@ -86,8 +98,11 @@
     col = lax.broadcasted_iota(jnp.int32, (tok_rows, tok_rows), 1)
     causal = (col >= start_ref[...]) & (col <= row)
     gram = jnp.where(causal, dot(c_ref[...], b_ref[...], ((1,), (1,))), 0.0)
-    logs = log_ref[...]
     steps = step_ref[...]
+    logs = exact(jnp.where(col <= row, 1.0, 0.0), -steps * rate_ref[...])
+    decay_ref[...] = logs - exact(jnp.where(col == start_ref[...] - 1, 1.0, 0.0), logs)
+    fill = jnp.zeros((tok_rows, 128 - 2 * head_count), jnp.float32)
+    as_rows = jnp.transpose(jnp.concatenate([logs, steps, fill], axis=1))
     last_log = logs[tok_rows - 1 :, :]
     last_start = start_ref[tok_rows - 1 :, :]
     place = lax.broadcasted_iota(jnp.int32, (tok_rows, 1), 0)
@@ -97,8 +112,8 @@
         x_pair = x_ref[:, span]
         sides = []
         for head in range(first, min(first + 2, head_count)):
-            gap = jnp.minimum(logs[:, head : head + 1] - log_row_ref[head : head + 1, :], 0.0)
-            mixing = jnp.exp(gap) * gram * step_row_ref[head : head + 1, :]
+            gap = jnp.minimum(logs[:, head : head + 1] - as_rows[head : head + 1, :], 0.0)
+            mixing = jnp.exp(gap) * gram * as_rows[head_count + head : head_count + head + 1, :]
             sides.append(dot(mixing.astype(jnp.bfloat16), x_pair))
         x_wide = x_pair.astype(jnp.float32)
         lane = lax.broadcasted_iota(jnp.int32, x_pair.shape, 1)
@@ -161,51 +176,51 @@
 
 def head_kernel(parts, limit_ref, *refs):
     row_refs = refs[:parts]
-    weight_ref, target_ref, out_ref, total = refs[parts:]
-    step = pl.program_id(0)
+    weight_ref, target_ref, out_ref, held, logits_ref, arrived = refs[parts:]
     each = row_refs[0].shape[0]
-
-    @pl.when(step == 0)
-    def _():
-        total[...] = jnp.zeros_like(total)
-
-    total[...] += dot(jnp.concatenate([rows[...] for rows in row_refs], axis=0), weight_ref[...])
-
-    @pl.when(step == pl.num_programs(0) - 1)
-    def _():
-        count = total.shape[1]
-        for part in range(parts):
-            rows = slice(part * each, (part + 1) * each)
-            column = lax.broadcasted_iota(jnp.int32, (each, count), 1)
-            in_range = column < limit_ref[0]
-            logits = jnp.where(in_range, total[rows, :], -jnp.inf)
-            top = jnp.max(logits, axis=1, keepdims=True)
-            sums = jnp.sum(jnp.exp(logits - top), axis=1, keepdims=True)
-            hit = (target_ref[rows, :] - limit_ref[1] == column) & in_range
-            target = jnp.sum(jnp.where(hit, logits, 0.0), axis=1, keepdims=True)
-            lane = lax.broadcasted_iota(jnp.int32, (each, 128), 1)
-            stats = jnp.where(lane == 0, top, jnp.where(lane == 1, sums, target))
-            out_ref[:, rows] = jnp.transpose(stats)[:8]
+    tiles, _, tile = held.shape
+    copies = [
+        pltpu.make_async_copy(
+            weight_ref.at[:, pl.ds(i * tile, tile)], held.at[i], arrived.at[i]
+        )
+        for i in range(tiles)
+    ]
+    for copy in copies:
+        copy.start()
+    spans = [slice(part * each, (part + 1) * each) for part in range(parts)]
+    for i in range(tiles):
+        copies[i].wait()
+        for rows, row_ref in zip(spans, row_refs):
+            logits_ref[rows, i * tile : (i + 1) * tile] = dot(row_ref[...], held[i])
+    for rows in spans:
+        logits = logits_ref[rows, :]
+        column = lax.broadcasted_iota(jnp.int32, logits.shape, 1)
+        in_range = column < limit_ref[0]
+        logits = jnp.where(in_range, logits, -jnp.inf)
+        top = jnp.max(logits, axis=1, keepdims=True)
+        sums = jnp.sum(jnp.exp(logits - top), axis=1, keepdims=True)
+        hit = (target_ref[rows, :] - limit_ref[1] == column) & in_range
+        target = jnp.sum(jnp.where(hit, logits, 0.0), axis=1, keepdims=True)
+        lane = lax.broadcasted_iota(jnp.int32, (each, 128), 1)
+        stats = jnp.where(lane == 0, top, jnp.where(lane == 1, sums, target))
+        out_ref[:, rows] = jnp.transpose(stats)[:8]
 
 
 def place_kernel(count, first_ref, *refs):
-    whole, held, arrived, left = refs[count:]
-    into, out = [], []
+    whole, arrived = refs[count:]
+    copies = []
     for i in range(count):
         blocks, size = refs[i].shape[:2]
-        into.append(pltpu.make_async_copy(refs[i], held.at[i], arrived.at[i]))
         for j in range(blocks):
             rows = pl.ds(pl.multiple_of(first_ref[i * blocks + j], 16), size)
-            out.append(
-                pltpu.make_async_copy(held.at[i, j], whole.at[rows, :], left.at[i * blocks + j])
+            copies.append(
+                pltpu.make_async_copy(
+                    refs[i].at[j], whole.at[rows, :], arrived.at[i * blocks + j]
+                )
             )
-    for copy in into:
+    for copy in copies:
         copy.start()
-    for i in range(count):
-        into[i].wait()
-        for copy in out[i * blocks : (i + 1) * blocks]:
-            copy.start()
-    for copy in out:
+    for copy in copies:
         copy.wait()
 
 
@@ -219,8 +234,13 @@
     return pl.CostEstimate(flops=flops, bytes_accessed=moved, transcendentals=exps)
 
 
-def whole_spec():
-    return pl.BlockSpec(memory_space=pltpu.VMEM)
+def whole(value):
+    return pl.BlockSpec(value.shape, lambda *_: (0,) * value.ndim)
+
+
+def across(x, by):
+    count = lax.axis_size("mp")
+    return lax.ppermute(x, "mp", [(i, (i + 2 * by) % count ^ 1) for i in range(count)])
 
 
 def shards(
@@ -275,9 +295,6 @@
     states = [held, turn(held, 1), turn(held, 2)]
     states.append(turn(states[2], 1))
     beside_held = beside(held)
-    targets = lax.all_gather(
-        scored_token_targets, "seq", axis_index_groups=chain_groups(), tiled=False
-    )
 
     first_row = seq_index * tok_rows
     offsets = jnp.arange(tok_rows, dtype=jnp.int32)
@@ -294,16 +311,21 @@
             for source in [seq_index] + [from_partner(side, block) for side, block in partners]
         ]
     )
+    last_rollout = (offsets >= start_local[-1]).astype(jnp.float32)
+    local_tail = -head_decay_rate * jnp.sum(
+        token_step_sizes * last_rollout[None, :, None], axis=1
+    )
+    next_one = [(i, i + 1) for i in range(seq_count - 1)]
+    tail = lax.ppermute(local_tail, "seq", next_one)
     pick = (holder_tok[:, None] == prompt_holder[None, :]).astype(jnp.float32)
     inherited = (start_local < 0).astype(jnp.float32)
-    neg_rates = -head_decay_rate
-    log_decay = jnp.cumsum(token_step_sizes * neg_rates[:, None, :], axis=1)
-    before = jnp.take(log_decay, jnp.maximum(start_local - 1, 0), axis=1)
-    before = jnp.where((start_local >= 1)[None, :, None], before, 0.0)
-
-    mixer_x, states[1], *beside_held = tied(mixer_input_x, states[1], *beside_held)
+    beside_next = beside(states[1])
+    mixer_x, states[1], tail, *beside_held = tied(
+        mixer_input_x, states[1], tail, *beside_held
+    )
+
     per_model = lambda *shape: pl.BlockSpec((None,) + shape, lambda m: (m,) + (0,) * len(shape))
-    local_out, local_end = pl.pallas_call(
+    local_out, local_end, decay = pl.pallas_call(
         local_kernel,
         grid=(models,),
         in_specs=[
@@ -311,16 +333,19 @@
             per_model(tok_rows, state_dim),
             per_model(tok_rows, state_dim),
             per_model(tok_rows, head_count),
-            per_model(head_count, tok_rows),
-            per_model(tok_rows, head_count),
-            per_model(head_count, tok_rows),
+            per_model(1, head_count),
             pl.BlockSpec((tok_rows, 1), lambda m: (0, 0)),
             per_model(1, head_count),
         ],
-        out_specs=[per_model(tok_rows, inner_local), per_model(state_dim, inner_local)],
+        out_specs=[
+            per_model(tok_rows, inner_local),
+            per_model(state_dim, inner_local),
+            per_model(tok_rows, head_count),
+        ],
         out_shape=[
             jax.ShapeDtypeStruct((models, tok_rows, inner_local), jnp.float32),
             jax.ShapeDtypeStruct((models, state_dim, inner_local), jnp.bfloat16),
+            jax.ShapeDtypeStruct((models, tok_rows, head_count), jnp.float32),
         ],
         compiler_params=pltpu.CompilerParams(vmem_limit_bytes=32 * 2**20),
         cost_estimate=cost(10**9, 8 * 2**20, 2 * 10**6),
@@ -330,20 +355,15 @@
         input_projection_b,
         output_projection_c,
         token_step_sizes,
-        jnp.swapaxes(token_step_sizes, 1, 2),
-        log_decay,
-        jnp.swapaxes(log_decay, 1, 2),
+        head_decay_rate[:, None, :],
         start_local[:, None],
         head_skip_scale[:, None, :],
     )
 
     hops = max(1, -(-(seq_count * tok_rows // 8) // tok_rows))
-    next_one = [(i, i + 1) for i in range(seq_count - 1)]
-    local_tail = log_decay[:, -1] - before[:, -1]
     arriving = lax.ppermute(local_end, "seq", next_one)
-    tail = lax.ppermute(local_tail, "seq", next_one)
     if hops > 1:
-        through = jnp.repeat(jnp.exp(log_decay[:, -1]), inner_local // head_count, axis=1)
+        through = jnp.repeat(jnp.exp(local_tail), inner_local // head_count, axis=1)
         through = through[:, None, :] * inherited[-1]
         for _ in range(hops - 1):
             moved = through * arriving.astype(jnp.float32) + local_end.astype(jnp.float32)
@@ -363,29 +383,43 @@
         cost_estimate=cost(0, 2 * vocab_head_weight.size * 2),
         name="split_head_columns",
     )(vocab_head_weight)
-    arriving, tail, states[2], states[3], *head = tied(arriving, tail, states[2], states[3], *head)
+    targets = jnp.stack([scored_token_targets, turn(scored_token_targets, 1)])
+    targets = jnp.concatenate([targets, turn(targets, 2)])
+    arriving, states[3], targets, *head = tied(arriving, states[3], targets, *head)
     came_head = [
         lax.all_to_all(head[cut], "seq", 0, 0, axis_index_groups=chain_groups())
         for cut in range(cuts)
     ]
 
-    prompts = [held] + beside_held
-    for state in states[1:]:
-        prompts += [state] + beside(state)
+    besides = [beside_held, beside_next, beside(states[2]), beside(states[3])]
+    prompts = []
+    for state, others in zip(states, besides):
+        prompts += [state] + list(others)
 
     quarter = jnp.arange(mp_count, dtype=jnp.int32)
     order = (quarter % 2 != core) * x_count + (quarter // 2 - x_index) % x_count
     order = order.astype(jnp.int32) * (models * share_rows)
     half = models * tok_rows // 2
     tile = 512 if width % 512 == 0 else width
+    resident = [
+        *prompts,
+        local_out,
+        output_projection_c,
+        pick,
+        inherited[:, None],
+        decay,
+        arriving,
+        tail[:, None, :],
+        mixer_gate_input,
+    ]
     kept, sent = pl.pallas_call(
         functools.partial(project_kernel, len(prompts)),
         grid=(width // tile,),
         in_specs=[pl.BlockSpec(memory_space=pltpu.SMEM)]
-        + [whole_spec()] * (len(prompts) + 8)
+        + [whole(value) for value in resident]
         + [
             pl.BlockSpec((inner_local, tile), lambda j: (0, j)),
-            whole_spec(),
+            whole(adapter_down_weight),
             pl.BlockSpec((adapter_up_weight.shape[0], tile), lambda j: (0, j)),
         ],
         out_specs=[pl.BlockSpec((half, tile), lambda j: (0, j))] * 2,
@@ -394,67 +428,30 @@
             pltpu.VMEM((models * tok_rows, inner_local), jnp.bfloat16),
             pltpu.VMEM((models * tok_rows, adapter_up_weight.shape[0]), jnp.bfloat16),
         ],
-        compiler_params=pltpu.CompilerParams(vmem_limit_bytes=48 * 2**20),
+        compiler_params=pltpu.CompilerParams(vmem_limit_bytes=56 * 2**20),
         cost_estimate=cost(
             2 * models * tok_rows * inner_local * width, 4 * inner_local * width, 2 * 10**6
         ),
         name="gate_and_project",
-    )(
-        order,
-        *prompts,
-        local_out,
-        output_projection_c,
-        pick,
-        inherited[:, None],
-        log_decay - before,
-        arriving,
-        tail[:, None, :],
-        mixer_gate_input,
-        shared_output_weight,
-        adapter_down_weight,
-        adapter_up_weight,
-    )
-
-    came, targets = tied(other_core(sent), targets)
+    )(order, *resident, shared_output_weight, adapter_down_weight, adapter_up_weight)
+
+    sent, came_head[0] = tied(sent, came_head[0])
+    came = other_core(sent)
     each = models * share_rows
-    chip_sum = kept.astype(jnp.float32) + came.astype(jnp.float32)
-    mixed = chip_sum[:each]
+
+    def chip_sum(by):
+        rows = slice(by * each, (by + 1) * each)
+        return kept[rows].astype(jnp.float32) + came[rows].astype(jnp.float32)
+
+    mixed = chip_sum(0)
     for by in range(1, x_count):
-        away = chip_sum[by * each : (by + 1) * each].astype(jnp.bfloat16)
-        mixed = mixed + along_x(away, by).astype(jnp.float32)
+        mixed = mixed + along_x(chip_sum(by).astype(jnp.bfloat16), by).astype(jnp.float32)
+    besides_head = [beside(came_head[0])]
+    mixed, came_head[-1], *besides_head[0] = tied(mixed, came_head[-1], *besides_head[0])
     own_rows = lax.dynamic_slice_in_dim(residual, mp_index * share_rows, share_rows, 0)
     hidden = jnp.transpose(own_rows, (1, 0, 2)).reshape(each, width).astype(jnp.float32) + mixed
     mean_sq = jnp.mean(hidden * hidden, axis=-1, keepdims=True)
     normed_own = (hidden * lax.rsqrt(mean_sq + 1e-05) * final_norm_scale).astype(jnp.bfloat16)
-
-    came_head[-1], _ = tied(came_head[-1], normed_own)
-    rows_of = [normed_own, turn(normed_own, 1), turn(normed_own, 2)]
-    pieces, firsts = [], []
-    for cut in range(cuts):
-        sources = [seq_index] + [from_partner(side, block) for side, block in partners]
-        pieces += [came_head[cut]] + beside(came_head[cut])
-        for source in sources:
-            first_of_chain = source - place_of(source) * SIDE
-            firsts += [
-                (first_of_chain + k * SIDE) * head_rows + cut * cut_rows for k in range(CHAIN)
-            ]
-    head_part = pl.pallas_call(
-        functools.partial(place_kernel, len(pieces)),
-        in_specs=[pl.BlockSpec(memory_space=pltpu.SMEM)]
-        + [pl.BlockSpec(memory_space=pl.ANY)] * len(pieces),
-        out_specs=pl.BlockSpec(memory_space=pl.ANY),
-        out_shape=jax.ShapeDtypeStruct((seq_count * head_rows, part), vocab_head_weight.dtype),
-        scratch_shapes=[
-            pltpu.VMEM((len(pieces), CHAIN, cut_rows, part), vocab_head_weight.dtype),
-            pltpu.SemaphoreType.DMA((len(pieces),)),
-            pltpu.SemaphoreType.DMA((len(pieces) * CHAIN,)),
-        ],
-        compiler_params=pltpu.CompilerParams(vmem_limit_bytes=16 * 2**20),
-        cost_estimate=cost(0, 4 * seq_count * head_rows * part),
-        name="place_head_rows",
-    )(jnp.stack(firsts).astype(jnp.int32), *pieces)
-    last_rows, head_part = tied(turn(rows_of[2], 1), head_part)
-    rows_of.append(last_rows)
 
     limit = jnp.stack(
         [
@@ -462,36 +459,131 @@
             mp_index * vocab_local + place * part,
         ]
     ).astype(jnp.int32)
-    depth = 512 if width % 512 == 0 else width
-    parts = mp_count
-    chain_stats = []
     mp_order = jnp.stack(
         [(x_index - k) % x_count * 2 + (core + other) % 2 for other in (0, 1) for k in range(x_count)]
     )
-    def head_stats(rows, targets):
-        near = [rows] + [along_x(rows, by) for by in range(1, x_count)]
-        all_rows = near + [other_core(value) for value in near]
-        targets = jnp.repeat(targets.reshape(mp_count, 1, share_rows)[mp_order], models, axis=1)
-        stats = pl.pallas_call(
-            functools.partial(head_kernel, parts),
-            grid=(width // depth,),
+
+    def words_of(targets):
+        targets = targets.reshape(CHAIN, mp_count, 1, share_rows)[:, mp_order]
+        targets = jnp.broadcast_to(targets, (CHAIN, mp_count, models, share_rows))
+        return targets.reshape(CHAIN, 2, x_count, each)
+
+    tiles = 2 if part % 256 == 0 else 1
+
+    def place_head():
+        pieces, firsts = [], []
+        for cut, others in enumerate(besides_head):
+            pieces += [came_head[cut]] + others
+            for source in [seq_index] + [from_partner(side, block) for side, block in partners]:
+                first_of_chain = source - place_of(source) * SIDE
+                firsts += [
+                    (first_of_chain + k * SIDE) * head_rows + cut * cut_rows for k in range(CHAIN)
+                ]
+        return pl.pallas_call(
+            functools.partial(place_kernel, len(pieces)),
             in_specs=[pl.BlockSpec(memory_space=pltpu.SMEM)]
-            + [pl.BlockSpec((each, depth), lambda j: (0, j))] * parts
-            + [pl.BlockSpec((depth, part), lambda j: (j, 0)), whole_spec()],
-            out_specs=whole_spec(),
-            out_shape=jax.ShapeDtypeStruct((8, parts * each), jnp.float32),
-            scratch_shapes=[pltpu.VMEM((parts * each, part), jnp.float32)],
-            compiler_params=pltpu.CompilerParams(vmem_limit_bytes=48 * 2**20),
+            + [pl.BlockSpec(memory_space=pl.ANY)] * len(pieces),
+            out_specs=pl.BlockSpec(memory_space=pltpu.VMEM),
+            out_shape=jax.ShapeDtypeStruct((seq_count * head_rows, part), vocab_head_weight.dtype),
+            scratch_shapes=[pltpu.SemaphoreType.DMA((len(pieces) * CHAIN,))],
+            compiler_params=pltpu.CompilerParams(vmem_limit_bytes=16 * 2**20),
+            cost_estimate=cost(0, 4 * seq_count * head_rows * part),
+            name="place_head_rows",
+        )(jnp.stack(firsts).astype(jnp.int32), *pieces)
+
+    def head_stats(head_part, rows, words):
+        count = len(rows)
+        words = words.reshape(count * each, 1)
+        stats_shape = jax.ShapeDtypeStruct((8, count * each), jnp.float32)
+        return pl.pallas_call(
+            functools.partial(head_kernel, count),
+            in_specs=[pl.BlockSpec(memory_space=pltpu.SMEM)]
+            + [pl.BlockSpec(memory_space=pltpu.VMEM)] * count
+            + [pl.BlockSpec(memory_space=pl.ANY), pl.BlockSpec(memory_space=pltpu.VMEM)],
+            out_specs=pl.BlockSpec(memory_space=pltpu.VMEM),
+            out_shape=stats_shape,
+            scratch_shapes=[
+                pltpu.VMEM((tiles, width, part // tiles), jnp.bfloat16),
+                pltpu.VMEM((count * each, part), jnp.float32),
+                pltpu.SemaphoreType.DMA((tiles,)),
+            ],
+            compiler_params=pltpu.CompilerParams(vmem_limit_bytes=56 * 2**20),
             cost_estimate=cost(
-                2 * parts * each * width * part, 2 * (parts * each + part) * width, parts * each * part
+                2 * count * each * width * part,
+                2 * (count * each + part) * width,
+                count * each * part,
             ),
             name="head_stats",
-        )(limit, *all_rows, head_part, targets.reshape(parts * each, 1))
-        return stats.reshape(8, 2, x_count, models, share_rows)
-
-    for k in range(CHAIN):
-        stats = head_stats(rows_of[k], targets[place ^ k])
-        chain_stats.append(stats if k == 0 else turn(stats, k))
+        )(limit, *rows, head_part, words).reshape(8, count, models, share_rows)
+
+    def both_cores(values):
+        return values + [other_core(value) for value in values]
+
+    def crossed(rows):
+        return [along_x(rows, by) for by in range(1, x_count)]
+
+    halves = [came_head[-1][: CHAIN // 2], came_head[-1][CHAIN // 2 :]] if cuts == 2 else []
+    blocks_of = [normed_own]
+    nears = [crossed(normed_own)]
+    up, down = normed_own, normed_own
+    ups, downs, late = [], [], []
+    words = words_of(targets)
+    for step in range(1, CHAIN):
+        up, down = passed_on(up, down, step)
+        count = len(nears[-1])
+        extra = []
+        if step <= len(halves):
+            late.append(beside(halves[step - 1]))
+            extra = late[-1]
+        if step == CHAIN - 2:
+            if cuts == 2:
+                besides_head.append([jnp.concatenate(both) for both in zip(late[0], late[1])])
+            extra = [place_head()]
+        elif step == CHAIN - 1:
+            rows = [both_cores([blocks_of[k]] + nears[k]) for k in (0, 1)]
+            extra = [head_stats(head_part, rows[0] + rows[1], words[:2])]
+        up, down, *came = tied(up, down, *nears[-1], *extra)
+        nears[-1], extra = came[:count], came[count:]
+        if step <= len(halves) and step < CHAIN - 2:
+            late[-1] = extra
+        elif step == CHAIN - 2:
+            head_part = extra[0]
+        elif step == CHAIN - 1:
+            early = extra[0]
+        ups.append(up)
+        downs.append(down)
+        if step == 1:
+            block = jnp.where(place % 2 == 1, up, down)
+        elif step == 2:
+            block = jnp.where(place >= 2, up, down)
+        else:
+            near = jnp.where(place == 1, downs[0], ups[0])
+            block = jnp.where(place == 0, down, jnp.where(place == 3, up, near))
+        blocks_of.append(block)
+        nears.append(crossed(block))
+
+    last = CHAIN - 1
+    middle = head_stats(
+        head_part,
+        both_cores([blocks_of[last - 1]] + nears[last - 1]) + both_cores([blocks_of[last]]),
+        jnp.concatenate([words[last - 1].reshape(-1, each), words[last, :, 0]]),
+    )
+    *nears[last], early, middle = tied(*nears[last], early, middle)
+    rest = head_stats(head_part, both_cores(nears[last]), words[last, :, 1:])
+    grid_shape = (8, 2, x_count, models, share_rows)
+    stats_of = [
+        early[:, :mp_count].reshape(grid_shape),
+        early[:, mp_count:].reshape(grid_shape),
+        middle[:, :mp_count].reshape(grid_shape),
+        jnp.concatenate(
+            [
+                middle[:, mp_count:].reshape(8, 2, 1, models, share_rows),
+                rest.reshape(8, 2, x_count - 1, models, share_rows),
+            ],
+            axis=2,
+        ),
+    ]
+    chain_stats = [stats_of[0]] + [turn(stats_of[k], k) for k in range(1, CHAIN)]
 
     def merged(several):
         top = functools.reduce(jnp.maximum, [stats[0] for stats in several])
@@ -499,10 +591,11 @@
         return jnp.stack([top, total, sum(stats[2] for stats in several)])
 
     stats = merged(chain_stats)
-    stats = merged([stats, other_core(stats)[:, ::-1]])
-    stats = merged(
-        [stats] + [jnp.roll(along_x(stats, by), by, axis=2) for by in range(1, x_count)]
-    )
+    several = [stats, other_core(stats)[:, ::-1]]
+    for by in range(1, x_count):
+        several.append(jnp.roll(along_x(stats, by), by, axis=2))
+        several.append(jnp.roll(across(stats, by)[:, ::-1], by, axis=2))
+    stats = merged(several)
     logprob = stats[2] - stats[0] - jnp.log(stats[1])
     delta = (logprob[:, :, 0] - logprob[:, :, 1]).reshape(mp_count, share_rows)
     token_delta = jnp.sum(
@@ -510,11 +603,8 @@
     ).reshape(tok_rows)
     token_delta = token_delta * valid.astype(jnp.float32)
     roll_sums = jnp.dot(token_delta, member_table.astype(jnp.float32), precision=highest)
-    distance = 1
-    while distance < seq_count:
-        pairs = [(i, i ^ distance) for i in range(seq_count)]
-        roll_sums = roll_sums + lax.ppermute(roll_sums, "seq", pairs)
-        distance *= 2
+    roll_sums = roll_sums + sum(turn(roll_sums, k) for k in range(1, CHAIN))
+    roll_sums = roll_sums + sum(beside(roll_sums))
     owner_sums = jnp.where(owners == seq_index, roll_sums / lengths.astype(jnp.float32), 0.0)
     return (owner_sums[None, :], token_delta)
 

time: 306 us -> 291 us (0.951)
  waiting for transfers between devices: 135 us -> 112 us
  starting transfers between devices: 46.2 us -> 64.7 us
  other arithmetic: 12.2 us -> 24.9 us
  blocking collectives: 11.1 us -> 0 us
  Pallas kernels: 67.7 us -> 59.6 us
  local copies, waits for them, and re-layouts: 30.6 us -> 26.8 us
    ppermute x9 -> x11, waiting for transfers between devices: 43.4 us -> 10.4 us  [turn(): return lax.ppermute(x, 'seq', [(i, turned(i, by)) for i in range(count)])]
    ppermute x6, waiting for transfers between devices: 53.5 us -> 26.6 us  [along_x(): lax.ppermute(x, 'mp', [(i, (i + 2 * by) % count) for i in range(count)])]
    ppermute x3 -> x7, waiting for transfers between devices: 8.97 us -> 22.2 us  [the longest x6 21.1 us: passed_on(): return (lax.ppermute(up, 'seq', ups), lax.ppermute(down, 'seq', downs))]
    ppermute x6 -> x8, waiting for transfers between devices: 15.9 us -> 28.9 us  [to_partner(): lax.ppermute(x, 'seq', [(i, partner(i, side, block, count)) for i in rang...]
    all_gather x1 -> x0, blocking collectives: 11.1 us -> none  [shards(): lax.all_gather(scored_token_targets, 'seq', axis_index_groups=chain_group...]
    pallas_call x5 -> x4, Pallas kernels: 46 us -> 36 us  [the longest x3 32.9 us: head_stats(): pl.pallas_call(functools.partial(head_kernel, count), in_specs=[pl.BlockS...]
    all_to_all x2, waiting for transfers between devices: 12.5 us -> 22 us  [shards(): lax.all_to_all(head[cut], 'seq', 0, 0, axis_index_groups=chain_groups())]
    ppermute x6 -> x8, starting transfers between devices: 6.03 us -> 15.1 us  [to_partner(): lax.ppermute(x, 'seq', [(i, partner(i, side, block, count)) for i in rang...]
  transfers between devices with their start and end apart: 38 -> 46, of which waited for: 18 -> 25; matrix products, arithmetic and copies ran while one was open for 8% -> 12% of each run, Pallas kernels for 22% -> 21%
where the time goes in v2:
time: 291 us; the launch traced here: 290 us
  waiting for transfers between devices  112 us (38%)
  starting transfers between devices  64.7 us (22%)
  Pallas kernels  59.6 us (20%)
  local copies, waits for them, and re-layouts  26.8 us (9%)
  other arithmetic  24.9 us (9%)
    pallas_call x3, Pallas kernels, head_stats(): pl.pallas_call(functools.partial(head_kernel, count), in_specs=[pl.BlockS...  32.9 us
    ppermute x8, waiting for transfers between devices, to_partner(): lax.ppermute(x, 'seq', [(i, partner(i, side, block, count)) for i in rang...  28.9 us
    ppermute x6, waiting for transfers between devices, along_x(): lax.ppermute(x, 'mp', [(i, (i + 2 * by) % count) for i in range(count)])  26.6 us
    all_to_all x2, waiting for transfers between devices, shards(): lax.all_to_all(head[cut], 'seq', 0, 0, axis_index_groups=chain_groups())  22 us
    ppermute x6, waiting for transfers between devices, passed_on(): return (lax.ppermute(up, 'seq', ups), lax.ppermute(down, 'seq', downs))  21.1 us
    ppermute x11, starting transfers between devices, turn(): return lax.ppermute(x, 'seq', [(i, turned(i, by)) for i in range(count)])  17.6 us
    ppermute x8, starting transfers between devices, to_partner(): lax.ppermute(x, 'seq', [(i, partner(i, side, block, count)) for i in rang...  15.1 us
    pallas_call x1, Pallas kernels, shards(): pl.pallas_call(functools.partial(project_kernel, len(prompts)), grid=(wid...  14.9 us
  transfers between devices with their start and end apart: 46, of which 25 were waited for; matrix products, arithmetic and copies ran while one was open for 12% of the time, Pallas kernels for 21%

profile of v2, /device:TPU:0, one launch (start us, length us, event | category | flops | bytes accessed | tf_op | source)
XLA Modules:
  0.0 289.9 jit_solution(7270615256134922096)
XLA Ops:
  1.9 3.1 %collective-permute-start = (bf16[2,64,896]{2,1,0:T(8,128)(2,1)S(1)}, bf16[2,64,896]{2,1,0:T(8,128)(2,1)S(1)}, u32[]{:S(2)}, u32[]{:S(2)}) collective-permute-start(bf16[2,64,896]{2,1,0:T(8,128)(2,1)S(1)} %copy.156.refs_0_), channel_id=1, source_target_pairs={{0,8},{4,12},{8,0},{12,4},{16,24},{20,28},{24,16},{28,20},{1,9},{5... | collective-permute-start | bytes 688136 | tf_op jit(solution)/shard_map/ppermute | solution.py:30
  5.0 1.5 collective-permute-start.2
  6.5 2.6 collective-permute-start.4
  14.4 2.4 collective-permute-start.1
  22.4 4.2 %local_tokens.1 = (f32[2,256,896]{2,1,0:T(8,128)S(1)}, bf16[2,64,896]{2,1,0:T(8,128)(2,1)S(1)}, f32[2,256,14]{2,1,0:T(8,128)S(1)}) custom-call(bf16[2,256,896]{2,1,0:T(8,128)(2,1)S(1)} %copy-done.5, bf16[2,256,64]{2,1,0:T(8,128)(2,1)S(1)} %copy.133.b_ref, bf16[2,256,64]{2,1,0:T(8,128)(2,1)S(1)} %copy.134.c_ref.refs_9_, f32[2,256,14]{2,1,0:T(8,128)S(1)} %copy.135.step_ref, ...), custom_call_target="tpu_custom_call" | custom-call | flops 1000000000 | bytes 8388608 | tf_op jit(solution)/shard_map/local_tokens/pallas_call | solution.py:328
  28.7 3.3 %collective-permute-start.6 = (bf16[2,64,896]{2,1,0:T(8,128)(2,1)S(1)}, bf16[2,64,896]{2,1,0:T(8,128)(2,1)S(1)}, u32[]{:S(2)}, u32[]{:S(2)}) collective-permute-start(bf16[2,64,896]{2,1,0:T(8,128)(2,1)S(1)} %get-tuple-element.41), channel_id=1, source_target_pairs={{0,4},{4,8},{8,12},{12,16},{16,20},{20,24},{24,28},{1,5},{5,9},{9,... | collective-permute-start | bytes 688136 | tf_op jit(solution)/shard_map/ppermute | solution.py:364
  32.5 1.6 collective-permute-start.8
  34.1 4.0 %collective-permute-done.8 = s32[256]{0:T(256)S(1)} collective-permute-done((s32[256]{0:T(256)S(1)}, s32[256]{0:T(256)S(1)}, u32[]{:S(2)}, u32[]{:S(2)}) %collective-permute-start.8) | collective-permute-done | bytes 1056 | tf_op jit(solution)/shard_map/ppermute | solution.py:30
  38.5 4.4 %split_head_columns.1 = (bf16[4,224,1024]{2,1,0:T(8,128)(2,1)}, bf16[4,224,1024]{2,1,0:T(8,128)(2,1)}) custom-call(bf16[448,4000]{1,0:T(8,128)(2,1)} %head_ref.1), custom_call_target="tpu_custom_call" | custom-call | bytes 7168000 | tf_op jit(solution)/shard_map/split_head_columns/pallas_call | solution.py:377
  43.7 4.4 %all-to-all-start = ((bf16[4,224,1024]{2,1,0:T(8,128)(2,1)}), bf16[4,224,1024]{2,1,0:T(8,128)(2,1)}, u32[]{:S(2)}, u32[]{:S(2)}) async-start(bf16[4,224,1024]{2,1,0:T(8,128)(2,1)} %get-tuple-element.51), calls=%async_computation | async-start | bytes 3670016 | tf_op jit(solution)/shard_map/all_to_all | solution.py:390
  49.5 4.5 %collective-permute-start.5 = (bf16[2,64,896]{2,1,0:T(8,128)(2,1)S(1)}, bf16[2,64,896]{2,1,0:T(8,128)(2,1)S(1)}, u32[]{:S(2)}, u32[]{:S(2)}) collective-permute-start(bf16[2,64,896]{2,1,0:T(8,128)(2,1)S(1)} %collective-permute-done.4.refs_4_), channel_id=1, source_target_pairs={{0,4},{4,0},{8,12},{12,8},{16,20},{20,16},{24,28},{28,24},{1,5},{5... | collective-permute-start | bytes 688136 | tf_op jit(solution)/shard_map/ppermute | solution.py:35
  54.0 2.0 collective-permute-start.10
  57.3 3.2 %collective-permute-done.5.refs_5_ = bf16[2,64,896]{2,1,0:T(8,128)(2,1)S(1)} collective-permute-done((bf16[2,64,896]{2,1,0:T(8,128)(2,1)S(1)}, bf16[2,64,896]{2,1,0:T(8,128)(2,1)S(1)}, u32[]{:S(2)}, u32[]{:S(2)}) %collective-permute-start.5) | collective-permute-done | bytes 229408 | tf_op jit(solution)/shard_map/ppermute | solution.py:35
  60.5 2.7 collective-permute-done.3.refs_3_
  63.2 2.5 collective-permute-done.10.refs_7_
  66.3 14.9 %gate_and_project.1 = (bf16[256,3584]{1,0:T(8,128)(2,1)}, bf16[256,3584]{1,0:T(8,128)(2,1)}) custom-call(s32[4]{0:T(128)} %fusion.31.order_ref, bf16[2,64,896]{2,1,0:T(8,128)(2,1)} %copy-done.13, bf16[2,64,896]{2,1,0:T(8,128)(2,1)} %copy-done.15, bf16[2,64,896]{2,1,0:T(8,128)(2,1)} %copy-done.14, bf16[2,64,896]{2,1,0:T(8,128)(2,1)} %copy-done.20, ...), custom_call_target="tpu_custom_call" | custom-call | flops 3288334336 | bytes 12845056 | tf_op jit(solution)/shard_map/gate_and_project/pallas_call | solution.py:415
  81.2 7.0 %all-to-all-done.refs_0_ = bf16[4,224,1024]{2,1,0:T(8,128)(2,1)} async-done(((bf16[4,224,1024]{2,1,0:T(8,128)(2,1)}), bf16[4,224,1024]{2,1,0:T(8,128)(2,1)}, u32[]{:S(2)}, u32[]{:S(2)}) %all-to-all-start) | async-done | bytes 1835040 | tf_op jit(solution)/shard_map/all_to_all | solution.py:390
  88.2 3.6 %all-to-all-start.1 = ((bf16[4,224,1024]{2,1,0:T(8,128)(2,1)}), bf16[4,224,1024]{2,1,0:T(8,128)(2,1)S(1)}, u32[]{:S(2)}, u32[]{:S(2)}) async-start(bf16[4,224,1024]{2,1,0:T(8,128)(2,1)} %get-tuple-element.53), calls=%async_computation.1 | async-start | bytes 3670016 | tf_op jit(solution)/shard_map/all_to_all | solution.py:390
  92.3 2.6 add_convert_fusion
  94.9 1.5 collective-permute-start.12
  96.4 3.6 %collective-permute-start.13 = (bf16[4,224,1024]{2,1,0:T(8,128)(2,1)}, bf16[4,224,1024]{2,1,0:T(8,128)(2,1)}, u32[]{:S(2)}, u32[]{:S(2)}) collective-permute-start(bf16[4,224,1024]{2,1,0:T(8,128)(2,1)} %all-to-all-done.refs_0_), channel_id=1, source_target_pairs={{0,4},{4,0},{8,12},{12,8},{16,20},{20,16},{24,28},{28,24},{1,5},{5... | collective-permute-start | bytes 5505032 | tf_op jit(solution)/shard_map/ppermute | solution.py:35
  100.0 1.8 convert_bitcast_fusion
  101.8 1.6 copy.129
  103.4 14.1 %collective-permute-done.12 = bf16[128,3584]{1,0:T(8,128)(2,1)S(1)} collective-permute-done((bf16[128,3584]{1,0:T(8,128)(2,1)}, bf16[128,3584]{1,0:T(8,128)(2,1)S(1)}, u32[]{:S(2)}, u32[]{:S(2)}) %collective-permute-start.12) | collective-permute-done | bytes 917536 | tf_op jit(solution)/shard_map/ppermute | solution.py:59
  117.5 2.8 convert_add_fusion
  120.3 15.0 %all-to-all-done.1.refs_2_ = bf16[4,224,1024]{2,1,0:T(8,128)(2,1)S(1)} async-done(((bf16[4,224,1024]{2,1,0:T(8,128)(2,1)}), bf16[4,224,1024]{2,1,0:T(8,128)(2,1)S(1)}, u32[]{:S(2)}, u32[]{:S(2)}) %all-to-all-start.1) | async-done | bytes 1835040 | tf_op jit(solution)/shard_map/all_to_all | solution.py:390
  135.3 5.1 %collective-permute-done.13.refs_1_ = bf16[4,224,1024]{2,1,0:T(8,128)(2,1)} collective-permute-done((bf16[4,224,1024]{2,1,0:T(8,128)(2,1)}, bf16[4,224,1024]{2,1,0:T(8,128)(2,1)}, u32[]{:S(2)}, u32[]{:S(2)}) %collective-permute-start.13) | collective-permute-done | bytes 1835040 | tf_op jit(solution)/shard_map/ppermute | solution.py:35
  140.3 2.3 multiply_reduce_fusion
  144.0 3.5 %collective-permute-start.14 = (bf16[128,3584]{1,0:T(8,128)(2,1)}, bf16[128,3584]{1,0:T(8,128)(2,1)S(1)}, u32[]{:S(2)}, u32[]{:S(2)}) collective-permute-start(bf16[128,3584]{1,0:T(8,128)(2,1)} %multiply_convert_fusion.refs_0_), channel_id=1, source_target_pairs={{0,8},{4,12},{8,16},{12,20},{16,24},{20,28},{1,9},{5,13},{9,17},{1... | collective-permute-start | bytes 2752520 | tf_op jit(solution)/shard_map/ppermute | solution.py:42
  147.5 1.3 collective-permute-start.15
  149.4 1.4 fusion.33
  150.8 1.7 collective-permute-start.17
  152.8 14.1 %collective-permute-done.14 = bf16[128,3584]{1,0:T(8,128)(2,1)S(1)} collective-permute-done((bf16[128,3584]{1,0:T(8,128)(2,1)}, bf16[128,3584]{1,0:T(8,128)(2,1)S(1)}, u32[]{:S(2)}, u32[]{:S(2)}) %collective-permute-start.14) | collective-permute-done | bytes 917536 | tf_op jit(solution)/shard_map/ppermute | solution.py:42
  166.9 4.2 %collective-permute-done.15 = bf16[128,3584]{1,0:T(8,128)(2,1)} collective-permute-done((bf16[128,3584]{1,0:T(8,128)(2,1)}, bf16[128,3584]{1,0:T(8,128)(2,1)}, u32[]{:S(2)}, u32[]{:S(2)}) %collective-permute-start.15) | collective-permute-done | bytes 917536 | tf_op jit(solution)/shard_map/ppermute | solution.py:42
  171.1 3.3 %collective-permute-done.17 = bf16[2,224,1024]{2,1,0:T(8,128)(2,1)} collective-permute-done((bf16[2,224,1024]{2,1,0:T(8,128)(2,1)}, bf16[2,224,1024]{2,1,0:T(8,128)(2,1)}, u32[]{:S(2)}, u32[]{:S(2)}) %collective-permute-start.17) | collective-permute-done | bytes 917536 | tf_op jit(solution)/shard_map/ppermute | solution.py:35
  174.4 2.3 broadcast_select_fusion.1.refs_4_
  176.7 1.5 collective-permute-start.20
  178.2 1.6 collective-permute-start.18
  179.7 1.3 collective-permute-start.19
  181.9 10.0 %collective-permute-done.21 = bf16[2,224,1024]{2,1,0:T(8,128)(2,1)} collective-permute-done((bf16[2,224,1024]{2,1,0:T(8,128)(2,1)}, bf16[2,224,1024]{2,1,0:T(8,128)(2,1)}, u32[]{:S(2)}, u32[]{:S(2)}) %collective-permute-start.21) | collective-permute-done | bytes 917536 | tf_op jit(solution)/shard_map/ppermute | solution.py:35
  191.9 1.6 pad_maximum_fusion.refs_3_
  193.5 3.1 %place_head_rows.1.refs_8_.refs_6_.refs_2_ = bf16[3584,1024]{1,0:T(8,128)(2,1)S(1)} custom-call(s32[16]{0:T(128)S(1)} %stack.160.first_ref, bf16[4,224,1024]{2,1,0:T(8,128)(2,1)} %all-to-all-done.refs_0_, bf16[4,224,1024]{2,1,0:T(8,128)(2,1)} %collective-permute-done.13.refs_1_, bf16[4,224,1024]{2,1,0:T(8,128)(2,1)S(1)} %all-to-all-done.1.refs_2_, ...), custom_call_target="tpu_custom_call" | custom-call | bytes 14680064 | tf_op jit(solution)/shard_map/place_head_rows/pallas_call | solution.py:482
  196.6 2.9 copy-done
  200.1 2.3 collective-permute-done.19
  203.1 1.3 broadcast_select_fusion.refs_0_
  204.4 1.5 collective-permute-start.23
  207.5 1.3 reshape.355.refs_9_
  209.4 14.3 %head_stats.3 = f32[8,1024]{1,0:T(8,128)} custom-call(s32[2]{0:T(128)} %pad_add_fusion.3.limit_ref, bf16[128,3584]{1,0:T(8,128)(2,1)} %multiply_convert_fusion.refs_0_, bf16[128,3584]{1,0:T(8,128)(2,1)} %collective-permute-done.16.refs_1_, bf16[128,3584]{1,0:T(8,128)(2,1)} %copy-done.28, bf16[128,3584]{1,0:T(8,128)(2,1)} %collective-permute-done.26.refs_3_, ...), custom_call_target="tpu_custom_call" | custom-call | flops 7516192768 | bytes 14680064 | tf_op jit(solution)/shard_map/head_stats/pallas_call | solution.py:498
  224.5 4.3 %collective-permute-done.24.refs_1_ = bf16[128,3584]{1,0:T(8,128)(2,1)} collective-permute-done((bf16[128,3584]{1,0:T(8,128)(2,1)S(1)}, bf16[128,3584]{1,0:T(8,128)(2,1)}, u32[]{:S(2)}, u32[]{:S(2)}) %collective-permute-start.24) | collective-permute-done | bytes 917536 | tf_op jit(solution)/shard_map/ppermute | solution.py:59
  229.4 2.3 select_select_fusion.refs_4_
  234.5 1.3 collective-permute-done.31.refs_3_
  235.8 12.0 %head_stats.4 = f32[8,768]{1,0:T(8,128)} custom-call(s32[2]{0:T(128)} %pad_add_fusion.3.limit_ref, bf16[128,3584]{1,0:T(8,128)(2,1)} %copy-done.10, bf16[128,3584]{1,0:T(8,128)(2,1)} %collective-permute-done.24.refs_1_, bf16[128,3584]{1,0:T(8,128)(2,1)} %collective-permute-done.30.refs_2_, bf16[128,3584]{1,0:T(8,128)(2,1)} %collective-permute-done.31.refs_3_, ...), custom_call_target="tpu_custom_call" | custom-call | flops 5637144576 | bytes 12845056 | tf_op jit(solution)/shard_map/head_stats/pallas_call | solution.py:498
  248.7 6.0 %collective-permute-done.29.refs_0_ = bf16[128,3584]{1,0:T(8,128)(2,1)S(1)} collective-permute-done((bf16[128,3584]{1,0:T(8,128)(2,1)}, bf16[128,3584]{1,0:T(8,128)(2,1)S(1)}, u32[]{:S(2)}, u32[]{:S(2)}) %collective-permute-start.29) | collective-permute-done | bytes 917536 | tf_op jit(solution)/shard_map/ppermute | solution.py:59
  255.7 2.6 collective-permute-start.33
  259.5 6.7 %head_stats.5 = f32[8,256]{1,0:T(8,128)} custom-call(s32[2]{0:T(128)} %pad_add_fusion.3.limit_ref, bf16[128,3584]{1,0:T(8,128)(2,1)} %copy-done.11, bf16[128,3584]{1,0:T(8,128)(2,1)} %copy-done.12, bf16[3584,1024]{1,0:T(8,128)(2,1)} %copy-done, s32[256,1]{1,0:T(8,128)} %copy.154.refs_3_), custom_call_target="tpu_custom_call" | custom-call | flops 1879048192 | bytes 9175040 | tf_op jit(solution)/shard_map/head_stats/pallas_call | solution.py:498
  266.9 2.3 collective-permute-start.36
  269.3 3.4 %collective-permute-done.36 = f32[8,2,2,2,64]{4,3,2,1,0:T(2,128)S(1)} collective-permute-done((f32[8,2,2,2,64]{4,3,2,1,0:T(2,128)S(1)}, f32[8,2,2,2,64]{4,3,2,1,0:T(2,128)S(1)}, u32[]{:S(2)}, u32[]{:S(2)}) %collective-permute-start.36) | collective-permute-done | bytes 16416 | tf_op jit(solution)/shard_map/ppermute | solution.py:30
  272.9 1.6 collective-permute-start.37
  276.1 2.1 collective-permute-done.38
  278.7 1.8 collective-permute-start.41
  280.5 2.4 collective-permute-start.42
  283.2 2.7 collective-permute-done.42
  285.9 1.4 collective-permute-start.43
  287.3 2.1 collective-permute-done.43
  (182 shorter events, 36.7 us)
Async XLA Ops:
  1.9 24.8 %copy-start.13 = (bf16[2,64,896]{2,1,0:T(8,128)(2,1)}, bf16[2,64,896]{2,1,0:T(8,128)(2,1)S(1)}, u32[]{:S(2)}) copy-start(bf16[2,64,896]{2,1,0:T(8,128)(2,1)S(1)} %copy.156.refs_0_) | copy-start | bytes 688132
  1.9 18.0 %collective-permute-start = (bf16[2,64,896]{2,1,0:T(8,128)(2,1)S(1)}, bf16[2,64,896]{2,1,0:T(8,128)(2,1)S(1)}, u32[]{:S(2)}, u32[]{:S(2)}) collective-permute-start(bf16[2,64,896]{2,1,0:T(8,128)(2,1)S(1)} %copy.156.refs_0_), channel_id=1, source_target_pairs={{0,8},{4,12},{8,0},{12,4},{16,24},{20,28},{24,16},{28,20},{1,9},{5... | collective-permute-start | bytes 688136 | tf_op jit(solution)/shard_map/ppermute | solution.py:30
  5.0 14.9 %collective-permute-start.2 = (bf16[2,64,896]{2,1,0:T(8,128)(2,1)S(1)}, bf16[2,64,896]{2,1,0:T(8,128)(2,1)S(1)}, u32[]{:S(2)}, u32[]{:S(2)}) collective-permute-start(bf16[2,64,896]{2,1,0:T(8,128)(2,1)S(1)} %copy.156.refs_0_), channel_id=1, source_target_pairs={{0,4},{4,0},{8,12},{12,8},{16,20},{20,16},{24,28},{28,24},{1,5},{5... | collective-permute-start | bytes 688136 | tf_op jit(solution)/shard_map/ppermute | solution.py:35
  6.5 25.5 %collective-permute-start.4 = (bf16[2,64,896]{2,1,0:T(8,128)(2,1)S(1)}, bf16[2,64,896]{2,1,0:T(8,128)(2,1)S(1)}, u32[]{:S(2)}, u32[]{:S(2)}) collective-permute-start(bf16[2,64,896]{2,1,0:T(8,128)(2,1)S(1)} %copy.156.refs_0_), channel_id=1, source_target_pairs={{0,16},{4,20},{8,24},{12,28},{16,0},{20,4},{24,8},{28,12},{1,17},{... | collective-permute-start | bytes 688136 | tf_op jit(solution)/shard_map/ppermute | solution.py:30
  14.4 5.4 %collective-permute-start.1 = (f32[2,14]{0,1:T(8,128)S(1)}, f32[2,14]{0,1:T(8,128)S(1)}, u32[]{:S(2)}, u32[]{:S(2)}) collective-permute-start(f32[2,14]{0,1:T(8,128)S(1)} %negate_multiply_fusion), channel_id=1, source_target_pairs={{0,4},{4,8},{8,12},{12,16},{16,20},{20,24},{24,28},{1,5},{5,9},{9,... | collective-permute-start | bytes 344 | tf_op jit(solution)/shard_map/ppermute | solution.py:319
  18.8 7.9 %copy-start.2 = (bf16[2,256,64]{2,1,0:T(8,128)(2,1)}, bf16[2,256,64]{2,1,0:T(8,128)(2,1)S(1)}, u32[]{:S(2)}) copy-start(bf16[2,256,64]{2,1,0:T(8,128)(2,1)S(1)} %copy.134.c_ref.refs_9_) | copy-start | bytes 196612
  19.8 34.1 %copy-start.14 = (bf16[2,64,896]{2,1,0:T(8,128)(2,1)}, bf16[2,64,896]{2,1,0:T(8,128)(2,1)S(1)}, u32[]{:S(2)}) copy-start(bf16[2,64,896]{2,1,0:T(8,128)(2,1)S(1)} %collective-permute-done.refs_2_) | copy-start | bytes 688132
  19.9 6.9 %copy-start.15 = (bf16[2,64,896]{2,1,0:T(8,128)(2,1)}, bf16[2,64,896]{2,1,0:T(8,128)(2,1)S(1)}, u32[]{:S(2)}) copy-start(bf16[2,64,896]{2,1,0:T(8,128)(2,1)S(1)} %collective-permute-done.2.refs_1_) | copy-start | bytes 688132
  22.4 10.1 %copy-start.23 = (s32[256]{0:T(256)S(1)}, s32[256]{0:T(256)}, u32[]{:S(2)}) copy-start(s32[256]{0:T(256)} %param.19) | copy-start | bytes 3076
  28.7 14.3 %collective-permute-start.6 = (bf16[2,64,896]{2,1,0:T(8,128)(2,1)S(1)}, bf16[2,64,896]{2,1,0:T(8,128)(2,1)S(1)}, u32[]{:S(2)}, u32[]{:S(2)}) collective-permute-start(bf16[2,64,896]{2,1,0:T(8,128)(2,1)S(1)} %get-tuple-element.41), channel_id=1, source_target_pairs={{0,4},{4,8},{8,12},{12,16},{16,20},{20,24},{24,28},{1,5},{5,9},{9,... | collective-permute-start | bytes 688136 | tf_op jit(solution)/shard_map/ppermute | solution.py:364
  32.0 17.5 %copy-start.16 = (bf16[2,64,896]{2,1,0:T(8,128)(2,1)}, bf16[2,64,896]{2,1,0:T(8,128)(2,1)S(1)}, u32[]{:S(2)}) copy-start(bf16[2,64,896]{2,1,0:T(8,128)(2,1)S(1)} %collective-permute-done.4.refs_4_) | copy-start | bytes 688132
  32.0 10.9 %collective-permute-start.7 = (bf16[2,64,896]{2,1,0:T(8,128)(2,1)S(1)}, bf16[2,64,896]{2,1,0:T(8,128)(2,1)S(1)}, u32[]{:S(2)}, u32[]{:S(2)}) collective-permute-start(bf16[2,64,896]{2,1,0:T(8,128)(2,1)S(1)} %collective-permute-done.4.refs_4_), channel_id=1, source_target_pairs={{0,8},{4,12},{8,0},{12,4},{16,24},{20,28},{24,16},{28,20},{1,9},{5... | collective-permute-start | bytes 688136 | tf_op jit(solution)/shard_map/ppermute | solution.py:30
  32.5 5.6 %collective-permute-start.8 = (s32[256]{0:T(256)S(1)}, s32[256]{0:T(256)S(1)}, u32[]{:S(2)}, u32[]{:S(2)}) collective-permute-start(s32[256]{0:T(256)S(1)} %copy-done.23), channel_id=1, source_target_pairs={{0,8},{4,12},{8,0},{12,4},{16,24},{20,28},{24,16},{28,20},{1,9},{5... | collective-permute-start | bytes 3080 | tf_op jit(solution)/shard_map/ppermute | solution.py:30
  38.2 4.8 %collective-permute-start.9 = (s32[2,256]{1,0:T(2,128)S(1)}, s32[2,256]{1,0:T(2,128)S(1)}, u32[]{:S(2)}, u32[]{:S(2)}) collective-permute-start(s32[2,256]{1,0:T(2,128)S(1)} %pad_add_fusion.1), channel_id=1, source_target_pairs={{0,16},{4,20},{8,24},{12,28},{16,0},{20,4},{24,8},{28,12},{1,17},{... | collective-permute-start | bytes 6152 | tf_op jit(solution)/shard_map/ppermute | solution.py:30
  43.0 11.1 %copy-start.18 = (bf16[2,64,896]{2,1,0:T(8,128)(2,1)}, bf16[2,64,896]{2,1,0:T(8,128)(2,1)S(1)}, u32[]{:S(2)}) copy-start(bf16[2,64,896]{2,1,0:T(8,128)(2,1)S(1)} %collective-permute-done.7.refs_6_) | copy-start | bytes 688132
  43.7 44.5 %all-to-all-start = ((bf16[4,224,1024]{2,1,0:T(8,128)(2,1)}), bf16[4,224,1024]{2,1,0:T(8,128)(2,1)}, u32[]{:S(2)}, u32[]{:S(2)}) async-start(bf16[4,224,1024]{2,1,0:T(8,128)(2,1)} %get-tuple-element.51), calls=%async_computation | async-start | bytes 3670016 | tf_op jit(solution)/shard_map/all_to_all | solution.py:390
  49.5 11.0 %collective-permute-start.5 = (bf16[2,64,896]{2,1,0:T(8,128)(2,1)S(1)}, bf16[2,64,896]{2,1,0:T(8,128)(2,1)S(1)}, u32[]{:S(2)}, u32[]{:S(2)}) collective-permute-start(bf16[2,64,896]{2,1,0:T(8,128)(2,1)S(1)} %collective-permute-done.4.refs_4_), channel_id=1, source_target_pairs={{0,4},{4,0},{8,12},{12,8},{16,20},{20,16},{24,28},{28,24},{1,5},{5... | collective-permute-start | bytes 688136 | tf_op jit(solution)/shard_map/ppermute | solution.py:35
  54.0 9.2 %collective-permute-start.3 = (bf16[2,64,896]{2,1,0:T(8,128)(2,1)S(1)}, bf16[2,64,896]{2,1,0:T(8,128)(2,1)S(1)}, u32[]{:S(2)}, u32[]{:S(2)}) collective-permute-start(bf16[2,64,896]{2,1,0:T(8,128)(2,1)S(1)} %collective-permute-done.refs_2_), channel_id=1, source_target_pairs={{0,4},{4,0},{8,12},{12,8},{16,20},{20,16},{24,28},{28,24},{1,5},{5... | collective-permute-start | bytes 688136 | tf_op jit(solution)/shard_map/ppermute | solution.py:35
  54.0 11.6 %collective-permute-start.10 = (bf16[2,64,896]{2,1,0:T(8,128)(2,1)S(1)}, bf16[2,64,896]{2,1,0:T(8,128)(2,1)S(1)}, u32[]{:S(2)}, u32[]{:S(2)}) collective-permute-start(bf16[2,64,896]{2,1,0:T(8,128)(2,1)S(1)} %collective-permute-done.7.refs_6_), channel_id=1, source_target_pairs={{0,4},{4,0},{8,12},{12,8},{16,20},{20,16},{24,28},{28,24},{1,5},{5... | collective-permute-start | bytes 688136 | tf_op jit(solution)/shard_map/ppermute | solution.py:35
  60.5 5.1 %copy-start.19 = (bf16[2,64,896]{2,1,0:T(8,128)(2,1)}, bf16[2,64,896]{2,1,0:T(8,128)(2,1)S(1)}, u32[]{:S(2)}) copy-start(bf16[2,64,896]{2,1,0:T(8,128)(2,1)S(1)} %collective-permute-done.5.refs_5_) | copy-start | bytes 688132
  88.2 4.1 %collective-permute-start.11 = (bf16[256,3584]{1,0:T(8,128)(2,1)}, bf16[256,3584]{1,0:T(8,128)(2,1)}, u32[]{:S(2)}, u32[]{:S(2)}) collective-permute-start(bf16[256,3584]{1,0:T(8,128)(2,1)} %get-tuple-element.52), channel_id=1, source_target_pairs={{0,1},{1,0},{2,3},{3,2},{4,5},{5,4},{6,7},{7,6},{8,9},{9,8},{10,11... | collective-permute-start | bytes 5505032 | tf_op jit(solution)/shard_map/ppermute | solution.py:54
  88.2 47.1 %all-to-all-start.1 = ((bf16[4,224,1024]{2,1,0:T(8,128)(2,1)}), bf16[4,224,1024]{2,1,0:T(8,128)(2,1)S(1)}, u32[]{:S(2)}, u32[]{:S(2)}) async-start(bf16[4,224,1024]{2,1,0:T(8,128)(2,1)} %get-tuple-element.53), calls=%async_computation.1 | async-start | bytes 3670016 | tf_op jit(solution)/shard_map/all_to_all | solution.py:390
  94.9 22.6 %collective-permute-start.12 = (bf16[128,3584]{1,0:T(8,128)(2,1)}, bf16[128,3584]{1,0:T(8,128)(2,1)S(1)}, u32[]{:S(2)}, u32[]{:S(2)}) collective-permute-start(bf16[128,3584]{1,0:T(8,128)(2,1)} %add_convert_fusion), channel_id=1, source_target_pairs={{0,2},{1,3},{2,0},{3,1},{4,6},{5,7},{6,4},{7,5},{8,10},{9,11},{10,... | collective-permute-start | bytes 2752520 | tf_op jit(solution)/shard_map/ppermute | solution.py:59
  96.4 44.0 %collective-permute-start.13 = (bf16[4,224,1024]{2,1,0:T(8,128)(2,1)}, bf16[4,224,1024]{2,1,0:T(8,128)(2,1)}, u32[]{:S(2)}, u32[]{:S(2)}) collective-permute-start(bf16[4,224,1024]{2,1,0:T(8,128)(2,1)} %all-to-all-done.refs_0_), channel_id=1, source_target_pairs={{0,4},{4,0},{8,12},{12,8},{16,20},{20,16},{24,28},{28,24},{1,5},{5... | collective-permute-start | bytes 5505032 | tf_op jit(solution)/shard_map/ppermute | solution.py:35
  101.8 15.7 %copy-start.9 = (bf16[256,3584]{1,0:T(8,128)(2,1)S(1)}, bf16[256,3584]{1,0:T(8,128)(2,1)}, u32[]{:S(2)}) copy-start(bf16[256,3584]{1,0:T(8,128)(2,1)} %get-tuple-element.49) | copy-start | bytes 5505028
  117.5 25.2 %copy-start.22 = (f32[3584]{0:T(1024)S(1)}, f32[3584]{0:T(1024)}, u32[]{:S(2)}) copy-start(f32[3584]{0:T(1024)} %param.36) | copy-start | bytes 43012
  135.3 7.4 %copy-start.7 = (f32[2,64,3584]{2,1,0:T(8,128)S(1)}, f32[2,64,3584]{2,1,0:T(8,128)}, u32[]{:S(2)}) copy-start(f32[2,64,3584]{2,1,0:T(8,128)} %copy.129) | copy-start | bytes 5505028
  135.3 7.4 %copy-start.8 = (f32[128,3584]{1,0:T(8,128)S(1)}, f32[128,3584]{1,0:T(8,128)}, u32[]{:S(2)}) copy-start(f32[128,3584]{1,0:T(8,128)} %convert_add_fusion) | copy-start | bytes 5505028
  144.0 22.9 %collective-permute-start.14 = (bf16[128,3584]{1,0:T(8,128)(2,1)}, bf16[128,3584]{1,0:T(8,128)(2,1)S(1)}, u32[]{:S(2)}, u32[]{:S(2)}) collective-permute-start(bf16[128,3584]{1,0:T(8,128)(2,1)} %multiply_convert_fusion.refs_0_), channel_id=1, source_target_pairs={{0,8},{4,12},{8,16},{12,20},{16,24},{20,28},{1,9},{5,13},{9,17},{1... | collective-permute-start | bytes 2752520 | tf_op jit(solution)/shard_map/ppermute | solution.py:42
  147.5 23.6 %collective-permute-start.15 = (bf16[128,3584]{1,0:T(8,128)(2,1)}, bf16[128,3584]{1,0:T(8,128)(2,1)}, u32[]{:S(2)}, u32[]{:S(2)}) collective-permute-start(bf16[128,3584]{1,0:T(8,128)(2,1)} %multiply_convert_fusion.refs_0_), channel_id=1, source_target_pairs={{8,0},{12,4},{16,8},{20,12},{24,16},{28,20},{9,1},{13,5},{17,9},{2... | collective-permute-start | bytes 2752520 | tf_op jit(solution)/shard_map/ppermute | solution.py:42
  148.8 22.3 %collective-permute-start.16 = (bf16[128,3584]{1,0:T(8,128)(2,1)}, bf16[128,3584]{1,0:T(8,128)(2,1)}, u32[]{:S(2)}, u32[]{:S(2)}) collective-permute-start(bf16[128,3584]{1,0:T(8,128)(2,1)} %multiply_convert_fusion.refs_0_), channel_id=1, source_target_pairs={{0,2},{1,3},{2,0},{3,1},{4,6},{5,7},{6,4},{7,5},{8,10},{9,11},{10,... | collective-permute-start | bytes 2752520 | tf_op jit(solution)/shard_map/ppermute | solution.py:59
  150.8 23.6 %collective-permute-start.17 = (bf16[2,224,1024]{2,1,0:T(8,128)(2,1)}, bf16[2,224,1024]{2,1,0:T(8,128)(2,1)}, u32[]{:S(2)}, u32[]{:S(2)}) collective-permute-start(bf16[2,224,1024]{2,1,0:T(8,128)(2,1)} %get-tuple-element.79), channel_id=1, source_target_pairs={{0,4},{4,0},{8,12},{12,8},{16,20},{20,16},{24,28},{28,24},{1,5},{5... | collective-permute-start | bytes 2752520 | tf_op jit(solution)/shard_map/ppermute | solution.py:35
  152.6 39.3 %collective-permute-start.21 = (bf16[2,224,1024]{2,1,0:T(8,128)(2,1)}, bf16[2,224,1024]{2,1,0:T(8,128)(2,1)}, u32[]{:S(2)}, u32[]{:S(2)}) collective-permute-start(bf16[2,224,1024]{2,1,0:T(8,128)(2,1)} %get-tuple-element.78), channel_id=1, source_target_pairs={{0,4},{4,0},{8,12},{12,8},{16,20},{20,16},{24,28},{28,24},{1,5},{5... | collective-permute-start | bytes 2752520 | tf_op jit(solution)/shard_map/ppermute | solution.py:35
  176.7 22.9 %collective-permute-start.20 = (bf16[128,3584]{1,0:T(8,128)(2,1)}, bf16[128,3584]{1,0:T(8,128)(2,1)}, u32[]{:S(2)}, u32[]{:S(2)}) collective-permute-start(bf16[128,3584]{1,0:T(8,128)(2,1)} %broadcast_select_fusion.1.refs_4_), channel_id=1, source_target_pairs={{0,2},{1,3},{2,0},{3,1},{4,6},{5,7},{6,4},{7,5},{8,10},{9,11},{10,... | collective-permute-start | bytes 2752520 | tf_op jit(solution)/shard_map/ppermute | solution.py:59
  178.2 21.9 %collective-permute-start.18 = (bf16[128,3584]{1,0:T(8,128)(2,1)S(1)}, bf16[128,3584]{1,0:T(8,128)(2,1)}, u32[]{:S(2)}, u32[]{:S(2)}) collective-permute-start(bf16[128,3584]{1,0:T(8,128)(2,1)S(1)} %collective-permute-done.14), channel_id=1, source_target_pairs={{8,16},{12,20},{16,24},{20,28},{9,17},{13,21},{17,25},{21,29},{10,... | collective-permute-start | bytes 2752520 | tf_op jit(solution)/shard_map/ppermute | solution.py:42
  179.7 22.6 %collective-permute-start.19 = (bf16[128,3584]{1,0:T(8,128)(2,1)}, bf16[128,3584]{1,0:T(8,128)(2,1)}, u32[]{:S(2)}, u32[]{:S(2)}) collective-permute-start(bf16[128,3584]{1,0:T(8,128)(2,1)} %collective-permute-done.15), channel_id=1, source_target_pairs={{8,0},{12,4},{16,8},{20,12},{9,1},{13,5},{17,9},{21,13},{10,2},{14... | collective-permute-start | bytes 2752520 | tf_op jit(solution)/shard_map/ppermute | solution.py:42
  181.9 22.5 %collective-permute-start.25 = (bf16[128,3584]{1,0:T(8,128)(2,1)}, bf16[128,3584]{1,0:T(8,128)(2,1)S(1)}, u32[]{:S(2)}, u32[]{:S(2)}) collective-permute-start(bf16[128,3584]{1,0:T(8,128)(2,1)} %multiply_convert_fusion.refs_0_), channel_id=1, source_target_pairs={{0,1},{1,0},{2,3},{3,2},{4,5},{5,4},{6,7},{7,6},{8,9},{9,8},{10,11... | collective-permute-start | bytes 2752520 | tf_op jit(solution)/shard_map/ppermute | solution.py:54
  191.9 14.0 %collective-permute-start.27 = (bf16[128,3584]{1,0:T(8,128)(2,1)}, bf16[128,3584]{1,0:T(8,128)(2,1)S(1)}, u32[]{:S(2)}, u32[]{:S(2)}) collective-permute-start(bf16[128,3584]{1,0:T(8,128)(2,1)} %broadcast_select_fusion.1.refs_4_), channel_id=1, source_target_pairs={{0,1},{1,0},{2,3},{3,2},{4,5},{5,4},{6,7},{7,6},{8,9},{9,8},{10,11... | collective-permute-start | bytes 2752520 | tf_op jit(solution)/shard_map/ppermute | solution.py:54
  199.5 9.3 %collective-permute-start.26 = (bf16[128,3584]{1,0:T(8,128)(2,1)}, bf16[128,3584]{1,0:T(8,128)(2,1)}, u32[]{:S(2)}, u32[]{:S(2)}) collective-permute-start(bf16[128,3584]{1,0:T(8,128)(2,1)} %collective-permute-done.16.refs_1_), channel_id=1, source_target_pairs={{0,1},{1,0},{2,3},{3,2},{4,5},{5,4},{6,7},{7,6},{8,9},{9,8},{10,11... | collective-permute-start | bytes 2752520 | tf_op jit(solution)/shard_map/ppermute | solution.py:54
  202.4 7.0 %collective-permute-start.28 = (bf16[128,3584]{1,0:T(8,128)(2,1)}, bf16[128,3584]{1,0:T(8,128)(2,1)}, u32[]{:S(2)}, u32[]{:S(2)}) collective-permute-start(bf16[128,3584]{1,0:T(8,128)(2,1)} %collective-permute-done.20.refs_5_), channel_id=1, source_target_pairs={{0,1},{1,0},{2,3},{3,2},{4,5},{5,4},{6,7},{7,6},{8,9},{9,8},{10,11... | collective-permute-start | bytes 2752520 | tf_op jit(solution)/shard_map/ppermute | solution.py:54
  202.4 26.5 %collective-permute-start.22 = (bf16[128,3584]{1,0:T(8,128)(2,1)}, bf16[128,3584]{1,0:T(8,128)(2,1)S(1)}, u32[]{:S(2)}, u32[]{:S(2)}) collective-permute-start(bf16[128,3584]{1,0:T(8,128)(2,1)} %collective-permute-done.18), channel_id=1, source_target_pairs={{16,24},{20,28},{17,25},{21,29},{18,26},{22,30},{19,27},{23,31}} | collective-permute-start | bytes 2752520 | tf_op jit(solution)/shard_map/ppermute | solution.py:42
  204.4 19.2 %copy-start.10 = (bf16[128,3584]{1,0:T(8,128)(2,1)}, bf16[128,3584]{1,0:T(8,128)(2,1)S(1)}, u32[]{:S(2)}) copy-start(bf16[128,3584]{1,0:T(8,128)(2,1)S(1)} %broadcast_select_fusion.refs_0_) | copy-start | bytes 2752516
  204.4 25.0 %collective-permute-start.23 = (bf16[128,3584]{1,0:T(8,128)(2,1)}, bf16[128,3584]{1,0:T(8,128)(2,1)}, u32[]{:S(2)}, u32[]{:S(2)}) collective-permute-start(bf16[128,3584]{1,0:T(8,128)(2,1)} %collective-permute-done.19), channel_id=1, source_target_pairs={{8,0},{12,4},{9,1},{13,5},{10,2},{14,6},{11,3},{15,7}} | collective-permute-start | bytes 2752520 | tf_op jit(solution)/shard_map/ppermute | solution.py:42
  205.9 22.9 %collective-permute-start.24 = (bf16[128,3584]{1,0:T(8,128)(2,1)S(1)}, bf16[128,3584]{1,0:T(8,128)(2,1)}, u32[]{:S(2)}, u32[]{:S(2)}) collective-permute-start(bf16[128,3584]{1,0:T(8,128)(2,1)S(1)} %broadcast_select_fusion.refs_0_), channel_id=1, source_target_pairs={{0,2},{1,3},{2,0},{3,1},{4,6},{5,7},{6,4},{7,5},{8,10},{9,11},{10,... | collective-permute-start | bytes 2752520 | tf_op jit(solution)/shard_map/ppermute | solution.py:59
  208.9 25.0 %collective-permute-start.30 = (bf16[128,3584]{1,0:T(8,128)(2,1)S(1)}, bf16[128,3584]{1,0:T(8,128)(2,1)}, u32[]{:S(2)}, u32[]{:S(2)}) collective-permute-start(bf16[128,3584]{1,0:T(8,128)(2,1)S(1)} %broadcast_select_fusion.refs_0_), channel_id=1, source_target_pairs={{0,1},{1,0},{2,3},{3,2},{4,5},{5,4},{6,7},{7,6},{8,9},{9,8},{10,11... | collective-permute-start | bytes 2752520 | tf_op jit(solution)/shard_map/ppermute | solution.py:54
  231.7 2.8 collective-permute-start.32
  231.7 4.1 %collective-permute-start.31 = (bf16[128,3584]{1,0:T(8,128)(2,1)}, bf16[128,3584]{1,0:T(8,128)(2,1)}, u32[]{:S(2)}, u32[]{:S(2)}) collective-permute-start(bf16[128,3584]{1,0:T(8,128)(2,1)} %collective-permute-done.24.refs_1_), channel_id=1, source_target_pairs={{0,1},{1,0},{2,3},{3,2},{4,5},{5,4},{6,7},{7,6},{8,9},{9,8},{10,11... | collective-permute-start | bytes 2752520 | tf_op jit(solution)/shard_map/ppermute | solution.py:54
  232.2 22.5 %collective-permute-start.29 = (bf16[128,3584]{1,0:T(8,128)(2,1)}, bf16[128,3584]{1,0:T(8,128)(2,1)S(1)}, u32[]{:S(2)}, u32[]{:S(2)}) collective-permute-start(bf16[128,3584]{1,0:T(8,128)(2,1)} %select_select_fusion.refs_4_), channel_id=1, source_target_pairs={{0,2},{1,3},{2,0},{3,1},{4,6},{5,7},{6,4},{7,5},{8,10},{9,11},{10,... | collective-permute-start | bytes 2752520 | tf_op jit(solution)/shard_map/ppermute | solution.py:59
  254.7 3.9 %copy-start.11 = (bf16[128,3584]{1,0:T(8,128)(2,1)}, bf16[128,3584]{1,0:T(8,128)(2,1)S(1)}, u32[]{:S(2)}) copy-start(bf16[128,3584]{1,0:T(8,128)(2,1)S(1)} %collective-permute-done.29.refs_0_) | copy-start | bytes 2752516
  254.7 3.9 %collective-permute-start.35 = (bf16[128,3584]{1,0:T(8,128)(2,1)S(1)}, bf16[128,3584]{1,0:T(8,128)(2,1)S(1)}, u32[]{:S(2)}, u32[]{:S(2)}) collective-permute-start(bf16[128,3584]{1,0:T(8,128)(2,1)S(1)} %collective-permute-done.29.refs_0_), channel_id=1, source_target_pairs={{0,1},{1,0},{2,3},{3,2},{4,5},{5,4},{6,7},{7,6},{8,9},{9,8},{10,11... | collective-permute-start | bytes 2752520 | tf_op jit(solution)/shard_map/ppermute | solution.py:54
  255.7 13.6 %collective-permute-start.33 = (f32[8,2,2,2,64]{4,3,2,1,0:T(2,128)S(1)}, f32[8,2,2,2,64]{4,3,2,1,0:T(2,128)S(1)}, u32[]{:S(2)}, u32[]{:S(2)}) collective-permute-start(f32[8,2,2,2,64]{4,3,2,1,0:T(2,128)S(1)} %copy.151), channel_id=1, source_target_pairs={{0,8},{4,12},{8,0},{12,4},{16,24},{20,28},{24,16},{28,20},{1,9},{5... | collective-permute-start | bytes 49160 | tf_op jit(solution)/shard_map/ppermute | solution.py:30
  258.3 11.0 %collective-permute-start.34 = (f32[8,2,2,2,64]{4,3,2,1,0:T(2,128)S(1)}, f32[8,2,2,2,64]{4,3,2,1,0:T(2,128)S(1)}, u32[]{:S(2)}, u32[]{:S(2)}) collective-permute-start(f32[8,2,2,2,64]{4,3,2,1,0:T(2,128)S(1)} %bitcast.256), channel_id=1, source_target_pairs={{0,16},{4,20},{8,24},{12,28},{16,0},{20,4},{24,8},{28,12},{1,17},{... | collective-permute-start | bytes 49160 | tf_op jit(solution)/shard_map/ppermute | solution.py:30
  258.5 19.9 %copy-start.25 = (s32[256]{0:T(256)S(1)}, s32[256]{0:T(256)}, u32[]{:S(2)}) copy-start(s32[256]{0:T(256)} %param.20) | copy-start | bytes 3076
  258.5 30.9 %copy-start.24 = (s32[48]{0:T(128)S(1)}, s32[48]{0:T(128)}, u32[]{:S(2)}) copy-start(s32[48]{0:T(128)} %param.21) | copy-start | bytes 580
  258.5 30.9 %copy-start.27 = (s32[48]{0:T(128)S(1)}, s32[48]{0:T(128)}, u32[]{:S(2)}) copy-start(s32[48]{0:T(128)} %param.22) | copy-start | bytes 580
  266.9 5.8 %collective-permute-start.36 = (f32[8,2,2,2,64]{4,3,2,1,0:T(2,128)S(1)}, f32[8,2,2,2,64]{4,3,2,1,0:T(2,128)S(1)}, u32[]{:S(2)}, u32[]{:S(2)}) collective-permute-start(f32[8,2,2,2,64]{4,3,2,1,0:T(2,128)S(1)} %pad_maximum_fusion.1), channel_id=1, source_target_pairs={{0,24},{4,28},{8,16},{12,20},{16,8},{20,12},{24,0},{28,4},{1,25},{... | collective-permute-start | bytes 49160 | tf_op jit(solution)/shard_map/ppermute | solution.py:30
  272.8 3.3 %collective-permute-start.39 = (f32[3,2,2,2,64]{4,3,2,1,0:T(2,128)S(1)}, f32[3,2,2,2,64]{4,3,2,1,0:T(2,128)S(1)}, u32[]{:S(2)}, u32[]{:S(2)}) collective-permute-start(f32[3,2,2,2,64]{4,3,2,1,0:T(2,128)S(1)} %pad_maximum_fusion.2), channel_id=1, source_target_pairs={{0,3},{1,2},{2,1},{3,0},{4,7},{5,6},{6,5},{7,4},{8,11},{9,10},{10,... | collective-permute-start | bytes 18440 | tf_op jit(solution)/shard_map/ppermute | solution.py:243
  272.9 3.2 %collective-permute-start.37 = (f32[3,2,2,2,64]{4,3,2,1,0:T(2,128)S(1)}, f32[3,2,2,2,64]{4,3,2,1,0:T(2,128)S(1)}, u32[]{:S(2)}, u32[]{:S(2)}) collective-permute-start(f32[3,2,2,2,64]{4,3,2,1,0:T(2,128)S(1)} %pad_maximum_fusion.2), channel_id=1, source_target_pairs={{0,1},{1,0},{2,3},{3,2},{4,5},{5,4},{6,7},{7,6},{8,9},{9,8},{10,11... | collective-permute-start | bytes 18440 | tf_op jit(solution)/shard_map/ppermute | solution.py:54
  274.5 3.7 %collective-permute-start.38 = (f32[3,2,2,2,64]{4,3,2,1,0:T(2,128)S(1)}, f32[3,2,2,2,64]{4,3,2,1,0:T(2,128)S(1)}, u32[]{:S(2)}, u32[]{:S(2)}) collective-permute-start(f32[3,2,2,2,64]{4,3,2,1,0:T(2,128)S(1)} %pad_maximum_fusion.2), channel_id=1, source_target_pairs={{0,2},{1,3},{2,0},{3,1},{4,6},{5,7},{6,4},{7,5},{8,10},{9,11},{10,... | collective-permute-start | bytes 18440 | tf_op jit(solution)/shard_map/ppermute | solution.py:59
  278.4 11.5 %copy-start.26 = (f32[256]{0:T(256)}, f32[256]{0:T(256)S(1)}, u32[]{:S(2)}) copy-start(f32[256]{0:T(256)S(1)} %convert_multiply_fusion) | copy-start | bytes 3076
  278.5 4.4 %collective-permute-start.40 = (f32[48]{0:T(128)S(1)}, f32[48]{0:T(128)S(1)}, u32[]{:S(2)}, u32[]{:S(2)}) collective-permute-start(f32[48]{0:T(128)S(1)} %convolution_bitcast_fusion), channel_id=1, source_target_pairs={{0,8},{4,12},{8,0},{12,4},{16,24},{20,28},{24,16},{28,20},{1,9},{5... | collective-permute-start | bytes 584 | tf_op jit(solution)/shard_map/ppermute | solution.py:30
  278.7 4.4 %collective-permute-start.41 = (f32[48]{0:T(128)S(1)}, f32[48]{0:T(128)S(1)}, u32[]{:S(2)}, u32[]{:S(2)}) collective-permute-start(f32[48]{0:T(128)S(1)} %convolution_bitcast_fusion), channel_id=1, source_target_pairs={{0,16},{4,20},{8,24},{12,28},{16,0},{20,4},{24,8},{28,12},{1,17},{... | collective-permute-start | bytes 584 | tf_op jit(solution)/shard_map/ppermute | solution.py:30
  280.5 5.3 %collective-permute-start.42 = (f32[48]{0:T(128)S(1)}, f32[48]{0:T(128)S(1)}, u32[]{:S(2)}, u32[]{:S(2)}) collective-permute-start(f32[48]{0:T(128)S(1)} %convolution_bitcast_fusion), channel_id=1, source_target_pairs={{0,24},{4,28},{8,16},{12,20},{16,8},{20,12},{24,0},{28,4},{1,25},{... | collective-permute-start | bytes 584 | tf_op jit(solution)/shard_map/ppermute | solution.py:30
  285.9 3.5 %collective-permute-start.43 = (f32[48]{0:T(128)S(1)}, f32[48]{0:T(128)S(1)}, u32[]{:S(2)}, u32[]{:S(2)}) collective-permute-start(f32[48]{0:T(128)S(1)} %add_add_fusion.1), channel_id=1, source_target_pairs={{0,4},{4,0},{8,12},{12,8},{16,20},{20,16},{24,28},{28,24},{1,5},{5... | collective-permute-start | bytes 584 | tf_op jit(solution)/shard_map/ppermute | solution.py:35
  (12 other events, 15.3 us)

commit v3 on v2

--- a/solution.py
+++ b/solution.py
@@ -35,11 +35,15 @@
     return lax.ppermute(x, "seq", [(i, partner(i, side, block, count)) for i in range(count)])
 
 
-def passed_on(up, down, step):
+def between(x, pairs):
     count = lax.axis_size("seq")
-    ups = [(i, i + SIDE) for i in range(count) if step - 1 <= place_of(i) < CHAIN - 1]
-    downs = [(i, i - SIDE) for i in range(count) if 0 < place_of(i) <= CHAIN - step]
-    return lax.ppermute(up, "seq", ups), lax.ppermute(down, "seq", downs)
+    sends = [
+        (i, i + (to - place) * SIDE)
+        for i in range(count)
+        for place, to in pairs
+        if place_of(i) == place
+    ]
+    return lax.ppermute(x, "seq", sends)
 
 
 def chain_groups():
@@ -60,7 +64,7 @@
 
 
 def tied(*values):
-    return lax.optimization_barrier(values)
+    return list(lax.optimization_barrier(values))
 
 
 def dot(a, b, over=((1,), (0,))):
@@ -222,6 +226,13 @@
         copy.start()
     for copy in copies:
         copy.wait()
+
+
+def norm_kernel(*refs):
+    *term_refs, scale_ref, out_ref = refs
+    hidden = sum(term[...].astype(jnp.float32) for term in term_refs)
+    mean_sq = jnp.mean(hidden * hidden, axis=1, keepdims=True)
+    out_ref[...] = (hidden * lax.rsqrt(mean_sq + 1e-05) * scale_ref[...]).astype(out_ref.dtype)
 
 
 def split_kernel(head_ref, *out_refs):
@@ -383,9 +394,7 @@
         cost_estimate=cost(0, 2 * vocab_head_weight.size * 2),
         name="split_head_columns",
     )(vocab_head_weight)
-    targets = jnp.stack([scored_token_targets, turn(scored_token_targets, 1)])
-    targets = jnp.concatenate([targets, turn(targets, 2)])
-    arriving, states[3], targets, *head = tied(arriving, states[3], targets, *head)
+    arriving, states[3], *head = tied(arriving, states[3], *head)
     came_head = [
         lax.all_to_all(head[cut], "seq", 0, 0, axis_index_groups=chain_groups())
         for cut in range(cuts)
@@ -435,7 +444,9 @@
         name="gate_and_project",
     )(order, *resident, shared_output_weight, adapter_down_weight, adapter_up_weight)
 
-    sent, came_head[0] = tied(sent, came_head[0])
+    own_words = jnp.stack([scored_token_targets, valid])
+    sent, came_head[0], own_words = tied(sent, came_head[0], own_words)
+    words_and_valid = [own_words] + [turn(own_words, k) for k in range(1, CHAIN)]
     came = other_core(sent)
     each = models * share_rows
 
@@ -443,15 +454,26 @@
         rows = slice(by * each, (by + 1) * each)
         return kept[rows].astype(jnp.float32) + came[rows].astype(jnp.float32)
 
-    mixed = chip_sum(0)
-    for by in range(1, x_count):
-        mixed = mixed + along_x(chip_sum(by).astype(jnp.bfloat16), by).astype(jnp.float32)
+    own_rows = lax.dynamic_slice_in_dim(residual, mp_index * share_rows, share_rows, 0)
+    own_rows = jnp.transpose(own_rows, (1, 0, 2)).reshape(each, width)
+    crossing = [along_x(chip_sum(by).astype(jnp.bfloat16), by) for by in range(1, x_count)]
     besides_head = [beside(came_head[0])]
-    mixed, came_head[-1], *besides_head[0] = tied(mixed, came_head[-1], *besides_head[0])
-    own_rows = lax.dynamic_slice_in_dim(residual, mp_index * share_rows, share_rows, 0)
-    hidden = jnp.transpose(own_rows, (1, 0, 2)).reshape(each, width).astype(jnp.float32) + mixed
-    mean_sq = jnp.mean(hidden * hidden, axis=-1, keepdims=True)
-    normed_own = (hidden * lax.rsqrt(mean_sq + 1e-05) * final_norm_scale).astype(jnp.bfloat16)
+    crossing[0], own_rows, came_head[-1], *came_small = tied(
+        crossing[0], own_rows, came_head[-1], *words_and_valid, *besides_head[0]
+    )
+    words_and_valid, besides_head[0] = jnp.stack(came_small[:CHAIN]), came_small[CHAIN:]
+    besides_head += [beside(piece) for piece in came_head[1:]]
+    half_block = pl.BlockSpec((each, width), lambda i: (0, 0))
+    normed_own = pl.pallas_call(
+        norm_kernel,
+        grid=(1,),
+        in_specs=[half_block] * (3 + len(crossing)) + [pl.BlockSpec((1, width), lambda i: (0, 0))],
+        out_specs=half_block,
+        out_shape=jax.ShapeDtypeStruct((each, width), jnp.bfloat16),
+        compiler_params=pltpu.CompilerParams(vmem_limit_bytes=32 * 2**20),
+        cost_estimate=cost(0, 10 * each * width),
+        name="add_and_norm",
+    )(own_rows, kept, came, *crossing, final_norm_scale[None, :])
 
     limit = jnp.stack(
         [
@@ -522,43 +544,38 @@
     def crossed(rows):
         return [along_x(rows, by) for by in range(1, x_count)]
 
-    halves = [came_head[-1][: CHAIN // 2], came_head[-1][CHAIN // 2 :]] if cuts == 2 else []
     blocks_of = [normed_own]
     nears = [crossed(normed_own)]
-    up, down = normed_own, normed_own
-    ups, downs, late = [], [], []
-    words = words_of(targets)
+    words = words_of(words_and_valid[:, 0])
+    at_end = (place == 0) | (place == CHAIN - 1)
     for step in range(1, CHAIN):
-        up, down = passed_on(up, down, step)
+        if step == 1:
+            moved = [turn(normed_own, 1), between(normed_own, [(1, 2), (2, 1)])]
+        elif step == 2:
+            moved = [between(inner, [(1, 0), (2, 3)]), between(blocks_of[1], [(1, 2), (2, 1)])]
+        else:
+            moved = [between(passed, [(1, 0), (2, 3)])]
         count = len(nears[-1])
         extra = []
-        if step <= len(halves):
-            late.append(beside(halves[step - 1]))
-            extra = late[-1]
         if step == CHAIN - 2:
-            if cuts == 2:
-                besides_head.append([jnp.concatenate(both) for both in zip(late[0], late[1])])
-            extra = [place_head()]
+            extra = besides_head[-1]
         elif step == CHAIN - 1:
+            head_part = place_head()
             rows = [both_cores([blocks_of[k]] + nears[k]) for k in (0, 1)]
             extra = [head_stats(head_part, rows[0] + rows[1], words[:2])]
-        up, down, *came = tied(up, down, *nears[-1], *extra)
-        nears[-1], extra = came[:count], came[count:]
-        if step <= len(halves) and step < CHAIN - 2:
-            late[-1] = extra
-        elif step == CHAIN - 2:
-            head_part = extra[0]
+        came = tied(*nears[-1], *extra, *moved)
+        nears[-1], extra, moved = came[:count], came[count : -len(moved)], came[-len(moved) :]
+        if step == CHAIN - 2:
+            besides_head[-1] = extra
         elif step == CHAIN - 1:
             early = extra[0]
-        ups.append(up)
-        downs.append(down)
         if step == 1:
-            block = jnp.where(place % 2 == 1, up, down)
+            block, inner = moved
         elif step == 2:
-            block = jnp.where(place >= 2, up, down)
+            passed = moved[1]
+            block = jnp.where(at_end, moved[0], passed)
         else:
-            near = jnp.where(place == 1, downs[0], ups[0])
-            block = jnp.where(place == 0, down, jnp.where(place == 3, up, near))
+            block = jnp.where(at_end, moved[0], inner)
         blocks_of.append(block)
         nears.append(crossed(block))
 
@@ -568,42 +585,47 @@
         both_cores([blocks_of[last - 1]] + nears[last - 1]) + both_cores([blocks_of[last]]),
         jnp.concatenate([words[last - 1].reshape(-1, each), words[last, :, 0]]),
     )
-    *nears[last], early, middle = tied(*nears[last], early, middle)
+    def blocks(stats):
+        return stats[:3].reshape(3, -1, 2, x_count, models, share_rows)
+
+    first = blocks(early)
+    firsts = [first] + [turn(first, by) for by in range(1, CHAIN)]
+    came = tied(*nears[last], middle, *firsts)
+    nears[last], middle, firsts = came[: -CHAIN - 1], came[-CHAIN - 1], came[-CHAIN:]
     rest = head_stats(head_part, both_cores(nears[last]), words[last, :, 1:])
-    grid_shape = (8, 2, x_count, models, share_rows)
-    stats_of = [
-        early[:, :mp_count].reshape(grid_shape),
-        early[:, mp_count:].reshape(grid_shape),
-        middle[:, :mp_count].reshape(grid_shape),
-        jnp.concatenate(
-            [
-                middle[:, mp_count:].reshape(8, 2, 1, models, share_rows),
-                rest.reshape(8, 2, x_count - 1, models, share_rows),
-            ],
-            axis=2,
-        ),
-    ]
-    chain_stats = [stats_of[0]] + [turn(stats_of[k], k) for k in range(1, CHAIN)]
+    own_side = middle[:3, mp_count:].reshape(3, 1, 2, 1, models, share_rows)
+    other_side = rest[:3].reshape(3, 1, 2, x_count - 1, models, share_rows)
+    late = jnp.concatenate(
+        [blocks(middle[:, :mp_count]), jnp.concatenate([own_side, other_side], axis=3)], axis=1
+    )
 
     def merged(several):
         top = functools.reduce(jnp.maximum, [stats[0] for stats in several])
         total = sum(stats[1] * jnp.exp(stats[0] - top) for stats in several)
         return jnp.stack([top, total, sum(stats[2] for stats in several)])
 
-    stats = merged(chain_stats)
-    several = [stats, other_core(stats)[:, ::-1]]
+    several = [jnp.concatenate([firsts[0], late], axis=1)]
+    for by in range(1, CHAIN):
+        stats = jnp.concatenate([firsts[by], turn(late, by)], axis=1)
+        several.append(jnp.stack([stats[:, k ^ by] for k in range(CHAIN)], axis=1))
+    stats = merged(several)
+    several = [stats, other_core(stats)[:, :, ::-1]]
     for by in range(1, x_count):
-        several.append(jnp.roll(along_x(stats, by), by, axis=2))
-        several.append(jnp.roll(across(stats, by)[:, ::-1], by, axis=2))
+        several.append(jnp.roll(along_x(stats, by), by, axis=3))
+        several.append(jnp.roll(across(stats, by)[:, :, ::-1], by, axis=3))
     stats = merged(several)
     logprob = stats[2] - stats[0] - jnp.log(stats[1])
-    delta = (logprob[:, :, 0] - logprob[:, :, 1]).reshape(mp_count, share_rows)
-    token_delta = jnp.sum(
-        jnp.where(mp_order[None, :, None] == quarter[:, None, None], delta[None], 0.0), axis=1
-    ).reshape(tok_rows)
-    token_delta = token_delta * valid.astype(jnp.float32)
-    roll_sums = jnp.dot(token_delta, member_table.astype(jnp.float32), precision=highest)
-    roll_sums = roll_sums + sum(turn(roll_sums, k) for k in range(1, CHAIN))
+    delta = (logprob[:, :, :, 0] - logprob[:, :, :, 1]).reshape(CHAIN, mp_count, share_rows)
+    in_order = mp_order[None, :] == quarter[:, None]
+    delta = jnp.sum(jnp.where(in_order[None, :, :, None], delta[:, None], 0.0), axis=2)
+    delta = delta.reshape(CHAIN, tok_rows) * words_and_valid[:, 1].astype(jnp.float32)
+    token_delta = delta[0]
+    first_rows = jnp.stack([turned(seq_index, k) for k in range(CHAIN)]) * tok_rows
+    since = (first_rows[:, None] + offsets[None, :])[:, :, None] - starts
+    member = ((since >= 0) & (since < lengths)).astype(jnp.float32)
+    roll_sums = jnp.dot(
+        delta.reshape(-1), member.reshape(-1, roll_count), precision=highest
+    )
     roll_sums = roll_sums + sum(beside(roll_sums))
     owner_sums = jnp.where(owners == seq_index, roll_sums / lengths.astype(jnp.float32), 0.0)
     return (owner_sums[None, :], token_delta)

time: 291 us -> 270 us (0.928)
  waiting for transfers between devices: 112 us -> 98.3 us
  other arithmetic: 24.9 us -> 13.3 us
  Pallas kernels: 59.6 us -> 63.3 us
    ppermute x8 -> x7, waiting for transfers between devices: 28.9 us -> 11.1 us  [to_partner(): lax.ppermute(x, 'seq', [(i, partner(i, side, block, count)) for i in rang...]
    ppermute x6 -> x4, waiting for transfers between devices: 21.1 us -> 3.72 us  [between(): return lax.ppermute(x, 'seq', sends)]
    all_to_all x2, waiting for transfers between devices: 22 us -> 38.3 us  [shards(): lax.all_to_all(head[cut], 'seq', 0, 0, axis_index_groups=chain_groups())]
    ppermute x6, waiting for transfers between devices: 26.6 us -> 35.8 us  [along_x(): lax.ppermute(x, 'mp', [(i, (i + 2 * by) % count) for i in range(count)])]
    ppermute x11 -> x13, starting transfers between devices: 17.6 us -> 25.2 us  [turn(): return lax.ppermute(x, 'seq', [(i, turned(i, by)) for i in range(count)])]
    ppermute x6 -> x4, starting transfers between devices: 9.82 us -> 4.93 us  [between(): return lax.ppermute(x, 'seq', sends)]
    ppermute x11 -> x13, waiting for transfers between devices: 10.4 us -> 6.67 us  [turn(): return lax.ppermute(x, 'seq', [(i, turned(i, by)) for i in range(count)])]
    ppermute x8 -> x7, starting transfers between devices: 15.1 us -> 11.7 us  [to_partner(): lax.ppermute(x, 'seq', [(i, partner(i, side, block, count)) for i in rang...]
  transfers between devices with their start and end apart: 46 -> 45, of which waited for: 25 -> 18; matrix products, arithmetic and copies ran while one was open for 12% -> 10% of each run, Pallas kernels for 21% -> 20%
where the time goes in v3:
time: 270 us; the launch traced here: 268 us
  waiting for transfers between devices  98.3 us (36%)
  starting transfers between devices  66 us (24%)
  Pallas kernels  63.3 us (23%)
  local copies, waits for them, and re-layouts  25.6 us (9%)
  other arithmetic  13.3 us (5%)
    all_to_all x2, waiting for transfers between devices, shards(): lax.all_to_all(head[cut], 'seq', 0, 0, axis_index_groups=chain_groups())  38.3 us
    ppermute x6, waiting for transfers between devices, along_x(): lax.ppermute(x, 'mp', [(i, (i + 2 * by) % count) for i in range(count)])  35.8 us
    pallas_call x3, Pallas kernels, head_stats(): pl.pallas_call(functools.partial(head_kernel, count), in_specs=[pl.BlockS...  32.9 us
    ppermute x13, starting transfers between devices, turn(): return lax.ppermute(x, 'seq', [(i, turned(i, by)) for i in range(count)])  25.2 us
    pallas_call x1, Pallas kernels, shards(): pl.pallas_call(functools.partial(project_kernel, len(prompts)), grid=(wid...  14.8 us
    unnamed x61, local copies, waits for them, and re-layouts  13.9 us
    ppermute x7, starting transfers between devices, to_partner(): lax.ppermute(x, 'seq', [(i, partner(i, side, block, count)) for i in rang...  11.7 us
    ppermute x7, waiting for transfers between devices, to_partner(): lax.ppermute(x, 'seq', [(i, partner(i, side, block, count)) for i in rang...  11.1 us
  transfers between devices with their start and end apart: 45, of which 18 were waited for; matrix products, arithmetic and copies ran while one was open for 10% of the time, Pallas kernels for 20%

profile of v3, /device:TPU:0, one launch (start us, length us, event | category | flops | bytes accessed | tf_op | source)
XLA Modules:
  0.0 268.5 jit_solution(15929047149306082790)
XLA Ops:
  0.6 1.2 copy.175.refs_0_
  1.9 3.1 %collective-permute-start = (bf16[2,64,896]{2,1,0:T(8,128)(2,1)S(1)}, bf16[2,64,896]{2,1,0:T(8,128)(2,1)S(1)}, u32[]{:S(2)}, u32[]{:S(2)}) collective-permute-start(bf16[2,64,896]{2,1,0:T(8,128)(2,1)S(1)} %copy.175.refs_0_), channel_id=1, source_target_pairs={{0,8},{4,12},{8,0},{12,4},{16,24},{20,28},{24,16},{28,20},{1,9},{5... | collective-permute-start | bytes 688136 | tf_op jit(solution)/shard_map/ppermute | solution.py:30
  5.0 1.5 collective-permute-start.2
  6.5 2.6 collective-permute-start.4
  14.4 2.4 collective-permute-start.1
  17.8 1.0 copy.148.c_ref.refs_9_
  18.8 1.0 copy.147.b_ref
  20.6 1.2 copy-done.7
  22.4 4.2 %local_tokens.1 = (f32[2,256,896]{2,1,0:T(8,128)S(1)}, bf16[2,64,896]{2,1,0:T(8,128)(2,1)S(1)}, f32[2,256,14]{2,1,0:T(8,128)S(1)}) custom-call(bf16[2,256,896]{2,1,0:T(8,128)(2,1)S(1)} %copy-done.7, bf16[2,256,64]{2,1,0:T(8,128)(2,1)S(1)} %copy.147.b_ref, bf16[2,256,64]{2,1,0:T(8,128)(2,1)S(1)} %copy.148.c_ref.refs_9_, f32[2,256,14]{2,1,0:T(8,128)S(1)} %copy.149.step_ref, ...), custom_call_target="tpu_custom_call" | custom-call | flops 1000000000 | bytes 8388608 | tf_op jit(solution)/shard_map/local_tokens/pallas_call | solution.py:339
  27.4 3.3 %collective-permute-start.6 = (bf16[2,64,896]{2,1,0:T(8,128)(2,1)S(1)}, bf16[2,64,896]{2,1,0:T(8,128)(2,1)S(1)}, u32[]{:S(2)}, u32[]{:S(2)}) collective-permute-start(bf16[2,64,896]{2,1,0:T(8,128)(2,1)S(1)} %get-tuple-element.47), channel_id=1, source_target_pairs={{0,4},{4,8},{8,12},{12,16},{16,20},{20,24},{24,28},{1,5},{5,9},{9,... | collective-permute-start | bytes 688136 | tf_op jit(solution)/shard_map/ppermute | solution.py:375
  31.3 4.5 %split_head_columns.1 = (bf16[4,224,1024]{2,1,0:T(8,128)(2,1)}, bf16[4,224,1024]{2,1,0:T(8,128)(2,1)}) custom-call(bf16[448,4000]{1,0:T(8,128)(2,1)} %head_ref.1), custom_call_target="tpu_custom_call" | custom-call | bytes 7168000 | tf_op jit(solution)/shard_map/split_head_columns/pallas_call | solution.py:388
  35.7 1.3 collective-permute-done.7.refs_6_
  37.1 4.5 %all-to-all-start = ((bf16[4,224,1024]{2,1,0:T(8,128)(2,1)}), bf16[4,224,1024]{2,1,0:T(8,128)(2,1)S(1)}, u32[]{:S(2)}, u32[]{:S(2)}) async-start(bf16[4,224,1024]{2,1,0:T(8,128)(2,1)} %get-tuple-element.57), calls=%async_computation | async-start | bytes 3670016 | tf_op jit(solution)/shard_map/all_to_all | solution.py:399
  43.0 2.5 collective-permute-start.5
  45.5 2.0 collective-permute-start.8
  48.8 3.4 %collective-permute-done.5.refs_5_ = bf16[2,64,896]{2,1,0:T(8,128)(2,1)S(1)} collective-permute-done((bf16[2,64,896]{2,1,0:T(8,128)(2,1)}, bf16[2,64,896]{2,1,0:T(8,128)(2,1)S(1)}, u32[]{:S(2)}, u32[]{:S(2)}) %collective-permute-start.5) | collective-permute-done | bytes 229408 | tf_op jit(solution)/shard_map/ppermute | solution.py:35
  52.2 3.4 %collective-permute-done.3.refs_3_ = bf16[2,64,896]{2,1,0:T(8,128)(2,1)S(1)} collective-permute-done((bf16[2,64,896]{2,1,0:T(8,128)(2,1)S(1)}, bf16[2,64,896]{2,1,0:T(8,128)(2,1)S(1)}, u32[]{:S(2)}, u32[]{:S(2)}) %collective-permute-start.3) | collective-permute-done | bytes 229408 | tf_op jit(solution)/shard_map/ppermute | solution.py:35
  55.5 2.5 collective-permute-done.8.refs_7_
  58.7 14.8 %gate_and_project.1 = (bf16[256,3584]{1,0:T(8,128)(2,1)}, bf16[256,3584]{1,0:T(8,128)(2,1)}) custom-call(s32[4]{0:T(128)} %fusion.41.order_ref, bf16[2,64,896]{2,1,0:T(8,128)(2,1)} %copy-done.12, bf16[2,64,896]{2,1,0:T(8,128)(2,1)} %copy-done.14, bf16[2,64,896]{2,1,0:T(8,128)(2,1)} %copy-done.13, bf16[2,64,896]{2,1,0:T(8,128)(2,1)} %copy-done.18, ...), custom_call_target="tpu_custom_call" | custom-call | flops 3288334336 | bytes 12845056 | tf_op jit(solution)/shard_map/gate_and_project/pallas_call | solution.py:424
  73.5 7.6 %all-to-all-done.refs_0_ = bf16[4,224,1024]{2,1,0:T(8,128)(2,1)S(1)} async-done(((bf16[4,224,1024]{2,1,0:T(8,128)(2,1)}), bf16[4,224,1024]{2,1,0:T(8,128)(2,1)S(1)}, u32[]{:S(2)}, u32[]{:S(2)}) %all-to-all-start) | async-done | bytes 1835040 | tf_op jit(solution)/shard_map/all_to_all | solution.py:399
  81.2 4.4 %all-to-all-start.1 = ((bf16[4,224,1024]{2,1,0:T(8,128)(2,1)}), bf16[4,224,1024]{2,1,0:T(8,128)(2,1)}, u32[]{:S(2)}, u32[]{:S(2)}) async-start(bf16[4,224,1024]{2,1,0:T(8,128)(2,1)} %get-tuple-element.59), calls=%async_computation.1 | async-start | bytes 3670016 | tf_op jit(solution)/shard_map/all_to_all | solution.py:399
  85.6 2.7 collective-permute-start.14
  88.3 2.6 add_convert_fusion
  90.8 1.5 collective-permute-start.10
  92.3 1.9 collective-permute-start.11
  94.2 2.4 collective-permute-start.12
  96.7 1.8 dynamic-slice_bitcast_fusion
  98.7 30.7 %all-to-all-done.1.refs_2_ = bf16[4,224,1024]{2,1,0:T(8,128)(2,1)} async-done(((bf16[4,224,1024]{2,1,0:T(8,128)(2,1)}), bf16[4,224,1024]{2,1,0:T(8,128)(2,1)}, u32[]{:S(2)}, u32[]{:S(2)}) %all-to-all-start.1) | async-done | bytes 1835040 | tf_op jit(solution)/shard_map/all_to_all | solution.py:399
  129.4 1.5 copy-done.1
  130.9 2.3 add_and_norm.1.refs_0_
  133.2 1.6 collective-permute-start.15
  134.8 1.3 collective-permute-start.16
  136.8 1.8 collective-permute-start.19
  138.6 16.6 %collective-permute-done.15.refs_1_ = bf16[128,3584]{1,0:T(8,128)(2,1)S(1)} collective-permute-done((bf16[128,3584]{1,0:T(8,128)(2,1)S(1)}, bf16[128,3584]{1,0:T(8,128)(2,1)S(1)}, u32[]{:S(2)}, u32[]{:S(2)}) %collective-permute-start.15) | collective-permute-done | bytes 917536 | tf_op jit(solution)/shard_map/ppermute | solution.py:63
  155.2 1.3 collective-permute-done.16.refs_4_
  156.6 1.1 collective-permute-start.18
  157.6 1.3 collective-permute-start.20
  158.9 1.7 collective-permute-start.21
  160.8 16.8 %collective-permute-done.18.refs_5_ = bf16[128,3584]{1,0:T(8,128)(2,1)} collective-permute-done((bf16[128,3584]{1,0:T(8,128)(2,1)}, bf16[128,3584]{1,0:T(8,128)(2,1)}, u32[]{:S(2)}, u32[]{:S(2)}) %collective-permute-start.18) | collective-permute-done | bytes 917536 | tf_op jit(solution)/shard_map/ppermute | solution.py:63
  177.6 3.7 %collective-permute-done.20 = bf16[128,3584]{1,0:T(8,128)(2,1)} collective-permute-done((bf16[128,3584]{1,0:T(8,128)(2,1)S(1)}, bf16[128,3584]{1,0:T(8,128)(2,1)}, u32[]{:S(2)}, u32[]{:S(2)}) %collective-permute-start.20) | collective-permute-done | bytes 917536 | tf_op jit(solution)/shard_map/ppermute | solution.py:46
  181.9 1.3 collective-permute-start.27
  183.2 2.3 broadcast_select_fusion.1.refs_0_
  185.4 1.5 collective-permute-start.22
  188.2 1.3 reshape.401.refs_9_
  189.5 4.5 %place_head_rows.1.refs_8_.refs_6_.refs_2_ = bf16[3584,1024]{1,0:T(8,128)(2,1)S(1)} custom-call(s32[16]{0:T(128)S(1)} %stack.195.first_ref, bf16[4,224,1024]{2,1,0:T(8,128)(2,1)S(1)} %all-to-all-done.refs_0_, bf16[4,224,1024]{2,1,0:T(8,128)(2,1)} %collective-permute-done.14.refs_1_, bf16[4,224,1024]{2,1,0:T(8,128)(2,1)} %all-to-all-done.1.refs_2_, ...), custom_call_target="tpu_custom_call" | custom-call | bytes 14680064 | tf_op jit(solution)/shard_map/place_head_rows/pallas_call | solution.py:504
  194.0 2.9 %copy-done = bf16[3584,1024]{1,0:T(8,128)(2,1)} copy-done((bf16[3584,1024]{1,0:T(8,128)(2,1)}, bf16[3584,1024]{1,0:T(8,128)(2,1)S(1)}, u32[]{:S(2)}) %copy-start) | copy-done | bytes 7340056
  197.0 14.3 %head_stats.3 = f32[8,1024]{1,0:T(8,128)} custom-call(s32[2]{0:T(128)} %pad_add_fusion.3.limit_ref, bf16[128,3584]{1,0:T(8,128)(2,1)} %copy-done.3, bf16[128,3584]{1,0:T(8,128)(2,1)} %copy-done.25, bf16[128,3584]{1,0:T(8,128)(2,1)} %copy-done.26, bf16[128,3584]{1,0:T(8,128)(2,1)} %collective-permute-done.24.refs_3_, ...), custom_call_target="tpu_custom_call" | custom-call | flops 7516192768 | bytes 14680064 | tf_op jit(solution)/shard_map/head_stats/pallas_call | solution.py:520
  212.1 1.3 broadcast_select_fusion.refs_4_
  215.8 4.4 %collective-permute-start.32 = (f32[3,2,2,2,2,64]{5,3,2,1,4,0:T(2,128)S(1)}, f32[3,2,2,2,2,64]{5,3,2,1,4,0:T(2,128)S(1)}, u32[]{:S(2)}, u32[]{:S(2)}) collective-permute-start(f32[3,2,2,2,2,64]{5,3,2,1,4,0:T(2,128)S(1)} %bitcast.233), channel_id=1, source_target_pairs={{0,8},{4,12},{8,0},{12,4},{16,24},{20,28},{24,16},{28,20},{1,9},{5... | collective-permute-start | bytes 36872 | tf_op jit(solution)/shard_map/ppermute | solution.py:30
  220.2 1.0 collective-permute-start.33
  221.1 1.5 collective-permute-start.34
  222.6 12.0 %head_stats.4 = f32[8,768]{1,0:T(8,128)} custom-call(s32[2]{0:T(128)} %pad_add_fusion.3.limit_ref, bf16[128,3584]{1,0:T(8,128)(2,1)} %broadcast_select_fusion.1.refs_0_, bf16[128,3584]{1,0:T(8,128)(2,1)} %collective-permute-done.22.refs_1_, bf16[128,3584]{1,0:T(8,128)(2,1)} %collective-permute-done.29.refs_2_, ...), custom_call_target="tpu_custom_call" | custom-call | flops 5637144576 | bytes 12845056 | tf_op jit(solution)/shard_map/head_stats/pallas_call | solution.py:520
  235.5 1.3 collective-permute-done.28.refs_0_
  237.9 1.3 collective-permute-done.35.refs_1_
  240.2 6.6 %head_stats.5 = f32[8,256]{1,0:T(8,128)} custom-call(s32[2]{0:T(128)} %pad_add_fusion.3.limit_ref, bf16[128,3584]{1,0:T(8,128)(2,1)} %copy-done.10, bf16[128,3584]{1,0:T(8,128)(2,1)} %copy-done.11, bf16[3584,1024]{1,0:T(8,128)(2,1)} %copy-done, s32[256,1]{1,0:T(8,128)} %copy.170.refs_3_), custom_call_target="tpu_custom_call" | custom-call | flops 1879048192 | bytes 9175040 | tf_op jit(solution)/shard_map/head_stats/pallas_call | solution.py:520
  247.7 5.0 %collective-permute-start.37 = (f32[3,2,2,2,2,64]{5,3,2,1,4,0:T(2,128)S(1)}, f32[3,2,2,2,2,64]{5,3,2,1,4,0:T(2,128)S(1)}, u32[]{:S(2)}, u32[]{:S(2)}) collective-permute-start(f32[3,2,2,2,2,64]{5,3,2,1,4,0:T(2,128)S(1)} %maximum_maximum_fusion.1), channel_id=1, source_target_pairs={{0,16},{4,20},{8,24},{12,28},{16,0},{20,4},{24,8},{28,12},{1,17},{... | collective-permute-start | bytes 36872 | tf_op jit(solution)/shard_map/ppermute | solution.py:30
  252.7 1.5 collective-permute-start.38
  254.5 2.0 collective-permute-done.36
  256.5 1.8 collective-permute-done.38
  259.2 1.5 collective-permute-start.40
  260.7 1.4 collective-permute-done.41
  262.2 1.1 collective-permute-done.40
  264.4 1.2 collective-permute-start.42
  266.1 1.9 collective-permute-done.42
  (186 shorter events, 25.6 us)
Async XLA Ops:
  1.9 24.8 %copy-start.12 = (bf16[2,64,896]{2,1,0:T(8,128)(2,1)}, bf16[2,64,896]{2,1,0:T(8,128)(2,1)S(1)}, u32[]{:S(2)}) copy-start(bf16[2,64,896]{2,1,0:T(8,128)(2,1)S(1)} %copy.175.refs_0_) | copy-start | bytes 688132
  1.9 18.0 %collective-permute-start = (bf16[2,64,896]{2,1,0:T(8,128)(2,1)S(1)}, bf16[2,64,896]{2,1,0:T(8,128)(2,1)S(1)}, u32[]{:S(2)}, u32[]{:S(2)}) collective-permute-start(bf16[2,64,896]{2,1,0:T(8,128)(2,1)S(1)} %copy.175.refs_0_), channel_id=1, source_target_pairs={{0,8},{4,12},{8,0},{12,4},{16,24},{20,28},{24,16},{28,20},{1,9},{5... | collective-permute-start | bytes 688136 | tf_op jit(solution)/shard_map/ppermute | solution.py:30
  5.0 14.9 %collective-permute-start.2 = (bf16[2,64,896]{2,1,0:T(8,128)(2,1)S(1)}, bf16[2,64,896]{2,1,0:T(8,128)(2,1)S(1)}, u32[]{:S(2)}, u32[]{:S(2)}) collective-permute-start(bf16[2,64,896]{2,1,0:T(8,128)(2,1)S(1)} %copy.175.refs_0_), channel_id=1, source_target_pairs={{0,4},{4,0},{8,12},{12,8},{16,20},{20,16},{24,28},{28,24},{1,5},{5... | collective-permute-start | bytes 688136 | tf_op jit(solution)/shard_map/ppermute | solution.py:35
  6.5 24.3 %collective-permute-start.4 = (bf16[2,64,896]{2,1,0:T(8,128)(2,1)S(1)}, bf16[2,64,896]{2,1,0:T(8,128)(2,1)}, u32[]{:S(2)}, u32[]{:S(2)}) collective-permute-start(bf16[2,64,896]{2,1,0:T(8,128)(2,1)S(1)} %copy.175.refs_0_), channel_id=1, source_target_pairs={{0,16},{4,20},{8,24},{12,28},{16,0},{20,4},{24,8},{28,12},{1,17},{... | collective-permute-start | bytes 688136 | tf_op jit(solution)/shard_map/ppermute | solution.py:30
  14.4 5.4 %collective-permute-start.1 = (f32[2,14]{0,1:T(8,128)S(1)}, f32[2,14]{0,1:T(8,128)S(1)}, u32[]{:S(2)}, u32[]{:S(2)}) collective-permute-start(f32[2,14]{0,1:T(8,128)S(1)} %negate_multiply_fusion), channel_id=1, source_target_pairs={{0,4},{4,8},{8,12},{12,16},{16,20},{20,24},{24,28},{1,5},{5,9},{9,... | collective-permute-start | bytes 344 | tf_op jit(solution)/shard_map/ppermute | solution.py:330
  18.8 7.9 %copy-start.4 = (bf16[2,256,64]{2,1,0:T(8,128)(2,1)}, bf16[2,256,64]{2,1,0:T(8,128)(2,1)S(1)}, u32[]{:S(2)}) copy-start(bf16[2,256,64]{2,1,0:T(8,128)(2,1)S(1)} %copy.148.c_ref.refs_9_) | copy-start | bytes 196612
  19.8 25.6 %copy-start.13 = (bf16[2,64,896]{2,1,0:T(8,128)(2,1)}, bf16[2,64,896]{2,1,0:T(8,128)(2,1)S(1)}, u32[]{:S(2)}) copy-start(bf16[2,64,896]{2,1,0:T(8,128)(2,1)S(1)} %collective-permute-done.refs_2_) | copy-start | bytes 688132
  19.9 6.9 %copy-start.14 = (bf16[2,64,896]{2,1,0:T(8,128)(2,1)}, bf16[2,64,896]{2,1,0:T(8,128)(2,1)S(1)}, u32[]{:S(2)}) copy-start(bf16[2,64,896]{2,1,0:T(8,128)(2,1)S(1)} %collective-permute-done.2.refs_1_) | copy-start | bytes 688132
  27.4 8.3 %copy-start.2 = (f32[2,256,896]{2,1,0:T(8,128)}, f32[2,256,896]{2,1,0:T(8,128)S(1)}, u32[]{:S(2)}) copy-start(f32[2,256,896]{2,1,0:T(8,128)S(1)} %get-tuple-element.51.refs_8_) | copy-start | bytes 5505028
  27.4 8.3 %collective-permute-start.6 = (bf16[2,64,896]{2,1,0:T(8,128)(2,1)S(1)}, bf16[2,64,896]{2,1,0:T(8,128)(2,1)S(1)}, u32[]{:S(2)}, u32[]{:S(2)}) collective-permute-start(bf16[2,64,896]{2,1,0:T(8,128)(2,1)S(1)} %get-tuple-element.47), channel_id=1, source_target_pairs={{0,4},{4,8},{8,12},{12,16},{16,20},{20,24},{24,28},{1,5},{5,9},{9,... | collective-permute-start | bytes 688136 | tf_op jit(solution)/shard_map/ppermute | solution.py:375
  30.8 6.3 %collective-permute-start.7 = (bf16[2,64,896]{2,1,0:T(8,128)(2,1)}, bf16[2,64,896]{2,1,0:T(8,128)(2,1)S(1)}, u32[]{:S(2)}, u32[]{:S(2)}) collective-permute-start(bf16[2,64,896]{2,1,0:T(8,128)(2,1)} %collective-permute-done.4.refs_4_), channel_id=1, source_target_pairs={{0,8},{4,12},{8,0},{12,4},{16,24},{20,28},{24,16},{28,20},{1,9},{5... | collective-permute-start | bytes 688136 | tf_op jit(solution)/shard_map/ppermute | solution.py:30
  37.1 8.4 %copy-start.16 = (bf16[2,64,896]{2,1,0:T(8,128)(2,1)}, bf16[2,64,896]{2,1,0:T(8,128)(2,1)S(1)}, u32[]{:S(2)}) copy-start(bf16[2,64,896]{2,1,0:T(8,128)(2,1)S(1)} %collective-permute-done.7.refs_6_) | copy-start | bytes 688132
  37.1 5.1 %copy-start.22 = (s32[256]{0:T(256)S(1)}, s32[256]{0:T(256)}, u32[]{:S(2)}) copy-start(s32[256]{0:T(256)} %param.20) | copy-start | bytes 3076
  37.1 5.1 %copy-start.23 = (s32[256]{0:T(256)S(1)}, s32[256]{0:T(256)}, u32[]{:S(2)}) copy-start(s32[256]{0:T(256)} %param.19) | copy-start | bytes 3076
  37.1 44.1 %all-to-all-start = ((bf16[4,224,1024]{2,1,0:T(8,128)(2,1)}), bf16[4,224,1024]{2,1,0:T(8,128)(2,1)S(1)}, u32[]{:S(2)}, u32[]{:S(2)}) async-start(bf16[4,224,1024]{2,1,0:T(8,128)(2,1)} %get-tuple-element.57), calls=%async_computation | async-start | bytes 3670016 | tf_op jit(solution)/shard_map/all_to_all | solution.py:399
  43.0 9.2 %collective-permute-start.5 = (bf16[2,64,896]{2,1,0:T(8,128)(2,1)}, bf16[2,64,896]{2,1,0:T(8,128)(2,1)S(1)}, u32[]{:S(2)}, u32[]{:S(2)}) collective-permute-start(bf16[2,64,896]{2,1,0:T(8,128)(2,1)} %collective-permute-done.4.refs_4_), channel_id=1, source_target_pairs={{0,4},{4,0},{8,12},{12,8},{16,20},{20,16},{24,28},{28,24},{1,5},{5... | collective-permute-start | bytes 688136 | tf_op jit(solution)/shard_map/ppermute | solution.py:35
  45.4 10.1 %collective-permute-start.3 = (bf16[2,64,896]{2,1,0:T(8,128)(2,1)S(1)}, bf16[2,64,896]{2,1,0:T(8,128)(2,1)S(1)}, u32[]{:S(2)}, u32[]{:S(2)}) collective-permute-start(bf16[2,64,896]{2,1,0:T(8,128)(2,1)S(1)} %collective-permute-done.refs_2_), channel_id=1, source_target_pairs={{0,4},{4,0},{8,12},{12,8},{16,20},{20,16},{24,28},{28,24},{1,5},{5... | collective-permute-start | bytes 688136 | tf_op jit(solution)/shard_map/ppermute | solution.py:35
  45.5 12.5 %collective-permute-start.8 = (bf16[2,64,896]{2,1,0:T(8,128)(2,1)S(1)}, bf16[2,64,896]{2,1,0:T(8,128)(2,1)S(1)}, u32[]{:S(2)}, u32[]{:S(2)}) collective-permute-start(bf16[2,64,896]{2,1,0:T(8,128)(2,1)S(1)} %collective-permute-done.7.refs_6_), channel_id=1, source_target_pairs={{0,4},{4,0},{8,12},{12,8},{16,20},{20,16},{24,28},{28,24},{1,5},{5... | collective-permute-start | bytes 688136 | tf_op jit(solution)/shard_map/ppermute | solution.py:35
  52.2 5.8 %copy-start.17 = (bf16[2,64,896]{2,1,0:T(8,128)(2,1)}, bf16[2,64,896]{2,1,0:T(8,128)(2,1)S(1)}, u32[]{:S(2)}) copy-start(bf16[2,64,896]{2,1,0:T(8,128)(2,1)S(1)} %collective-permute-done.5.refs_5_) | copy-start | bytes 688132
  55.5 2.5 copy-start.18
  81.2 7.1 %collective-permute-start.9 = (bf16[256,3584]{1,0:T(8,128)(2,1)}, bf16[256,3584]{1,0:T(8,128)(2,1)}, u32[]{:S(2)}, u32[]{:S(2)}) collective-permute-start(bf16[256,3584]{1,0:T(8,128)(2,1)} %get-tuple-element.58), channel_id=1, source_target_pairs={{0,1},{1,0},{2,3},{3,2},{4,5},{5,4},{6,7},{7,6},{8,9},{9,8},{10,11... | collective-permute-start | bytes 5505032 | tf_op jit(solution)/shard_map/ppermute | solution.py:58
  81.2 48.1 %all-to-all-start.1 = ((bf16[4,224,1024]{2,1,0:T(8,128)(2,1)}), bf16[4,224,1024]{2,1,0:T(8,128)(2,1)}, u32[]{:S(2)}, u32[]{:S(2)}) async-start(bf16[4,224,1024]{2,1,0:T(8,128)(2,1)} %get-tuple-element.59), calls=%async_computation.1 | async-start | bytes 3670016 | tf_op jit(solution)/shard_map/all_to_all | solution.py:399
  85.6 43.7 %collective-permute-start.14 = (bf16[4,224,1024]{2,1,0:T(8,128)(2,1)S(1)}, bf16[4,224,1024]{2,1,0:T(8,128)(2,1)}, u32[]{:S(2)}, u32[]{:S(2)}) collective-permute-start(bf16[4,224,1024]{2,1,0:T(8,128)(2,1)S(1)} %all-to-all-done.refs_0_), channel_id=1, source_target_pairs={{0,4},{4,0},{8,12},{12,8},{16,20},{20,16},{24,28},{28,24},{1,5},{5... | collective-permute-start | bytes 5505032 | tf_op jit(solution)/shard_map/ppermute | solution.py:35
  90.8 38.5 %collective-permute-start.10 = (bf16[128,3584]{1,0:T(8,128)(2,1)}, bf16[128,3584]{1,0:T(8,128)(2,1)}, u32[]{:S(2)}, u32[]{:S(2)}) collective-permute-start(bf16[128,3584]{1,0:T(8,128)(2,1)} %add_convert_fusion), channel_id=1, source_target_pairs={{0,2},{1,3},{2,0},{3,1},{4,6},{5,7},{6,4},{7,5},{8,10},{9,11},{10,... | collective-permute-start | bytes 2752520 | tf_op jit(solution)/shard_map/ppermute | solution.py:63
  92.3 6.3 %copy-start.20 = (f32[3584]{0:T(1024)S(1)}, f32[3584]{0:T(1024)}, u32[]{:S(2)}) copy-start(f32[3584]{0:T(1024)} %param.36) | copy-start | bytes 43012
  92.3 37.0 %collective-permute-start.11 = (s32[2,256]{1,0:T(2,128)S(1)}, s32[2,256]{1,0:T(2,128)S(1)}, u32[]{:S(2)}, u32[]{:S(2)}) collective-permute-start(s32[2,256]{1,0:T(2,128)S(1)} %pad_add_fusion.1), channel_id=1, source_target_pairs={{0,8},{4,12},{8,0},{12,4},{16,24},{20,28},{24,16},{28,20},{1,9},{5... | collective-permute-start | bytes 6152 | tf_op jit(solution)/shard_map/ppermute | solution.py:30
  94.2 35.1 %collective-permute-start.12 = (s32[2,256]{1,0:T(2,128)S(1)}, s32[2,256]{1,0:T(2,128)S(1)}, u32[]{:S(2)}, u32[]{:S(2)}) collective-permute-start(s32[2,256]{1,0:T(2,128)S(1)} %pad_add_fusion.1), channel_id=1, source_target_pairs={{0,16},{4,20},{8,24},{12,28},{16,0},{20,4},{24,8},{28,12},{1,17},{... | collective-permute-start | bytes 6152 | tf_op jit(solution)/shard_map/ppermute | solution.py:30
  96.6 32.7 %collective-permute-start.13 = (s32[2,256]{1,0:T(2,128)S(1)}, s32[2,256]{1,0:T(2,128)S(1)}, u32[]{:S(2)}, u32[]{:S(2)}) collective-permute-start(s32[2,256]{1,0:T(2,128)S(1)} %pad_add_fusion.1), channel_id=1, source_target_pairs={{0,24},{4,28},{8,16},{12,20},{16,8},{20,12},{24,0},{28,4},{1,25},{... | collective-permute-start | bytes 6152 | tf_op jit(solution)/shard_map/ppermute | solution.py:30
  129.4 1.5 copy-start.1
  133.2 2.9 %copy-start.3 = (bf16[128,3584]{1,0:T(8,128)(2,1)}, bf16[128,3584]{1,0:T(8,128)(2,1)S(1)}, u32[]{:S(2)}) copy-start(bf16[128,3584]{1,0:T(8,128)(2,1)S(1)} %add_and_norm.1.refs_0_) | copy-start | bytes 2752516
  133.2 22.0 %collective-permute-start.15 = (bf16[128,3584]{1,0:T(8,128)(2,1)S(1)}, bf16[128,3584]{1,0:T(8,128)(2,1)S(1)}, u32[]{:S(2)}, u32[]{:S(2)}) collective-permute-start(bf16[128,3584]{1,0:T(8,128)(2,1)S(1)} %add_and_norm.1.refs_0_), channel_id=1, source_target_pairs={{0,2},{1,3},{2,0},{3,1},{4,6},{5,7},{6,4},{7,5},{8,10},{9,11},{10,... | collective-permute-start | bytes 2752520 | tf_op jit(solution)/shard_map/ppermute | solution.py:63
  134.8 21.8 %collective-permute-start.16 = (bf16[128,3584]{1,0:T(8,128)(2,1)S(1)}, bf16[128,3584]{1,0:T(8,128)(2,1)}, u32[]{:S(2)}, u32[]{:S(2)}) collective-permute-start(bf16[128,3584]{1,0:T(8,128)(2,1)S(1)} %add_and_norm.1.refs_0_), channel_id=1, source_target_pairs={{0,8},{4,12},{8,0},{12,4},{16,24},{20,28},{24,16},{28,20},{1,9},{5... | collective-permute-start | bytes 2752520 | tf_op jit(solution)/shard_map/ppermute | solution.py:30
  136.1 20.5 %collective-permute-start.17 = (bf16[128,3584]{1,0:T(8,128)(2,1)S(1)}, bf16[128,3584]{1,0:T(8,128)(2,1)S(1)}, u32[]{:S(2)}, u32[]{:S(2)}) collective-permute-start(bf16[128,3584]{1,0:T(8,128)(2,1)S(1)} %add_and_norm.1.refs_0_), channel_id=1, source_target_pairs={{8,16},{12,20},{16,8},{20,12},{9,17},{13,21},{17,9},{21,13},{10,18... | collective-permute-start | bytes 2752520 | tf_op jit(solution)/shard_map/ppermute | solution.py:46
  136.8 44.6 %collective-permute-start.19 = (bf16[4,224,1024]{2,1,0:T(8,128)(2,1)}, bf16[4,224,1024]{2,1,0:T(8,128)(2,1)}, u32[]{:S(2)}, u32[]{:S(2)}) collective-permute-start(bf16[4,224,1024]{2,1,0:T(8,128)(2,1)} %all-to-all-done.1.refs_2_), channel_id=1, source_target_pairs={{0,4},{4,0},{8,12},{12,8},{16,20},{20,16},{24,28},{28,24},{1,5},{5... | collective-permute-start | bytes 5505032 | tf_op jit(solution)/shard_map/ppermute | solution.py:35
  156.6 21.1 %collective-permute-start.18 = (bf16[128,3584]{1,0:T(8,128)(2,1)}, bf16[128,3584]{1,0:T(8,128)(2,1)}, u32[]{:S(2)}, u32[]{:S(2)}) collective-permute-start(bf16[128,3584]{1,0:T(8,128)(2,1)} %collective-permute-done.16.refs_4_), channel_id=1, source_target_pairs={{0,2},{1,3},{2,0},{3,1},{4,6},{5,7},{6,4},{7,5},{8,10},{9,11},{10,... | collective-permute-start | bytes 2752520 | tf_op jit(solution)/shard_map/ppermute | solution.py:63
  157.6 23.7 %collective-permute-start.20 = (bf16[128,3584]{1,0:T(8,128)(2,1)S(1)}, bf16[128,3584]{1,0:T(8,128)(2,1)}, u32[]{:S(2)}, u32[]{:S(2)}) collective-permute-start(bf16[128,3584]{1,0:T(8,128)(2,1)S(1)} %collective-permute-done.17), channel_id=1, source_target_pairs={{8,0},{12,4},{16,24},{20,28},{9,1},{13,5},{17,25},{21,29},{10,2},{... | collective-permute-start | bytes 2752520 | tf_op jit(solution)/shard_map/ppermute | solution.py:46
  158.9 22.4 %collective-permute-start.21 = (bf16[128,3584]{1,0:T(8,128)(2,1)}, bf16[128,3584]{1,0:T(8,128)(2,1)}, u32[]{:S(2)}, u32[]{:S(2)}) collective-permute-start(bf16[128,3584]{1,0:T(8,128)(2,1)} %collective-permute-done.16.refs_4_), channel_id=1, source_target_pairs={{8,16},{12,20},{16,8},{20,12},{9,17},{13,21},{17,9},{21,13},{10,18... | collective-permute-start | bytes 2752520 | tf_op jit(solution)/shard_map/ppermute | solution.py:46
  160.8 24.7 %collective-permute-start.23 = (bf16[128,3584]{1,0:T(8,128)(2,1)}, bf16[128,3584]{1,0:T(8,128)(2,1)S(1)}, u32[]{:S(2)}, u32[]{:S(2)}) collective-permute-start(bf16[128,3584]{1,0:T(8,128)(2,1)} %copy-done.3), channel_id=1, source_target_pairs={{0,1},{1,0},{2,3},{3,2},{4,5},{5,4},{6,7},{7,6},{8,9},{9,8},{10,11... | collective-permute-start | bytes 2752520 | tf_op jit(solution)/shard_map/ppermute | solution.py:58
  177.6 19.3 %collective-permute-start.25 = (bf16[128,3584]{1,0:T(8,128)(2,1)}, bf16[128,3584]{1,0:T(8,128)(2,1)}, u32[]{:S(2)}, u32[]{:S(2)}) collective-permute-start(bf16[128,3584]{1,0:T(8,128)(2,1)} %collective-permute-done.16.refs_4_), channel_id=1, source_target_pairs={{0,1},{1,0},{2,3},{3,2},{4,5},{5,4},{6,7},{7,6},{8,9},{9,8},{10,11... | collective-permute-start | bytes 2752520 | tf_op jit(solution)/shard_map/ppermute | solution.py:58
  181.4 15.6 %collective-permute-start.24 = (bf16[128,3584]{1,0:T(8,128)(2,1)}, bf16[128,3584]{1,0:T(8,128)(2,1)}, u32[]{:S(2)}, u32[]{:S(2)}) collective-permute-start(bf16[128,3584]{1,0:T(8,128)(2,1)} %copy-done.25), channel_id=1, source_target_pairs={{0,1},{1,0},{2,3},{3,2},{4,5},{5,4},{6,7},{7,6},{8,9},{9,8},{10,11... | collective-permute-start | bytes 2752520 | tf_op jit(solution)/shard_map/ppermute | solution.py:58
  181.4 15.6 %collective-permute-start.26 = (bf16[128,3584]{1,0:T(8,128)(2,1)}, bf16[128,3584]{1,0:T(8,128)(2,1)}, u32[]{:S(2)}, u32[]{:S(2)}) collective-permute-start(bf16[128,3584]{1,0:T(8,128)(2,1)} %collective-permute-done.18.refs_5_), channel_id=1, source_target_pairs={{0,1},{1,0},{2,3},{3,2},{4,5},{5,4},{6,7},{7,6},{8,9},{9,8},{10,11... | collective-permute-start | bytes 2752520 | tf_op jit(solution)/shard_map/ppermute | solution.py:58
  181.9 30.2 %collective-permute-start.27 = (bf16[128,3584]{1,0:T(8,128)(2,1)}, bf16[128,3584]{1,0:T(8,128)(2,1)}, u32[]{:S(2)}, u32[]{:S(2)}) collective-permute-start(bf16[128,3584]{1,0:T(8,128)(2,1)} %collective-permute-done.21), channel_id=1, source_target_pairs={{8,0},{12,4},{16,24},{20,28},{9,1},{13,5},{17,25},{21,29},{10,2},{... | collective-permute-start | bytes 2752520 | tf_op jit(solution)/shard_map/ppermute | solution.py:46
  185.4 2.1 copy-start.26
  185.4 26.7 %collective-permute-start.22 = (bf16[128,3584]{1,0:T(8,128)(2,1)}, bf16[128,3584]{1,0:T(8,128)(2,1)}, u32[]{:S(2)}, u32[]{:S(2)}) collective-permute-start(bf16[128,3584]{1,0:T(8,128)(2,1)} %broadcast_select_fusion.1.refs_0_), channel_id=1, source_target_pairs={{0,2},{1,3},{2,0},{3,1},{4,6},{5,7},{6,4},{7,5},{8,10},{9,11},{10,... | collective-permute-start | bytes 2752520 | tf_op jit(solution)/shard_map/ppermute | solution.py:63
  194.0 2.9 %copy-start = (bf16[3584,1024]{1,0:T(8,128)(2,1)}, bf16[3584,1024]{1,0:T(8,128)(2,1)S(1)}, u32[]{:S(2)}) copy-start(bf16[3584,1024]{1,0:T(8,128)(2,1)S(1)} %place_head_rows.1.refs_8_.refs_6_.refs_2_) | copy-start | bytes 22020100
  196.9 23.2 %collective-permute-start.29 = (bf16[128,3584]{1,0:T(8,128)(2,1)}, bf16[128,3584]{1,0:T(8,128)(2,1)}, u32[]{:S(2)}, u32[]{:S(2)}) collective-permute-start(bf16[128,3584]{1,0:T(8,128)(2,1)} %broadcast_select_fusion.1.refs_0_), channel_id=1, source_target_pairs={{0,1},{1,0},{2,3},{3,2},{4,5},{5,4},{6,7},{7,6},{8,9},{9,8},{10,11... | collective-permute-start | bytes 2752520 | tf_op jit(solution)/shard_map/ppermute | solution.py:58
  213.4 9.2 %copy-start.9 = (bf16[128,3584]{1,0:T(8,128)(2,1)}, bf16[128,3584]{1,0:T(8,128)(2,1)S(1)}, u32[]{:S(2)}) copy-start(bf16[128,3584]{1,0:T(8,128)(2,1)S(1)} %broadcast_select_fusion.refs_4_) | copy-start | bytes 2752516
  213.4 7.7 %collective-permute-start.31 = (bf16[128,3584]{1,0:T(8,128)(2,1)S(1)}, bf16[128,3584]{1,0:T(8,128)(2,1)}, u32[]{:S(2)}, u32[]{:S(2)}) collective-permute-start(bf16[128,3584]{1,0:T(8,128)(2,1)S(1)} %broadcast_select_fusion.refs_4_), channel_id=1, source_target_pairs={{0,1},{1,0},{2,3},{3,2},{4,5},{5,4},{6,7},{7,6},{8,9},{9,8},{10,11... | collective-permute-start | bytes 2752520 | tf_op jit(solution)/shard_map/ppermute | solution.py:58
  214.0 8.6 %collective-permute-start.30 = (bf16[128,3584]{1,0:T(8,128)(2,1)}, bf16[128,3584]{1,0:T(8,128)(2,1)}, u32[]{:S(2)}, u32[]{:S(2)}) collective-permute-start(bf16[128,3584]{1,0:T(8,128)(2,1)} %collective-permute-done.22.refs_1_), channel_id=1, source_target_pairs={{0,1},{1,0},{2,3},{3,2},{4,5},{5,4},{6,7},{7,6},{8,9},{9,8},{10,11... | collective-permute-start | bytes 2752520 | tf_op jit(solution)/shard_map/ppermute | solution.py:58
  214.1 22.7 %collective-permute-start.28 = (bf16[128,3584]{1,0:T(8,128)(2,1)S(1)}, bf16[128,3584]{1,0:T(8,128)(2,1)S(1)}, u32[]{:S(2)}, u32[]{:S(2)}) collective-permute-start(bf16[128,3584]{1,0:T(8,128)(2,1)S(1)} %broadcast_select_fusion.refs_4_), channel_id=1, source_target_pairs={{0,2},{1,3},{2,0},{3,1},{4,6},{5,7},{6,4},{7,5},{8,10},{9,11},{10,... | collective-permute-start | bytes 2752520 | tf_op jit(solution)/shard_map/ppermute | solution.py:63
  215.8 19.7 %collective-permute-start.32 = (f32[3,2,2,2,2,64]{5,3,2,1,4,0:T(2,128)S(1)}, f32[3,2,2,2,2,64]{5,3,2,1,4,0:T(2,128)S(1)}, u32[]{:S(2)}, u32[]{:S(2)}) collective-permute-start(f32[3,2,2,2,2,64]{5,3,2,1,4,0:T(2,128)S(1)} %bitcast.233), channel_id=1, source_target_pairs={{0,8},{4,12},{8,0},{12,4},{16,24},{20,28},{24,16},{28,20},{1,9},{5... | collective-permute-start | bytes 36872 | tf_op jit(solution)/shard_map/ppermute | solution.py:30
  220.2 15.3 %collective-permute-start.33 = (f32[3,2,2,2,2,64]{5,3,2,1,4,0:T(2,128)S(1)}, f32[3,2,2,2,2,64]{5,3,2,1,4,0:T(2,128)S(1)}, u32[]{:S(2)}, u32[]{:S(2)}) collective-permute-start(f32[3,2,2,2,2,64]{5,3,2,1,4,0:T(2,128)S(1)} %bitcast.234), channel_id=1, source_target_pairs={{0,16},{4,20},{8,24},{12,28},{16,0},{20,4},{24,8},{28,12},{1,17},{... | collective-permute-start | bytes 36872 | tf_op jit(solution)/shard_map/ppermute | solution.py:30
  221.1 14.4 %collective-permute-start.34 = (f32[3,2,2,2,2,64]{5,3,2,1,4,0:T(2,128)S(1)}, f32[3,2,2,2,2,64]{5,3,2,1,4,0:T(2,128)S(1)}, u32[]{:S(2)}, u32[]{:S(2)}) collective-permute-start(f32[3,2,2,2,2,64]{5,3,2,1,4,0:T(2,128)S(1)} %bitcast.235), channel_id=1, source_target_pairs={{0,24},{4,28},{8,16},{12,20},{16,8},{20,12},{24,0},{28,4},{1,25},{... | collective-permute-start | bytes 36872 | tf_op jit(solution)/shard_map/ppermute | solution.py:30
  236.8 2.5 copy-start.10
  236.8 2.5 collective-permute-start.35
  237.9 25.9 %copy-start.21 = (s32[48]{0:T(128)S(1)}, s32[48]{0:T(128)}, u32[]{:S(2)}) copy-start(s32[48]{0:T(128)} %param.21) | copy-start | bytes 580
  246.8 21.2 %copy-start.24 = (s32[48]{0:T(128)S(1)}, s32[48]{0:T(128)}, u32[]{:S(2)}) copy-start(s32[48]{0:T(128)} %param.22) | copy-start | bytes 580
  247.7 6.8 %collective-permute-start.37 = (f32[3,2,2,2,2,64]{5,3,2,1,4,0:T(2,128)S(1)}, f32[3,2,2,2,2,64]{5,3,2,1,4,0:T(2,128)S(1)}, u32[]{:S(2)}, u32[]{:S(2)}) collective-permute-start(f32[3,2,2,2,2,64]{5,3,2,1,4,0:T(2,128)S(1)} %maximum_maximum_fusion.1), channel_id=1, source_target_pairs={{0,16},{4,20},{8,24},{12,28},{16,0},{20,4},{24,8},{28,12},{1,17},{... | collective-permute-start | bytes 36872 | tf_op jit(solution)/shard_map/ppermute | solution.py:30
  252.7 3.8 %collective-permute-start.36 = (f32[3,2,2,2,2,64]{5,3,2,1,4,0:T(2,128)S(1)}, f32[3,2,2,2,2,64]{5,3,2,1,4,0:T(2,128)S(1)}, u32[]{:S(2)}, u32[]{:S(2)}) collective-permute-start(f32[3,2,2,2,2,64]{5,3,2,1,4,0:T(2,128)S(1)} %maximum_maximum_fusion.1), channel_id=1, source_target_pairs={{0,8},{4,12},{8,0},{12,4},{16,24},{20,28},{24,16},{28,20},{1,9},{5... | collective-permute-start | bytes 36872 | tf_op jit(solution)/shard_map/ppermute | solution.py:30
  252.7 5.6 %collective-permute-start.38 = (f32[3,2,2,2,2,64]{5,3,2,1,4,0:T(2,128)S(1)}, f32[3,2,2,2,2,64]{5,3,2,1,4,0:T(2,128)S(1)}, u32[]{:S(2)}, u32[]{:S(2)}) collective-permute-start(f32[3,2,2,2,2,64]{5,3,2,1,4,0:T(2,128)S(1)} %maximum_maximum_fusion.1), channel_id=1, source_target_pairs={{0,24},{4,28},{8,16},{12,20},{16,8},{20,12},{24,0},{28,4},{1,25},{... | collective-permute-start | bytes 36872 | tf_op jit(solution)/shard_map/ppermute | solution.py:30
  258.5 3.6 %collective-permute-start.41 = (f32[3,4,2,2,2,64]{5,3,2,1,4,0:T(2,128)S(1)}, f32[3,4,2,2,2,64]{5,3,2,1,4,0:T(2,128)S(1)}, u32[]{:S(2)}, u32[]{:S(2)}) collective-permute-start(f32[3,4,2,2,2,64]{5,3,2,1,4,0:T(2,128)S(1)} %pad_maximum_fusion.2), channel_id=1, source_target_pairs={{0,3},{1,2},{2,1},{3,0},{4,7},{5,6},{6,5},{7,4},{8,11},{9,10},{10,... | collective-permute-start | bytes 73736 | tf_op jit(solution)/shard_map/ppermute | solution.py:254
  258.6 3.5 %collective-permute-start.39 = (f32[3,4,2,2,2,64]{5,3,2,1,4,0:T(2,128)S(1)}, f32[3,4,2,2,2,64]{5,3,2,1,4,0:T(2,128)S(1)}, u32[]{:S(2)}, u32[]{:S(2)}) collective-permute-start(f32[3,4,2,2,2,64]{5,3,2,1,4,0:T(2,128)S(1)} %pad_maximum_fusion.2), channel_id=1, source_target_pairs={{0,1},{1,0},{2,3},{3,2},{4,5},{5,4},{6,7},{7,6},{8,9},{9,8},{10,11... | collective-permute-start | bytes 73736 | tf_op jit(solution)/shard_map/ppermute | solution.py:58
  259.2 4.1 %collective-permute-start.40 = (f32[3,4,2,2,2,64]{5,3,2,1,4,0:T(2,128)S(1)}, f32[3,4,2,2,2,64]{5,3,2,1,4,0:T(2,128)S(1)}, u32[]{:S(2)}, u32[]{:S(2)}) collective-permute-start(f32[3,4,2,2,2,64]{5,3,2,1,4,0:T(2,128)S(1)} %pad_maximum_fusion.2), channel_id=1, source_target_pairs={{0,2},{1,3},{2,0},{3,1},{4,6},{5,7},{6,4},{7,5},{8,10},{9,11},{10,... | collective-permute-start | bytes 73736 | tf_op jit(solution)/shard_map/ppermute | solution.py:63
  264.4 3.6 %collective-permute-start.42 = (f32[48]{0:T(128)S(1)}, f32[48]{0:T(128)S(1)}, u32[]{:S(2)}, u32[]{:S(2)}) collective-permute-start(f32[48]{0:T(128)S(1)} %convolution_bitcast_fusion), channel_id=1, source_target_pairs={{0,4},{4,0},{8,12},{12,8},{16,20},{20,16},{24,28},{28,24},{1,5},{5... | collective-permute-start | bytes 584 | tf_op jit(solution)/shard_map/ppermute | solution.py:35
  (8 other events, 7.5 us)

commit v4 on v3

--- a/solution.py
+++ b/solution.py
@@ -10,6 +10,7 @@
 
 highest = lax.Precision.HIGHEST
 CHAIN = 4
+TAIL_ROWS = 16
 SIDE = 2
 
 
@@ -92,19 +93,27 @@
 
 
 def local_kernel(
-    x_ref, b_ref, c_ref, step_ref, rate_ref, start_ref, skip_ref, out_ref, end_ref, decay_ref,
+    x_ref, both_ref, step_ref, rate_ref, start_ref, skip_ref, out_ref, end_ref, decay_ref,
 ):
     tok_rows, inner = x_ref.shape
     head_count = step_ref.shape[1]
     head_dim = inner // head_count
-    state_dim = b_ref.shape[1]
+    state_dim = both_ref.shape[1] // 2
+    b_values, c_values = both_ref[:, :state_dim], both_ref[:, state_dim:]
     row = lax.broadcasted_iota(jnp.int32, (tok_rows, tok_rows), 0)
     col = lax.broadcasted_iota(jnp.int32, (tok_rows, tok_rows), 1)
     causal = (col >= start_ref[...]) & (col <= row)
-    gram = jnp.where(causal, dot(c_ref[...], b_ref[...], ((1,), (1,))), 0.0)
+    gram = jnp.where(causal, dot(c_values, b_values, ((1,), (1,))), 0.0)
     steps = step_ref[...]
     logs = exact(jnp.where(col <= row, 1.0, 0.0), -steps * rate_ref[...])
-    decay_ref[...] = logs - exact(jnp.where(col == start_ref[...] - 1, 1.0, 0.0), logs)
+    decay = logs - exact(jnp.where(col == start_ref[...] - 1, 1.0, 0.0), logs)
+    decay_ref[...] = decay
+    since = jnp.broadcast_to(decay[tok_rows - 1 :, :], (TAIL_ROWS, head_count))
+    term = lax.broadcasted_iota(jnp.int32, since.shape, 0)
+    high = since.astype(jnp.bfloat16).astype(jnp.float32)
+    middle = (since - high).astype(jnp.bfloat16).astype(jnp.float32)
+    low = since - high - middle
+    since = jnp.where(term == 0, high, jnp.where(term == 1, middle, jnp.where(term == 2, low, 0.0)))
     fill = jnp.zeros((tok_rows, 128 - 2 * head_count), jnp.float32)
     as_rows = jnp.transpose(jnp.concatenate([logs, steps, fill], axis=1))
     last_log = logs[tok_rows - 1 :, :]
@@ -125,28 +134,34 @@
             jnp.where(lane < head_dim, sides[0], sides[-1])
             + pair_lanes(skip, first, head_dim)[:1] * x_wide
         )
+        tail = pair_lanes(since, first, head_dim)
+        end_ref[state_dim:, span] = tail.astype(end_ref.dtype)
         weighted = (pair_lanes(weight, first, head_dim) * x_wide).astype(jnp.bfloat16)
-        end_ref[:, span] = dot(b_ref[...], weighted, ((0,), (0,))).astype(end_ref.dtype)
-
-
-def project_kernel(slots, order_ref, *refs):
+        end_ref[:state_dim, span] = dot(b_values, weighted, ((0,), (0,))).astype(end_ref.dtype)
+
+
+def project_kernel(slots, joined, order_ref, *refs):
     prompt_refs = refs[:slots]
-    (local_ref, c_ref, pick_ref, inherited_ref, decay_ref, arriving_ref, tail_ref, gate_ref,
+    (local_ref, both_ref, pick_ref, inherited_ref, decay_ref, arriving_ref, tail_ref, gate_ref,
      weight_ref, down_ref, up_ref, kept_ref, sent_ref, gated, low_rank) = refs[slots:]
     models, tok_rows, inner = local_ref.shape
     head_count = decay_ref.shape[2]
     head_dim = inner // head_count
-    state_dim = c_ref.shape[2]
+    state_dim = both_ref.shape[2] // 2
     share = tok_rows // order_ref.shape[0]
     half = models * tok_rows // 2
 
     @pl.when(pl.program_id(0) == 0)
     def _():
         for model in range(models):
-            c_values = c_ref[model].astype(jnp.float32)
+            c_values = both_ref[model][:, state_dim:].astype(jnp.float32)
             inherited = inherited_ref[...]
+            mine = dot(
+                (c_values * inherited).astype(jnp.bfloat16), arriving_ref[model, :state_dim, :]
+            )
             tail = jnp.broadcast_to(tail_ref[model], (8, head_count))
-            mine = dot((c_values * inherited).astype(jnp.bfloat16), arriving_ref[model])
+            sent_tail = arriving_ref[model, state_dim:, :].astype(jnp.float32)
+            sent_tail = jnp.sum(sent_tail, axis=0, keepdims=True)
             borrowed = jnp.zeros((tok_rows, inner), jnp.float32)
             for slot in range(0, slots, 4):
                 chosen = [c_values * pick_ref[:, i : i + 1] for i in range(slot, slot + 4)]
@@ -158,7 +173,8 @@
             decay = decay_ref[model]
             for first, span in head_pairs(head_count, head_dim):
                 log_wide = pair_lanes(decay, first, head_dim)
-                log_prompt = log_wide + inherited * pair_lanes(tail, first, head_dim)[:1]
+                since = sent_tail[:, span] if joined else pair_lanes(tail, first, head_dim)[:1]
+                log_prompt = log_wide + inherited * since
                 output = (
                     local_ref[model, :, span]
                     + jnp.exp(log_wide) * mine[:, span]
@@ -322,18 +338,11 @@
             for source in [seq_index] + [from_partner(side, block) for side, block in partners]
         ]
     )
-    last_rollout = (offsets >= start_local[-1]).astype(jnp.float32)
-    local_tail = -head_decay_rate * jnp.sum(
-        token_step_sizes * last_rollout[None, :, None], axis=1
-    )
-    next_one = [(i, i + 1) for i in range(seq_count - 1)]
-    tail = lax.ppermute(local_tail, "seq", next_one)
+    both_projections = jnp.concatenate([input_projection_b, output_projection_c], axis=2)
     pick = (holder_tok[:, None] == prompt_holder[None, :]).astype(jnp.float32)
     inherited = (start_local < 0).astype(jnp.float32)
     beside_next = beside(states[1])
-    mixer_x, states[1], tail, *beside_held = tied(
-        mixer_input_x, states[1], tail, *beside_held
-    )
+    mixer_x, states[1], *beside_held = tied(mixer_input_x, states[1], *beside_held)
 
     per_model = lambda *shape: pl.BlockSpec((None,) + shape, lambda m: (m,) + (0,) * len(shape))
     local_out, local_end, decay = pl.pallas_call(
@@ -341,8 +350,7 @@
         grid=(models,),
         in_specs=[
             per_model(tok_rows, inner_local),
-            per_model(tok_rows, state_dim),
-            per_model(tok_rows, state_dim),
+            per_model(tok_rows, 2 * state_dim),
             per_model(tok_rows, head_count),
             per_model(1, head_count),
             pl.BlockSpec((tok_rows, 1), lambda m: (0, 0)),
@@ -350,12 +358,12 @@
         ],
         out_specs=[
             per_model(tok_rows, inner_local),
-            per_model(state_dim, inner_local),
+            per_model(state_dim + TAIL_ROWS, inner_local),
             per_model(tok_rows, head_count),
         ],
         out_shape=[
             jax.ShapeDtypeStruct((models, tok_rows, inner_local), jnp.float32),
-            jax.ShapeDtypeStruct((models, state_dim, inner_local), jnp.bfloat16),
+            jax.ShapeDtypeStruct((models, state_dim + TAIL_ROWS, inner_local), jnp.bfloat16),
             jax.ShapeDtypeStruct((models, tok_rows, head_count), jnp.float32),
         ],
         compiler_params=pltpu.CompilerParams(vmem_limit_bytes=32 * 2**20),
@@ -363,8 +371,7 @@
         name="local_tokens",
     )(
         mixer_x,
-        input_projection_b,
-        output_projection_c,
+        both_projections,
         token_step_sizes,
         head_decay_rate[:, None, :],
         start_local[:, None],
@@ -372,8 +379,12 @@
     )
 
     hops = max(1, -(-(seq_count * tok_rows // 8) // tok_rows))
+    next_one = [(i, i + 1) for i in range(seq_count - 1)]
     arriving = lax.ppermute(local_end, "seq", next_one)
+    tail = jnp.zeros((models, head_count), jnp.float32)
     if hops > 1:
+        local_tail = decay[:, -1]
+        tail = lax.ppermute(local_tail, "seq", next_one)
         through = jnp.repeat(jnp.exp(local_tail), inner_local // head_count, axis=1)
         through = through[:, None, :] * inherited[-1]
         for _ in range(hops - 1):
@@ -413,7 +424,7 @@
     resident = [
         *prompts,
         local_out,
-        output_projection_c,
+        both_projections,
         pick,
         inherited[:, None],
         decay,
@@ -422,7 +433,7 @@
         mixer_gate_input,
     ]
     kept, sent = pl.pallas_call(
-        functools.partial(project_kernel, len(prompts)),
+        functools.partial(project_kernel, len(prompts), hops == 1),
         grid=(width // tile,),
         in_specs=[pl.BlockSpec(memory_space=pltpu.SMEM)]
         + [whole(value) for value in resident]
@@ -458,10 +469,10 @@
     own_rows = jnp.transpose(own_rows, (1, 0, 2)).reshape(each, width)
     crossing = [along_x(chip_sum(by).astype(jnp.bfloat16), by) for by in range(1, x_count)]
     besides_head = [beside(came_head[0])]
-    crossing[0], own_rows, came_head[-1], *came_small = tied(
-        crossing[0], own_rows, came_head[-1], *words_and_valid, *besides_head[0]
-    )
-    words_and_valid, besides_head[0] = jnp.stack(came_small[:CHAIN]), came_small[CHAIN:]
+    crossing[0], own_rows, came_head[-1], *words_and_valid = tied(
+        crossing[0], own_rows, came_head[-1], *words_and_valid
+    )
+    words_and_valid = jnp.stack(words_and_valid)
     besides_head += [beside(piece) for piece in came_head[1:]]
     half_block = pl.BlockSpec((each, width), lambda i: (0, 0))
     normed_own = pl.pallas_call(
@@ -474,6 +485,7 @@
         cost_estimate=cost(0, 10 * each * width),
         name="add_and_norm",
     )(own_rows, kept, came, *crossing, final_norm_scale[None, :])
+    normed_own, *besides_head[0] = tied(normed_own, *besides_head[0])
 
     limit = jnp.stack(
         [
@@ -561,8 +573,8 @@
             extra = besides_head[-1]
         elif step == CHAIN - 1:
             head_part = place_head()
-            rows = [both_cores([blocks_of[k]] + nears[k]) for k in (0, 1)]
-            extra = [head_stats(head_part, rows[0] + rows[1], words[:2])]
+            rows = both_cores([blocks_of[0]] + nears[0])
+            extra = [head_stats(head_part, rows, words[0])]
         came = tied(*nears[-1], *extra, *moved)
         nears[-1], extra, moved = came[:count], came[count : -len(moved)], came[-len(moved) :]
         if step == CHAIN - 2:
@@ -580,23 +592,27 @@
         nears.append(crossed(block))
 
     last = CHAIN - 1
+    rows = [both_cores([blocks_of[k]] + nears[k]) for k in range(1, last)]
     middle = head_stats(
         head_part,
-        both_cores([blocks_of[last - 1]] + nears[last - 1]) + both_cores([blocks_of[last]]),
-        jnp.concatenate([words[last - 1].reshape(-1, each), words[last, :, 0]]),
+        [value for values in rows for value in values] + both_cores([blocks_of[last]]),
+        jnp.concatenate([words[1:last].reshape(-1, each), words[last, :, 0]]),
     )
     def blocks(stats):
         return stats[:3].reshape(3, -1, 2, x_count, models, share_rows)
 
-    first = blocks(early)
-    firsts = [first] + [turn(first, by) for by in range(1, CHAIN)]
-    came = tied(*nears[last], middle, *firsts)
-    nears[last], middle, firsts = came[: -CHAIN - 1], came[-CHAIN - 1], came[-CHAIN:]
+    *nears[last], middle, early = tied(*nears[last], middle, early)
     rest = head_stats(head_part, both_cores(nears[last]), words[last, :, 1:])
-    own_side = middle[:3, mp_count:].reshape(3, 1, 2, 1, models, share_rows)
+    whole_blocks = (last - 1) * mp_count
+    own_side = middle[:3, whole_blocks:].reshape(3, 1, 2, 1, models, share_rows)
     other_side = rest[:3].reshape(3, 1, 2, x_count - 1, models, share_rows)
-    late = jnp.concatenate(
-        [blocks(middle[:, :mp_count]), jnp.concatenate([own_side, other_side], axis=3)], axis=1
+    stats = jnp.concatenate(
+        [
+            blocks(early),
+            blocks(middle[:, :whole_blocks]),
+            jnp.concatenate([own_side, other_side], axis=3),
+        ],
+        axis=1,
     )
 
     def merged(several):
@@ -604,10 +620,10 @@
         total = sum(stats[1] * jnp.exp(stats[0] - top) for stats in several)
         return jnp.stack([top, total, sum(stats[2] for stats in several)])
 
-    several = [jnp.concatenate([firsts[0], late], axis=1)]
+    several = [stats]
     for by in range(1, CHAIN):
-        stats = jnp.concatenate([firsts[by], turn(late, by)], axis=1)
-        several.append(jnp.stack([stats[:, k ^ by] for k in range(CHAIN)], axis=1))
+        came = turn(stats, by)
+        several.append(jnp.stack([came[:, k ^ by] for k in range(CHAIN)], axis=1))
     stats = merged(several)
     several = [stats, other_core(stats)[:, :, ::-1]]
     for by in range(1, x_count):

time: 270 us -> 265 us (0.981)
  local copies, waits for them, and re-layouts: 25.6 us -> 22.4 us
    ppermute x7, waiting for transfers between devices: 11.1 us -> 32.6 us  [to_partner(): lax.ppermute(x, 'seq', [(i, partner(i, side, block, count)) for i in rang...]
    ppermute x6, waiting for transfers between devices: 35.8 us -> 16.1 us  [along_x(): lax.ppermute(x, 'mp', [(i, (i + 2 * by) % count) for i in range(count)])]
    ppermute x7, starting transfers between devices: 11.7 us -> 23.5 us  [to_partner(): lax.ppermute(x, 'seq', [(i, partner(i, side, block, count)) for i in rang...]
    ppermute x13 -> x10, starting transfers between devices: 25.2 us -> 14.6 us  [turn(): return lax.ppermute(x, 'seq', [(i, turned(i, by)) for i in range(count)])]
    all_to_all x2, waiting for transfers between devices: 38.3 us -> 32.7 us  [shards(): lax.all_to_all(head[cut], 'seq', 0, 0, axis_index_groups=chain_groups())]
    ppermute x13 -> x10, waiting for transfers between devices: 6.67 us -> 8.6 us  [turn(): return lax.ppermute(x, 'seq', [(i, turned(i, by)) for i in range(count)])]
  transfers between devices with their start and end apart: 45 -> 41, of which waited for: 18 -> 20; matrix products, arithmetic and copies ran while one was open for 10% -> 9% of each run, Pallas kernels for 20% -> 22%
where the time goes in v4:
time: 265 us; the launch traced here: 264 us
  waiting for transfers between devices  96.6 us (36%)
  starting transfers between devices  66.9 us (25%)
  Pallas kernels  64.2 us (24%)
  local copies, waits for them, and re-layouts  22.4 us (8%)
  other arithmetic  11.9 us (4%)
    pallas_call x3, Pallas kernels, head_stats(): pl.pallas_call(functools.partial(head_kernel, count), in_specs=[pl.BlockS...  32.9 us
    all_to_all x2, waiting for transfers between devices, shards(): lax.all_to_all(head[cut], 'seq', 0, 0, axis_index_groups=chain_groups())  32.7 us
    ppermute x7, waiting for transfers between devices, to_partner(): lax.ppermute(x, 'seq', [(i, partner(i, side, block, count)) for i in rang...  32.6 us
    ppermute x7, starting transfers between devices, to_partner(): lax.ppermute(x, 'seq', [(i, partner(i, side, block, count)) for i in rang...  23.5 us
    ppermute x6, waiting for transfers between devices, along_x(): lax.ppermute(x, 'mp', [(i, (i + 2 * by) % count) for i in range(count)])  16.1 us
    pallas_call x1, Pallas kernels, shards(): pl.pallas_call(functools.partial(project_kernel, len(prompts), hops == 1)...  14.8 us
    ppermute x10, starting transfers between devices, turn(): return lax.ppermute(x, 'seq', [(i, turned(i, by)) for i in range(count)])  14.6 us
    unnamed x61, local copies, waits for them, and re-layouts  11.7 us
  transfers between devices with their start and end apart: 41, of which 20 were waited for; matrix products, arithmetic and copies ran while one was open for 9% of the time, Pallas kernels for 22%

profile of v4, /device:TPU:0, one launch (start us, length us, event | category | flops | bytes accessed | tf_op | source)
XLA Modules:
  0.0 263.9 jit_solution(9251226597496677288)
XLA Ops:
  0.7 1.3 copy.114.refs_0_
  2.0 3.1 %collective-permute-start = (bf16[2,64,896]{2,1,0:T(8,128)(2,1)S(1)}, bf16[2,64,896]{2,1,0:T(8,128)(2,1)S(1)}, u32[]{:S(2)}, u32[]{:S(2)}) collective-permute-start(bf16[2,64,896]{2,1,0:T(8,128)(2,1)S(1)} %copy.114.refs_0_), channel_id=1, source_target_pairs={{0,8},{4,12},{8,0},{12,4},{16,24},{20,28},{24,16},{28,20},{1,9},{5... | collective-permute-start | bytes 688136 | tf_op jit(solution)/shard_map/ppermute | solution.py:31
  5.1 1.5 collective-permute-start.1
  6.6 2.6 collective-permute-start.3
  11.8 1.0 copy.91
  12.7 1.0 copy.92
  13.7 0.9 copy.94.step_ref
  15.5 5.2 %local_tokens.1 = (f32[2,256,896]{2,1,0:T(8,128)S(1)}, bf16[2,80,896]{2,1,0:T(8,128)(2,1)}, f32[2,256,14]{2,1,0:T(8,128)S(1)}) custom-call(bf16[2,256,896]{2,1,0:T(8,128)(2,1)S(1)} %copy-done.6, bf16[2,256,128]{2,1,0:T(8,128)(2,1)S(1)} %pad_maximum_fusion.both_ref.refs_9_, f32[2,256,14]{2,1,0:T(8,128)S(1)} %copy.94.step_ref, f32[2,1,14]{2,1,0:T(1,128)S(1)} %bitcast.230, ...), custom_call_target="tpu_custom_call" | custom-call | flops 1000000000 | bytes 8388608 | tf_op jit(solution)/shard_map/local_tokens/pallas_call | solution.py:348
  21.5 4.1 %collective-permute-start.5 = (bf16[2,80,896]{2,1,0:T(8,128)(2,1)}, bf16[2,80,896]{2,1,0:T(8,128)(2,1)S(1)}, u32[]{:S(2)}, u32[]{:S(2)}) collective-permute-start(bf16[2,80,896]{2,1,0:T(8,128)(2,1)} %get-tuple-element.44), channel_id=1, source_target_pairs={{0,4},{4,8},{8,12},{12,16},{16,20},{20,24},{24,28},{1,5},{5,9},{9,... | collective-permute-start | bytes 860168 | tf_op jit(solution)/shard_map/ppermute | solution.py:383
  25.6 4.5 %split_head_columns.1 = (bf16[4,224,1024]{2,1,0:T(8,128)(2,1)}, bf16[4,224,1024]{2,1,0:T(8,128)(2,1)}) custom-call(bf16[448,4000]{1,0:T(8,128)(2,1)} %head_ref.1), custom_call_target="tpu_custom_call" | custom-call | bytes 7168000 | tf_op jit(solution)/shard_map/split_head_columns/pallas_call | solution.py:399
  30.1 2.0 collective-permute-done.6.refs_6_
  32.9 5.4 %all-to-all-start = ((bf16[4,224,1024]{2,1,0:T(8,128)(2,1)}), bf16[4,224,1024]{2,1,0:T(8,128)(2,1)S(1)}, u32[]{:S(2)}, u32[]{:S(2)}) async-start(bf16[4,224,1024]{2,1,0:T(8,128)(2,1)} %get-tuple-element.53), calls=%async_computation | async-start | bytes 3670016 | tf_op jit(solution)/shard_map/all_to_all | solution.py:410
  39.8 3.6 %collective-permute-start.4 = (bf16[2,64,896]{2,1,0:T(8,128)(2,1)}, bf16[2,64,896]{2,1,0:T(8,128)(2,1)S(1)}, u32[]{:S(2)}, u32[]{:S(2)}) collective-permute-start(bf16[2,64,896]{2,1,0:T(8,128)(2,1)} %collective-permute-done.3.refs_4_), channel_id=1, source_target_pairs={{0,4},{4,0},{8,12},{12,8},{16,20},{20,16},{24,28},{28,24},{1,5},{5... | collective-permute-start | bytes 688136 | tf_op jit(solution)/shard_map/ppermute | solution.py:36
  43.4 2.0 collective-permute-start.7
  46.1 4.0 %collective-permute-done.4.refs_5_ = bf16[2,64,896]{2,1,0:T(8,128)(2,1)S(1)} collective-permute-done((bf16[2,64,896]{2,1,0:T(8,128)(2,1)}, bf16[2,64,896]{2,1,0:T(8,128)(2,1)S(1)}, u32[]{:S(2)}, u32[]{:S(2)}) %collective-permute-start.4) | collective-permute-done | bytes 229408 | tf_op jit(solution)/shard_map/ppermute | solution.py:36
  50.1 4.5 %collective-permute-done.2.refs_3_ = bf16[2,64,896]{2,1,0:T(8,128)(2,1)S(1)} collective-permute-done((bf16[2,64,896]{2,1,0:T(8,128)(2,1)S(1)}, bf16[2,64,896]{2,1,0:T(8,128)(2,1)S(1)}, u32[]{:S(2)}, u32[]{:S(2)}) %collective-permute-start.2) | collective-permute-done | bytes 229408 | tf_op jit(solution)/shard_map/ppermute | solution.py:36
  54.6 2.5 collective-permute-done.7.refs_7_
  57.7 14.8 %gate_and_project.1 = (bf16[256,3584]{1,0:T(8,128)(2,1)}, bf16[256,3584]{1,0:T(8,128)(2,1)}) custom-call(s32[4]{0:T(128)} %fusion.45.order_ref, bf16[2,64,896]{2,1,0:T(8,128)(2,1)} %copy-done.12, bf16[2,64,896]{2,1,0:T(8,128)(2,1)} %copy-done.16, bf16[2,64,896]{2,1,0:T(8,128)(2,1)} %copy-done.14, bf16[2,64,896]{2,1,0:T(8,128)(2,1)} %copy-done.19, ...), custom_call_target="tpu_custom_call" | custom-call | flops 3288334336 | bytes 12845056 | tf_op jit(solution)/shard_map/gate_and_project/pallas_call | solution.py:435
  72.5 4.9 %all-to-all-done.refs_0_ = bf16[4,224,1024]{2,1,0:T(8,128)(2,1)S(1)} async-done(((bf16[4,224,1024]{2,1,0:T(8,128)(2,1)}), bf16[4,224,1024]{2,1,0:T(8,128)(2,1)S(1)}, u32[]{:S(2)}, u32[]{:S(2)}) %all-to-all-start) | async-done | bytes 1835040 | tf_op jit(solution)/shard_map/all_to_all | solution.py:410
  77.4 4.4 %all-to-all-start.1 = ((bf16[4,224,1024]{2,1,0:T(8,128)(2,1)}), bf16[4,224,1024]{2,1,0:T(8,128)(2,1)}, u32[]{:S(2)}, u32[]{:S(2)}) async-start(bf16[4,224,1024]{2,1,0:T(8,128)(2,1)} %get-tuple-element.55), calls=%async_computation.1 | async-start | bytes 3670016 | tf_op jit(solution)/shard_map/all_to_all | solution.py:410
  81.8 5.5 %collective-permute-start.13 = (bf16[4,224,1024]{2,1,0:T(8,128)(2,1)S(1)}, bf16[4,224,1024]{2,1,0:T(8,128)(2,1)}, u32[]{:S(2)}, u32[]{:S(2)}) collective-permute-start(bf16[4,224,1024]{2,1,0:T(8,128)(2,1)S(1)} %all-to-all-done.refs_0_), channel_id=1, source_target_pairs={{0,4},{4,0},{8,12},{12,8},{16,20},{20,16},{24,28},{28,24},{1,5},{5... | collective-permute-start | bytes 5505032 | tf_op jit(solution)/shard_map/ppermute | solution.py:36
  87.3 2.6 add_convert_fusion
  89.9 1.5 collective-permute-start.9
  91.4 1.9 collective-permute-start.10
  93.3 2.4 collective-permute-start.11
  95.8 1.8 dynamic-slice_bitcast_fusion
  97.7 27.8 %all-to-all-done.1.refs_2_ = bf16[4,224,1024]{2,1,0:T(8,128)(2,1)} async-done(((bf16[4,224,1024]{2,1,0:T(8,128)(2,1)}), bf16[4,224,1024]{2,1,0:T(8,128)(2,1)}, u32[]{:S(2)}, u32[]{:S(2)}) %all-to-all-start.1) | async-done | bytes 1835040 | tf_op jit(solution)/shard_map/all_to_all | solution.py:410
  125.5 1.5 copy-done.1
  127.0 2.3 add_and_norm.1.refs_0_
  129.4 1.6 collective-permute-start.14
  132.2 5.5 %collective-permute-start.18 = (bf16[4,224,1024]{2,1,0:T(8,128)(2,1)}, bf16[4,224,1024]{2,1,0:T(8,128)(2,1)}, u32[]{:S(2)}, u32[]{:S(2)}) collective-permute-start(bf16[4,224,1024]{2,1,0:T(8,128)(2,1)} %all-to-all-done.1.refs_2_), channel_id=1, source_target_pairs={{0,4},{4,0},{8,12},{12,8},{16,20},{20,16},{24,28},{28,24},{1,5},{5... | collective-permute-start | bytes 5505032 | tf_op jit(solution)/shard_map/ppermute | solution.py:36
  137.7 13.8 %collective-permute-done.14.refs_1_ = bf16[128,3584]{1,0:T(8,128)(2,1)S(1)} collective-permute-done((bf16[128,3584]{1,0:T(8,128)(2,1)S(1)}, bf16[128,3584]{1,0:T(8,128)(2,1)S(1)}, u32[]{:S(2)}, u32[]{:S(2)}) %collective-permute-start.14) | collective-permute-done | bytes 917536 | tf_op jit(solution)/shard_map/ppermute | solution.py:64
  151.4 1.3 collective-permute-done.15.refs_0_
  152.8 1.1 collective-permute-start.17
  153.8 1.3 collective-permute-start.19
  155.1 1.6 collective-permute-start.20
  156.7 20.7 %collective-permute-done.18.refs_3_ = bf16[4,224,1024]{2,1,0:T(8,128)(2,1)} collective-permute-done((bf16[4,224,1024]{2,1,0:T(8,128)(2,1)}, bf16[4,224,1024]{2,1,0:T(8,128)(2,1)}, u32[]{:S(2)}, u32[]{:S(2)}) %collective-permute-start.18) | collective-permute-done | bytes 1835040 | tf_op jit(solution)/shard_map/ppermute | solution.py:36
  177.4 2.2 broadcast_select_fusion.1.refs_4_
  179.7 0.8 collective-permute-start.21
  180.5 1.3 collective-permute-start.24
  183.5 0.9 broadcast_in_dim.99.refs_5_
  184.6 4.5 %place_head_rows.1.refs_4_.refs_10_.refs_2_ = bf16[3584,1024]{1,0:T(8,128)(2,1)S(1)} custom-call(s32[16]{0:T(128)S(1)} %stack.195.first_ref, bf16[4,224,1024]{2,1,0:T(8,128)(2,1)S(1)} %all-to-all-done.refs_0_, bf16[4,224,1024]{2,1,0:T(8,128)(2,1)} %collective-permute-done.13.refs_1_, bf16[4,224,1024]{2,1,0:T(8,128)(2,1)} %all-to-all-done.1.refs_2_, ...), custom_call_target="tpu_custom_call" | custom-call | bytes 14680064 | tf_op jit(solution)/shard_map/place_head_rows/pallas_call | solution.py:516
  189.1 2.9 %copy-done = bf16[3584,1024]{1,0:T(8,128)(2,1)} copy-done((bf16[3584,1024]{1,0:T(8,128)(2,1)}, bf16[3584,1024]{1,0:T(8,128)(2,1)S(1)}, u32[]{:S(2)}) %copy-start) | copy-done | bytes 7340056
  192.3 9.2 %head_stats.3 = f32[8,512]{1,0:T(8,128)} custom-call(s32[2]{0:T(128)} %pad_add_fusion.3.limit_ref, bf16[128,3584]{1,0:T(8,128)(2,1)} %copy-done.3, bf16[128,3584]{1,0:T(8,128)(2,1)} %copy-done.27, bf16[128,3584]{1,0:T(8,128)(2,1)} %collective-permute-done.22.refs_2_, bf16[128,3584]{1,0:T(8,128)(2,1)} %collective-permute-done.23.refs_3_, ...), custom_call_target="tpu_custom_call" | custom-call | flops 3758096384 | bytes 11010048 | tf_op jit(solution)/shard_map/head_stats/pallas_call | solution.py:532
  202.7 2.7 %collective-permute-done.24 = bf16[128,3584]{1,0:T(8,128)(2,1)} collective-permute-done((bf16[128,3584]{1,0:T(8,128)(2,1)}, bf16[128,3584]{1,0:T(8,128)(2,1)}, u32[]{:S(2)}, u32[]{:S(2)}) %collective-permute-start.24) | collective-permute-done | bytes 917536 | tf_op jit(solution)/shard_map/ppermute | solution.py:47
  205.4 1.3 broadcast_select_fusion.refs_8_
  207.5 1.5 collective-permute-start.25
  209.0 1.2 copy.151
  210.9 17.0 %head_stats.4 = f32[8,1280]{1,0:T(8,128)} custom-call(s32[2]{0:T(128)} %pad_add_fusion.3.limit_ref, bf16[128,3584]{1,0:T(8,128)(2,1)} %collective-permute-done.15.refs_0_, bf16[128,3584]{1,0:T(8,128)(2,1)} %collective-permute-done.17.refs_1_, bf16[128,3584]{1,0:T(8,128)(2,1)} %collective-permute-done.26.refs_2_, ...), custom_call_target="tpu_custom_call" | custom-call | flops 9395240960 | bytes 16515072 | tf_op jit(solution)/shard_map/head_stats/pallas_call | solution.py:532
  228.0 0.9 reshape.372
  228.8 1.0 collective-permute-done.25.refs_0_
  230.0 0.8 copy.110.refs_3_
  230.9 1.4 collective-permute-done.31.refs_1_
  232.3 0.9 copy-done.11
  233.3 6.7 %head_stats.5 = f32[8,256]{1,0:T(8,128)} custom-call(s32[2]{0:T(128)} %pad_add_fusion.3.limit_ref, bf16[128,3584]{1,0:T(8,128)(2,1)} %copy-done.10, bf16[128,3584]{1,0:T(8,128)(2,1)} %copy-done.11, bf16[3584,1024]{1,0:T(8,128)(2,1)} %copy-done, s32[256,1]{1,0:T(8,128)} %copy.110.refs_3_), custom_call_target="tpu_custom_call" | custom-call | flops 1879048192 | bytes 9175040 | tf_op jit(solution)/shard_map/head_stats/pallas_call | solution.py:532
  240.8 1.9 collective-permute-start.32
  242.7 2.1 collective-permute-start.34
  244.9 3.7 %collective-permute-done.34 = f32[3,4,2,2,2,64]{5,4,3,2,1,0:T(2,128)S(1)} collective-permute-done((f32[3,4,2,2,2,64]{5,4,3,2,1,0:T(2,128)S(1)}, f32[3,4,2,2,2,64]{5,4,3,2,1,0:T(2,128)S(1)}, u32[]{:S(2)}, u32[]{:S(2)}) %collective-permute-start.34) | collective-permute-done | bytes 24608 | tf_op jit(solution)/shard_map/ppermute | solution.py:31
  248.7 1.4 collective-permute-done.33
  251.4 1.0 collective-permute-start.36
  252.4 1.8 collective-permute-done.37
  254.3 1.2 collective-permute-done.36
  256.5 5.4 %collective-permute-start.38 = (f32[48]{0:T(128)S(1)}, f32[48]{0:T(128)S(1)}, u32[]{:S(2)}, u32[]{:S(2)}) collective-permute-start(f32[48]{0:T(128)S(1)} %convolution_bitcast_fusion), channel_id=1, source_target_pairs={{0,4},{4,0},{8,12},{12,8},{16,20},{20,16},{24,28},{28,24},{1,5},{5... | collective-permute-start | bytes 584 | tf_op jit(solution)/shard_map/ppermute | solution.py:36
  262.5 1.0 collective-permute-done.38
  (169 shorter events, 18.7 us)
Async XLA Ops:
  0.6 14.9 %copy-start.6 = (bf16[2,256,896]{2,1,0:T(8,128)(2,1)S(1)}, bf16[2,256,896]{2,1,0:T(8,128)(2,1)}, u32[]{:S(2)}) copy-start(bf16[2,256,896]{2,1,0:T(8,128)(2,1)} %x_ref) | copy-start | bytes 2752516
  0.6 14.9 %copy-start.7 = (f32[2,14]{1,0:T(2,128)S(1)}, f32[2,14]{1,0:T(2,128)}, u32[]{:S(2)}) copy-start(f32[2,14]{1,0:T(2,128)} %param.29) | copy-start | bytes 340
  0.7 14.9 %copy-start.8 = (f32[2,14]{1,0:T(2,128)S(1)}, f32[2,14]{1,0:T(2,128)}, u32[]{:S(2)}) copy-start(f32[2,14]{1,0:T(2,128)} %param.30) | copy-start | bytes 340
  2.0 18.8 %copy-start.12 = (bf16[2,64,896]{2,1,0:T(8,128)(2,1)}, bf16[2,64,896]{2,1,0:T(8,128)(2,1)S(1)}, u32[]{:S(2)}) copy-start(bf16[2,64,896]{2,1,0:T(8,128)(2,1)S(1)} %copy.114.refs_0_) | copy-start | bytes 688132
  2.0 12.8 %collective-permute-start = (bf16[2,64,896]{2,1,0:T(8,128)(2,1)S(1)}, bf16[2,64,896]{2,1,0:T(8,128)(2,1)S(1)}, u32[]{:S(2)}, u32[]{:S(2)}) collective-permute-start(bf16[2,64,896]{2,1,0:T(8,128)(2,1)S(1)} %copy.114.refs_0_), channel_id=1, source_target_pairs={{0,8},{4,12},{8,0},{12,4},{16,24},{20,28},{24,16},{28,20},{1,9},{5... | collective-permute-start | bytes 688136 | tf_op jit(solution)/shard_map/ppermute | solution.py:31
  5.1 9.7 %collective-permute-start.1 = (bf16[2,64,896]{2,1,0:T(8,128)(2,1)S(1)}, bf16[2,64,896]{2,1,0:T(8,128)(2,1)S(1)}, u32[]{:S(2)}, u32[]{:S(2)}) collective-permute-start(bf16[2,64,896]{2,1,0:T(8,128)(2,1)S(1)} %copy.114.refs_0_), channel_id=1, source_target_pairs={{0,4},{4,0},{8,12},{12,8},{16,20},{20,16},{24,28},{28,24},{1,5},{5... | collective-permute-start | bytes 688136 | tf_op jit(solution)/shard_map/ppermute | solution.py:36
  6.6 19.0 %collective-permute-start.3 = (bf16[2,64,896]{2,1,0:T(8,128)(2,1)S(1)}, bf16[2,64,896]{2,1,0:T(8,128)(2,1)}, u32[]{:S(2)}, u32[]{:S(2)}) collective-permute-start(bf16[2,64,896]{2,1,0:T(8,128)(2,1)S(1)} %copy.114.refs_0_), channel_id=1, source_target_pairs={{0,16},{4,20},{8,24},{12,28},{16,0},{20,4},{24,8},{28,12},{1,17},{... | collective-permute-start | bytes 688136 | tf_op jit(solution)/shard_map/ppermute | solution.py:31
  14.7 6.1 %copy-start.4 = (bf16[2,256,128]{2,1,0:T(8,128)(2,1)}, bf16[2,256,128]{2,1,0:T(8,128)(2,1)S(1)}, u32[]{:S(2)}) copy-start(bf16[2,256,128]{2,1,0:T(8,128)(2,1)S(1)} %pad_maximum_fusion.both_ref.refs_9_) | copy-start | bytes 393220
  21.5 8.6 %copy-start.2 = (f32[2,256,896]{2,1,0:T(8,128)}, f32[2,256,896]{2,1,0:T(8,128)S(1)}, u32[]{:S(2)}) copy-start(f32[2,256,896]{2,1,0:T(8,128)S(1)} %get-tuple-element.48.refs_8_) | copy-start | bytes 5505028
  21.5 10.7 %collective-permute-start.5 = (bf16[2,80,896]{2,1,0:T(8,128)(2,1)}, bf16[2,80,896]{2,1,0:T(8,128)(2,1)S(1)}, u32[]{:S(2)}, u32[]{:S(2)}) collective-permute-start(bf16[2,80,896]{2,1,0:T(8,128)(2,1)} %get-tuple-element.44), channel_id=1, source_target_pairs={{0,4},{4,8},{8,12},{12,16},{16,20},{20,24},{24,28},{1,5},{5,9},{9,... | collective-permute-start | bytes 860168 | tf_op jit(solution)/shard_map/ppermute | solution.py:383
  25.6 6.6 %collective-permute-start.6 = (bf16[2,64,896]{2,1,0:T(8,128)(2,1)}, bf16[2,64,896]{2,1,0:T(8,128)(2,1)S(1)}, u32[]{:S(2)}, u32[]{:S(2)}) collective-permute-start(bf16[2,64,896]{2,1,0:T(8,128)(2,1)} %collective-permute-done.3.refs_4_), channel_id=1, source_target_pairs={{0,8},{4,12},{8,0},{12,4},{16,24},{20,28},{24,16},{28,20},{1,9},{5... | collective-permute-start | bytes 688136 | tf_op jit(solution)/shard_map/ppermute | solution.py:31
  32.1 11.3 %copy-start.17 = (bf16[2,64,896]{2,1,0:T(8,128)(2,1)}, bf16[2,64,896]{2,1,0:T(8,128)(2,1)S(1)}, u32[]{:S(2)}) copy-start(bf16[2,64,896]{2,1,0:T(8,128)(2,1)S(1)} %collective-permute-done.6.refs_6_) | copy-start | bytes 688132
  32.1 6.9 %copy-start.24 = (s32[256]{0:T(256)S(1)}, s32[256]{0:T(256)}, u32[]{:S(2)}) copy-start(s32[256]{0:T(256)} %param.20) | copy-start | bytes 3076
  32.2 6.9 %copy-start.25 = (s32[256]{0:T(256)S(1)}, s32[256]{0:T(256)}, u32[]{:S(2)}) copy-start(s32[256]{0:T(256)} %param.19) | copy-start | bytes 3076
  32.2 11.2 %copy-start.15 = (bf16[2,64,896]{2,1,0:T(8,128)(2,1)S(1)}, bf16[2,64,896]{2,1,0:T(8,128)(2,1)}, u32[]{:S(2)}) copy-start(bf16[2,64,896]{2,1,0:T(8,128)(2,1)} %copy-done.14) | copy-start | bytes 688132
  32.9 44.4 %all-to-all-start = ((bf16[4,224,1024]{2,1,0:T(8,128)(2,1)}), bf16[4,224,1024]{2,1,0:T(8,128)(2,1)S(1)}, u32[]{:S(2)}, u32[]{:S(2)}) async-start(bf16[4,224,1024]{2,1,0:T(8,128)(2,1)} %get-tuple-element.53), calls=%async_computation | async-start | bytes 3670016 | tf_op jit(solution)/shard_map/all_to_all | solution.py:410
  39.8 10.3 %collective-permute-start.4 = (bf16[2,64,896]{2,1,0:T(8,128)(2,1)}, bf16[2,64,896]{2,1,0:T(8,128)(2,1)S(1)}, u32[]{:S(2)}, u32[]{:S(2)}) collective-permute-start(bf16[2,64,896]{2,1,0:T(8,128)(2,1)} %collective-permute-done.3.refs_4_), channel_id=1, source_target_pairs={{0,4},{4,0},{8,12},{12,8},{16,20},{20,16},{24,28},{28,24},{1,5},{5... | collective-permute-start | bytes 688136 | tf_op jit(solution)/shard_map/ppermute | solution.py:36
  43.4 11.2 %collective-permute-start.2 = (bf16[2,64,896]{2,1,0:T(8,128)(2,1)S(1)}, bf16[2,64,896]{2,1,0:T(8,128)(2,1)S(1)}, u32[]{:S(2)}, u32[]{:S(2)}) collective-permute-start(bf16[2,64,896]{2,1,0:T(8,128)(2,1)S(1)} %copy-done.15), channel_id=1, source_target_pairs={{0,4},{4,0},{8,12},{12,8},{16,20},{20,16},{24,28},{28,24},{1,5},{5... | collective-permute-start | bytes 688136 | tf_op jit(solution)/shard_map/ppermute | solution.py:36
  43.4 13.6 %collective-permute-start.7 = (bf16[2,64,896]{2,1,0:T(8,128)(2,1)S(1)}, bf16[2,64,896]{2,1,0:T(8,128)(2,1)S(1)}, u32[]{:S(2)}, u32[]{:S(2)}) collective-permute-start(bf16[2,64,896]{2,1,0:T(8,128)(2,1)S(1)} %collective-permute-done.6.refs_6_), channel_id=1, source_target_pairs={{0,4},{4,0},{8,12},{12,8},{16,20},{20,16},{24,28},{28,24},{1,5},{5... | collective-permute-start | bytes 688136 | tf_op jit(solution)/shard_map/ppermute | solution.py:36
  50.1 7.5 %copy-start.18 = (bf16[2,64,896]{2,1,0:T(8,128)(2,1)}, bf16[2,64,896]{2,1,0:T(8,128)(2,1)S(1)}, u32[]{:S(2)}) copy-start(bf16[2,64,896]{2,1,0:T(8,128)(2,1)S(1)} %collective-permute-done.4.refs_5_) | copy-start | bytes 688132
  54.6 3.1 %copy-start.19 = (bf16[2,64,896]{2,1,0:T(8,128)(2,1)}, bf16[2,64,896]{2,1,0:T(8,128)(2,1)S(1)}, u32[]{:S(2)}) copy-start(bf16[2,64,896]{2,1,0:T(8,128)(2,1)S(1)} %collective-permute-done.2.refs_3_) | copy-start | bytes 688132
  77.4 9.9 %collective-permute-start.8 = (bf16[256,3584]{1,0:T(8,128)(2,1)}, bf16[256,3584]{1,0:T(8,128)(2,1)}, u32[]{:S(2)}, u32[]{:S(2)}) collective-permute-start(bf16[256,3584]{1,0:T(8,128)(2,1)} %get-tuple-element.54), channel_id=1, source_target_pairs={{0,1},{1,0},{2,3},{3,2},{4,5},{5,4},{6,7},{7,6},{8,9},{9,8},{10,11... | collective-permute-start | bytes 5505032 | tf_op jit(solution)/shard_map/ppermute | solution.py:59
  77.4 48.1 %all-to-all-start.1 = ((bf16[4,224,1024]{2,1,0:T(8,128)(2,1)}), bf16[4,224,1024]{2,1,0:T(8,128)(2,1)}, u32[]{:S(2)}, u32[]{:S(2)}) async-start(bf16[4,224,1024]{2,1,0:T(8,128)(2,1)} %get-tuple-element.55), calls=%async_computation.1 | async-start | bytes 3670016 | tf_op jit(solution)/shard_map/all_to_all | solution.py:410
  81.8 47.6 %collective-permute-start.13 = (bf16[4,224,1024]{2,1,0:T(8,128)(2,1)S(1)}, bf16[4,224,1024]{2,1,0:T(8,128)(2,1)}, u32[]{:S(2)}, u32[]{:S(2)}) collective-permute-start(bf16[4,224,1024]{2,1,0:T(8,128)(2,1)S(1)} %all-to-all-done.refs_0_), channel_id=1, source_target_pairs={{0,4},{4,0},{8,12},{12,8},{16,20},{20,16},{24,28},{28,24},{1,5},{5... | collective-permute-start | bytes 5505032 | tf_op jit(solution)/shard_map/ppermute | solution.py:36
  89.9 35.6 %collective-permute-start.9 = (bf16[128,3584]{1,0:T(8,128)(2,1)}, bf16[128,3584]{1,0:T(8,128)(2,1)}, u32[]{:S(2)}, u32[]{:S(2)}) collective-permute-start(bf16[128,3584]{1,0:T(8,128)(2,1)} %add_convert_fusion), channel_id=1, source_target_pairs={{0,2},{1,3},{2,0},{3,1},{4,6},{5,7},{6,4},{7,5},{8,10},{9,11},{10,... | collective-permute-start | bytes 2752520 | tf_op jit(solution)/shard_map/ppermute | solution.py:64
  91.4 6.3 %copy-start.22 = (f32[3584]{0:T(1024)S(1)}, f32[3584]{0:T(1024)}, u32[]{:S(2)}) copy-start(f32[3584]{0:T(1024)} %param.36) | copy-start | bytes 43012
  91.4 34.1 %collective-permute-start.10 = (s32[2,256]{1,0:T(2,128)S(1)}, s32[2,256]{1,0:T(2,128)S(1)}, u32[]{:S(2)}, u32[]{:S(2)}) collective-permute-start(s32[2,256]{1,0:T(2,128)S(1)} %pad_add_fusion.1), channel_id=1, source_target_pairs={{0,8},{4,12},{8,0},{12,4},{16,24},{20,28},{24,16},{28,20},{1,9},{5... | collective-permute-start | bytes 6152 | tf_op jit(solution)/shard_map/ppermute | solution.py:31
  93.3 32.2 %collective-permute-start.11 = (s32[2,256]{1,0:T(2,128)S(1)}, s32[2,256]{1,0:T(2,128)S(1)}, u32[]{:S(2)}, u32[]{:S(2)}) collective-permute-start(s32[2,256]{1,0:T(2,128)S(1)} %pad_add_fusion.1), channel_id=1, source_target_pairs={{0,16},{4,20},{8,24},{12,28},{16,0},{20,4},{24,8},{28,12},{1,17},{... | collective-permute-start | bytes 6152 | tf_op jit(solution)/shard_map/ppermute | solution.py:31
  95.6 29.9 %collective-permute-start.12 = (s32[2,256]{1,0:T(2,128)S(1)}, s32[2,256]{1,0:T(2,128)S(1)}, u32[]{:S(2)}, u32[]{:S(2)}) collective-permute-start(s32[2,256]{1,0:T(2,128)S(1)} %pad_add_fusion.1), channel_id=1, source_target_pairs={{0,24},{4,28},{8,16},{12,20},{16,8},{20,12},{24,0},{28,4},{1,25},{... | collective-permute-start | bytes 6152 | tf_op jit(solution)/shard_map/ppermute | solution.py:31
  125.5 1.5 copy-start.1
  129.4 2.1 copy-start.3
  129.4 22.0 %collective-permute-start.14 = (bf16[128,3584]{1,0:T(8,128)(2,1)S(1)}, bf16[128,3584]{1,0:T(8,128)(2,1)S(1)}, u32[]{:S(2)}, u32[]{:S(2)}) collective-permute-start(bf16[128,3584]{1,0:T(8,128)(2,1)S(1)} %add_and_norm.1.refs_0_), channel_id=1, source_target_pairs={{0,2},{1,3},{2,0},{3,1},{4,6},{5,7},{6,4},{7,5},{8,10},{9,11},{10,... | collective-permute-start | bytes 2752520 | tf_op jit(solution)/shard_map/ppermute | solution.py:64
  131.0 21.8 %collective-permute-start.15 = (bf16[128,3584]{1,0:T(8,128)(2,1)S(1)}, bf16[128,3584]{1,0:T(8,128)(2,1)}, u32[]{:S(2)}, u32[]{:S(2)}) collective-permute-start(bf16[128,3584]{1,0:T(8,128)(2,1)S(1)} %add_and_norm.1.refs_0_), channel_id=1, source_target_pairs={{0,8},{4,12},{8,0},{12,4},{16,24},{20,28},{24,16},{28,20},{1,9},{5... | collective-permute-start | bytes 2752520 | tf_op jit(solution)/shard_map/ppermute | solution.py:31
  131.4 21.3 %collective-permute-start.16 = (bf16[128,3584]{1,0:T(8,128)(2,1)S(1)}, bf16[128,3584]{1,0:T(8,128)(2,1)S(1)}, u32[]{:S(2)}, u32[]{:S(2)}) collective-permute-start(bf16[128,3584]{1,0:T(8,128)(2,1)S(1)} %add_and_norm.1.refs_0_), channel_id=1, source_target_pairs={{8,16},{12,20},{16,8},{20,12},{9,17},{13,21},{17,9},{21,13},{10,18... | collective-permute-start | bytes 2752520 | tf_op jit(solution)/shard_map/ppermute | solution.py:47
  132.2 45.3 %collective-permute-start.18 = (bf16[4,224,1024]{2,1,0:T(8,128)(2,1)}, bf16[4,224,1024]{2,1,0:T(8,128)(2,1)}, u32[]{:S(2)}, u32[]{:S(2)}) collective-permute-start(bf16[4,224,1024]{2,1,0:T(8,128)(2,1)} %all-to-all-done.1.refs_2_), channel_id=1, source_target_pairs={{0,4},{4,0},{8,12},{12,8},{16,20},{20,16},{24,28},{28,24},{1,5},{5... | collective-permute-start | bytes 5505032 | tf_op jit(solution)/shard_map/ppermute | solution.py:36
  151.4 1.3 copy-start.27
  152.8 24.7 %collective-permute-start.17 = (bf16[128,3584]{1,0:T(8,128)(2,1)}, bf16[128,3584]{1,0:T(8,128)(2,1)}, u32[]{:S(2)}, u32[]{:S(2)}) collective-permute-start(bf16[128,3584]{1,0:T(8,128)(2,1)} %collective-permute-done.15.refs_0_), channel_id=1, source_target_pairs={{0,2},{1,3},{2,0},{3,1},{4,6},{5,7},{6,4},{7,5},{8,10},{9,11},{10,... | collective-permute-start | bytes 2752520 | tf_op jit(solution)/shard_map/ppermute | solution.py:64
  153.8 23.6 %collective-permute-start.19 = (bf16[128,3584]{1,0:T(8,128)(2,1)S(1)}, bf16[128,3584]{1,0:T(8,128)(2,1)}, u32[]{:S(2)}, u32[]{:S(2)}) collective-permute-start(bf16[128,3584]{1,0:T(8,128)(2,1)S(1)} %collective-permute-done.16), channel_id=1, source_target_pairs={{8,0},{12,4},{16,24},{20,28},{9,1},{13,5},{17,25},{21,29},{10,2},{... | collective-permute-start | bytes 2752520 | tf_op jit(solution)/shard_map/ppermute | solution.py:47
  155.1 22.3 %collective-permute-start.20 = (bf16[128,3584]{1,0:T(8,128)(2,1)}, bf16[128,3584]{1,0:T(8,128)(2,1)}, u32[]{:S(2)}, u32[]{:S(2)}) collective-permute-start(bf16[128,3584]{1,0:T(8,128)(2,1)} %collective-permute-done.15.refs_0_), channel_id=1, source_target_pairs={{8,16},{12,20},{16,8},{20,12},{9,17},{13,21},{17,9},{21,13},{10,18... | collective-permute-start | bytes 2752520 | tf_op jit(solution)/shard_map/ppermute | solution.py:47
  156.7 35.3 %collective-permute-start.22 = (bf16[128,3584]{1,0:T(8,128)(2,1)}, bf16[128,3584]{1,0:T(8,128)(2,1)}, u32[]{:S(2)}, u32[]{:S(2)}) collective-permute-start(bf16[128,3584]{1,0:T(8,128)(2,1)} %copy-done.3), channel_id=1, source_target_pairs={{0,1},{1,0},{2,3},{3,2},{4,5},{5,4},{6,7},{7,6},{8,9},{9,8},{10,11... | collective-permute-start | bytes 2752520 | tf_op jit(solution)/shard_map/ppermute | solution.py:59
  177.4 14.9 %collective-permute-start.23 = (bf16[128,3584]{1,0:T(8,128)(2,1)}, bf16[128,3584]{1,0:T(8,128)(2,1)}, u32[]{:S(2)}, u32[]{:S(2)}) collective-permute-start(bf16[128,3584]{1,0:T(8,128)(2,1)} %copy-done.27), channel_id=1, source_target_pairs={{0,1},{1,0},{2,3},{3,2},{4,5},{5,4},{6,7},{7,6},{8,9},{9,8},{10,11... | collective-permute-start | bytes 2752520 | tf_op jit(solution)/shard_map/ppermute | solution.py:59
  179.7 23.1 %collective-permute-start.21 = (bf16[128,3584]{1,0:T(8,128)(2,1)}, bf16[128,3584]{1,0:T(8,128)(2,1)}, u32[]{:S(2)}, u32[]{:S(2)}) collective-permute-start(bf16[128,3584]{1,0:T(8,128)(2,1)} %broadcast_select_fusion.1.refs_4_), channel_id=1, source_target_pairs={{0,2},{1,3},{2,0},{3,1},{4,6},{5,7},{6,4},{7,5},{8,10},{9,11},{10,... | collective-permute-start | bytes 2752520 | tf_op jit(solution)/shard_map/ppermute | solution.py:64
  180.5 24.9 %collective-permute-start.24 = (bf16[128,3584]{1,0:T(8,128)(2,1)}, bf16[128,3584]{1,0:T(8,128)(2,1)}, u32[]{:S(2)}, u32[]{:S(2)}) collective-permute-start(bf16[128,3584]{1,0:T(8,128)(2,1)} %collective-permute-done.20), channel_id=1, source_target_pairs={{8,0},{12,4},{16,24},{20,28},{9,1},{13,5},{17,25},{21,29},{10,2},{... | collective-permute-start | bytes 2752520 | tf_op jit(solution)/shard_map/ppermute | solution.py:47
  184.4 23.1 %collective-permute-start.26 = (bf16[128,3584]{1,0:T(8,128)(2,1)}, bf16[128,3584]{1,0:T(8,128)(2,1)}, u32[]{:S(2)}, u32[]{:S(2)}) collective-permute-start(bf16[128,3584]{1,0:T(8,128)(2,1)} %collective-permute-done.15.refs_0_), channel_id=1, source_target_pairs={{0,1},{1,0},{2,3},{3,2},{4,5},{5,4},{6,7},{7,6},{8,9},{9,8},{10,11... | collective-permute-start | bytes 2752520 | tf_op jit(solution)/shard_map/ppermute | solution.py:59
  189.1 2.9 %copy-start = (bf16[3584,1024]{1,0:T(8,128)(2,1)}, bf16[3584,1024]{1,0:T(8,128)(2,1)S(1)}, u32[]{:S(2)}) copy-start(bf16[3584,1024]{1,0:T(8,128)(2,1)S(1)} %place_head_rows.1.refs_4_.refs_10_.refs_2_) | copy-start | bytes 22020100
  192.0 18.2 %collective-permute-start.28 = (bf16[128,3584]{1,0:T(8,128)(2,1)}, bf16[128,3584]{1,0:T(8,128)(2,1)}, u32[]{:S(2)}, u32[]{:S(2)}) collective-permute-start(bf16[128,3584]{1,0:T(8,128)(2,1)} %broadcast_select_fusion.1.refs_4_), channel_id=1, source_target_pairs={{0,1},{1,0},{2,3},{3,2},{4,5},{5,4},{6,7},{7,6},{8,9},{9,8},{10,11... | collective-permute-start | bytes 2752520 | tf_op jit(solution)/shard_map/ppermute | solution.py:59
  202.3 28.6 %copy-start.21 = (f32[8,4,2,64]{3,2,1,0:T(2,128)}, f32[8,4,2,64]{3,2,1,0:T(2,128)S(1)}, u32[]{:S(2)}) copy-start(f32[8,4,2,64]{3,2,1,0:T(2,128)S(1)} %reshape.368) | copy-start | bytes 49156
  202.3 7.9 %collective-permute-start.27 = (bf16[128,3584]{1,0:T(8,128)(2,1)}, bf16[128,3584]{1,0:T(8,128)(2,1)}, u32[]{:S(2)}, u32[]{:S(2)}) collective-permute-start(bf16[128,3584]{1,0:T(8,128)(2,1)} %collective-permute-done.17.refs_1_), channel_id=1, source_target_pairs={{0,1},{1,0},{2,3},{3,2},{4,5},{5,4},{6,7},{7,6},{8,9},{9,8},{10,11... | collective-permute-start | bytes 2752520 | tf_op jit(solution)/shard_map/ppermute | solution.py:59
  206.7 4.2 %copy-start.9 = (bf16[128,3584]{1,0:T(8,128)(2,1)}, bf16[128,3584]{1,0:T(8,128)(2,1)S(1)}, u32[]{:S(2)}) copy-start(bf16[128,3584]{1,0:T(8,128)(2,1)S(1)} %broadcast_select_fusion.refs_8_) | copy-start | bytes 2752516
  206.7 3.5 %collective-permute-start.30 = (bf16[128,3584]{1,0:T(8,128)(2,1)S(1)}, bf16[128,3584]{1,0:T(8,128)(2,1)}, u32[]{:S(2)}, u32[]{:S(2)}) collective-permute-start(bf16[128,3584]{1,0:T(8,128)(2,1)S(1)} %broadcast_select_fusion.refs_8_), channel_id=1, source_target_pairs={{0,1},{1,0},{2,3},{3,2},{4,5},{5,4},{6,7},{7,6},{8,9},{9,8},{10,11... | collective-permute-start | bytes 2752520 | tf_op jit(solution)/shard_map/ppermute | solution.py:59
  206.8 4.1 %collective-permute-start.29 = (bf16[128,3584]{1,0:T(8,128)(2,1)}, bf16[128,3584]{1,0:T(8,128)(2,1)}, u32[]{:S(2)}, u32[]{:S(2)}) collective-permute-start(bf16[128,3584]{1,0:T(8,128)(2,1)} %collective-permute-done.21.refs_5_), channel_id=1, source_target_pairs={{0,1},{1,0},{2,3},{3,2},{4,5},{5,4},{6,7},{7,6},{8,9},{9,8},{10,11... | collective-permute-start | bytes 2752520 | tf_op jit(solution)/shard_map/ppermute | solution.py:59
  207.5 22.4 %collective-permute-start.25 = (bf16[128,3584]{1,0:T(8,128)(2,1)S(1)}, bf16[128,3584]{1,0:T(8,128)(2,1)S(1)}, u32[]{:S(2)}, u32[]{:S(2)}) collective-permute-start(bf16[128,3584]{1,0:T(8,128)(2,1)S(1)} %broadcast_select_fusion.refs_8_), channel_id=1, source_target_pairs={{0,2},{1,3},{2,0},{3,1},{4,6},{5,7},{6,4},{7,5},{8,10},{9,11},{10,... | collective-permute-start | bytes 2752520 | tf_op jit(solution)/shard_map/ppermute | solution.py:64
  229.9 2.5 copy-start.10
  229.9 2.5 collective-permute-start.31
  230.9 9.8 %slice-start = ((f32[8,4,2,64]{3,2,1,0:T(2,128)}), f32[3,4,2,64]{3,2,1,0:T(2,128)S(1)}, s32[]{:S(2)}) async-start(f32[8,4,2,64]{3,2,1,0:T(2,128)} %copy-done.21), calls=%async_computation.2 | async-start | bytes 24576 | tf_op jit(solution)/shard_map/slice | solution.py:602
  230.9 25.0 %copy-start.23 = (s32[48]{0:T(128)S(1)}, s32[48]{0:T(128)}, u32[]{:S(2)}) copy-start(s32[48]{0:T(128)} %param.21) | copy-start | bytes 580
  239.9 23.5 %copy-start.26 = (s32[48]{0:T(128)S(1)}, s32[48]{0:T(128)}, u32[]{:S(2)}) copy-start(s32[48]{0:T(128)} %param.22) | copy-start | bytes 580
  240.8 4.2 %collective-permute-start.32 = (f32[3,4,2,2,2,64]{5,4,3,2,1,0:T(2,128)S(1)}, f32[3,4,2,2,2,64]{5,4,3,2,1,0:T(2,128)S(1)}, u32[]{:S(2)}, u32[]{:S(2)}) collective-permute-start(f32[3,4,2,2,2,64]{5,4,3,2,1,0:T(2,128)S(1)} %pad_maximum_fusion.1), channel_id=1, source_target_pairs={{0,8},{4,12},{8,0},{12,4},{16,24},{20,28},{24,16},{28,20},{1,9},{5... | collective-permute-start | bytes 73736 | tf_op jit(solution)/shard_map/ppermute | solution.py:31
  242.7 5.9 %collective-permute-start.34 = (f32[3,4,2,2,2,64]{5,4,3,2,1,0:T(2,128)S(1)}, f32[3,4,2,2,2,64]{5,4,3,2,1,0:T(2,128)S(1)}, u32[]{:S(2)}, u32[]{:S(2)}) collective-permute-start(f32[3,4,2,2,2,64]{5,4,3,2,1,0:T(2,128)S(1)} %pad_maximum_fusion.1), channel_id=1, source_target_pairs={{0,24},{4,28},{8,16},{12,20},{16,8},{20,12},{24,0},{28,4},{1,25},{... | collective-permute-start | bytes 73736 | tf_op jit(solution)/shard_map/ppermute | solution.py:31
  244.8 5.3 %collective-permute-start.33 = (f32[3,4,2,2,2,64]{5,4,3,2,1,0:T(2,128)S(1)}, f32[3,4,2,2,2,64]{5,4,3,2,1,0:T(2,128)S(1)}, u32[]{:S(2)}, u32[]{:S(2)}) collective-permute-start(f32[3,4,2,2,2,64]{5,4,3,2,1,0:T(2,128)S(1)} %pad_maximum_fusion.1), channel_id=1, source_target_pairs={{0,16},{4,20},{8,24},{12,28},{16,0},{20,4},{24,8},{28,12},{1,17},{... | collective-permute-start | bytes 73736 | tf_op jit(solution)/shard_map/ppermute | solution.py:31
  250.2 4.0 %collective-permute-start.37 = (f32[3,4,2,2,2,64]{5,4,3,2,1,0:T(2,128)S(1)}, f32[3,4,2,2,2,64]{5,4,3,2,1,0:T(2,128)S(1)}, u32[]{:S(2)}, u32[]{:S(2)}) collective-permute-start(f32[3,4,2,2,2,64]{5,4,3,2,1,0:T(2,128)S(1)} %pad_maximum_fusion.4), channel_id=1, source_target_pairs={{0,3},{1,2},{2,1},{3,0},{4,7},{5,6},{6,5},{7,4},{8,11},{9,10},{10,... | collective-permute-start | bytes 73736 | tf_op jit(solution)/shard_map/ppermute | solution.py:270
  250.8 3.5 %collective-permute-start.35 = (f32[3,4,2,2,2,64]{5,4,3,2,1,0:T(2,128)S(1)}, f32[3,4,2,2,2,64]{5,4,3,2,1,0:T(2,128)S(1)}, u32[]{:S(2)}, u32[]{:S(2)}) collective-permute-start(f32[3,4,2,2,2,64]{5,4,3,2,1,0:T(2,128)S(1)} %pad_maximum_fusion.4), channel_id=1, source_target_pairs={{0,1},{1,0},{2,3},{3,2},{4,5},{5,4},{6,7},{7,6},{8,9},{9,8},{10,11... | collective-permute-start | bytes 73736 | tf_op jit(solution)/shard_map/ppermute | solution.py:59
  251.4 4.1 %collective-permute-start.36 = (f32[3,4,2,2,2,64]{5,4,3,2,1,0:T(2,128)S(1)}, f32[3,4,2,2,2,64]{5,4,3,2,1,0:T(2,128)S(1)}, u32[]{:S(2)}, u32[]{:S(2)}) collective-permute-start(f32[3,4,2,2,2,64]{5,4,3,2,1,0:T(2,128)S(1)} %pad_maximum_fusion.4), channel_id=1, source_target_pairs={{0,2},{1,3},{2,0},{3,1},{4,6},{5,7},{6,4},{7,5},{8,10},{9,11},{10,... | collective-permute-start | bytes 73736 | tf_op jit(solution)/shard_map/ppermute | solution.py:64
  256.5 6.9 %collective-permute-start.38 = (f32[48]{0:T(128)S(1)}, f32[48]{0:T(128)S(1)}, u32[]{:S(2)}, u32[]{:S(2)}) collective-permute-start(f32[48]{0:T(128)S(1)} %convolution_bitcast_fusion), channel_id=1, source_target_pairs={{0,4},{4,0},{8,12},{12,8},{16,20},{20,16},{24,28},{28,24},{1,5},{5... | collective-permute-start | bytes 584 | tf_op jit(solution)/shard_map/ppermute | solution.py:36
  (6 other events, 4.6 us)

commit v5 on v4

--- a/solution.py
+++ b/solution.py
@@ -469,11 +469,6 @@
     own_rows = jnp.transpose(own_rows, (1, 0, 2)).reshape(each, width)
     crossing = [along_x(chip_sum(by).astype(jnp.bfloat16), by) for by in range(1, x_count)]
     besides_head = [beside(came_head[0])]
-    crossing[0], own_rows, came_head[-1], *words_and_valid = tied(
-        crossing[0], own_rows, came_head[-1], *words_and_valid
-    )
-    words_and_valid = jnp.stack(words_and_valid)
-    besides_head += [beside(piece) for piece in came_head[1:]]
     half_block = pl.BlockSpec((each, width), lambda i: (0, 0))
     normed_own = pl.pallas_call(
         norm_kernel,
@@ -482,10 +477,14 @@
         out_specs=half_block,
         out_shape=jax.ShapeDtypeStruct((each, width), jnp.bfloat16),
         compiler_params=pltpu.CompilerParams(vmem_limit_bytes=32 * 2**20),
-        cost_estimate=cost(0, 10 * each * width),
+        cost_estimate=cost(0, width),
         name="add_and_norm",
     )(own_rows, kept, came, *crossing, final_norm_scale[None, :])
-    normed_own, *besides_head[0] = tied(normed_own, *besides_head[0])
+    normed_own, came_head[-1], *words_and_valid = tied(
+        normed_own, came_head[-1], *words_and_valid
+    )
+    words_and_valid = jnp.stack(words_and_valid)
+    besides_head += [beside(piece) for piece in came_head[1:]]
 
     limit = jnp.stack(
         [
@@ -569,7 +568,9 @@
             moved = [between(passed, [(1, 0), (2, 3)])]
         count = len(nears[-1])
         extra = []
-        if step == CHAIN - 2:
+        if step == 1:
+            extra = besides_head[0]
+        elif step == CHAIN - 2:
             extra = besides_head[-1]
         elif step == CHAIN - 1:
             head_part = place_head()
@@ -577,7 +578,9 @@
             extra = [head_stats(head_part, rows, words[0])]
         came = tied(*nears[-1], *extra, *moved)
         nears[-1], extra, moved = came[:count], came[count : -len(moved)], came[-len(moved) :]
-        if step == CHAIN - 2:
+        if step == 1:
+            besides_head[0] = extra
+        elif step == CHAIN - 2:
             besides_head[-1] = extra
         elif step == CHAIN - 1:
             early = extra[0]

time: 265 us -> 262 us (0.989)
  waiting for transfers between devices: 96.6 us -> 92.4 us
    all_to_all x2, waiting for transfers between devices: 32.7 us -> 18.7 us  [shards(): lax.all_to_all(head[cut], 'seq', 0, 0, axis_index_groups=chain_groups())]
    ppermute x6, waiting for transfers between devices: 16.1 us -> 25.3 us  [along_x(): lax.ppermute(x, 'mp', [(i, (i + 2 * by) % count) for i in range(count)])]
    unnamed x61 -> x65, local copies, waits for them, and re-layouts: 11.7 us -> 12.4 us
  transfers between devices with their start and end apart: 41 -> 41, of which waited for: 20 -> 21; matrix products, arithmetic and copies ran while one was open for 9% -> 9% of each run, Pallas kernels for 22% -> 22%
where the time goes in v5:
time: 262 us; the launch traced here: 261 us
  waiting for transfers between devices  92.4 us (35%)
  starting transfers between devices  67.9 us (26%)
  Pallas kernels  63.9 us (24%)
  local copies, waits for them, and re-layouts  23.1 us (9%)
  other arithmetic  12 us (5%)
    ppermute x7, waiting for transfers between devices, to_partner(): lax.ppermute(x, 'seq', [(i, partner(i, side, block, count)) for i in rang...  33.2 us
    pallas_call x3, Pallas kernels, head_stats(): pl.pallas_call(functools.partial(head_kernel, count), in_specs=[pl.BlockS...  32.9 us
    ppermute x6, waiting for transfers between devices, along_x(): lax.ppermute(x, 'mp', [(i, (i + 2 * by) % count) for i in range(count)])  25.3 us
    ppermute x7, starting transfers between devices, to_partner(): lax.ppermute(x, 'seq', [(i, partner(i, side, block, count)) for i in rang...  23.4 us
    all_to_all x2, waiting for transfers between devices, shards(): lax.all_to_all(head[cut], 'seq', 0, 0, axis_index_groups=chain_groups())  18.7 us
    ppermute x10, starting transfers between devices, turn(): return lax.ppermute(x, 'seq', [(i, turned(i, by)) for i in range(count)])  15 us
    pallas_call x1, Pallas kernels, shards(): pl.pallas_call(functools.partial(project_kernel, len(prompts), hops == 1)...  14.7 us
    unnamed x65, local copies, waits for them, and re-layouts  12.4 us
  transfers between devices with their start and end apart: 41, of which 21 were waited for; matrix products, arithmetic and copies ran while one was open for 9% of the time, Pallas kernels for 22%

profile of v5, /device:TPU:0, one launch (start us, length us, event | category | flops | bytes accessed | tf_op | source)
XLA Modules:
  0.0 261.3 jit_solution(12786520958248901017)
XLA Ops:
  0.7 1.3 copy.114.refs_0_
  2.0 3.1 %collective-permute-start = (bf16[2,64,896]{2,1,0:T(8,128)(2,1)S(1)}, bf16[2,64,896]{2,1,0:T(8,128)(2,1)S(1)}, u32[]{:S(2)}, u32[]{:S(2)}) collective-permute-start(bf16[2,64,896]{2,1,0:T(8,128)(2,1)S(1)} %copy.114.refs_0_), channel_id=1, source_target_pairs={{0,8},{4,12},{8,0},{12,4},{16,24},{20,28},{24,16},{28,20},{1,9},{5... | collective-permute-start | bytes 688136 | tf_op jit(solution)/shard_map/ppermute | solution.py:31
  5.1 1.5 collective-permute-start.1
  6.6 2.6 collective-permute-start.3
  11.8 1.0 copy.92
  12.7 1.0 copy.93
  15.6 5.2 %local_tokens.1 = (f32[2,256,896]{2,1,0:T(8,128)S(1)}, bf16[2,80,896]{2,1,0:T(8,128)(2,1)}, f32[2,256,14]{2,1,0:T(8,128)S(1)}) custom-call(bf16[2,256,896]{2,1,0:T(8,128)(2,1)S(1)} %copy-done.8, bf16[2,256,128]{2,1,0:T(8,128)(2,1)S(1)} %pad_maximum_fusion.both_ref.refs_9_, f32[2,256,14]{2,1,0:T(8,128)S(1)} %copy.95.step_ref, f32[2,1,14]{2,1,0:T(1,128)S(1)} %bitcast.230, ...), custom_call_target="tpu_custom_call" | custom-call | flops 1000000000 | bytes 8388608 | tf_op jit(solution)/shard_map/local_tokens/pallas_call | solution.py:348
  21.5 4.0 %collective-permute-start.5 = (bf16[2,80,896]{2,1,0:T(8,128)(2,1)}, bf16[2,80,896]{2,1,0:T(8,128)(2,1)S(1)}, u32[]{:S(2)}, u32[]{:S(2)}) collective-permute-start(bf16[2,80,896]{2,1,0:T(8,128)(2,1)} %get-tuple-element.42), channel_id=1, source_target_pairs={{0,4},{4,8},{8,12},{12,16},{16,20},{20,24},{24,28},{1,5},{5,9},{9,... | collective-permute-start | bytes 860168 | tf_op jit(solution)/shard_map/ppermute | solution.py:383
  25.7 4.4 %split_head_columns.1 = (bf16[4,224,1024]{2,1,0:T(8,128)(2,1)}, bf16[4,224,1024]{2,1,0:T(8,128)(2,1)}) custom-call(bf16[448,4000]{1,0:T(8,128)(2,1)} %head_ref.1), custom_call_target="tpu_custom_call" | custom-call | bytes 7168000 | tf_op jit(solution)/shard_map/split_head_columns/pallas_call | solution.py:399
  30.1 2.0 collective-permute-done.6.refs_6_
  32.9 5.4 %all-to-all-start = ((bf16[4,224,1024]{2,1,0:T(8,128)(2,1)}), bf16[4,224,1024]{2,1,0:T(8,128)(2,1)S(1)}, u32[]{:S(2)}, u32[]{:S(2)}) async-start(bf16[4,224,1024]{2,1,0:T(8,128)(2,1)} %get-tuple-element.51), calls=%async_computation | async-start | bytes 3670016 | tf_op jit(solution)/shard_map/all_to_all | solution.py:410
  39.8 3.6 %collective-permute-start.4 = (bf16[2,64,896]{2,1,0:T(8,128)(2,1)}, bf16[2,64,896]{2,1,0:T(8,128)(2,1)S(1)}, u32[]{:S(2)}, u32[]{:S(2)}) collective-permute-start(bf16[2,64,896]{2,1,0:T(8,128)(2,1)} %collective-permute-done.3.refs_4_), channel_id=1, source_target_pairs={{0,4},{4,0},{8,12},{12,8},{16,20},{20,16},{24,28},{28,24},{1,5},{5... | collective-permute-start | bytes 688136 | tf_op jit(solution)/shard_map/ppermute | solution.py:36
  43.4 2.0 collective-permute-start.7
  46.1 4.0 %collective-permute-done.4.refs_5_ = bf16[2,64,896]{2,1,0:T(8,128)(2,1)S(1)} collective-permute-done((bf16[2,64,896]{2,1,0:T(8,128)(2,1)}, bf16[2,64,896]{2,1,0:T(8,128)(2,1)S(1)}, u32[]{:S(2)}, u32[]{:S(2)}) %collective-permute-start.4) | collective-permute-done | bytes 229408 | tf_op jit(solution)/shard_map/ppermute | solution.py:36
  50.1 4.5 %collective-permute-done.2.refs_3_ = bf16[2,64,896]{2,1,0:T(8,128)(2,1)S(1)} collective-permute-done((bf16[2,64,896]{2,1,0:T(8,128)(2,1)S(1)}, bf16[2,64,896]{2,1,0:T(8,128)(2,1)S(1)}, u32[]{:S(2)}, u32[]{:S(2)}) %collective-permute-start.2) | collective-permute-done | bytes 229408 | tf_op jit(solution)/shard_map/ppermute | solution.py:36
  54.6 2.5 collective-permute-done.7.refs_7_
  57.7 14.7 %gate_and_project.1 = (bf16[256,3584]{1,0:T(8,128)(2,1)}, bf16[256,3584]{1,0:T(8,128)(2,1)}) custom-call(s32[4]{0:T(128)} %fusion.45.order_ref, bf16[2,64,896]{2,1,0:T(8,128)(2,1)} %copy-done.14, bf16[2,64,896]{2,1,0:T(8,128)(2,1)} %copy-done.18, bf16[2,64,896]{2,1,0:T(8,128)(2,1)} %copy-done.16, bf16[2,64,896]{2,1,0:T(8,128)(2,1)} %copy-done.21, ...), custom_call_target="tpu_custom_call" | custom-call | flops 3288334336 | bytes 12845056 | tf_op jit(solution)/shard_map/gate_and_project/pallas_call | solution.py:435
  72.5 4.9 %all-to-all-done.refs_0_ = bf16[4,224,1024]{2,1,0:T(8,128)(2,1)S(1)} async-done(((bf16[4,224,1024]{2,1,0:T(8,128)(2,1)}), bf16[4,224,1024]{2,1,0:T(8,128)(2,1)S(1)}, u32[]{:S(2)}, u32[]{:S(2)}) %all-to-all-start) | async-done | bytes 1835040 | tf_op jit(solution)/shard_map/all_to_all | solution.py:410
  77.4 4.4 %all-to-all-start.1 = ((bf16[4,224,1024]{2,1,0:T(8,128)(2,1)}), bf16[4,224,1024]{2,1,0:T(8,128)(2,1)}, u32[]{:S(2)}, u32[]{:S(2)}) async-start(bf16[4,224,1024]{2,1,0:T(8,128)(2,1)} %get-tuple-element.53), calls=%async_computation.1 | async-start | bytes 3670016 | tf_op jit(solution)/shard_map/all_to_all | solution.py:410
  81.8 2.7 %add_convert_fusion = bf16[128,3584]{1,0:T(8,128)(2,1)} fusion(bf16[256,3584]{1,0:T(8,128)(2,1)} %collective-permute-done.8.refs_2_, bf16[256,3584]{1,0:T(8,128)(2,1)} %get-tuple-element.49.refs_1_), kind=kLoop, calls=%fused_computation.1 | loop fusion | flops 1835008 | bytes 2752512 | tf_op jit(solution)/shard_map/convert_element_type | solution.py:470
  84.5 1.5 collective-permute-start.9
  86.0 5.4 %collective-permute-start.14 = (bf16[4,224,1024]{2,1,0:T(8,128)(2,1)S(1)}, bf16[4,224,1024]{2,1,0:T(8,128)(2,1)}, u32[]{:S(2)}, u32[]{:S(2)}) collective-permute-start(bf16[4,224,1024]{2,1,0:T(8,128)(2,1)S(1)} %all-to-all-done.refs_0_), channel_id=1, source_target_pairs={{0,4},{4,0},{8,12},{12,8},{16,20},{20,16},{24,28},{28,24},{1,5},{5... | collective-permute-start | bytes 5505032 | tf_op jit(solution)/shard_map/ppermute | solution.py:36
  91.4 2.0 collective-permute-start.10
  93.4 2.4 collective-permute-start.11
  95.8 1.8 dynamic-slice_bitcast_fusion
  97.7 9.7 %collective-permute-done.9.refs_3_ = bf16[128,3584]{1,0:T(8,128)(2,1)S(1)} collective-permute-done((bf16[128,3584]{1,0:T(8,128)(2,1)}, bf16[128,3584]{1,0:T(8,128)(2,1)S(1)}, u32[]{:S(2)}, u32[]{:S(2)}) %collective-permute-start.9) | collective-permute-done | bytes 917536 | tf_op jit(solution)/shard_map/ppermute | solution.py:64
  107.4 1.0 copy-done.4
  108.5 1.2 copy-done.5
  109.6 2.1 add_and_norm.1.refs_0_
  111.7 13.8 %all-to-all-done.1.refs_2_ = bf16[4,224,1024]{2,1,0:T(8,128)(2,1)} async-done(((bf16[4,224,1024]{2,1,0:T(8,128)(2,1)}), bf16[4,224,1024]{2,1,0:T(8,128)(2,1)}, u32[]{:S(2)}, u32[]{:S(2)}) %all-to-all-start.1) | async-done | bytes 1835040 | tf_op jit(solution)/shard_map/all_to_all | solution.py:410
  125.5 1.6 collective-permute-start.13
  127.5 1.6 collective-permute-start.16
  129.1 5.4 %collective-permute-start.18 = (bf16[4,224,1024]{2,1,0:T(8,128)(2,1)}, bf16[4,224,1024]{2,1,0:T(8,128)(2,1)}, u32[]{:S(2)}, u32[]{:S(2)}) collective-permute-start(bf16[4,224,1024]{2,1,0:T(8,128)(2,1)} %all-to-all-done.1.refs_2_), channel_id=1, source_target_pairs={{0,4},{4,0},{8,12},{12,8},{16,20},{20,16},{24,28},{28,24},{1,5},{5... | collective-permute-start | bytes 5505032 | tf_op jit(solution)/shard_map/ppermute | solution.py:36
  134.5 13.0 %collective-permute-done.13.refs_1_ = bf16[128,3584]{1,0:T(8,128)(2,1)S(1)} collective-permute-done((bf16[128,3584]{1,0:T(8,128)(2,1)S(1)}, bf16[128,3584]{1,0:T(8,128)(2,1)S(1)}, u32[]{:S(2)}, u32[]{:S(2)}) %collective-permute-start.13) | collective-permute-done | bytes 917536 | tf_op jit(solution)/shard_map/ppermute | solution.py:64
  147.5 1.3 collective-permute-done.15.refs_0_
  148.8 1.1 collective-permute-start.17
  150.0 1.3 collective-permute-start.19
  151.3 1.7 collective-permute-start.20
  152.9 21.3 %collective-permute-done.18.refs_3_ = bf16[4,224,1024]{2,1,0:T(8,128)(2,1)} collective-permute-done((bf16[4,224,1024]{2,1,0:T(8,128)(2,1)}, bf16[4,224,1024]{2,1,0:T(8,128)(2,1)}, u32[]{:S(2)}, u32[]{:S(2)}) %collective-permute-start.18) | collective-permute-done | bytes 1835040 | tf_op jit(solution)/shard_map/ppermute | solution.py:36
  174.3 2.2 broadcast_select_fusion.1.refs_4_
  177.0 1.3 collective-permute-start.24
  180.0 0.9 broadcast_in_dim.99.refs_5_
  181.2 4.5 %place_head_rows.1.refs_4_.refs_10_.refs_2_ = bf16[3584,1024]{1,0:T(8,128)(2,1)S(1)} custom-call(s32[16]{0:T(128)S(1)} %stack.195.first_ref, bf16[4,224,1024]{2,1,0:T(8,128)(2,1)S(1)} %all-to-all-done.refs_0_, bf16[4,224,1024]{2,1,0:T(8,128)(2,1)} %collective-permute-done.14.refs_1_, bf16[4,224,1024]{2,1,0:T(8,128)(2,1)} %all-to-all-done.1.refs_2_, ...), custom_call_target="tpu_custom_call" | custom-call | bytes 14680064 | tf_op jit(solution)/shard_map/place_head_rows/pallas_call | solution.py:515
  185.7 2.9 %copy-done = bf16[3584,1024]{1,0:T(8,128)(2,1)} copy-done((bf16[3584,1024]{1,0:T(8,128)(2,1)}, bf16[3584,1024]{1,0:T(8,128)(2,1)S(1)}, u32[]{:S(2)}) %copy-start) | copy-done | bytes 7340056
  188.9 9.2 %head_stats.3 = f32[8,512]{1,0:T(8,128)} custom-call(s32[2]{0:T(128)} %pad_add_fusion.3.limit_ref, bf16[128,3584]{1,0:T(8,128)(2,1)} %copy-done.3, bf16[128,3584]{1,0:T(8,128)(2,1)} %copy-done.29, bf16[128,3584]{1,0:T(8,128)(2,1)} %collective-permute-done.22.refs_2_, bf16[128,3584]{1,0:T(8,128)(2,1)} %collective-permute-done.23.refs_3_, ...), custom_call_target="tpu_custom_call" | custom-call | flops 3758096384 | bytes 11010048 | tf_op jit(solution)/shard_map/head_stats/pallas_call | solution.py:531
  199.6 2.1 collective-permute-done.24
  201.7 1.3 broadcast_select_fusion.refs_8_
  203.8 1.5 collective-permute-start.25
  205.3 1.1 copy.151
  207.2 17.0 %head_stats.4 = f32[8,1280]{1,0:T(8,128)} custom-call(s32[2]{0:T(128)} %pad_add_fusion.3.limit_ref, bf16[128,3584]{1,0:T(8,128)(2,1)} %collective-permute-done.15.refs_0_, bf16[128,3584]{1,0:T(8,128)(2,1)} %collective-permute-done.17.refs_1_, bf16[128,3584]{1,0:T(8,128)(2,1)} %collective-permute-done.26.refs_2_, ...), custom_call_target="tpu_custom_call" | custom-call | flops 9395240960 | bytes 16515072 | tf_op jit(solution)/shard_map/head_stats/pallas_call | solution.py:531
  224.2 0.9 reshape.372
  225.1 1.0 collective-permute-done.25.refs_0_
  227.2 1.4 collective-permute-done.31.refs_1_
  228.6 0.9 copy-done.13
  229.5 6.6 %head_stats.5 = f32[8,256]{1,0:T(8,128)} custom-call(s32[2]{0:T(128)} %pad_add_fusion.3.limit_ref, bf16[128,3584]{1,0:T(8,128)(2,1)} %copy-done.12, bf16[128,3584]{1,0:T(8,128)(2,1)} %copy-done.13, bf16[3584,1024]{1,0:T(8,128)(2,1)} %copy-done, s32[256,1]{1,0:T(8,128)} %copy.110.refs_3_), custom_call_target="tpu_custom_call" | custom-call | flops 1879048192 | bytes 9175040 | tf_op jit(solution)/shard_map/head_stats/pallas_call | solution.py:531
  237.0 2.9 %collective-permute-start.32 = (f32[3,4,2,2,2,64]{5,4,3,2,1,0:T(2,128)S(1)}, f32[3,4,2,2,2,64]{5,4,3,2,1,0:T(2,128)S(1)}, u32[]{:S(2)}, u32[]{:S(2)}) collective-permute-start(f32[3,4,2,2,2,64]{5,4,3,2,1,0:T(2,128)S(1)} %pad_maximum_fusion.1), channel_id=1, source_target_pairs={{0,8},{4,12},{8,0},{12,4},{16,24},{20,28},{24,16},{28,20},{1,9},{5... | collective-permute-start | bytes 73736 | tf_op jit(solution)/shard_map/ppermute | solution.py:31
  240.0 1.5 collective-permute-start.34
  242.0 3.9 %collective-permute-done.34 = f32[3,4,2,2,2,64]{5,4,3,2,1,0:T(2,128)S(1)} collective-permute-done((f32[3,4,2,2,2,64]{5,4,3,2,1,0:T(2,128)S(1)}, f32[3,4,2,2,2,64]{5,4,3,2,1,0:T(2,128)S(1)}, u32[]{:S(2)}, u32[]{:S(2)}) %collective-permute-start.34) | collective-permute-done | bytes 24608 | tf_op jit(solution)/shard_map/ppermute | solution.py:31
  246.0 1.4 collective-permute-done.33
  248.3 1.5 collective-permute-start.36
  249.8 1.7 collective-permute-done.37
  251.6 1.2 collective-permute-done.36
  253.7 5.5 %collective-permute-start.38 = (f32[48]{0:T(128)S(1)}, f32[48]{0:T(128)S(1)}, u32[]{:S(2)}, u32[]{:S(2)}) collective-permute-start(f32[48]{0:T(128)S(1)} %convolution_bitcast_fusion), channel_id=1, source_target_pairs={{0,4},{4,0},{8,12},{12,8},{16,20},{20,16},{24,28},{28,24},{1,5},{5... | collective-permute-start | bytes 584 | tf_op jit(solution)/shard_map/ppermute | solution.py:36
  259.8 1.0 collective-permute-done.38
  (173 shorter events, 20.5 us)
Async XLA Ops:
  0.6 14.9 %copy-start.8 = (bf16[2,256,896]{2,1,0:T(8,128)(2,1)S(1)}, bf16[2,256,896]{2,1,0:T(8,128)(2,1)}, u32[]{:S(2)}) copy-start(bf16[2,256,896]{2,1,0:T(8,128)(2,1)} %x_ref) | copy-start | bytes 2752516
  0.6 14.9 %copy-start.9 = (f32[2,14]{1,0:T(2,128)S(1)}, f32[2,14]{1,0:T(2,128)}, u32[]{:S(2)}) copy-start(f32[2,14]{1,0:T(2,128)} %param.29) | copy-start | bytes 340
  0.7 14.9 %copy-start.10 = (f32[2,14]{1,0:T(2,128)S(1)}, f32[2,14]{1,0:T(2,128)}, u32[]{:S(2)}) copy-start(f32[2,14]{1,0:T(2,128)} %param.30) | copy-start | bytes 340
  2.0 18.8 %copy-start.14 = (bf16[2,64,896]{2,1,0:T(8,128)(2,1)}, bf16[2,64,896]{2,1,0:T(8,128)(2,1)S(1)}, u32[]{:S(2)}) copy-start(bf16[2,64,896]{2,1,0:T(8,128)(2,1)S(1)} %copy.114.refs_0_) | copy-start | bytes 688132
  2.0 12.8 %collective-permute-start = (bf16[2,64,896]{2,1,0:T(8,128)(2,1)S(1)}, bf16[2,64,896]{2,1,0:T(8,128)(2,1)S(1)}, u32[]{:S(2)}, u32[]{:S(2)}) collective-permute-start(bf16[2,64,896]{2,1,0:T(8,128)(2,1)S(1)} %copy.114.refs_0_), channel_id=1, source_target_pairs={{0,8},{4,12},{8,0},{12,4},{16,24},{20,28},{24,16},{28,20},{1,9},{5... | collective-permute-start | bytes 688136 | tf_op jit(solution)/shard_map/ppermute | solution.py:31
  5.1 9.7 %collective-permute-start.1 = (bf16[2,64,896]{2,1,0:T(8,128)(2,1)S(1)}, bf16[2,64,896]{2,1,0:T(8,128)(2,1)S(1)}, u32[]{:S(2)}, u32[]{:S(2)}) collective-permute-start(bf16[2,64,896]{2,1,0:T(8,128)(2,1)S(1)} %copy.114.refs_0_), channel_id=1, source_target_pairs={{0,4},{4,0},{8,12},{12,8},{16,20},{20,16},{24,28},{28,24},{1,5},{5... | collective-permute-start | bytes 688136 | tf_op jit(solution)/shard_map/ppermute | solution.py:36
  6.6 19.0 %collective-permute-start.3 = (bf16[2,64,896]{2,1,0:T(8,128)(2,1)S(1)}, bf16[2,64,896]{2,1,0:T(8,128)(2,1)}, u32[]{:S(2)}, u32[]{:S(2)}) collective-permute-start(bf16[2,64,896]{2,1,0:T(8,128)(2,1)S(1)} %copy.114.refs_0_), channel_id=1, source_target_pairs={{0,16},{4,20},{8,24},{12,28},{16,0},{20,4},{24,8},{28,12},{1,17},{... | collective-permute-start | bytes 688136 | tf_op jit(solution)/shard_map/ppermute | solution.py:31
  14.7 6.1 %copy-start.6 = (bf16[2,256,128]{2,1,0:T(8,128)(2,1)}, bf16[2,256,128]{2,1,0:T(8,128)(2,1)S(1)}, u32[]{:S(2)}) copy-start(bf16[2,256,128]{2,1,0:T(8,128)(2,1)S(1)} %pad_maximum_fusion.both_ref.refs_9_) | copy-start | bytes 393220
  21.5 8.6 %copy-start.2 = (f32[2,256,896]{2,1,0:T(8,128)}, f32[2,256,896]{2,1,0:T(8,128)S(1)}, u32[]{:S(2)}) copy-start(f32[2,256,896]{2,1,0:T(8,128)S(1)} %get-tuple-element.46.refs_8_) | copy-start | bytes 5505028
  21.5 10.6 %collective-permute-start.5 = (bf16[2,80,896]{2,1,0:T(8,128)(2,1)}, bf16[2,80,896]{2,1,0:T(8,128)(2,1)S(1)}, u32[]{:S(2)}, u32[]{:S(2)}) collective-permute-start(bf16[2,80,896]{2,1,0:T(8,128)(2,1)} %get-tuple-element.42), channel_id=1, source_target_pairs={{0,4},{4,8},{8,12},{12,16},{16,20},{20,24},{24,28},{1,5},{5,9},{9,... | collective-permute-start | bytes 860168 | tf_op jit(solution)/shard_map/ppermute | solution.py:383
  25.6 6.6 %collective-permute-start.6 = (bf16[2,64,896]{2,1,0:T(8,128)(2,1)}, bf16[2,64,896]{2,1,0:T(8,128)(2,1)S(1)}, u32[]{:S(2)}, u32[]{:S(2)}) collective-permute-start(bf16[2,64,896]{2,1,0:T(8,128)(2,1)} %collective-permute-done.3.refs_4_), channel_id=1, source_target_pairs={{0,8},{4,12},{8,0},{12,4},{16,24},{20,28},{24,16},{28,20},{1,9},{5... | collective-permute-start | bytes 688136 | tf_op jit(solution)/shard_map/ppermute | solution.py:31
  32.2 11.2 %copy-start.19 = (bf16[2,64,896]{2,1,0:T(8,128)(2,1)}, bf16[2,64,896]{2,1,0:T(8,128)(2,1)S(1)}, u32[]{:S(2)}) copy-start(bf16[2,64,896]{2,1,0:T(8,128)(2,1)S(1)} %collective-permute-done.6.refs_6_) | copy-start | bytes 688132
  32.2 6.9 %copy-start.26 = (s32[256]{0:T(256)S(1)}, s32[256]{0:T(256)}, u32[]{:S(2)}) copy-start(s32[256]{0:T(256)} %param.20) | copy-start | bytes 3076
  32.2 6.9 %copy-start.27 = (s32[256]{0:T(256)S(1)}, s32[256]{0:T(256)}, u32[]{:S(2)}) copy-start(s32[256]{0:T(256)} %param.19) | copy-start | bytes 3076
  32.2 11.2 %copy-start.17 = (bf16[2,64,896]{2,1,0:T(8,128)(2,1)S(1)}, bf16[2,64,896]{2,1,0:T(8,128)(2,1)}, u32[]{:S(2)}) copy-start(bf16[2,64,896]{2,1,0:T(8,128)(2,1)} %copy-done.16) | copy-start | bytes 688132
  32.9 44.4 %all-to-all-start = ((bf16[4,224,1024]{2,1,0:T(8,128)(2,1)}), bf16[4,224,1024]{2,1,0:T(8,128)(2,1)S(1)}, u32[]{:S(2)}, u32[]{:S(2)}) async-start(bf16[4,224,1024]{2,1,0:T(8,128)(2,1)} %get-tuple-element.51), calls=%async_computation | async-start | bytes 3670016 | tf_op jit(solution)/shard_map/all_to_all | solution.py:410
  39.8 10.3 %collective-permute-start.4 = (bf16[2,64,896]{2,1,0:T(8,128)(2,1)}, bf16[2,64,896]{2,1,0:T(8,128)(2,1)S(1)}, u32[]{:S(2)}, u32[]{:S(2)}) collective-permute-start(bf16[2,64,896]{2,1,0:T(8,128)(2,1)} %collective-permute-done.3.refs_4_), channel_id=1, source_target_pairs={{0,4},{4,0},{8,12},{12,8},{16,20},{20,16},{24,28},{28,24},{1,5},{5... | collective-permute-start | bytes 688136 | tf_op jit(solution)/shard_map/ppermute | solution.py:36
  43.4 11.2 %collective-permute-start.2 = (bf16[2,64,896]{2,1,0:T(8,128)(2,1)S(1)}, bf16[2,64,896]{2,1,0:T(8,128)(2,1)S(1)}, u32[]{:S(2)}, u32[]{:S(2)}) collective-permute-start(bf16[2,64,896]{2,1,0:T(8,128)(2,1)S(1)} %copy-done.17), channel_id=1, source_target_pairs={{0,4},{4,0},{8,12},{12,8},{16,20},{20,16},{24,28},{28,24},{1,5},{5... | collective-permute-start | bytes 688136 | tf_op jit(solution)/shard_map/ppermute | solution.py:36
  43.4 13.6 %collective-permute-start.7 = (bf16[2,64,896]{2,1,0:T(8,128)(2,1)S(1)}, bf16[2,64,896]{2,1,0:T(8,128)(2,1)S(1)}, u32[]{:S(2)}, u32[]{:S(2)}) collective-permute-start(bf16[2,64,896]{2,1,0:T(8,128)(2,1)S(1)} %collective-permute-done.6.refs_6_), channel_id=1, source_target_pairs={{0,4},{4,0},{8,12},{12,8},{16,20},{20,16},{24,28},{28,24},{1,5},{5... | collective-permute-start | bytes 688136 | tf_op jit(solution)/shard_map/ppermute | solution.py:36
  50.1 7.5 %copy-start.20 = (bf16[2,64,896]{2,1,0:T(8,128)(2,1)}, bf16[2,64,896]{2,1,0:T(8,128)(2,1)S(1)}, u32[]{:S(2)}) copy-start(bf16[2,64,896]{2,1,0:T(8,128)(2,1)S(1)} %collective-permute-done.4.refs_5_) | copy-start | bytes 688132
  54.6 3.1 %copy-start.21 = (bf16[2,64,896]{2,1,0:T(8,128)(2,1)}, bf16[2,64,896]{2,1,0:T(8,128)(2,1)S(1)}, u32[]{:S(2)}) copy-start(bf16[2,64,896]{2,1,0:T(8,128)(2,1)S(1)} %collective-permute-done.2.refs_3_) | copy-start | bytes 688132
  77.4 4.4 %collective-permute-start.8 = (bf16[256,3584]{1,0:T(8,128)(2,1)}, bf16[256,3584]{1,0:T(8,128)(2,1)}, u32[]{:S(2)}, u32[]{:S(2)}) collective-permute-start(bf16[256,3584]{1,0:T(8,128)(2,1)} %get-tuple-element.52), channel_id=1, source_target_pairs={{0,1},{1,0},{2,3},{3,2},{4,5},{5,4},{6,7},{7,6},{8,9},{9,8},{10,11... | collective-permute-start | bytes 5505032 | tf_op jit(solution)/shard_map/ppermute | solution.py:59
  77.4 48.1 %all-to-all-start.1 = ((bf16[4,224,1024]{2,1,0:T(8,128)(2,1)}), bf16[4,224,1024]{2,1,0:T(8,128)(2,1)}, u32[]{:S(2)}, u32[]{:S(2)}) async-start(bf16[4,224,1024]{2,1,0:T(8,128)(2,1)} %get-tuple-element.53), calls=%async_computation.1 | async-start | bytes 3670016 | tf_op jit(solution)/shard_map/all_to_all | solution.py:410
  84.5 23.0 %collective-permute-start.9 = (bf16[128,3584]{1,0:T(8,128)(2,1)}, bf16[128,3584]{1,0:T(8,128)(2,1)S(1)}, u32[]{:S(2)}, u32[]{:S(2)}) collective-permute-start(bf16[128,3584]{1,0:T(8,128)(2,1)} %add_convert_fusion), channel_id=1, source_target_pairs={{0,2},{1,3},{2,0},{3,1},{4,6},{5,7},{6,4},{7,5},{8,10},{9,11},{10,... | collective-permute-start | bytes 2752520 | tf_op jit(solution)/shard_map/ppermute | solution.py:64
  86.0 48.5 %collective-permute-start.14 = (bf16[4,224,1024]{2,1,0:T(8,128)(2,1)S(1)}, bf16[4,224,1024]{2,1,0:T(8,128)(2,1)}, u32[]{:S(2)}, u32[]{:S(2)}) collective-permute-start(bf16[4,224,1024]{2,1,0:T(8,128)(2,1)S(1)} %all-to-all-done.refs_0_), channel_id=1, source_target_pairs={{0,4},{4,0},{8,12},{12,8},{16,20},{20,16},{24,28},{28,24},{1,5},{5... | collective-permute-start | bytes 5505032 | tf_op jit(solution)/shard_map/ppermute | solution.py:36
  91.4 6.3 %copy-start.24 = (f32[3584]{0:T(1024)S(1)}, f32[3584]{0:T(1024)}, u32[]{:S(2)}) copy-start(f32[3584]{0:T(1024)} %param.36) | copy-start | bytes 43012
  91.4 17.1 %copy-start.1 = (bf16[256,3584]{1,0:T(8,128)(2,1)S(1)}, bf16[256,3584]{1,0:T(8,128)(2,1)}, u32[]{:S(2)}) copy-start(bf16[256,3584]{1,0:T(8,128)(2,1)} %get-tuple-element.49.refs_1_) | copy-start | bytes 5505028
  91.4 34.1 %collective-permute-start.10 = (s32[2,256]{1,0:T(2,128)S(1)}, s32[2,256]{1,0:T(2,128)S(1)}, u32[]{:S(2)}, u32[]{:S(2)}) collective-permute-start(s32[2,256]{1,0:T(2,128)S(1)} %pad_add_fusion.1), channel_id=1, source_target_pairs={{0,8},{4,12},{8,0},{12,4},{16,24},{20,28},{24,16},{28,20},{1,9},{5... | collective-permute-start | bytes 6152 | tf_op jit(solution)/shard_map/ppermute | solution.py:31
  93.4 32.1 %collective-permute-start.11 = (s32[2,256]{1,0:T(2,128)S(1)}, s32[2,256]{1,0:T(2,128)S(1)}, u32[]{:S(2)}, u32[]{:S(2)}) collective-permute-start(s32[2,256]{1,0:T(2,128)S(1)} %pad_add_fusion.1), channel_id=1, source_target_pairs={{0,16},{4,20},{8,24},{12,28},{16,0},{20,4},{24,8},{28,12},{1,17},{... | collective-permute-start | bytes 6152 | tf_op jit(solution)/shard_map/ppermute | solution.py:31
  95.7 29.8 %collective-permute-start.12 = (s32[2,256]{1,0:T(2,128)S(1)}, s32[2,256]{1,0:T(2,128)S(1)}, u32[]{:S(2)}, u32[]{:S(2)}) collective-permute-start(s32[2,256]{1,0:T(2,128)S(1)} %pad_add_fusion.1), channel_id=1, source_target_pairs={{0,24},{4,28},{8,16},{12,20},{16,8},{20,12},{24,0},{28,4},{1,25},{... | collective-permute-start | bytes 6152 | tf_op jit(solution)/shard_map/ppermute | solution.py:31
  111.7 74.0 %copy-start.3 = (bf16[128,3584]{1,0:T(8,128)(2,1)}, bf16[128,3584]{1,0:T(8,128)(2,1)S(1)}, u32[]{:S(2)}) copy-start(bf16[128,3584]{1,0:T(8,128)(2,1)S(1)} %add_and_norm.1.refs_0_) | copy-start | bytes 2752516
  125.5 22.0 %collective-permute-start.13 = (bf16[128,3584]{1,0:T(8,128)(2,1)S(1)}, bf16[128,3584]{1,0:T(8,128)(2,1)S(1)}, u32[]{:S(2)}, u32[]{:S(2)}) collective-permute-start(bf16[128,3584]{1,0:T(8,128)(2,1)S(1)} %add_and_norm.1.refs_0_), channel_id=1, source_target_pairs={{0,2},{1,3},{2,0},{3,1},{4,6},{5,7},{6,4},{7,5},{8,10},{9,11},{10,... | collective-permute-start | bytes 2752520 | tf_op jit(solution)/shard_map/ppermute | solution.py:64
  127.1 21.8 %collective-permute-start.15 = (bf16[128,3584]{1,0:T(8,128)(2,1)S(1)}, bf16[128,3584]{1,0:T(8,128)(2,1)}, u32[]{:S(2)}, u32[]{:S(2)}) collective-permute-start(bf16[128,3584]{1,0:T(8,128)(2,1)S(1)} %add_and_norm.1.refs_0_), channel_id=1, source_target_pairs={{0,8},{4,12},{8,0},{12,4},{16,24},{20,28},{24,16},{28,20},{1,9},{5... | collective-permute-start | bytes 2752520 | tf_op jit(solution)/shard_map/ppermute | solution.py:31
  127.5 21.3 %collective-permute-start.16 = (bf16[128,3584]{1,0:T(8,128)(2,1)S(1)}, bf16[128,3584]{1,0:T(8,128)(2,1)}, u32[]{:S(2)}, u32[]{:S(2)}) collective-permute-start(bf16[128,3584]{1,0:T(8,128)(2,1)S(1)} %add_and_norm.1.refs_0_), channel_id=1, source_target_pairs={{8,16},{12,20},{16,8},{20,12},{9,17},{13,21},{17,9},{21,13},{10,18... | collective-permute-start | bytes 2752520 | tf_op jit(solution)/shard_map/ppermute | solution.py:47
  129.1 45.2 %collective-permute-start.18 = (bf16[4,224,1024]{2,1,0:T(8,128)(2,1)}, bf16[4,224,1024]{2,1,0:T(8,128)(2,1)}, u32[]{:S(2)}, u32[]{:S(2)}) collective-permute-start(bf16[4,224,1024]{2,1,0:T(8,128)(2,1)} %all-to-all-done.1.refs_2_), channel_id=1, source_target_pairs={{0,4},{4,0},{8,12},{12,8},{16,20},{20,16},{24,28},{28,24},{1,5},{5... | collective-permute-start | bytes 5505032 | tf_op jit(solution)/shard_map/ppermute | solution.py:36
  147.5 1.3 copy-start.29
  148.8 25.4 %collective-permute-start.17 = (bf16[128,3584]{1,0:T(8,128)(2,1)}, bf16[128,3584]{1,0:T(8,128)(2,1)}, u32[]{:S(2)}, u32[]{:S(2)}) collective-permute-start(bf16[128,3584]{1,0:T(8,128)(2,1)} %collective-permute-done.15.refs_0_), channel_id=1, source_target_pairs={{0,2},{1,3},{2,0},{3,1},{4,6},{5,7},{6,4},{7,5},{8,10},{9,11},{10,... | collective-permute-start | bytes 2752520 | tf_op jit(solution)/shard_map/ppermute | solution.py:64
  150.0 24.3 %collective-permute-start.19 = (bf16[128,3584]{1,0:T(8,128)(2,1)}, bf16[128,3584]{1,0:T(8,128)(2,1)}, u32[]{:S(2)}, u32[]{:S(2)}) collective-permute-start(bf16[128,3584]{1,0:T(8,128)(2,1)} %collective-permute-done.16), channel_id=1, source_target_pairs={{8,0},{12,4},{16,24},{20,28},{9,1},{13,5},{17,25},{21,29},{10,2},{... | collective-permute-start | bytes 2752520 | tf_op jit(solution)/shard_map/ppermute | solution.py:47
  151.3 23.0 %collective-permute-start.20 = (bf16[128,3584]{1,0:T(8,128)(2,1)}, bf16[128,3584]{1,0:T(8,128)(2,1)}, u32[]{:S(2)}, u32[]{:S(2)}) collective-permute-start(bf16[128,3584]{1,0:T(8,128)(2,1)} %collective-permute-done.15.refs_0_), channel_id=1, source_target_pairs={{8,16},{12,20},{16,8},{20,12},{9,17},{13,21},{17,9},{21,13},{10,18... | collective-permute-start | bytes 2752520 | tf_op jit(solution)/shard_map/ppermute | solution.py:47
  152.9 35.7 %collective-permute-start.22 = (bf16[128,3584]{1,0:T(8,128)(2,1)S(1)}, bf16[128,3584]{1,0:T(8,128)(2,1)}, u32[]{:S(2)}, u32[]{:S(2)}) collective-permute-start(bf16[128,3584]{1,0:T(8,128)(2,1)S(1)} %add_and_norm.1.refs_0_), channel_id=1, source_target_pairs={{0,1},{1,0},{2,3},{3,2},{4,5},{5,4},{6,7},{7,6},{8,9},{9,8},{10,11... | collective-permute-start | bytes 2752520 | tf_op jit(solution)/shard_map/ppermute | solution.py:59
  174.2 14.7 %collective-permute-start.23 = (bf16[128,3584]{1,0:T(8,128)(2,1)}, bf16[128,3584]{1,0:T(8,128)(2,1)}, u32[]{:S(2)}, u32[]{:S(2)}) collective-permute-start(bf16[128,3584]{1,0:T(8,128)(2,1)} %copy-done.29), channel_id=1, source_target_pairs={{0,1},{1,0},{2,3},{3,2},{4,5},{5,4},{6,7},{7,6},{8,9},{9,8},{10,11... | collective-permute-start | bytes 2752520 | tf_op jit(solution)/shard_map/ppermute | solution.py:59
  176.5 23.1 %collective-permute-start.21 = (bf16[128,3584]{1,0:T(8,128)(2,1)}, bf16[128,3584]{1,0:T(8,128)(2,1)}, u32[]{:S(2)}, u32[]{:S(2)}) collective-permute-start(bf16[128,3584]{1,0:T(8,128)(2,1)} %broadcast_select_fusion.1.refs_4_), channel_id=1, source_target_pairs={{0,2},{1,3},{2,0},{3,1},{4,6},{5,7},{6,4},{7,5},{8,10},{9,11},{10,... | collective-permute-start | bytes 2752520 | tf_op jit(solution)/shard_map/ppermute | solution.py:64
  177.0 24.7 %collective-permute-start.24 = (bf16[128,3584]{1,0:T(8,128)(2,1)}, bf16[128,3584]{1,0:T(8,128)(2,1)}, u32[]{:S(2)}, u32[]{:S(2)}) collective-permute-start(bf16[128,3584]{1,0:T(8,128)(2,1)} %collective-permute-done.20), channel_id=1, source_target_pairs={{8,0},{12,4},{16,24},{20,28},{9,1},{13,5},{17,25},{21,29},{10,2},{... | collective-permute-start | bytes 2752520 | tf_op jit(solution)/shard_map/ppermute | solution.py:47
  181.0 22.8 %collective-permute-start.26 = (bf16[128,3584]{1,0:T(8,128)(2,1)}, bf16[128,3584]{1,0:T(8,128)(2,1)}, u32[]{:S(2)}, u32[]{:S(2)}) collective-permute-start(bf16[128,3584]{1,0:T(8,128)(2,1)} %collective-permute-done.15.refs_0_), channel_id=1, source_target_pairs={{0,1},{1,0},{2,3},{3,2},{4,5},{5,4},{6,7},{7,6},{8,9},{9,8},{10,11... | collective-permute-start | bytes 2752520 | tf_op jit(solution)/shard_map/ppermute | solution.py:59
  185.7 2.9 %copy-start = (bf16[3584,1024]{1,0:T(8,128)(2,1)}, bf16[3584,1024]{1,0:T(8,128)(2,1)S(1)}, u32[]{:S(2)}) copy-start(bf16[3584,1024]{1,0:T(8,128)(2,1)S(1)} %place_head_rows.1.refs_4_.refs_10_.refs_2_) | copy-start | bytes 22020100
  188.6 17.8 %collective-permute-start.28 = (bf16[128,3584]{1,0:T(8,128)(2,1)}, bf16[128,3584]{1,0:T(8,128)(2,1)}, u32[]{:S(2)}, u32[]{:S(2)}) collective-permute-start(bf16[128,3584]{1,0:T(8,128)(2,1)} %broadcast_select_fusion.1.refs_4_), channel_id=1, source_target_pairs={{0,1},{1,0},{2,3},{3,2},{4,5},{5,4},{6,7},{7,6},{8,9},{9,8},{10,11... | collective-permute-start | bytes 2752520 | tf_op jit(solution)/shard_map/ppermute | solution.py:59
  198.9 28.3 %copy-start.23 = (f32[8,4,2,64]{3,2,1,0:T(2,128)}, f32[8,4,2,64]{3,2,1,0:T(2,128)S(1)}, u32[]{:S(2)}) copy-start(f32[8,4,2,64]{3,2,1,0:T(2,128)S(1)} %reshape.368) | copy-start | bytes 49156
  198.9 7.5 %collective-permute-start.27 = (bf16[128,3584]{1,0:T(8,128)(2,1)}, bf16[128,3584]{1,0:T(8,128)(2,1)}, u32[]{:S(2)}, u32[]{:S(2)}) collective-permute-start(bf16[128,3584]{1,0:T(8,128)(2,1)} %collective-permute-done.17.refs_1_), channel_id=1, source_target_pairs={{0,1},{1,0},{2,3},{3,2},{4,5},{5,4},{6,7},{7,6},{8,9},{9,8},{10,11... | collective-permute-start | bytes 2752520 | tf_op jit(solution)/shard_map/ppermute | solution.py:59
  203.0 4.2 %copy-start.11 = (bf16[128,3584]{1,0:T(8,128)(2,1)}, bf16[128,3584]{1,0:T(8,128)(2,1)S(1)}, u32[]{:S(2)}) copy-start(bf16[128,3584]{1,0:T(8,128)(2,1)S(1)} %broadcast_select_fusion.refs_8_) | copy-start | bytes 2752516
  203.0 3.5 %collective-permute-start.30 = (bf16[128,3584]{1,0:T(8,128)(2,1)S(1)}, bf16[128,3584]{1,0:T(8,128)(2,1)}, u32[]{:S(2)}, u32[]{:S(2)}) collective-permute-start(bf16[128,3584]{1,0:T(8,128)(2,1)S(1)} %broadcast_select_fusion.refs_8_), channel_id=1, source_target_pairs={{0,1},{1,0},{2,3},{3,2},{4,5},{5,4},{6,7},{7,6},{8,9},{9,8},{10,11... | collective-permute-start | bytes 2752520 | tf_op jit(solution)/shard_map/ppermute | solution.py:59
  203.1 4.1 %collective-permute-start.29 = (bf16[128,3584]{1,0:T(8,128)(2,1)}, bf16[128,3584]{1,0:T(8,128)(2,1)}, u32[]{:S(2)}, u32[]{:S(2)}) collective-permute-start(bf16[128,3584]{1,0:T(8,128)(2,1)} %collective-permute-done.21.refs_5_), channel_id=1, source_target_pairs={{0,1},{1,0},{2,3},{3,2},{4,5},{5,4},{6,7},{7,6},{8,9},{9,8},{10,11... | collective-permute-start | bytes 2752520 | tf_op jit(solution)/shard_map/ppermute | solution.py:59
  203.8 22.4 %collective-permute-start.25 = (bf16[128,3584]{1,0:T(8,128)(2,1)S(1)}, bf16[128,3584]{1,0:T(8,128)(2,1)S(1)}, u32[]{:S(2)}, u32[]{:S(2)}) collective-permute-start(bf16[128,3584]{1,0:T(8,128)(2,1)S(1)} %broadcast_select_fusion.refs_8_), channel_id=1, source_target_pairs={{0,2},{1,3},{2,0},{3,1},{4,6},{5,7},{6,4},{7,5},{8,10},{9,11},{10,... | collective-permute-start | bytes 2752520 | tf_op jit(solution)/shard_map/ppermute | solution.py:64
  226.1 2.5 copy-start.12
  226.1 2.5 collective-permute-start.31
  227.2 9.8 %slice-start = ((f32[8,4,2,64]{3,2,1,0:T(2,128)}), f32[3,4,2,64]{3,2,1,0:T(2,128)S(1)}, s32[]{:S(2)}) async-start(f32[8,4,2,64]{3,2,1,0:T(2,128)} %copy-done.23), calls=%async_computation.2 | async-start | bytes 24576 | tf_op jit(solution)/shard_map/slice | solution.py:605
  227.2 25.9 %copy-start.25 = (s32[48]{0:T(128)S(1)}, s32[48]{0:T(128)}, u32[]{:S(2)}) copy-start(s32[48]{0:T(128)} %param.21) | copy-start | bytes 580
  236.2 24.5 %copy-start.28 = (s32[48]{0:T(128)S(1)}, s32[48]{0:T(128)}, u32[]{:S(2)}) copy-start(s32[48]{0:T(128)} %param.22) | copy-start | bytes 580
  237.0 5.0 %collective-permute-start.32 = (f32[3,4,2,2,2,64]{5,4,3,2,1,0:T(2,128)S(1)}, f32[3,4,2,2,2,64]{5,4,3,2,1,0:T(2,128)S(1)}, u32[]{:S(2)}, u32[]{:S(2)}) collective-permute-start(f32[3,4,2,2,2,64]{5,4,3,2,1,0:T(2,128)S(1)} %pad_maximum_fusion.1), channel_id=1, source_target_pairs={{0,8},{4,12},{8,0},{12,4},{16,24},{20,28},{24,16},{28,20},{1,9},{5... | collective-permute-start | bytes 73736 | tf_op jit(solution)/shard_map/ppermute | solution.py:31
  240.0 5.9 %collective-permute-start.34 = (f32[3,4,2,2,2,64]{5,4,3,2,1,0:T(2,128)S(1)}, f32[3,4,2,2,2,64]{5,4,3,2,1,0:T(2,128)S(1)}, u32[]{:S(2)}, u32[]{:S(2)}) collective-permute-start(f32[3,4,2,2,2,64]{5,4,3,2,1,0:T(2,128)S(1)} %pad_maximum_fusion.1), channel_id=1, source_target_pairs={{0,24},{4,28},{8,16},{12,20},{16,8},{20,12},{24,0},{28,4},{1,25},{... | collective-permute-start | bytes 73736 | tf_op jit(solution)/shard_map/ppermute | solution.py:31
  241.5 5.9 %collective-permute-start.33 = (f32[3,4,2,2,2,64]{5,4,3,2,1,0:T(2,128)S(1)}, f32[3,4,2,2,2,64]{5,4,3,2,1,0:T(2,128)S(1)}, u32[]{:S(2)}, u32[]{:S(2)}) collective-permute-start(f32[3,4,2,2,2,64]{5,4,3,2,1,0:T(2,128)S(1)} %pad_maximum_fusion.1), channel_id=1, source_target_pairs={{0,16},{4,20},{8,24},{12,28},{16,0},{20,4},{24,8},{28,12},{1,17},{... | collective-permute-start | bytes 73736 | tf_op jit(solution)/shard_map/ppermute | solution.py:31
  247.6 3.9 %collective-permute-start.37 = (f32[3,4,2,2,2,64]{5,4,3,2,1,0:T(2,128)S(1)}, f32[3,4,2,2,2,64]{5,4,3,2,1,0:T(2,128)S(1)}, u32[]{:S(2)}, u32[]{:S(2)}) collective-permute-start(f32[3,4,2,2,2,64]{5,4,3,2,1,0:T(2,128)S(1)} %pad_maximum_fusion.4), channel_id=1, source_target_pairs={{0,3},{1,2},{2,1},{3,0},{4,7},{5,6},{6,5},{7,4},{8,11},{9,10},{10,... | collective-permute-start | bytes 73736 | tf_op jit(solution)/shard_map/ppermute | solution.py:270
  247.8 3.7 %collective-permute-start.35 = (f32[3,4,2,2,2,64]{5,4,3,2,1,0:T(2,128)S(1)}, f32[3,4,2,2,2,64]{5,4,3,2,1,0:T(2,128)S(1)}, u32[]{:S(2)}, u32[]{:S(2)}) collective-permute-start(f32[3,4,2,2,2,64]{5,4,3,2,1,0:T(2,128)S(1)} %pad_maximum_fusion.4), channel_id=1, source_target_pairs={{0,1},{1,0},{2,3},{3,2},{4,5},{5,4},{6,7},{7,6},{8,9},{9,8},{10,11... | collective-permute-start | bytes 73736 | tf_op jit(solution)/shard_map/ppermute | solution.py:59
  248.3 4.4 %collective-permute-start.36 = (f32[3,4,2,2,2,64]{5,4,3,2,1,0:T(2,128)S(1)}, f32[3,4,2,2,2,64]{5,4,3,2,1,0:T(2,128)S(1)}, u32[]{:S(2)}, u32[]{:S(2)}) collective-permute-start(f32[3,4,2,2,2,64]{5,4,3,2,1,0:T(2,128)S(1)} %pad_maximum_fusion.4), channel_id=1, source_target_pairs={{0,2},{1,3},{2,0},{3,1},{4,6},{5,7},{6,4},{7,5},{8,10},{9,11},{10,... | collective-permute-start | bytes 73736 | tf_op jit(solution)/shard_map/ppermute | solution.py:64
  253.7 7.0 %collective-permute-start.38 = (f32[48]{0:T(128)S(1)}, f32[48]{0:T(128)S(1)}, u32[]{:S(2)}, u32[]{:S(2)}) collective-permute-start(f32[48]{0:T(128)S(1)} %convolution_bitcast_fusion), channel_id=1, source_target_pairs={{0,4},{4,0},{8,12},{12,8},{16,20},{20,16},{24,28},{28,24},{1,5},{5... | collective-permute-start | bytes 584 | tf_op jit(solution)/shard_map/ppermute | solution.py:36
  (8 other events, 6.8 us)

commit v6 on v5

--- a/solution.py
+++ b/solution.py
@@ -252,9 +252,16 @@
 
 
 def split_kernel(head_ref, *out_refs):
-    size = out_refs[0].shape[0]
+    columns = head_ref.shape[1]
+    blocks, size, part = out_refs[0].shape
     for cut, out_ref in enumerate(out_refs):
-        out_ref[...] = head_ref[cut * size : (cut + 1) * size, :]
+        rows = slice(cut * size, (cut + 1) * size)
+        for block in range(blocks):
+            first = block * part
+            count = min(part, columns - first)
+            out_ref[block, :, :count] = head_ref[rows, first : first + count]
+            if count < part:
+                out_ref[block, :, count:] = jnp.zeros((size, part - count), out_ref.dtype)
 
 
 def cost(flops, moved, exps=0):
@@ -398,10 +405,11 @@
     cut_rows = head_rows // cuts
     head = pl.pallas_call(
         split_kernel,
-        grid=(CHAIN,),
-        in_specs=[pl.BlockSpec((head_rows, part), lambda j: (0, j))],
-        out_specs=[pl.BlockSpec((None, cut_rows, part), lambda j: (j, 0, 0))] * cuts,
+        grid=(1,),
+        in_specs=[whole(vocab_head_weight)],
+        out_specs=[pl.BlockSpec((CHAIN, cut_rows, part), lambda j: (0, 0, 0))] * cuts,
         out_shape=[jax.ShapeDtypeStruct((CHAIN, cut_rows, part), vocab_head_weight.dtype)] * cuts,
+        compiler_params=pltpu.CompilerParams(vmem_limit_bytes=32 * 2**20),
         cost_estimate=cost(0, 2 * vocab_head_weight.size * 2),
         name="split_head_columns",
     )(vocab_head_weight)

time: 262 us -> 262 us (level)
  Pallas kernels: 63.9 us -> 59 us
  local copies, waits for them, and re-layouts: 23.1 us -> 26.1 us
    pallas_call x1, Pallas kernels: 4.45 us -> 0.28 us  [shards(): pl.pallas_call(split_kernel, grid=(1,), in_specs=[whole(vocab_head_weight...]
    unnamed x65 -> x71, local copies, waits for them, and re-layouts: 12.4 us -> 15.4 us
  transfers between devices with their start and end apart: 41 -> 41, of which waited for: 21 -> 21; matrix products, arithmetic and copies ran while one was open for 9% -> 9% of each run, Pallas kernels for 22% -> 20%
where the time goes in v6:
time: 262 us; the launch traced here: 261 us
  waiting for transfers between devices  93.7 us (36%)
  starting transfers between devices  67.8 us (26%)
  Pallas kernels  59 us (23%)
  local copies, waits for them, and re-layouts  26.1 us (10%)
  other arithmetic  12 us (5%)
    ppermute x7, waiting for transfers between devices, to_partner(): lax.ppermute(x, 'seq', [(i, partner(i, side, block, count)) for i in rang...  33 us
    pallas_call x3, Pallas kernels, head_stats(): pl.pallas_call(functools.partial(head_kernel, count), in_specs=[pl.BlockS...  32.9 us
    ppermute x6, waiting for transfers between devices, along_x(): lax.ppermute(x, 'mp', [(i, (i + 2 * by) % count) for i in range(count)])  25.3 us
    ppermute x7, starting transfers between devices, to_partner(): lax.ppermute(x, 'seq', [(i, partner(i, side, block, count)) for i in rang...  23.3 us
    all_to_all x2, waiting for transfers between devices, shards(): lax.all_to_all(head[cut], 'seq', 0, 0, axis_index_groups=chain_groups())  18.9 us
    unnamed x71, local copies, waits for them, and re-layouts  15.4 us
    ppermute x10, starting transfers between devices, turn(): return lax.ppermute(x, 'seq', [(i, turned(i, by)) for i in range(count)])  14.9 us
    pallas_call x1, Pallas kernels, shards(): pl.pallas_call(functools.partial(project_kernel, len(prompts), hops == 1)...  14.8 us
  transfers between devices with their start and end apart: 41, of which 21 were waited for; matrix products, arithmetic and copies ran while one was open for 9% of the time, Pallas kernels for 20%

profile of v6, /device:TPU:0, one launch (start us, length us, event | category | flops | bytes accessed | tf_op | source)
XLA Modules:
  0.0 260.7 jit_solution(14115105469255738310)
XLA Ops:
  0.7 1.3 copy.114.refs_0_
  2.0 3.1 %collective-permute-start = (bf16[2,64,896]{2,1,0:T(8,128)(2,1)S(1)}, bf16[2,64,896]{2,1,0:T(8,128)(2,1)S(1)}, u32[]{:S(2)}, u32[]{:S(2)}) collective-permute-start(bf16[2,64,896]{2,1,0:T(8,128)(2,1)S(1)} %copy.114.refs_0_), channel_id=1, source_target_pairs={{0,8},{4,12},{8,0},{12,4},{16,24},{20,28},{24,16},{28,20},{1,9},{5... | collective-permute-start | bytes 688136 | tf_op jit(solution)/shard_map/ppermute | solution.py:31
  5.1 1.5 collective-permute-start.1
  6.6 2.6 collective-permute-start.3
  11.8 1.0 copy.92
  12.7 1.0 copy.93
  14.8 4.6 %local_tokens.1 = (f32[2,256,896]{2,1,0:T(8,128)S(1)}, bf16[2,80,896]{2,1,0:T(8,128)(2,1)S(1)}, f32[2,256,14]{2,1,0:T(8,128)S(1)}) custom-call(bf16[2,256,896]{2,1,0:T(8,128)(2,1)S(1)} %copy-done.11, bf16[2,256,128]{2,1,0:T(8,128)(2,1)S(1)} %pad_maximum_fusion.both_ref.refs_9_, f32[2,256,14]{2,1,0:T(8,128)S(1)} %copy.95.step_ref, f32[2,1,14]{2,1,0:T(1,128)S(1)} %bitcast.230, ...), custom_call_target="tpu_custom_call" | custom-call | flops 1000000000 | bytes 8388608 | tf_op jit(solution)/shard_map/local_tokens/pallas_call | solution.py:355
  19.4 1.2 copy-done.3
  21.4 4.1 %collective-permute-start.5 = (bf16[2,80,896]{2,1,0:T(8,128)(2,1)S(1)}, bf16[2,80,896]{2,1,0:T(8,128)(2,1)S(1)}, u32[]{:S(2)}, u32[]{:S(2)}) collective-permute-start(bf16[2,80,896]{2,1,0:T(8,128)(2,1)S(1)} %get-tuple-element.42), channel_id=1, source_target_pairs={{0,4},{4,8},{8,12},{12,16},{16,20},{20,24},{24,28},{1,5},{5,9},{9,... | collective-permute-start | bytes 860168 | tf_op jit(solution)/shard_map/ppermute | solution.py:390
  25.9 1.3 copy-done.4
  27.1 1.3 copy-done.5
  28.4 3.3 %collective-permute-done.6.refs_6_ = bf16[2,64,896]{2,1,0:T(8,128)(2,1)S(1)} collective-permute-done((bf16[2,64,896]{2,1,0:T(8,128)(2,1)S(1)}, bf16[2,64,896]{2,1,0:T(8,128)(2,1)S(1)}, u32[]{:S(2)}, u32[]{:S(2)}) %collective-permute-start.6) | collective-permute-done | bytes 229408 | tf_op jit(solution)/shard_map/ppermute | solution.py:31
  32.5 5.5 %all-to-all-start = ((bf16[4,224,1024]{2,1,0:T(8,128)(2,1)}), bf16[4,224,1024]{2,1,0:T(8,128)(2,1)S(1)}, u32[]{:S(2)}, u32[]{:S(2)}) async-start(bf16[4,224,1024]{2,1,0:T(8,128)(2,1)} %copy-done.5), calls=%async_computation | async-start | bytes 3670016 | tf_op jit(solution)/shard_map/all_to_all | solution.py:418
  39.5 3.4 %collective-permute-start.4 = (bf16[2,64,896]{2,1,0:T(8,128)(2,1)S(1)}, bf16[2,64,896]{2,1,0:T(8,128)(2,1)S(1)}, u32[]{:S(2)}, u32[]{:S(2)}) collective-permute-start(bf16[2,64,896]{2,1,0:T(8,128)(2,1)S(1)} %collective-permute-done.3.refs_4_), channel_id=1, source_target_pairs={{0,4},{4,0},{8,12},{12,8},{16,20},{20,16},{24,28},{28,24},{1,5},{5... | collective-permute-start | bytes 688136 | tf_op jit(solution)/shard_map/ppermute | solution.py:36
  43.0 2.0 collective-permute-start.7
  45.6 3.8 %collective-permute-done.4.refs_5_ = bf16[2,64,896]{2,1,0:T(8,128)(2,1)S(1)} collective-permute-done((bf16[2,64,896]{2,1,0:T(8,128)(2,1)S(1)}, bf16[2,64,896]{2,1,0:T(8,128)(2,1)S(1)}, u32[]{:S(2)}, u32[]{:S(2)}) %collective-permute-start.4) | collective-permute-done | bytes 229408 | tf_op jit(solution)/shard_map/ppermute | solution.py:36
  49.4 4.4 %collective-permute-done.2.refs_3_ = bf16[2,64,896]{2,1,0:T(8,128)(2,1)S(1)} collective-permute-done((bf16[2,64,896]{2,1,0:T(8,128)(2,1)S(1)}, bf16[2,64,896]{2,1,0:T(8,128)(2,1)S(1)}, u32[]{:S(2)}, u32[]{:S(2)}) %collective-permute-start.2) | collective-permute-done | bytes 229408 | tf_op jit(solution)/shard_map/ppermute | solution.py:36
  53.8 2.5 collective-permute-done.7.refs_7_
  57.0 14.8 %gate_and_project.1 = (bf16[256,3584]{1,0:T(8,128)(2,1)}, bf16[256,3584]{1,0:T(8,128)(2,1)}) custom-call(s32[4]{0:T(128)} %fusion.45.order_ref, bf16[2,64,896]{2,1,0:T(8,128)(2,1)} %copy-done.17, bf16[2,64,896]{2,1,0:T(8,128)(2,1)} %copy-done.20, bf16[2,64,896]{2,1,0:T(8,128)(2,1)} %copy-done.19, bf16[2,64,896]{2,1,0:T(8,128)(2,1)} %copy-done.24, ...), custom_call_target="tpu_custom_call" | custom-call | flops 3288334336 | bytes 12845056 | tf_op jit(solution)/shard_map/gate_and_project/pallas_call | solution.py:443
  71.7 5.1 %all-to-all-done.refs_0_ = bf16[4,224,1024]{2,1,0:T(8,128)(2,1)S(1)} async-done(((bf16[4,224,1024]{2,1,0:T(8,128)(2,1)}), bf16[4,224,1024]{2,1,0:T(8,128)(2,1)S(1)}, u32[]{:S(2)}, u32[]{:S(2)}) %all-to-all-start) | async-done | bytes 1835040 | tf_op jit(solution)/shard_map/all_to_all | solution.py:418
  76.8 4.4 %all-to-all-start.1 = ((bf16[4,224,1024]{2,1,0:T(8,128)(2,1)}), bf16[4,224,1024]{2,1,0:T(8,128)(2,1)}, u32[]{:S(2)}, u32[]{:S(2)}) async-start(bf16[4,224,1024]{2,1,0:T(8,128)(2,1)} %copy-done.4), calls=%async_computation.1 | async-start | bytes 3670016 | tf_op jit(solution)/shard_map/all_to_all | solution.py:418
  81.2 2.7 %add_convert_fusion = bf16[128,3584]{1,0:T(8,128)(2,1)} fusion(bf16[256,3584]{1,0:T(8,128)(2,1)} %collective-permute-done.8.refs_2_, bf16[256,3584]{1,0:T(8,128)(2,1)} %get-tuple-element.49.refs_1_), kind=kLoop, calls=%fused_computation.1 | loop fusion | flops 1835008 | bytes 2752512 | tf_op jit(solution)/shard_map/convert_element_type | solution.py:478
  83.9 1.5 collective-permute-start.9
  85.4 5.4 %collective-permute-start.14 = (bf16[4,224,1024]{2,1,0:T(8,128)(2,1)S(1)}, bf16[4,224,1024]{2,1,0:T(8,128)(2,1)}, u32[]{:S(2)}, u32[]{:S(2)}) collective-permute-start(bf16[4,224,1024]{2,1,0:T(8,128)(2,1)S(1)} %all-to-all-done.refs_0_), channel_id=1, source_target_pairs={{0,4},{4,0},{8,12},{12,8},{16,20},{20,16},{24,28},{28,24},{1,5},{5... | collective-permute-start | bytes 5505032 | tf_op jit(solution)/shard_map/ppermute | solution.py:36
  90.8 2.0 collective-permute-start.10
  92.8 2.4 collective-permute-start.11
  95.2 1.8 dynamic-slice_bitcast_fusion
  97.2 9.7 %collective-permute-done.9.refs_3_ = bf16[128,3584]{1,0:T(8,128)(2,1)S(1)} collective-permute-done((bf16[128,3584]{1,0:T(8,128)(2,1)}, bf16[128,3584]{1,0:T(8,128)(2,1)S(1)}, u32[]{:S(2)}, u32[]{:S(2)}) %collective-permute-start.9) | collective-permute-done | bytes 917536 | tf_op jit(solution)/shard_map/ppermute | solution.py:64
  106.9 1.0 copy-done.7
  107.9 1.2 copy-done.8
  109.1 2.1 add_and_norm.1.refs_0_
  111.1 13.8 %all-to-all-done.1.refs_2_ = bf16[4,224,1024]{2,1,0:T(8,128)(2,1)} async-done(((bf16[4,224,1024]{2,1,0:T(8,128)(2,1)}), bf16[4,224,1024]{2,1,0:T(8,128)(2,1)}, u32[]{:S(2)}, u32[]{:S(2)}) %all-to-all-start.1) | async-done | bytes 1835040 | tf_op jit(solution)/shard_map/all_to_all | solution.py:418
  125.0 1.6 collective-permute-start.13
  127.0 1.6 collective-permute-start.16
  128.5 5.4 %collective-permute-start.18 = (bf16[4,224,1024]{2,1,0:T(8,128)(2,1)}, bf16[4,224,1024]{2,1,0:T(8,128)(2,1)}, u32[]{:S(2)}, u32[]{:S(2)}) collective-permute-start(bf16[4,224,1024]{2,1,0:T(8,128)(2,1)} %all-to-all-done.1.refs_2_), channel_id=1, source_target_pairs={{0,4},{4,0},{8,12},{12,8},{16,20},{20,16},{24,28},{28,24},{1,5},{5... | collective-permute-start | bytes 5505032 | tf_op jit(solution)/shard_map/ppermute | solution.py:36
  133.9 13.0 %collective-permute-done.13.refs_1_ = bf16[128,3584]{1,0:T(8,128)(2,1)S(1)} collective-permute-done((bf16[128,3584]{1,0:T(8,128)(2,1)S(1)}, bf16[128,3584]{1,0:T(8,128)(2,1)S(1)}, u32[]{:S(2)}, u32[]{:S(2)}) %collective-permute-start.13) | collective-permute-done | bytes 917536 | tf_op jit(solution)/shard_map/ppermute | solution.py:64
  147.0 1.3 collective-permute-done.15.refs_0_
  148.3 1.1 collective-permute-start.17
  149.4 1.3 collective-permute-start.19
  150.7 1.6 collective-permute-start.20
  152.4 21.4 %collective-permute-done.18.refs_3_ = bf16[4,224,1024]{2,1,0:T(8,128)(2,1)} collective-permute-done((bf16[4,224,1024]{2,1,0:T(8,128)(2,1)}, bf16[4,224,1024]{2,1,0:T(8,128)(2,1)}, u32[]{:S(2)}, u32[]{:S(2)}) %collective-permute-start.18) | collective-permute-done | bytes 1835040 | tf_op jit(solution)/shard_map/ppermute | solution.py:36
  173.7 2.2 broadcast_select_fusion.1.refs_4_
  176.5 1.3 collective-permute-start.24
  180.6 4.5 %place_head_rows.1.refs_4_.refs_10_.refs_2_ = bf16[3584,1024]{1,0:T(8,128)(2,1)S(1)} custom-call(s32[16]{0:T(128)S(1)} %stack.195.first_ref, bf16[4,224,1024]{2,1,0:T(8,128)(2,1)S(1)} %all-to-all-done.refs_0_, bf16[4,224,1024]{2,1,0:T(8,128)(2,1)} %collective-permute-done.14.refs_1_, bf16[4,224,1024]{2,1,0:T(8,128)(2,1)} %all-to-all-done.1.refs_2_, ...), custom_call_target="tpu_custom_call" | custom-call | bytes 14680064 | tf_op jit(solution)/shard_map/place_head_rows/pallas_call | solution.py:523
  185.1 2.9 %copy-done = bf16[3584,1024]{1,0:T(8,128)(2,1)} copy-done((bf16[3584,1024]{1,0:T(8,128)(2,1)}, bf16[3584,1024]{1,0:T(8,128)(2,1)S(1)}, u32[]{:S(2)}) %copy-start) | copy-done | bytes 7340056
  188.3 9.2 %head_stats.3 = f32[8,512]{1,0:T(8,128)} custom-call(s32[2]{0:T(128)} %pad_add_fusion.3.limit_ref, bf16[128,3584]{1,0:T(8,128)(2,1)} %copy-done.6, bf16[128,3584]{1,0:T(8,128)(2,1)} %copy-done.32, bf16[128,3584]{1,0:T(8,128)(2,1)} %collective-permute-done.22.refs_2_, bf16[128,3584]{1,0:T(8,128)(2,1)} %collective-permute-done.23.refs_3_, ...), custom_call_target="tpu_custom_call" | custom-call | flops 3758096384 | bytes 11010048 | tf_op jit(solution)/shard_map/head_stats/pallas_call | solution.py:539
  199.0 2.1 collective-permute-done.24
  201.2 1.3 broadcast_select_fusion.refs_8_
  203.2 1.5 collective-permute-start.25
  204.8 1.1 copy.151
  206.6 17.0 %head_stats.4 = f32[8,1280]{1,0:T(8,128)} custom-call(s32[2]{0:T(128)} %pad_add_fusion.3.limit_ref, bf16[128,3584]{1,0:T(8,128)(2,1)} %collective-permute-done.15.refs_0_, bf16[128,3584]{1,0:T(8,128)(2,1)} %collective-permute-done.17.refs_1_, bf16[128,3584]{1,0:T(8,128)(2,1)} %collective-permute-done.26.refs_2_, ...), custom_call_target="tpu_custom_call" | custom-call | flops 9395240960 | bytes 16515072 | tf_op jit(solution)/shard_map/head_stats/pallas_call | solution.py:539
  224.6 1.0 collective-permute-done.25.refs_0_
  226.7 1.4 collective-permute-done.31.refs_1_
  228.1 0.9 copy-done.16
  229.0 6.6 %head_stats.5 = f32[8,256]{1,0:T(8,128)} custom-call(s32[2]{0:T(128)} %pad_add_fusion.3.limit_ref, bf16[128,3584]{1,0:T(8,128)(2,1)} %copy-done.15, bf16[128,3584]{1,0:T(8,128)(2,1)} %copy-done.16, bf16[3584,1024]{1,0:T(8,128)(2,1)} %copy-done, s32[256,1]{1,0:T(8,128)} %copy.110.refs_3_), custom_call_target="tpu_custom_call" | custom-call | flops 1879048192 | bytes 9175040 | tf_op jit(solution)/shard_map/head_stats/pallas_call | solution.py:539
  236.5 2.9 %collective-permute-start.32 = (f32[3,4,2,2,2,64]{5,4,3,2,1,0:T(2,128)S(1)}, f32[3,4,2,2,2,64]{5,4,3,2,1,0:T(2,128)S(1)}, u32[]{:S(2)}, u32[]{:S(2)}) collective-permute-start(f32[3,4,2,2,2,64]{5,4,3,2,1,0:T(2,128)S(1)} %pad_maximum_fusion.1), channel_id=1, source_target_pairs={{0,8},{4,12},{8,0},{12,4},{16,24},{20,28},{24,16},{28,20},{1,9},{5... | collective-permute-start | bytes 73736 | tf_op jit(solution)/shard_map/ppermute | solution.py:31
  239.5 1.5 collective-permute-start.34
  241.5 3.9 %collective-permute-done.34 = f32[3,4,2,2,2,64]{5,4,3,2,1,0:T(2,128)S(1)} collective-permute-done((f32[3,4,2,2,2,64]{5,4,3,2,1,0:T(2,128)S(1)}, f32[3,4,2,2,2,64]{5,4,3,2,1,0:T(2,128)S(1)}, u32[]{:S(2)}, u32[]{:S(2)}) %collective-permute-start.34) | collective-permute-done | bytes 24608 | tf_op jit(solution)/shard_map/ppermute | solution.py:31
  245.4 1.4 collective-permute-done.33
  247.7 1.5 collective-permute-start.36
  249.2 1.7 collective-permute-done.37
  251.0 1.2 collective-permute-done.36
  253.1 5.5 %collective-permute-start.38 = (f32[48]{0:T(128)S(1)}, f32[48]{0:T(128)S(1)}, u32[]{:S(2)}, u32[]{:S(2)}) collective-permute-start(f32[48]{0:T(128)S(1)} %convolution_bitcast_fusion), channel_id=1, source_target_pairs={{0,4},{4,0},{8,12},{12,8},{16,20},{20,16},{24,28},{28,24},{1,5},{5... | collective-permute-start | bytes 584 | tf_op jit(solution)/shard_map/ppermute | solution.py:36
  259.2 1.0 collective-permute-done.38
  (179 shorter events, 21.8 us)
Async XLA Ops:
  0.6 14.1 %copy-start.11 = (bf16[2,256,896]{2,1,0:T(8,128)(2,1)S(1)}, bf16[2,256,896]{2,1,0:T(8,128)(2,1)}, u32[]{:S(2)}) copy-start(bf16[2,256,896]{2,1,0:T(8,128)(2,1)} %x_ref) | copy-start | bytes 2752516
  0.6 14.1 %copy-start.12 = (f32[2,14]{1,0:T(2,128)S(1)}, f32[2,14]{1,0:T(2,128)}, u32[]{:S(2)}) copy-start(f32[2,14]{1,0:T(2,128)} %param.29) | copy-start | bytes 340
  0.7 14.1 %copy-start.13 = (f32[2,14]{1,0:T(2,128)S(1)}, f32[2,14]{1,0:T(2,128)}, u32[]{:S(2)}) copy-start(f32[2,14]{1,0:T(2,128)} %param.30) | copy-start | bytes 340
  2.0 17.4 %copy-start.17 = (bf16[2,64,896]{2,1,0:T(8,128)(2,1)}, bf16[2,64,896]{2,1,0:T(8,128)(2,1)S(1)}, u32[]{:S(2)}) copy-start(bf16[2,64,896]{2,1,0:T(8,128)(2,1)S(1)} %copy.114.refs_0_) | copy-start | bytes 688132
  2.0 12.8 %collective-permute-start = (bf16[2,64,896]{2,1,0:T(8,128)(2,1)S(1)}, bf16[2,64,896]{2,1,0:T(8,128)(2,1)S(1)}, u32[]{:S(2)}, u32[]{:S(2)}) collective-permute-start(bf16[2,64,896]{2,1,0:T(8,128)(2,1)S(1)} %copy.114.refs_0_), channel_id=1, source_target_pairs={{0,8},{4,12},{8,0},{12,4},{16,24},{20,28},{24,16},{28,20},{1,9},{5... | collective-permute-start | bytes 688136 | tf_op jit(solution)/shard_map/ppermute | solution.py:31
  5.1 9.7 %collective-permute-start.1 = (bf16[2,64,896]{2,1,0:T(8,128)(2,1)S(1)}, bf16[2,64,896]{2,1,0:T(8,128)(2,1)S(1)}, u32[]{:S(2)}, u32[]{:S(2)}) collective-permute-start(bf16[2,64,896]{2,1,0:T(8,128)(2,1)S(1)} %copy.114.refs_0_), channel_id=1, source_target_pairs={{0,4},{4,0},{8,12},{12,8},{16,20},{20,16},{24,28},{28,24},{1,5},{5... | collective-permute-start | bytes 688136 | tf_op jit(solution)/shard_map/ppermute | solution.py:36
  6.6 18.9 %collective-permute-start.3 = (bf16[2,64,896]{2,1,0:T(8,128)(2,1)S(1)}, bf16[2,64,896]{2,1,0:T(8,128)(2,1)S(1)}, u32[]{:S(2)}, u32[]{:S(2)}) collective-permute-start(bf16[2,64,896]{2,1,0:T(8,128)(2,1)S(1)} %copy.114.refs_0_), channel_id=1, source_target_pairs={{0,16},{4,20},{8,24},{12,28},{16,0},{20,4},{24,8},{28,12},{1,17},{... | collective-permute-start | bytes 688136 | tf_op jit(solution)/shard_map/ppermute | solution.py:31
  14.7 4.7 %copy-start.9 = (bf16[2,256,128]{2,1,0:T(8,128)(2,1)}, bf16[2,256,128]{2,1,0:T(8,128)(2,1)S(1)}, u32[]{:S(2)}) copy-start(bf16[2,256,128]{2,1,0:T(8,128)(2,1)S(1)} %pad_maximum_fusion.both_ref.refs_9_) | copy-start | bytes 393220
  14.7 28.2 %copy-start.19 = (bf16[2,64,896]{2,1,0:T(8,128)(2,1)}, bf16[2,64,896]{2,1,0:T(8,128)(2,1)S(1)}, u32[]{:S(2)}) copy-start(bf16[2,64,896]{2,1,0:T(8,128)(2,1)S(1)} %collective-permute-done.refs_2_) | copy-start | bytes 688132
  14.8 4.6 %copy-start.20 = (bf16[2,64,896]{2,1,0:T(8,128)(2,1)}, bf16[2,64,896]{2,1,0:T(8,128)(2,1)S(1)}, u32[]{:S(2)}) copy-start(bf16[2,64,896]{2,1,0:T(8,128)(2,1)S(1)} %collective-permute-done.1.refs_1_) | copy-start | bytes 688132
  14.8 10.7 %copy-start.2 = (bf16[448,4000]{1,0:T(8,128)(2,1)S(1)}, bf16[448,4000]{1,0:T(8,128)(2,1)}, u32[]{:S(2)}) copy-start(bf16[448,4000]{1,0:T(8,128)(2,1)} %head_ref.1) | copy-start | bytes 10752004
  21.4 10.4 %collective-permute-start.5 = (bf16[2,80,896]{2,1,0:T(8,128)(2,1)S(1)}, bf16[2,80,896]{2,1,0:T(8,128)(2,1)S(1)}, u32[]{:S(2)}, u32[]{:S(2)}) collective-permute-start(bf16[2,80,896]{2,1,0:T(8,128)(2,1)S(1)} %get-tuple-element.42), channel_id=1, source_target_pairs={{0,4},{4,8},{8,12},{12,16},{16,20},{20,24},{24,28},{1,5},{5,9},{9,... | collective-permute-start | bytes 860168 | tf_op jit(solution)/shard_map/ppermute | solution.py:390
  25.5 14.0 %copy-start.21 = (bf16[2,64,896]{2,1,0:T(8,128)(2,1)}, bf16[2,64,896]{2,1,0:T(8,128)(2,1)S(1)}, u32[]{:S(2)}) copy-start(bf16[2,64,896]{2,1,0:T(8,128)(2,1)S(1)} %collective-permute-done.3.refs_4_) | copy-start | bytes 688132
  25.5 6.3 %collective-permute-start.6 = (bf16[2,64,896]{2,1,0:T(8,128)(2,1)S(1)}, bf16[2,64,896]{2,1,0:T(8,128)(2,1)S(1)}, u32[]{:S(2)}, u32[]{:S(2)}) collective-permute-start(bf16[2,64,896]{2,1,0:T(8,128)(2,1)S(1)} %collective-permute-done.3.refs_4_), channel_id=1, source_target_pairs={{0,8},{4,12},{8,0},{12,4},{16,24},{20,28},{24,16},{28,20},{1,9},{5... | collective-permute-start | bytes 688136 | tf_op jit(solution)/shard_map/ppermute | solution.py:31
  31.7 11.3 %copy-start.22 = (bf16[2,64,896]{2,1,0:T(8,128)(2,1)}, bf16[2,64,896]{2,1,0:T(8,128)(2,1)S(1)}, u32[]{:S(2)}) copy-start(bf16[2,64,896]{2,1,0:T(8,128)(2,1)S(1)} %collective-permute-done.6.refs_6_) | copy-start | bytes 688132
  31.7 7.0 %copy-start.29 = (s32[256]{0:T(256)S(1)}, s32[256]{0:T(256)}, u32[]{:S(2)}) copy-start(s32[256]{0:T(256)} %param.20) | copy-start | bytes 3076
  31.7 7.0 %copy-start.30 = (s32[256]{0:T(256)S(1)}, s32[256]{0:T(256)}, u32[]{:S(2)}) copy-start(s32[256]{0:T(256)} %param.19) | copy-start | bytes 3076
  32.5 44.3 %all-to-all-start = ((bf16[4,224,1024]{2,1,0:T(8,128)(2,1)}), bf16[4,224,1024]{2,1,0:T(8,128)(2,1)S(1)}, u32[]{:S(2)}, u32[]{:S(2)}) async-start(bf16[4,224,1024]{2,1,0:T(8,128)(2,1)} %copy-done.5), calls=%async_computation | async-start | bytes 3670016 | tf_op jit(solution)/shard_map/all_to_all | solution.py:418
  39.5 10.0 %collective-permute-start.4 = (bf16[2,64,896]{2,1,0:T(8,128)(2,1)S(1)}, bf16[2,64,896]{2,1,0:T(8,128)(2,1)S(1)}, u32[]{:S(2)}, u32[]{:S(2)}) collective-permute-start(bf16[2,64,896]{2,1,0:T(8,128)(2,1)S(1)} %collective-permute-done.3.refs_4_), channel_id=1, source_target_pairs={{0,4},{4,0},{8,12},{12,8},{16,20},{20,16},{24,28},{28,24},{1,5},{5... | collective-permute-start | bytes 688136 | tf_op jit(solution)/shard_map/ppermute | solution.py:36
  42.9 10.9 %collective-permute-start.2 = (bf16[2,64,896]{2,1,0:T(8,128)(2,1)S(1)}, bf16[2,64,896]{2,1,0:T(8,128)(2,1)S(1)}, u32[]{:S(2)}, u32[]{:S(2)}) collective-permute-start(bf16[2,64,896]{2,1,0:T(8,128)(2,1)S(1)} %collective-permute-done.refs_2_), channel_id=1, source_target_pairs={{0,4},{4,0},{8,12},{12,8},{16,20},{20,16},{24,28},{28,24},{1,5},{5... | collective-permute-start | bytes 688136 | tf_op jit(solution)/shard_map/ppermute | solution.py:36
  43.0 13.3 %collective-permute-start.7 = (bf16[2,64,896]{2,1,0:T(8,128)(2,1)S(1)}, bf16[2,64,896]{2,1,0:T(8,128)(2,1)S(1)}, u32[]{:S(2)}, u32[]{:S(2)}) collective-permute-start(bf16[2,64,896]{2,1,0:T(8,128)(2,1)S(1)} %collective-permute-done.6.refs_6_), channel_id=1, source_target_pairs={{0,4},{4,0},{8,12},{12,8},{16,20},{20,16},{24,28},{28,24},{1,5},{5... | collective-permute-start | bytes 688136 | tf_op jit(solution)/shard_map/ppermute | solution.py:36
  49.4 7.4 %copy-start.23 = (bf16[2,64,896]{2,1,0:T(8,128)(2,1)}, bf16[2,64,896]{2,1,0:T(8,128)(2,1)S(1)}, u32[]{:S(2)}) copy-start(bf16[2,64,896]{2,1,0:T(8,128)(2,1)S(1)} %collective-permute-done.4.refs_5_) | copy-start | bytes 688132
  53.8 3.1 %copy-start.24 = (bf16[2,64,896]{2,1,0:T(8,128)(2,1)}, bf16[2,64,896]{2,1,0:T(8,128)(2,1)S(1)}, u32[]{:S(2)}) copy-start(bf16[2,64,896]{2,1,0:T(8,128)(2,1)S(1)} %collective-permute-done.2.refs_3_) | copy-start | bytes 688132
  76.8 4.4 %collective-permute-start.8 = (bf16[256,3584]{1,0:T(8,128)(2,1)}, bf16[256,3584]{1,0:T(8,128)(2,1)}, u32[]{:S(2)}, u32[]{:S(2)}) collective-permute-start(bf16[256,3584]{1,0:T(8,128)(2,1)} %get-tuple-element.52), channel_id=1, source_target_pairs={{0,1},{1,0},{2,3},{3,2},{4,5},{5,4},{6,7},{7,6},{8,9},{9,8},{10,11... | collective-permute-start | bytes 5505032 | tf_op jit(solution)/shard_map/ppermute | solution.py:59
  76.8 48.1 %all-to-all-start.1 = ((bf16[4,224,1024]{2,1,0:T(8,128)(2,1)}), bf16[4,224,1024]{2,1,0:T(8,128)(2,1)}, u32[]{:S(2)}, u32[]{:S(2)}) async-start(bf16[4,224,1024]{2,1,0:T(8,128)(2,1)} %copy-done.4), calls=%async_computation.1 | async-start | bytes 3670016 | tf_op jit(solution)/shard_map/all_to_all | solution.py:418
  83.9 23.0 %collective-permute-start.9 = (bf16[128,3584]{1,0:T(8,128)(2,1)}, bf16[128,3584]{1,0:T(8,128)(2,1)S(1)}, u32[]{:S(2)}, u32[]{:S(2)}) collective-permute-start(bf16[128,3584]{1,0:T(8,128)(2,1)} %add_convert_fusion), channel_id=1, source_target_pairs={{0,2},{1,3},{2,0},{3,1},{4,6},{5,7},{6,4},{7,5},{8,10},{9,11},{10,... | collective-permute-start | bytes 2752520 | tf_op jit(solution)/shard_map/ppermute | solution.py:64
  85.4 48.5 %collective-permute-start.14 = (bf16[4,224,1024]{2,1,0:T(8,128)(2,1)S(1)}, bf16[4,224,1024]{2,1,0:T(8,128)(2,1)}, u32[]{:S(2)}, u32[]{:S(2)}) collective-permute-start(bf16[4,224,1024]{2,1,0:T(8,128)(2,1)S(1)} %all-to-all-done.refs_0_), channel_id=1, source_target_pairs={{0,4},{4,0},{8,12},{12,8},{16,20},{20,16},{24,28},{28,24},{1,5},{5... | collective-permute-start | bytes 5505032 | tf_op jit(solution)/shard_map/ppermute | solution.py:36
  90.8 6.3 %copy-start.27 = (f32[3584]{0:T(1024)S(1)}, f32[3584]{0:T(1024)}, u32[]{:S(2)}) copy-start(f32[3584]{0:T(1024)} %param.36) | copy-start | bytes 43012
  90.8 17.1 %copy-start.1 = (bf16[256,3584]{1,0:T(8,128)(2,1)S(1)}, bf16[256,3584]{1,0:T(8,128)(2,1)}, u32[]{:S(2)}) copy-start(bf16[256,3584]{1,0:T(8,128)(2,1)} %get-tuple-element.49.refs_1_) | copy-start | bytes 5505028
  90.8 34.1 %collective-permute-start.10 = (s32[2,256]{1,0:T(2,128)S(1)}, s32[2,256]{1,0:T(2,128)S(1)}, u32[]{:S(2)}, u32[]{:S(2)}) collective-permute-start(s32[2,256]{1,0:T(2,128)S(1)} %pad_add_fusion.1), channel_id=1, source_target_pairs={{0,8},{4,12},{8,0},{12,4},{16,24},{20,28},{24,16},{28,20},{1,9},{5... | collective-permute-start | bytes 6152 | tf_op jit(solution)/shard_map/ppermute | solution.py:31
  92.8 32.2 %collective-permute-start.11 = (s32[2,256]{1,0:T(2,128)S(1)}, s32[2,256]{1,0:T(2,128)S(1)}, u32[]{:S(2)}, u32[]{:S(2)}) collective-permute-start(s32[2,256]{1,0:T(2,128)S(1)} %pad_add_fusion.1), channel_id=1, source_target_pairs={{0,16},{4,20},{8,24},{12,28},{16,0},{20,4},{24,8},{28,12},{1,17},{... | collective-permute-start | bytes 6152 | tf_op jit(solution)/shard_map/ppermute | solution.py:31
  95.2 29.8 %collective-permute-start.12 = (s32[2,256]{1,0:T(2,128)S(1)}, s32[2,256]{1,0:T(2,128)S(1)}, u32[]{:S(2)}, u32[]{:S(2)}) collective-permute-start(s32[2,256]{1,0:T(2,128)S(1)} %pad_add_fusion.1), channel_id=1, source_target_pairs={{0,24},{4,28},{8,16},{12,20},{16,8},{20,12},{24,0},{28,4},{1,25},{... | collective-permute-start | bytes 6152 | tf_op jit(solution)/shard_map/ppermute | solution.py:31
  111.1 74.0 %copy-start.6 = (bf16[128,3584]{1,0:T(8,128)(2,1)}, bf16[128,3584]{1,0:T(8,128)(2,1)S(1)}, u32[]{:S(2)}) copy-start(bf16[128,3584]{1,0:T(8,128)(2,1)S(1)} %add_and_norm.1.refs_0_) | copy-start | bytes 2752516
  125.0 22.0 %collective-permute-start.13 = (bf16[128,3584]{1,0:T(8,128)(2,1)S(1)}, bf16[128,3584]{1,0:T(8,128)(2,1)S(1)}, u32[]{:S(2)}, u32[]{:S(2)}) collective-permute-start(bf16[128,3584]{1,0:T(8,128)(2,1)S(1)} %add_and_norm.1.refs_0_), channel_id=1, source_target_pairs={{0,2},{1,3},{2,0},{3,1},{4,6},{5,7},{6,4},{7,5},{8,10},{9,11},{10,... | collective-permute-start | bytes 2752520 | tf_op jit(solution)/shard_map/ppermute | solution.py:64
  126.5 21.8 %collective-permute-start.15 = (bf16[128,3584]{1,0:T(8,128)(2,1)S(1)}, bf16[128,3584]{1,0:T(8,128)(2,1)}, u32[]{:S(2)}, u32[]{:S(2)}) collective-permute-start(bf16[128,3584]{1,0:T(8,128)(2,1)S(1)} %add_and_norm.1.refs_0_), channel_id=1, source_target_pairs={{0,8},{4,12},{8,0},{12,4},{16,24},{20,28},{24,16},{28,20},{1,9},{5... | collective-permute-start | bytes 2752520 | tf_op jit(solution)/shard_map/ppermute | solution.py:31
  127.0 21.3 %collective-permute-start.16 = (bf16[128,3584]{1,0:T(8,128)(2,1)S(1)}, bf16[128,3584]{1,0:T(8,128)(2,1)}, u32[]{:S(2)}, u32[]{:S(2)}) collective-permute-start(bf16[128,3584]{1,0:T(8,128)(2,1)S(1)} %add_and_norm.1.refs_0_), channel_id=1, source_target_pairs={{8,16},{12,20},{16,8},{20,12},{9,17},{13,21},{17,9},{21,13},{10,18... | collective-permute-start | bytes 2752520 | tf_op jit(solution)/shard_map/ppermute | solution.py:47
  128.5 45.2 %collective-permute-start.18 = (bf16[4,224,1024]{2,1,0:T(8,128)(2,1)}, bf16[4,224,1024]{2,1,0:T(8,128)(2,1)}, u32[]{:S(2)}, u32[]{:S(2)}) collective-permute-start(bf16[4,224,1024]{2,1,0:T(8,128)(2,1)} %all-to-all-done.1.refs_2_), channel_id=1, source_target_pairs={{0,4},{4,0},{8,12},{12,8},{16,20},{20,16},{24,28},{28,24},{1,5},{5... | collective-permute-start | bytes 5505032 | tf_op jit(solution)/shard_map/ppermute | solution.py:36
  148.3 25.4 %collective-permute-start.17 = (bf16[128,3584]{1,0:T(8,128)(2,1)}, bf16[128,3584]{1,0:T(8,128)(2,1)}, u32[]{:S(2)}, u32[]{:S(2)}) collective-permute-start(bf16[128,3584]{1,0:T(8,128)(2,1)} %collective-permute-done.15.refs_0_), channel_id=1, source_target_pairs={{0,2},{1,3},{2,0},{3,1},{4,6},{5,7},{6,4},{7,5},{8,10},{9,11},{10,... | collective-permute-start | bytes 2752520 | tf_op jit(solution)/shard_map/ppermute | solution.py:64
  149.4 24.3 %collective-permute-start.19 = (bf16[128,3584]{1,0:T(8,128)(2,1)}, bf16[128,3584]{1,0:T(8,128)(2,1)}, u32[]{:S(2)}, u32[]{:S(2)}) collective-permute-start(bf16[128,3584]{1,0:T(8,128)(2,1)} %collective-permute-done.16), channel_id=1, source_target_pairs={{8,0},{12,4},{16,24},{20,28},{9,1},{13,5},{17,25},{21,29},{10,2},{... | collective-permute-start | bytes 2752520 | tf_op jit(solution)/shard_map/ppermute | solution.py:47
  150.7 23.0 %collective-permute-start.20 = (bf16[128,3584]{1,0:T(8,128)(2,1)}, bf16[128,3584]{1,0:T(8,128)(2,1)}, u32[]{:S(2)}, u32[]{:S(2)}) collective-permute-start(bf16[128,3584]{1,0:T(8,128)(2,1)} %collective-permute-done.15.refs_0_), channel_id=1, source_target_pairs={{8,16},{12,20},{16,8},{20,12},{9,17},{13,21},{17,9},{21,13},{10,18... | collective-permute-start | bytes 2752520 | tf_op jit(solution)/shard_map/ppermute | solution.py:47
  152.4 35.7 %collective-permute-start.22 = (bf16[128,3584]{1,0:T(8,128)(2,1)S(1)}, bf16[128,3584]{1,0:T(8,128)(2,1)}, u32[]{:S(2)}, u32[]{:S(2)}) collective-permute-start(bf16[128,3584]{1,0:T(8,128)(2,1)S(1)} %add_and_norm.1.refs_0_), channel_id=1, source_target_pairs={{0,1},{1,0},{2,3},{3,2},{4,5},{5,4},{6,7},{7,6},{8,9},{9,8},{10,11... | collective-permute-start | bytes 2752520 | tf_op jit(solution)/shard_map/ppermute | solution.py:59
  173.7 14.6 %collective-permute-start.23 = (bf16[128,3584]{1,0:T(8,128)(2,1)}, bf16[128,3584]{1,0:T(8,128)(2,1)}, u32[]{:S(2)}, u32[]{:S(2)}) collective-permute-start(bf16[128,3584]{1,0:T(8,128)(2,1)} %copy-done.32), channel_id=1, source_target_pairs={{0,1},{1,0},{2,3},{3,2},{4,5},{5,4},{6,7},{7,6},{8,9},{9,8},{10,11... | collective-permute-start | bytes 2752520 | tf_op jit(solution)/shard_map/ppermute | solution.py:59
  175.9 23.1 %collective-permute-start.21 = (bf16[128,3584]{1,0:T(8,128)(2,1)}, bf16[128,3584]{1,0:T(8,128)(2,1)}, u32[]{:S(2)}, u32[]{:S(2)}) collective-permute-start(bf16[128,3584]{1,0:T(8,128)(2,1)} %broadcast_select_fusion.1.refs_4_), channel_id=1, source_target_pairs={{0,2},{1,3},{2,0},{3,1},{4,6},{5,7},{6,4},{7,5},{8,10},{9,11},{10,... | collective-permute-start | bytes 2752520 | tf_op jit(solution)/shard_map/ppermute | solution.py:64
  176.5 24.7 %collective-permute-start.24 = (bf16[128,3584]{1,0:T(8,128)(2,1)}, bf16[128,3584]{1,0:T(8,128)(2,1)}, u32[]{:S(2)}, u32[]{:S(2)}) collective-permute-start(bf16[128,3584]{1,0:T(8,128)(2,1)} %collective-permute-done.20), channel_id=1, source_target_pairs={{8,0},{12,4},{16,24},{20,28},{9,1},{13,5},{17,25},{21,29},{10,2},{... | collective-permute-start | bytes 2752520 | tf_op jit(solution)/shard_map/ppermute | solution.py:47
  180.4 22.8 %collective-permute-start.26 = (bf16[128,3584]{1,0:T(8,128)(2,1)}, bf16[128,3584]{1,0:T(8,128)(2,1)}, u32[]{:S(2)}, u32[]{:S(2)}) collective-permute-start(bf16[128,3584]{1,0:T(8,128)(2,1)} %collective-permute-done.15.refs_0_), channel_id=1, source_target_pairs={{0,1},{1,0},{2,3},{3,2},{4,5},{5,4},{6,7},{7,6},{8,9},{9,8},{10,11... | collective-permute-start | bytes 2752520 | tf_op jit(solution)/shard_map/ppermute | solution.py:59
  185.1 2.9 %copy-start = (bf16[3584,1024]{1,0:T(8,128)(2,1)}, bf16[3584,1024]{1,0:T(8,128)(2,1)S(1)}, u32[]{:S(2)}) copy-start(bf16[3584,1024]{1,0:T(8,128)(2,1)S(1)} %place_head_rows.1.refs_4_.refs_10_.refs_2_) | copy-start | bytes 22020100
  188.1 17.9 %collective-permute-start.28 = (bf16[128,3584]{1,0:T(8,128)(2,1)}, bf16[128,3584]{1,0:T(8,128)(2,1)}, u32[]{:S(2)}, u32[]{:S(2)}) collective-permute-start(bf16[128,3584]{1,0:T(8,128)(2,1)} %broadcast_select_fusion.1.refs_4_), channel_id=1, source_target_pairs={{0,1},{1,0},{2,3},{3,2},{4,5},{5,4},{6,7},{7,6},{8,9},{9,8},{10,11... | collective-permute-start | bytes 2752520 | tf_op jit(solution)/shard_map/ppermute | solution.py:59
  198.4 28.3 %copy-start.26 = (f32[8,4,2,64]{3,2,1,0:T(2,128)}, f32[8,4,2,64]{3,2,1,0:T(2,128)S(1)}, u32[]{:S(2)}) copy-start(f32[8,4,2,64]{3,2,1,0:T(2,128)S(1)} %reshape.368) | copy-start | bytes 49156
  198.4 7.5 %collective-permute-start.27 = (bf16[128,3584]{1,0:T(8,128)(2,1)}, bf16[128,3584]{1,0:T(8,128)(2,1)}, u32[]{:S(2)}, u32[]{:S(2)}) collective-permute-start(bf16[128,3584]{1,0:T(8,128)(2,1)} %collective-permute-done.17.refs_1_), channel_id=1, source_target_pairs={{0,1},{1,0},{2,3},{3,2},{4,5},{5,4},{6,7},{7,6},{8,9},{9,8},{10,11... | collective-permute-start | bytes 2752520 | tf_op jit(solution)/shard_map/ppermute | solution.py:59
  202.4 4.2 %copy-start.14 = (bf16[128,3584]{1,0:T(8,128)(2,1)}, bf16[128,3584]{1,0:T(8,128)(2,1)S(1)}, u32[]{:S(2)}) copy-start(bf16[128,3584]{1,0:T(8,128)(2,1)S(1)} %broadcast_select_fusion.refs_8_) | copy-start | bytes 2752516
  202.4 3.5 %collective-permute-start.30 = (bf16[128,3584]{1,0:T(8,128)(2,1)S(1)}, bf16[128,3584]{1,0:T(8,128)(2,1)}, u32[]{:S(2)}, u32[]{:S(2)}) collective-permute-start(bf16[128,3584]{1,0:T(8,128)(2,1)S(1)} %broadcast_select_fusion.refs_8_), channel_id=1, source_target_pairs={{0,1},{1,0},{2,3},{3,2},{4,5},{5,4},{6,7},{7,6},{8,9},{9,8},{10,11... | collective-permute-start | bytes 2752520 | tf_op jit(solution)/shard_map/ppermute | solution.py:59
  202.5 4.1 %collective-permute-start.29 = (bf16[128,3584]{1,0:T(8,128)(2,1)}, bf16[128,3584]{1,0:T(8,128)(2,1)}, u32[]{:S(2)}, u32[]{:S(2)}) collective-permute-start(bf16[128,3584]{1,0:T(8,128)(2,1)} %collective-permute-done.21.refs_5_), channel_id=1, source_target_pairs={{0,1},{1,0},{2,3},{3,2},{4,5},{5,4},{6,7},{7,6},{8,9},{9,8},{10,11... | collective-permute-start | bytes 2752520 | tf_op jit(solution)/shard_map/ppermute | solution.py:59
  203.2 22.4 %collective-permute-start.25 = (bf16[128,3584]{1,0:T(8,128)(2,1)S(1)}, bf16[128,3584]{1,0:T(8,128)(2,1)S(1)}, u32[]{:S(2)}, u32[]{:S(2)}) collective-permute-start(bf16[128,3584]{1,0:T(8,128)(2,1)S(1)} %broadcast_select_fusion.refs_8_), channel_id=1, source_target_pairs={{0,2},{1,3},{2,0},{3,1},{4,6},{5,7},{6,4},{7,5},{8,10},{9,11},{10,... | collective-permute-start | bytes 2752520 | tf_op jit(solution)/shard_map/ppermute | solution.py:64
  225.6 2.5 collective-permute-start.31
  226.6 9.8 %slice-start = ((f32[8,4,2,64]{3,2,1,0:T(2,128)}), f32[3,4,2,64]{3,2,1,0:T(2,128)S(1)}, s32[]{:S(2)}) async-start(f32[8,4,2,64]{3,2,1,0:T(2,128)} %copy-done.26), calls=%async_computation.2 | async-start | bytes 24576 | tf_op jit(solution)/shard_map/slice | solution.py:613
  226.6 25.9 %copy-start.28 = (s32[48]{0:T(128)S(1)}, s32[48]{0:T(128)}, u32[]{:S(2)}) copy-start(s32[48]{0:T(128)} %param.21) | copy-start | bytes 580
  235.6 24.5 %copy-start.31 = (s32[48]{0:T(128)S(1)}, s32[48]{0:T(128)}, u32[]{:S(2)}) copy-start(s32[48]{0:T(128)} %param.22) | copy-start | bytes 580
  236.5 5.0 %collective-permute-start.32 = (f32[3,4,2,2,2,64]{5,4,3,2,1,0:T(2,128)S(1)}, f32[3,4,2,2,2,64]{5,4,3,2,1,0:T(2,128)S(1)}, u32[]{:S(2)}, u32[]{:S(2)}) collective-permute-start(f32[3,4,2,2,2,64]{5,4,3,2,1,0:T(2,128)S(1)} %pad_maximum_fusion.1), channel_id=1, source_target_pairs={{0,8},{4,12},{8,0},{12,4},{16,24},{20,28},{24,16},{28,20},{1,9},{5... | collective-permute-start | bytes 73736 | tf_op jit(solution)/shard_map/ppermute | solution.py:31
  239.5 5.9 %collective-permute-start.34 = (f32[3,4,2,2,2,64]{5,4,3,2,1,0:T(2,128)S(1)}, f32[3,4,2,2,2,64]{5,4,3,2,1,0:T(2,128)S(1)}, u32[]{:S(2)}, u32[]{:S(2)}) collective-permute-start(f32[3,4,2,2,2,64]{5,4,3,2,1,0:T(2,128)S(1)} %pad_maximum_fusion.1), channel_id=1, source_target_pairs={{0,24},{4,28},{8,16},{12,20},{16,8},{20,12},{24,0},{28,4},{1,25},{... | collective-permute-start | bytes 73736 | tf_op jit(solution)/shard_map/ppermute | solution.py:31
  240.9 5.9 %collective-permute-start.33 = (f32[3,4,2,2,2,64]{5,4,3,2,1,0:T(2,128)S(1)}, f32[3,4,2,2,2,64]{5,4,3,2,1,0:T(2,128)S(1)}, u32[]{:S(2)}, u32[]{:S(2)}) collective-permute-start(f32[3,4,2,2,2,64]{5,4,3,2,1,0:T(2,128)S(1)} %pad_maximum_fusion.1), channel_id=1, source_target_pairs={{0,16},{4,20},{8,24},{12,28},{16,0},{20,4},{24,8},{28,12},{1,17},{... | collective-permute-start | bytes 73736 | tf_op jit(solution)/shard_map/ppermute | solution.py:31
  247.0 3.9 %collective-permute-start.37 = (f32[3,4,2,2,2,64]{5,4,3,2,1,0:T(2,128)S(1)}, f32[3,4,2,2,2,64]{5,4,3,2,1,0:T(2,128)S(1)}, u32[]{:S(2)}, u32[]{:S(2)}) collective-permute-start(f32[3,4,2,2,2,64]{5,4,3,2,1,0:T(2,128)S(1)} %pad_maximum_fusion.4), channel_id=1, source_target_pairs={{0,3},{1,2},{2,1},{3,0},{4,7},{5,6},{6,5},{7,4},{8,11},{9,10},{10,... | collective-permute-start | bytes 73736 | tf_op jit(solution)/shard_map/ppermute | solution.py:277
  247.2 3.7 %collective-permute-start.35 = (f32[3,4,2,2,2,64]{5,4,3,2,1,0:T(2,128)S(1)}, f32[3,4,2,2,2,64]{5,4,3,2,1,0:T(2,128)S(1)}, u32[]{:S(2)}, u32[]{:S(2)}) collective-permute-start(f32[3,4,2,2,2,64]{5,4,3,2,1,0:T(2,128)S(1)} %pad_maximum_fusion.4), channel_id=1, source_target_pairs={{0,1},{1,0},{2,3},{3,2},{4,5},{5,4},{6,7},{7,6},{8,9},{9,8},{10,11... | collective-permute-start | bytes 73736 | tf_op jit(solution)/shard_map/ppermute | solution.py:59
  247.7 4.4 %collective-permute-start.36 = (f32[3,4,2,2,2,64]{5,4,3,2,1,0:T(2,128)S(1)}, f32[3,4,2,2,2,64]{5,4,3,2,1,0:T(2,128)S(1)}, u32[]{:S(2)}, u32[]{:S(2)}) collective-permute-start(f32[3,4,2,2,2,64]{5,4,3,2,1,0:T(2,128)S(1)} %pad_maximum_fusion.4), channel_id=1, source_target_pairs={{0,2},{1,3},{2,0},{3,1},{4,6},{5,7},{6,4},{7,5},{8,10},{9,11},{10,... | collective-permute-start | bytes 73736 | tf_op jit(solution)/shard_map/ppermute | solution.py:64
  253.1 7.0 %collective-permute-start.38 = (f32[48]{0:T(128)S(1)}, f32[48]{0:T(128)S(1)}, u32[]{:S(2)}, u32[]{:S(2)}) collective-permute-start(f32[48]{0:T(128)S(1)} %convolution_bitcast_fusion), channel_id=1, source_target_pairs={{0,4},{4,0},{8,12},{12,8},{16,20},{20,16},{24,28},{28,24},{1,5},{5... | collective-permute-start | bytes 584 | tf_op jit(solution)/shard_map/ppermute | solution.py:36
  (11 other events, 12.9 us)
